TPU v7x, 32 devices: a whole 2x2x4 slice. The times are simulated.
32 devices in a mesh: grp: 1, head: 16 (over z, x, core), tile: 2 (over y).
Axes of the slice: x: 2, y: 2, z: 4, core: 2. Of those that a mesh axis runs over, the one named last changes fastest.
Arguments:
- attention: bfloat16 [144, 256, 256], P(('grp', 'head'), None, 'tile'), may hold values from 0 to 16, as said below
- proj_weight: bfloat16 [64, 144], replicated, may hold values from -0.5 to 0.5
- proj_bias: float32 [64], replicated, may hold values from -1.8 to 1.8
- conv_weight: bfloat16 [2, 2, 64, 64, 3, 3], replicated, may hold values from -0.25 to 0.25
- conv_bias: float32 [2, 2, 64], replicated, may hold values from -1.8 to 1.8
- out_weight: float32 [64], replicated, may hold values from -0.75 to 0.75
Outputs:
- logits: float32 [256, 256], P(('grp', 'head'), 'tile')
Inputs may be any that keep to these rules, and one draw needn't show every extreme that they name: `attention`: every entry is positive.
All inputs are finite; a program needn't handle non-finite values.
Results may differ from a plain program's by a relative error of at most 0.007.
Values may be sent and summed in bfloat16 or wider, within the bound.
No kernel may reach another device: no remote copies, remote signals or barrier semaphores. Data moves between devices by JAX's collectives and lax.ppermute only.
A program may use at most 128 MiB of HBM per device.

v0:
```python
import jax
import jax.numpy as jnp
from jax import lax
from jax.sharding import PartitionSpec as P


def extended(cells, sides, width):
    for axis, dim in sides:
        count = lax.axis_size(axis)
        ends = count - 1
        head = lax.slice_in_dim(cells, 0, width, axis=dim)
        tail = lax.slice_in_dim(cells, cells.shape[dim] - width, cells.shape[dim], axis=dim)
        cells = jnp.concatenate(
            [
                lax.ppermute(tail, axis, [(i, (i + 1) % count) for i in range(ends)]),
                cells,
                lax.ppermute(head, axis, [((i + 1) % count, i) for i in range(ends)]),
            ],
            axis=dim,
        )
    return cells


def convolve(padded, kernel, offsets):
    result = lax.conv_general_dilated(
        padded[None], kernel, (1, 1), "VALID", preferred_element_type=jnp.float32
    )[0]
    return result + offsets[:, None, None]


def with_edges(field):
    banded = extended(field, ((("head", "tile"), 1),), 1)
    return jnp.pad(banded, ((0, 0), (0, 0), (1, 1)))


def on_device(attention, proj_weight, proj_bias, conv_weight, conv_bias, out_weight):
    columns = attention.shape[2]
    offset = lax.axis_index("tile") * columns
    swapped = lax.all_to_all(attention, "tile", split_axis=1, concat_axis=2, tiled=True)
    mirror = jnp.swapaxes(swapped, 1, 2)
    symmetric = attention.astype(jnp.float32) + mirror.astype(jnp.float32)
    column_part = jnp.sum(symmetric, axis=1)
    rowsum = lax.all_gather(column_part, "tile", axis=1, tiled=True)
    grand_total = jnp.sum(rowsum, axis=1)
    symmetric = attention.astype(jnp.float32) + mirror.astype(jnp.float32)
    own_totals = lax.dynamic_slice_in_dim(rowsum, offset, columns, 1)
    corrected = (
        symmetric - rowsum[:, :, None] * own_totals[:, None, :] / grand_total[:, None, None]
    ).astype(jnp.bfloat16)
    grouped = lax.all_to_all(
        lax.all_to_all(corrected, "head", split_axis=1, concat_axis=0, tiled=True),
        "tile",
        split_axis=1,
        concat_axis=2,
        tiled=True,
    )
    stream = jnp.einsum("kc,crs->krs", proj_weight, grouped, preferred_element_type=jnp.float32)
    stream = (stream + proj_bias[:, None, None]).astype(jnp.bfloat16)
    for layer_index in range(conv_weight.shape[0]):
        hidden = jax.nn.elu(
            convolve(with_edges(stream), conv_weight[layer_index, 0], conv_bias[layer_index, 0])
        ).astype(jnp.bfloat16)
        update = convolve(
            with_edges(hidden), conv_weight[layer_index, 1], conv_bias[layer_index, 1]
        )
        stream = (stream.astype(jnp.float32) + update).astype(jnp.bfloat16)
    logits = jnp.einsum(
        "k,krs->rs", out_weight, stream.astype(jnp.float32), precision=lax.Precision.HIGHEST
    )
    logits = lax.all_to_all(
        logits.astype(jnp.bfloat16), "tile", split_axis=1, concat_axis=0, tiled=True
    ).astype(logits.dtype)
    return logits


def solution(mesh):
    return jax.shard_map(
        on_device,
        mesh=mesh,
        in_specs=(P(("grp", "head"), None, "tile"), P(), P(), P(), P(), P()),
        out_specs=P(("grp", "head"), "tile"),
        check_vma=False,
    )
```

profile of v0, /device:TPU:0, one launch (start us, length us, event | category | flops | bytes accessed | tf_op | source)
XLA Modules:
  0.0 138.3 jit_solution(11967543169565332876)
XLA Ops:
  0.0 2.5 %copy.55 = bf16[9,256,128]{2,0,1:T(8,128)(2,1)} copy(bf16[9,256,128]{2,1,0:T(8,128)(2,1)} %param.6) | data formatting | bytes 1179648 | tf_op args[0]
  2.5 4.2 %all-to-all-start = ((bf16[9,256,128]{2,0,1:T(8,128)(2,1)}), bf16[9,256,128]{2,0,1:T(8,128)(2,1)S(1)}, u32[]{:S(2)}, u32[]{:S(2)}) async-start(bf16[9,256,128]{2,0,1:T(8,128)(2,1)} %copy.55), calls=%async_computation | async-start | bytes 2097152 | tf_op jit(solution)/shard_map/all_to_all | solution.py:39
  6.7 14.4 %all-to-all-done = bf16[9,256,128]{2,0,1:T(8,128)(2,1)S(1)} async-done(((bf16[9,256,128]{2,0,1:T(8,128)(2,1)}), bf16[9,256,128]{2,0,1:T(8,128)(2,1)S(1)}, u32[]{:S(2)}, u32[]{:S(2)}) %all-to-all-start) | async-done | bytes 589856 | tf_op jit(solution)/shard_map/all_to_all | solution.py:39
  21.2 1.5 %convert_bitcast_fusion = f32[9,128,2,128]{3,0,1,2:T(8,128)} fusion(bf16[9,2,128,128]{3,0,2,1:T(8,128)(2,1)S(1)} %bitcast.140), kind=kLoop, calls=%fused_computation.5 | loop fusion | flops 294912 | bytes 1769472 | tf_op jit(solution)/shard_map/convert_element_type | solution.py:45
  22.6 2.6 %copy.57 = f32[9,128,2,128]{1,0,3,2:T(8,128)S(1)} copy(f32[9,128,2,128]{3,0,1,2:T(8,128)} %convert_bitcast_fusion) | data formatting | bytes 2359296 | tf_op jit(solution)/shard_map/convert_element_type | solution.py:45
  25.7 4.4 %all_gather.3 = f32[9,256]{1,0:T(8,128)S(1)} all-gather(f32[9,128]{1,0:T(8,128)S(1)} %fusion), channel_id=1, replica_groups=mesh['grp'=1,'head'=16,'tile'=2] {'tile'}, dimensions={1}, use_global_device_ids=true | all-gather | bytes 13824 | tf_op jit(solution)/shard_map/all_gather | solution.py:43
  30.3 1.1 subtract_convert_fusion
  31.4 30.8 %all_to_all.58 = bf16[9,256,128]{2,0,1:T(8,128)(2,1)S(1)} all-to-all(bf16[9,256,128]{2,0,1:T(8,128)(2,1)S(1)} %subtract_convert_fusion), channel_id=1, replica_groups=mesh['grp'=1,'head'=16,'tile'=2] {'head'}, dimensions={1} | all-to-all | bytes 1179648 | tf_op jit(solution)/shard_map/all_to_all | solution.py:51
  62.5 12.3 %all_to_all.59 = bf16[144,16,128]{2,0,1:T(8,128)(2,1)S(1)} all-to-all(bf16[144,16,128]{2,0,1:T(8,128)(2,1)S(1)} %copy.61), channel_id=1, replica_groups=mesh['grp'=1,'head'=16,'tile'=2] {'tile'}, dimensions={1} | all-to-all | bytes 1179648 | tf_op jit(solution)/shard_map/all_to_all | solution.py:50
  75.1 1.3 collective-permute-start.1
  76.4 4.5 %collective-permute-start = (bf16[64,1,256]{2,0,1:T(8,128)(2,1)S(1)}, bf16[64,1,256]{2,0,1:T(8,128)(2,1)S(1)}, u32[]{:S(2)}, u32[]{:S(2)}) collective-permute-start(bf16[64,1,256]{2,0,1:T(8,128)(2,1)S(1)} %get-tuple-element.11), channel_id=1, source_target_pairs={{0,1},{1,2},{2,3},{3,4},{4,5},{5,6},{6,7},{7,8},{8,9},{9,10},{10,1... | collective-permute-start | bytes 98312 | tf_op jit(solution)/shard_map/ppermute | solution.py:15
  81.0 1.5 %collective-permute-done = bf16[64,1,256]{2,0,1:T(8,128)(2,1)S(1)} collective-permute-done((bf16[64,1,256]{2,0,1:T(8,128)(2,1)S(1)}, bf16[64,1,256]{2,0,1:T(8,128)(2,1)S(1)}, u32[]{:S(2)}, u32[]{:S(2)}) %collective-permute-start) | collective-permute-done | bytes 32800 | tf_op jit(solution)/shard_map/ppermute | solution.py:15
  82.9 1.1 reshape.71
  84.0 1.0 copy.66
  85.1 1.4 %convolution_select_fusion.3 = f32[8,8,33,64]{3,1,2,0:T(8,128)S(1)} fusion(bf16[64,10,1,7,2]{0,3,4,1,2:T(8,128)(2,1)S(1)} %slice.74, bf16[64,10,1,8,33]{0,3,4,1,2:T(8,128)(2,1)S(1)} %copy.66, pred[8,33]{0,1:T(8,128)(4,1)S(1)} %copy-done.6, bf16[2,2,64,64,3,3]{3,2,5,4,1,0:T(8,128)(2,1)S(1)} %copy-done.4), kind=kOutput, calls=%fused_computation.18 | convolution fusion | flops 156923904 | bytes 1410048 | tf_op jit(solution)/shard_map/conv_general_dilated | solution.py:25
  87.3 1.3 collective-permute-start.3
  88.6 4.8 %collective-permute-start.2 = (bf16[64,1,256]{0,1,2:T(2,128)(2,1)S(1)}, bf16[64,1,256]{0,1,2:T(2,128)(2,1)S(1)}, u32[]{:S(2)}, u32[]{:S(2)}) collective-permute-start(bf16[64,1,256]{0,1,2:T(2,128)(2,1)S(1)} %get-tuple-element.7), channel_id=1, source_target_pairs={{0,1},{1,2},{2,3},{3,4},{4,5},{5,6},{6,7},{7,8},{8,9},{9,10},{10,1... | collective-permute-start | bytes 98312 | tf_op jit(solution)/shard_map/ppermute | solution.py:15
  94.9 2.5 %collective-permute-done.2 = bf16[64,1,256]{0,1,2:T(2,128)(2,1)S(1)} collective-permute-done((bf16[64,1,256]{0,1,2:T(2,128)(2,1)S(1)}, bf16[64,1,256]{0,1,2:T(2,128)(2,1)S(1)}, u32[]{:S(2)}, u32[]{:S(2)}) %collective-permute-start.2) | collective-permute-done | bytes 32800 | tf_op jit(solution)/shard_map/ppermute | solution.py:15
  97.7 1.1 reshape.72
  99.9 1.4 %convolution_select_fusion.2 = f32[8,8,33,64]{3,1,2,0:T(8,128)S(1)} fusion(bf16[64,10,1,7,2]{0,3,4,1,2:T(8,128)(2,1)S(1)} %slice.78, bf16[64,10,1,8,33]{0,3,4,1,2:T(8,128)(2,1)S(1)} %copy.73, pred[8,33]{0,1:T(8,128)(4,1)S(1)} %copy-done.6, bf16[2,2,64,64,3,3]{3,2,5,4,1,0:T(8,128)(2,1)S(1)} %copy-done.4), kind=kOutput, calls=%fused_computation.17 | convolution fusion | flops 156923904 | bytes 1410048 | tf_op jit(solution)/shard_map/conv_general_dilated | solution.py:25
  102.1 1.3 collective-permute-start.5
  103.4 5.2 %collective-permute-start.4 = (bf16[64,1,256]{2,0,1:T(8,128)(2,1)S(1)}, bf16[64,1,256]{2,0,1:T(8,128)(2,1)S(1)}, u32[]{:S(2)}, u32[]{:S(2)}) collective-permute-start(bf16[64,1,256]{2,0,1:T(8,128)(2,1)S(1)} %get-tuple-element.9), channel_id=1, source_target_pairs={{0,1},{1,2},{2,3},{3,4},{4,5},{5,6},{6,7},{7,8},{8,9},{9,10},{10,1... | collective-permute-start | bytes 98312 | tf_op jit(solution)/shard_map/ppermute | solution.py:15
  108.7 1.4 %collective-permute-done.4 = bf16[64,1,256]{2,0,1:T(8,128)(2,1)S(1)} collective-permute-done((bf16[64,1,256]{2,0,1:T(8,128)(2,1)S(1)}, bf16[64,1,256]{2,0,1:T(8,128)(2,1)S(1)}, u32[]{:S(2)}, u32[]{:S(2)}) %collective-permute-start.4) | collective-permute-done | bytes 32800 | tf_op jit(solution)/shard_map/ppermute | solution.py:15
  110.4 1.1 reshape.73
  112.5 1.4 %convolution_select_fusion.1 = f32[8,8,33,64]{3,1,2,0:T(8,128)S(1)} fusion(bf16[64,10,1,7,2]{0,3,4,1,2:T(8,128)(2,1)S(1)} %slice.82, bf16[64,10,1,8,33]{0,3,4,1,2:T(8,128)(2,1)S(1)} %copy.78, pred[8,33]{0,1:T(8,128)(4,1)S(1)} %copy-done.6, bf16[2,2,64,64,3,3]{3,2,5,4,1,0:T(8,128)(2,1)S(1)} %copy-done.4), kind=kOutput, calls=%fused_computation.16 | convolution fusion | flops 156923904 | bytes 1410048 | tf_op jit(solution)/shard_map/conv_general_dilated | solution.py:25
  114.8 1.3 collective-permute-start.7
  116.1 4.9 %collective-permute-start.6 = (bf16[64,1,256]{0,1,2:T(2,128)(2,1)S(1)}, bf16[64,1,256]{0,1,2:T(2,128)(2,1)S(1)}, u32[]{:S(2)}, u32[]{:S(2)}) collective-permute-start(bf16[64,1,256]{0,1,2:T(2,128)(2,1)S(1)} %get-tuple-element.5), channel_id=1, source_target_pairs={{0,1},{1,2},{2,3},{3,4},{4,5},{5,6},{6,7},{7,8},{8,9},{9,10},{10,1... | collective-permute-start | bytes 98312 | tf_op jit(solution)/shard_map/ppermute | solution.py:15
  121.3 1.6 %collective-permute-done.7 = bf16[64,1,256]{0,1,2:T(2,128)(2,1)S(1)} collective-permute-done((bf16[64,1,256]{0,1,2:T(2,128)(2,1)S(1)}, bf16[64,1,256]{0,1,2:T(2,128)(2,1)S(1)}, u32[]{:S(2)}, u32[]{:S(2)}) %collective-permute-start.7) | collective-permute-done | bytes 32800 | tf_op jit(solution)/shard_map/ppermute | solution.py:17
  123.0 2.2 %collective-permute-done.6 = bf16[64,1,256]{0,1,2:T(2,128)(2,1)S(1)} collective-permute-done((bf16[64,1,256]{0,1,2:T(2,128)(2,1)S(1)}, bf16[64,1,256]{0,1,2:T(2,128)(2,1)S(1)}, u32[]{:S(2)}, u32[]{:S(2)}) %collective-permute-start.6) | collective-permute-done | bytes 32800 | tf_op jit(solution)/shard_map/ppermute | solution.py:15
  125.6 1.1 reshape.74
  127.7 1.4 %convolution_select_fusion = f32[8,8,33,64]{3,1,2,0:T(8,128)S(1)} fusion(bf16[64,10,1,7,2]{0,3,4,1,2:T(8,128)(2,1)S(1)} %slice.86, bf16[64,10,1,8,33]{0,3,4,1,2:T(8,128)(2,1)S(1)} %copy.85, pred[8,33]{0,1:T(8,128)(4,1)S(1)} %copy-done.6, bf16[2,2,64,64,3,3]{3,2,5,4,1,0:T(8,128)(2,1)S(1)} %copy-done.4), kind=kOutput, calls=%fused_computation.15 | convolution fusion | flops 156923904 | bytes 1410048 | tf_op jit(solution)/shard_map/conv_general_dilated | solution.py:25
  130.3 7.3 %all_to_all.60 = bf16[8,2,128]{2,0,1:T(8,128)(2,1)S(1)} all-to-all(bf16[8,2,128]{2,0,1:T(8,128)(2,1)S(1)} %bitcast.144), channel_id=1, replica_groups=mesh['grp'=1,'head'=16,'tile'=2] {'tile'}, dimensions={1} | all-to-all | bytes 8192 | tf_op jit(solution)/shard_map/all_to_all | solution.py:70
  (64 shorter events, 11.9 us)
Async XLA Ops:
  0.0 74.9 %copy-start = (bf16[64,144]{1,0:T(8,128)(2,1)S(1)}, bf16[64,144]{1,0:T(8,128)(2,1)}, u32[]{:S(2)}) copy-start(bf16[64,144]{1,0:T(8,128)(2,1)} %param.7) | copy-start | bytes 55300
  2.5 18.7 %all-to-all-start = ((bf16[9,256,128]{2,0,1:T(8,128)(2,1)}), bf16[9,256,128]{2,0,1:T(8,128)(2,1)S(1)}, u32[]{:S(2)}, u32[]{:S(2)}) async-start(bf16[9,256,128]{2,0,1:T(8,128)(2,1)} %copy.55), calls=%async_computation | async-start | bytes 2097152 | tf_op jit(solution)/shard_map/all_to_all | solution.py:39
  22.6 2.6 %copy-start.1 = (bf16[9,256,128]{2,1,0:T(8,128)(2,1)S(1)}, bf16[9,256,128]{2,1,0:T(8,128)(2,1)}, u32[]{:S(2)}) copy-start(bf16[9,256,128]{2,1,0:T(8,128)(2,1)} %param.6) | copy-start | bytes 1769476
  62.4 12.5 %copy-start.5 = (f32[64]{0:T(128)S(1)}, f32[64]{0:T(128)}, u32[]{:S(2)}) copy-start(f32[64]{0:T(128)} %param.8) | copy-start | bytes 772
  62.4 18.6 %copy-start.2 = (f32[2,2,64]{2,1,0:T(2,128)S(1)}, f32[2,2,64]{2,1,0:T(2,128)}, u32[]{:S(2)}) copy-start(f32[2,2,64]{2,1,0:T(2,128)} %param.10) | copy-start | bytes 3076
  75.1 5.9 %collective-permute-start.1 = (bf16[64,1,256]{2,0,1:T(8,128)(2,1)S(1)}, bf16[64,1,256]{2,0,1:T(8,128)(2,1)S(1)}, u32[]{:S(2)}, u32[]{:S(2)}) collective-permute-start(bf16[64,1,256]{2,0,1:T(8,128)(2,1)S(1)} %get-tuple-element.12), channel_id=1, source_target_pairs={{1,0},{2,1},{3,2},{4,3},{5,4},{6,5},{7,6},{8,7},{9,8},{10,9},{11,1... | collective-permute-start | bytes 98312 | tf_op jit(solution)/shard_map/ppermute | solution.py:17
  76.4 6.1 %collective-permute-start = (bf16[64,1,256]{2,0,1:T(8,128)(2,1)S(1)}, bf16[64,1,256]{2,0,1:T(8,128)(2,1)S(1)}, u32[]{:S(2)}, u32[]{:S(2)}) collective-permute-start(bf16[64,1,256]{2,0,1:T(8,128)(2,1)S(1)} %get-tuple-element.11), channel_id=1, source_target_pairs={{0,1},{1,2},{2,3},{3,4},{4,5},{5,6},{6,7},{7,8},{8,9},{9,10},{10,1... | collective-permute-start | bytes 98312 | tf_op jit(solution)/shard_map/ppermute | solution.py:15
  84.0 1.1 copy-start.4
  84.0 1.1 copy-start.6
  87.3 7.4 %collective-permute-start.3 = (bf16[64,1,256]{0,1,2:T(2,128)(2,1)S(1)}, bf16[64,1,256]{0,1,2:T(2,128)(2,1)S(1)}, u32[]{:S(2)}, u32[]{:S(2)}) collective-permute-start(bf16[64,1,256]{0,1,2:T(2,128)(2,1)S(1)} %get-tuple-element.8), channel_id=1, source_target_pairs={{1,0},{2,1},{3,2},{4,3},{5,4},{6,5},{7,6},{8,7},{9,8},{10,9},{11,1... | collective-permute-start | bytes 98312 | tf_op jit(solution)/shard_map/ppermute | solution.py:17
  88.6 8.7 %collective-permute-start.2 = (bf16[64,1,256]{0,1,2:T(2,128)(2,1)S(1)}, bf16[64,1,256]{0,1,2:T(2,128)(2,1)S(1)}, u32[]{:S(2)}, u32[]{:S(2)}) collective-permute-start(bf16[64,1,256]{0,1,2:T(2,128)(2,1)S(1)} %get-tuple-element.7), channel_id=1, source_target_pairs={{0,1},{1,2},{2,3},{3,4},{4,5},{5,6},{6,7},{7,8},{8,9},{9,10},{10,1... | collective-permute-start | bytes 98312 | tf_op jit(solution)/shard_map/ppermute | solution.py:15
  102.1 6.5 %collective-permute-start.5 = (bf16[64,1,256]{2,0,1:T(8,128)(2,1)S(1)}, bf16[64,1,256]{2,0,1:T(8,128)(2,1)S(1)}, u32[]{:S(2)}, u32[]{:S(2)}) collective-permute-start(bf16[64,1,256]{2,0,1:T(8,128)(2,1)S(1)} %get-tuple-element.10), channel_id=1, source_target_pairs={{1,0},{2,1},{3,2},{4,3},{5,4},{6,5},{7,6},{8,7},{9,8},{10,9},{11,1... | collective-permute-start | bytes 98312 | tf_op jit(solution)/shard_map/ppermute | solution.py:17
  103.4 6.6 %collective-permute-start.4 = (bf16[64,1,256]{2,0,1:T(8,128)(2,1)S(1)}, bf16[64,1,256]{2,0,1:T(8,128)(2,1)S(1)}, u32[]{:S(2)}, u32[]{:S(2)}) collective-permute-start(bf16[64,1,256]{2,0,1:T(8,128)(2,1)S(1)} %get-tuple-element.9), channel_id=1, source_target_pairs={{0,1},{1,2},{2,3},{3,4},{4,5},{5,6},{6,7},{7,8},{8,9},{9,10},{10,1... | collective-permute-start | bytes 98312 | tf_op jit(solution)/shard_map/ppermute | solution.py:15
  114.8 8.1 %collective-permute-start.7 = (bf16[64,1,256]{0,1,2:T(2,128)(2,1)S(1)}, bf16[64,1,256]{0,1,2:T(2,128)(2,1)S(1)}, u32[]{:S(2)}, u32[]{:S(2)}) collective-permute-start(bf16[64,1,256]{0,1,2:T(2,128)(2,1)S(1)} %get-tuple-element.6), channel_id=1, source_target_pairs={{1,0},{2,1},{3,2},{4,3},{5,4},{6,5},{7,6},{8,7},{9,8},{10,9},{11,1... | collective-permute-start | bytes 98312 | tf_op jit(solution)/shard_map/ppermute | solution.py:17
  116.1 9.0 %collective-permute-start.6 = (bf16[64,1,256]{0,1,2:T(2,128)(2,1)S(1)}, bf16[64,1,256]{0,1,2:T(2,128)(2,1)S(1)}, u32[]{:S(2)}, u32[]{:S(2)}) collective-permute-start(bf16[64,1,256]{0,1,2:T(2,128)(2,1)S(1)} %get-tuple-element.5), channel_id=1, source_target_pairs={{0,1},{1,2},{2,3},{3,4},{4,5},{5,6},{6,7},{7,8},{8,9},{9,10},{10,1... | collective-permute-start | bytes 98312 | tf_op jit(solution)/shard_map/ppermute | solution.py:15
  129.4 0.7 copy-start.3
where the time goes:
time: 140 us; the launch traced here: 138 us
  blocking collectives  54.8 us (39%)
  starting transfers between devices  28.9 us (21%)
  waiting for transfers between devices  24.5 us (18%)
  local copies, waits for them, and re-layouts  17.6 us (13%)
  matrix products  6.19 us (4%)
  other arithmetic  5.83 us (4%)
    all_to_all x1, blocking collectives, on_device(): lax.all_to_all(corrected, 'head', split_axis=1, concat_axis=0, tiled=True)  30.8 us
    ppermute x4, starting transfers between devices, extended(): lax.ppermute(tail, axis, [(i, (i + 1) % count) for i in range(ends)])  19.4 us
    all_to_all x1, waiting for transfers between devices, on_device(): lax.all_to_all(attention, 'tile', split_axis=1, concat_axis=2, tiled=True)  14.4 us
    all_to_all x1, blocking collectives, on_device(): lax.all_to_all(lax.all_to_all(corrected, 'head', split_axis=1, concat_axi...  12.3 us
    conv_general_dilated x18, local copies, waits for them, and re-layouts, convolve(): lax.conv_general_dilated(padded[None], kernel, (1, 1), 'VALID', preferred...  9.49 us
    ppermute x4, waiting for transfers between devices, extended(): lax.ppermute(tail, axis, [(i, (i + 1) % count) for i in range(ends)])  7.55 us
    all_to_all x1, blocking collectives, on_device(): lax.all_to_all(logits.astype(jnp.bfloat16), 'tile', split_axis=1, concat_...  7.34 us
    conv_general_dilated x4, matrix products, convolve(): lax.conv_general_dilated(padded[None], kernel, (1, 1), 'VALID', preferred...  5.66 us
  transfers between devices with their start and end apart: 9, of which 7 were waited for; matrix products, arithmetic and copies ran while one was open for 1% of the time, Pallas kernels for 0%

commit v1 on v0

v1 whole, which is shorter than its diff:
```python
import functools
from typing import NamedTuple

import jax
import jax.numpy as jnp
import numpy as np
from jax import lax
from jax.experimental import pallas as pl
from jax.experimental.pallas import tpu as pltpu
from jax.sharding import PartitionSpec as P

BF16, F32 = jnp.bfloat16, jnp.float32
LANES = 128
VMEM_LIMIT = 40 * 1024 * 1024


def up(value, step):
    return -(-value // step) * step


class Plan(NamedTuple):
    maps: int
    width: int
    cols: int
    tiles: int
    heads: int
    feat: int
    convs: int

    @property
    def halo(self):
        return self.convs

    @property
    def sides(self):
        return min(2, self.tiles - 1)

    @property
    def edges(self):
        return self.sides * self.halo

    @property
    def edge_rows(self):
        return up(self.maps * self.edges, 8)

    @property
    def map_rows(self):
        return up(self.maps, 16)

    @property
    def tail_rows(self):
        return up((1 + self.tiles) * self.edge_rows + 3 * self.tiles * self.map_rows, 16)

    @property
    def band(self):
        return self.width // self.heads

    @property
    def rows(self):
        return self.band + 2 * self.halo

    @property
    def slots(self):
        return self.cols // self.rows

    @property
    def groups(self):
        return -(-self.maps // self.slots)

    @property
    def side_rows(self):
        return self.groups * self.edges

    @property
    def block_rows(self):
        return up(self.maps * self.rows + self.side_rows, 16)

    @property
    def stride(self):
        return self.cols + 2 * self.halo

    @property
    def start(self):
        return up(self.stride, LANES) - LANES

    @property
    def chunk(self):
        return 256

    @property
    def lanes(self):
        return up(self.start + self.rows * self.stride, LANES) + 2 * self.chunk + 3 * LANES


def edge_start(plan, tile, side):
    left, right = plan.cols * tile - plan.halo, plan.cols * (tile + 1)
    if plan.sides == 1:
        return jnp.where(tile > 0, left, right)
    return (left, right)[side]


def edge_select(plan, tile, row, position, index):
    hit = None
    for side in range(plan.sides):
        first = index * plan.edges + side * plan.halo
        inside = (row >= first) & (row < first + plan.halo)
        one = inside & (position == row - first + edge_start(plan, tile, side))
        hit = one if hit is None else hit | one
    return hit


def across(a, b):
    return lax.dot_general(a, b, (((1,), (1,)), ((), ())), preferred_element_type=F32)


def dot(a, b):
    return jnp.dot(a, b, preferred_element_type=F32)


def mirror_pack(plan, tile_ref, maps_ref, out_ref, sums_ref, edge_ref):
    me = tile_ref[0]
    count, cols, width, tiles = plan.maps, plan.cols, plan.width, plan.tiles
    head, edge = plan.map_rows, plan.edge_rows

    def pick(rows, span, base, tile, index):
        row = lax.broadcasted_iota(jnp.int32, (rows, span), 0)
        position = lax.broadcasted_iota(jnp.int32, (rows, span), 1) + base
        return edge_select(plan, tile, row, position, index).astype(F32)

    def total(span, index):
        return (lax.broadcasted_iota(jnp.int32, (head, span), 0) == index).astype(F32)

    for shift in range(1, tiles):
        dest = lax.rem(me + shift, tiles)
        by_col = by_row = None
        for index in range(count):
            block = maps_ref[index]
            out_ref[shift - 1, index * cols : (index + 1) * cols, :] = maps_ref[
                index, pl.ds(pl.multiple_of(dest * cols, cols), cols), :
            ]
            left = [pick(edge, cols, me * cols, dest, index)]
            upper = [pick(edge, width, 0, dest, index)]
            if shift == 1:
                left.append(total(cols, index))
                upper.append(total(width, index))
                upper.append(pick(edge, width, 0, me, index))
            by_c = across(jnp.concatenate(left, axis=0).astype(BF16), block)
            by_r = dot(jnp.concatenate(upper, axis=0).astype(BF16), block)
            by_col = by_c if by_col is None else by_col + by_c
            by_row = by_r if by_row is None else by_row + by_r
        if shift == 1:
            sums_ref[...] = by_col[edge : edge + head]
            own = pl.ds(pl.multiple_of(me * cols, cols), cols)
            sums_ref[:, own] = sums_ref[:, own] + by_row[edge : edge + head]
            edge_ref[...] = by_row[edge + head :]
            sums = sums_ref[...]
            high = sums.astype(BF16).astype(F32)
            middle = (sums - high).astype(BF16).astype(F32)
            low = sums - high - middle
        pieces = [by_row[:edge]]
        for wide in (by_col[:edge], high, middle, low):
            pieces += [wide[:, k * cols : (k + 1) * cols] for k in range(tiles)]
        used = (1 + tiles) * edge + 3 * tiles * head
        if plan.tail_rows > used:
            pieces.append(jnp.zeros((plan.tail_rows - used, cols), F32))
        out_ref[shift - 1, count * cols :, :] = jnp.concatenate(pieces, axis=0).astype(BF16)


def correct_pack(
    plan, tile_ref, maps_ref, recv_ref, sums_ref, edge_ref, out_ref, field_ref, turned_ref
):
    me = tile_ref[0]
    count, cols, width, tiles = plan.maps, plan.cols, plan.width, plan.tiles
    head, edge, halo = plan.map_rows, plan.edge_rows, plan.halo
    tails = [recv_ref[k, count * cols :, :].astype(F32) for k in range(tiles - 1)]

    rowsum = []
    for b in range(tiles):
        value = sums_ref[:, b * cols : (b + 1) * cols]
        for tail in tails:
            base = (1 + tiles) * edge
            parts = [
                tail[base + (k * tiles + b) * head : base + (k * tiles + b + 1) * head]
                for k in range(3)
            ]
            value = value + ((parts[0] + parts[1]) + parts[2])
        rowsum.append(value)
    grand = sum(jnp.sum(value, axis=1, keepdims=True) for value in rowsum)
    grand = jnp.where(lax.broadcasted_iota(jnp.int32, (head, 1), 0) < count, grand, 1.0)
    scaled = [value / grand for value in rowsum]
    for b in range(tiles):
        square = jnp.concatenate([rowsum[b], jnp.zeros((LANES - head, cols), F32)], axis=0)
        turned_ref[b * cols : (b + 1) * cols, :] = square.T
    mine = scaled[0]
    for b in range(1, tiles):
        mine = jnp.where(me == b, scaled[b], mine)

    eye = (
        lax.broadcasted_iota(jnp.int32, (cols, cols), 0)
        == lax.broadcasted_iota(jnp.int32, (cols, cols), 1)
    ).astype(F32).astype(BF16)
    margin = 8
    for index in range(count):
        field_ref[index, :margin, :] = jnp.zeros((margin, cols), F32)
        field_ref[index, margin + width :, :] = jnp.zeros((margin, cols), F32)
        for b in range(tiles):
            shift = lax.rem(b - me + tiles, tiles)
            other = recv_ref[
                jnp.maximum(shift - 1, 0), index * cols : (index + 1) * cols, :
            ]
            own = maps_ref[index, b * cols : (b + 1) * cols, :]
            mirror = across(eye, jnp.where(shift == 0, own, other))
            column = turned_ref[b * cols : (b + 1) * cols, index : index + 1]
            field_ref[index, margin + b * cols : margin + (b + 1) * cols, :] = (
                own.astype(F32) + mirror - column * mine[index : index + 1]
            )

    strips = []
    for b in range(tiles):
        strip = edge_ref[...]
        for k, tail in enumerate(tails):
            strip = jnp.where(lax.rem(me + k + 1, tiles) == b, tail[:edge], strip)
        for tail in tails:
            strip = strip + tail[(1 + b) * edge : (2 + b) * edge]
        strips.append(strip)
    strip = jnp.concatenate(strips, axis=1)
    wide = jnp.concatenate(scaled, axis=1)
    before = pl.multiple_of(jnp.maximum(me * cols - 8, 0), 8)
    after = pl.multiple_of(jnp.minimum((me + 1) * cols, width - 8), 8)
    left = turned_ref[pl.ds(before, 8), :][8 - halo :]
    right = turned_ref[pl.ds(after, 8), :][:halo]
    if plan.sides == 1:
        beside = jnp.where(me > 0, left, right)
    else:
        beside = jnp.concatenate([left, right], axis=0)
    lines = [
        strip[k * plan.edges : (k + 1) * plan.edges] - beside[:, k : k + 1] * wide[k : k + 1]
        for k in range(count)
    ]
    rows, slots = plan.rows, plan.slots
    stacks = []
    for slot in range(slots):
        members = []
        for group in range(plan.groups):
            k = group * slots + slot
            members.append(lines[k] if k < count else jnp.zeros((plan.edges, width), F32))
        stacks.append(jnp.concatenate(members, axis=0))
    lane = lax.broadcasted_iota(jnp.int32, (plan.side_rows, cols), 1)
    spare = plan.block_rows - count * rows - plan.side_rows
    for h in range(plan.heads):
        first = h * plan.band - halo
        pieces = [field_ref[k, margin + first : margin + first + rows, :] for k in range(count)]
        side = jnp.zeros((plan.side_rows, cols), F32)
        for slot in range(slots):
            moved = pltpu.roll(stacks[slot], (slot * rows - first) % width, 1)[:, :cols]
            side = jnp.where((lane >= slot * rows) & (lane < (slot + 1) * rows), moved, side)
        pieces.append(side)
        if spare:
            pieces.append(jnp.zeros((spare, cols), F32))
        out_ref[h] = jnp.concatenate(pieces, axis=0).astype(BF16)


def shifted(ref, rows, base, offset, size):
    low = offset // LANES * LANES
    rest = offset - low
    if rest == 0:
        return ref[rows, pl.ds(pl.multiple_of(base + low, LANES), size)]
    value = ref[rows, pl.ds(pl.multiple_of(base + low, LANES), size + LANES)]
    return pltpu.roll(value, size + LANES - rest, 1)[:, :size]


def stack(
    plan, recv_ref, proj_ref, side_ref, kernel_ref, vector_ref, mask_ref, out_ref,
    maps_ref, sides_ref, field_ref, stream_ref, hidden_ref, taps_ref, logit_ref,
):
    count, cols, rows, halo = plan.maps, plan.cols, plan.rows, plan.halo
    heads, feat, chunk, stride = plan.heads, plan.feat, plan.chunk, plan.stride
    body = count * rows
    for s in range(heads):
        block = recv_ref[s].astype(F32)
        maps_ref[s * body : (s + 1) * body, :] = block[:body]
        sides_ref[s * plan.side_rows : (s + 1) * plan.side_rows, :] = block[
            body : body + plan.side_rows
        ]
    bias = vector_ref[:, 0:1]

    slots, members = plan.slots, heads * plan.groups
    lane = lax.broadcasted_iota(jnp.int32, (members, cols), 1)
    placed = []
    for first in range(0, plan.edges, slots):
        parts = [jnp.zeros((members, cols), F32) for _ in range(slots)]
        for at in range(min(slots, plan.edges - first)):
            value = sides_ref[pl.ds(first + at, members, stride=plan.edges), :]
            keep = (lane >= at * rows) & (lane < (at + 1) * rows)
            for slot in range(slots):
                moved = value
                if at != slot:
                    moved = pltpu.roll(value, ((at - slot) * rows) % cols, 1)
                parts[slot] = jnp.where(keep, moved, parts[slot])
        stacked = jnp.concatenate(parts, axis=0).astype(BF16)
        placed.append((first, (dot(side_ref[...], stacked) + bias).astype(BF16)))

    key = lax.broadcasted_iota(jnp.int32, (cols, chunk), 0)
    at = sum((key >= k * rows).astype(jnp.int32) for k in range(1, slots + 1))
    base_target = plan.start + (key - at * rows) * stride
    spots = lax.broadcasted_iota(jnp.int32, (cols, chunk), 1)
    chunks = -(-(rows * stride + plan.start) // chunk)

    def place(i, carry):
        here = spots + i * chunk
        value = None
        for first, columns in placed:
            column = at + first
            fits = (at < slots) & (column < plan.edges)
            if plan.sides == 1:
                target = base_target + column
                hit = (here == target) | (here == target + halo + cols)
            else:
                target = base_target + column + jnp.where(column < halo, 0, cols)
                hit = here == target
            one = dot(columns, (hit & fits).astype(F32).astype(BF16))
            value = one if value is None else value + one
        field_ref[:, pl.ds(pl.multiple_of(i * chunk, chunk), chunk)] = value
        return carry

    lax.fori_loop(0, chunks, place, 0)

    weight = proj_ref[...]
    spot = lax.broadcasted_iota(jnp.int32, (feat, cols), 1)
    per = 2
    for r in range(0, rows, per):
        blocks = [
            maps_ref[pl.ds(r + k, heads * count, stride=rows), :].astype(BF16)
            for k in range(per)
        ]
        pair = dot(weight, jnp.concatenate(blocks, axis=1)) + bias
        for k in range(per):
            begin = plan.start + (r + k) * stride + halo
            low, rest = begin // LANES * LANES, begin % LANES
            value = pair[:, k * cols : (k + 1) * cols]
            if rest == 0:
                field_ref[:, low : low + cols] += value
                continue
            value = pltpu.roll(value, rest, 1)
            field_ref[:, low : low + cols] += jnp.where(spot >= rest, value, 0.0)
            field_ref[:, low + cols : low + 2 * cols] += jnp.where(spot < rest, value, 0.0)

    def settle(i, carry):
        here = pl.ds(pl.multiple_of(i * chunk, chunk), chunk)
        stream_ref[:, here] = jnp.where(mask_ref[:, here] > 0, field_ref[:, here], 0.0).astype(BF16)
        return carry

    lax.fori_loop(0, chunks, settle, 0)

    everything = slice(None)
    for n in range(plan.convs):
        source = hidden_ref if n % 2 else stream_ref
        low = (plan.start + (n + 1) * stride) // LANES * LANES
        steps = -(-(plan.start + (rows - n - 1) * stride - low) // chunk)
        offsets = vector_ref[:, n + 1 : n + 2]

        def multiply(i, carry):
            base = low + i * chunk
            window = jnp.concatenate(
                [shifted(source, everything, base, d * stride, chunk) for d in (-1, 0, 1)], axis=0
            )
            taps_ref[:, pl.ds(pl.multiple_of(base, LANES), chunk)] = dot(kernel_ref[n], window)
            return carry

        lax.fori_loop(0, steps, multiply, 0)

        def finish(i, carry):
            base = low + i * chunk
            here = pl.ds(pl.multiple_of(base, LANES), chunk)
            value = taps_ref[feat : 2 * feat, here]
            value = value + shifted(taps_ref, slice(0, feat), base, -1, chunk)
            value = value + shifted(taps_ref, slice(2 * feat, 3 * feat), base, 1, chunk)
            value = value + offsets
            keep = mask_ref[:, here] > 0
            if n % 2 == 0:
                value = jnp.where(value > 0, value, jnp.exp(jnp.minimum(value, 0.0)) - 1.0)
                hidden_ref[:, here] = jnp.where(keep, value, 0.0).astype(BF16)
                return carry
            value = (stream_ref[:, here].astype(F32) + value).astype(BF16)
            if n < plan.convs - 1:
                stream_ref[:, here] = jnp.where(keep, value.astype(F32), 0.0).astype(BF16)
                return carry
            readout = vector_ref[:, plan.convs + 1 : plan.convs + 2]
            logit_ref[0:1, here] = jnp.sum(value.astype(F32) * readout, axis=0, keepdims=True)
            return carry

        lax.fori_loop(0, steps, finish, 0)

    for r in range(plan.band):
        begin = plan.start + (r + halo) * stride + halo
        low = begin // LANES * LANES
        out_ref[r : r + 1, :] = shifted(logit_ref, slice(0, 1), low, begin - low, cols)


def whole(space=pltpu.VMEM):
    return pl.BlockSpec(memory_space=space)


def on_device(attention, proj_weight, proj_bias, conv_weight, conv_bias, out_weight):
    maps, width, cols = attention.shape
    feat = proj_weight.shape[0]
    blocks, convs = conv_weight.shape[:2]
    tiles, heads = lax.axis_size("tile"), lax.axis_size("head")
    plan = Plan(maps, width, cols, tiles, heads, feat, blocks * convs)
    me = lax.axis_index("tile").astype(jnp.int32)
    tile = me.reshape(1)
    params = pltpu.CompilerParams(vmem_limit_bytes=VMEM_LIMIT)

    payload_rows = maps * cols + plan.tail_rows
    payload, sums, edge = pl.pallas_call(
        functools.partial(mirror_pack, plan),
        out_shape=[
            jax.ShapeDtypeStruct((tiles - 1, payload_rows, cols), BF16),
            jax.ShapeDtypeStruct((plan.map_rows, width), F32),
            jax.ShapeDtypeStruct((plan.edge_rows, cols), F32),
        ],
        in_specs=[whole(pltpu.SMEM), whole()],
        out_specs=[whole()] * 3,
        compiler_params=params,
        name="mirror_pack",
    )(tile, attention)
    received = jnp.stack(
        [
            lax.ppermute(payload[s - 1], "tile", [(i, (i + s) % tiles) for i in range(tiles)])
            for s in range(tiles - 1, 0, -1)
        ]
    )

    stride, start = plan.stride, plan.start
    side_weight = proj_weight.reshape(feat, heads, maps)
    side_weight = jnp.pad(side_weight, ((0, 0), (0, 0), (0, plan.groups * plan.slots - maps)))
    side_weight = side_weight.reshape(feat, heads, plan.groups, plan.slots)
    side_weight = side_weight.transpose(0, 3, 1, 2).reshape(feat, -1)
    kernels = conv_weight.transpose(0, 1, 5, 2, 4, 3).reshape(plan.convs, 3 * feat, 3 * feat)
    vectors = jnp.concatenate(
        [proj_bias[None], conv_bias.reshape(-1, feat), out_weight[None]], axis=0
    ).T
    spot = np.arange(plan.lanes) - start
    row = lax.axis_index("head") * plan.band - plan.halo + (spot // stride).astype(np.int32)
    col = me * cols - plan.halo + (spot % stride).astype(np.int32)
    mask = (row >= 0) & (row < width) & (col >= 0) & (col < width)
    mask = mask.astype(F32)[None]

    packed = pl.pallas_call(
        functools.partial(correct_pack, plan),
        out_shape=jax.ShapeDtypeStruct((heads, plan.block_rows, cols), BF16),
        in_specs=[whole(pltpu.SMEM)] + [whole()] * 4,
        out_specs=whole(),
        scratch_shapes=[
            pltpu.VMEM((maps, width + 16, cols), F32),
            pltpu.VMEM((width, LANES), F32),
        ],
        compiler_params=params,
        name="correct_pack",
    )(tile, attention, received, sums, edge)
    grouped = lax.all_to_all(packed, "head", split_axis=0, concat_axis=0, tiled=True)

    return pl.pallas_call(
        functools.partial(stack, plan),
        out_shape=jax.ShapeDtypeStruct((plan.band, cols), F32),
        in_specs=[whole()] * 6,
        out_specs=whole(),
        scratch_shapes=[
            pltpu.VMEM((heads * maps * plan.rows, cols), F32),
            pltpu.VMEM((heads * plan.side_rows, cols), F32),
            pltpu.VMEM((feat, plan.lanes), F32),
            pltpu.VMEM((feat, plan.lanes), BF16),
            pltpu.VMEM((feat, plan.lanes), BF16),
            pltpu.VMEM((3 * feat, plan.lanes), F32),
            pltpu.VMEM((8, plan.lanes), F32),
        ],
        compiler_params=params,
        name="stack",
    )(grouped, proj_weight, side_weight, kernels, vectors, mask)


def solution(mesh):
    return jax.shard_map(
        on_device,
        mesh=mesh,
        in_specs=(P(("grp", "head"), None, "tile"), P(), P(), P(), P(), P()),
        out_specs=P(("grp", "head"), "tile"),
        check_vma=False,
    )
```

time: 140 us -> 62.7 us (0.45)
  blocking collectives: 54.8 us -> 0 us
  Pallas kernels: 0 us -> 22.4 us
  starting transfers between devices: 28.9 us -> 9.29 us
  local copies, waits for them, and re-layouts: 17.6 us -> 3.39 us
  matrix products: 6.19 us -> 0 us
  other arithmetic: 5.83 us -> 0.02 us
  waiting for transfers between devices: 24.5 us -> 26.6 us
    all_to_all x3 -> x0, blocking collectives: 50.4 us -> none  [the longest x1 30.8 us: on_device(): lax.all_to_all(corrected, 'head', split_axis=1, concat_axis=0, tiled=True)]
    pallas_call x0 -> x3, Pallas kernels: none -> 22.4 us  [the longest x1 20.1 us: on_device(): pl.pallas_call(functools.partial(stack, plan), out_shape=jax.ShapeDtypeSt...]
    ppermute x8 -> x1, starting transfers between devices: 24.6 us -> 3.03 us  [on_device(): lax.ppermute(payload[s - 1], 'tile', [(i, (i + s) % tiles) for i in range...]
    conv_general_dilated x18 -> x0, local copies, waits for them, and re-layouts: 9.49 us -> none  [convolve(): lax.conv_general_dilated(padded[None], kernel, (1, 1), 'VALID', preferred...]
    conv_general_dilated x4 -> x0, matrix products: 5.66 us -> none  [convolve(): lax.conv_general_dilated(padded[None], kernel, (1, 1), 'VALID', preferred...]
    all_gather x1 -> x0, blocking collectives: 4.36 us -> none  [on_device(): rowsum = lax.all_gather(column_part, 'tile', axis=1, tiled=True)]
    convert_element_type x6 -> x0, other arithmetic: 4.2 us -> none  [the longest x1 1.49 us: on_device(): symmetric = attention.astype(jnp.float32) + mirror.astype(jnp.float32)]
    all_to_all x1, waiting for transfers between devices: 14.4 us -> 18.3 us  [on_device(): lax.all_to_all(packed, 'head', split_axis=0, concat_axis=0, tiled=True)]
  transfers between devices with their start and end apart: 9 -> 2, of which waited for: 7 -> 2; matrix products, arithmetic and copies ran while one was open for 1% -> 2% of each run, Pallas kernels for 0% -> 0%
where the time goes in v1:
time: 62.7 us; the launch traced here: 61.8 us
  waiting for transfers between devices  26.6 us (42%)
  Pallas kernels  22.4 us (36%)
  starting transfers between devices  9.29 us (15%)
  local copies, waits for them, and re-layouts  3.39 us (5%)
    pallas_call x1, Pallas kernels, on_device(): pl.pallas_call(functools.partial(stack, plan), out_shape=jax.ShapeDtypeSt...  20.1 us
    all_to_all x1, waiting for transfers between devices, on_device(): lax.all_to_all(packed, 'head', split_axis=0, concat_axis=0, tiled=True)  18.3 us
    ppermute x1, waiting for transfers between devices, on_device(): lax.ppermute(payload[s - 1], 'tile', [(i, (i + s) % tiles) for i in range...  8.23 us
    all_to_all x1, starting transfers between devices, on_device(): lax.all_to_all(packed, 'head', split_axis=0, concat_axis=0, tiled=True)  6.26 us
    ppermute x1, starting transfers between devices, on_device(): lax.ppermute(payload[s - 1], 'tile', [(i, (i + s) % tiles) for i in range...  3.03 us
    unnamed x18, local copies, waits for them, and re-layouts  2.16 us
    pallas_call x1, Pallas kernels, on_device(): pl.pallas_call(functools.partial(correct_pack, plan), out_shape=jax.Shape...  1.79 us
  transfers between devices with their start and end apart: 2, of which 2 were waited for; matrix products, arithmetic and copies ran while one was open for 2% of the time, Pallas kernels for 0%

profile of v1, /device:TPU:0, one launch (start us, length us, event | category | flops | bytes accessed | tf_op | source)
XLA Modules:
  0.0 61.8 jit_solution(6291983577642423828)
XLA Ops:
  0.0 0.0 copy-start
  0.0 1.1 %copy-done = bf16[9,256,128]{2,1,0:T(8,128)(2,1)S(1)} copy-done((bf16[9,256,128]{2,1,0:T(8,128)(2,1)S(1)}, bf16[9,256,128]{2,1,0:T(8,128)(2,1)}, u32[]{:S(2)}) %copy-start) | copy-done | bytes 589848
  1.1 0.5 mirror_pack.1
  1.5 3.0 %collective-permute-start = (bf16[1376,128]{1,0:T(8,128)(2,1)S(1)}, bf16[1376,128]{1,0:T(8,128)(2,1)S(1)}, u32[]{:S(2)}, u32[]{:S(2)}) collective-permute-start(bf16[1376,128]{1,0:T(8,128)(2,1)S(1)} %bitcast.16), channel_id=1, source_target_pairs={{0,1},{1,0},{2,3},{3,2},{4,5},{5,4},{6,7},{7,6},{8,9},{9,8},{10,11... | collective-permute-start | bytes 1056776 | tf_op jit(solution)/shard_map/ppermute | solution.py:429
  4.6 8.2 %collective-permute-done = bf16[1376,128]{1,0:T(8,128)(2,1)S(1)} collective-permute-done((bf16[1376,128]{1,0:T(8,128)(2,1)S(1)}, bf16[1376,128]{1,0:T(8,128)(2,1)S(1)}, u32[]{:S(2)}, u32[]{:S(2)}) %collective-permute-start) | collective-permute-done | bytes 352288 | tf_op jit(solution)/shard_map/ppermute | solution.py:429
  12.8 1.8 %correct_pack.1 = bf16[16,224,128]{2,1,0:T(8,128)(2,1)} custom-call(s32[1]{0:T(128)} %bitcast.tile_ref, bf16[9,256,128]{2,1,0:T(8,128)(2,1)S(1)} %copy-done, bf16[1,1376,128]{2,1,0:T(8,128)(2,1)S(1)} %bitcast.14, f32[16,256]{1,0:T(8,128)S(1)} %get-tuple-element.9.sums_ref, f32[40,128]{1,0:T(8,128)S(1)} %get-tuple-element.10.edge_ref), custom_call_target="tpu_custom_call" | custom-call | tf_op jit(solution)/shard_map/correct_pack/pallas_call | solution.py:449
  14.6 0.0 copy-start.3
  14.6 0.0 copy-start.4
  14.6 0.0 copy-start.2
  14.6 6.3 %all-to-all-start = ((bf16[16,224,128]{2,1,0:T(8,128)(2,1)}), bf16[16,224,128]{2,1,0:T(8,128)(2,1)S(1)}, u32[]{:S(2)}, u32[]{:S(2)}) async-start(bf16[16,224,128]{2,1,0:T(8,128)(2,1)} %correct_pack.1), calls=%async_computation | async-start | bytes 1835008 | tf_op jit(solution)/shard_map/all_to_all | solution.py:461
  20.9 0.0 copy-done.3
  20.9 0.0 copy-done.4
  20.9 0.0 copy-done.2
  20.9 0.5 copy.24
  21.5 0.0 copy-start.1
  21.5 0.5 reshape.22.kernel_ref
  21.9 0.3 copy-done.1
  22.2 0.1 copy.21
  22.4 0.1 copy.26.side_ref
  22.5 0.0 copy-start.5
  22.6 0.0 copy-start.6
  22.6 0.0 copy-start.7
  22.6 0.6 %copy-done.5 = f32[2,2,64]{2,1,0:T(2,128)S(1)} copy-done((f32[2,2,64]{2,1,0:T(2,128)S(1)}, f32[2,2,64]{2,1,0:T(2,128)}, u32[]{:S(2)}) %copy-start.5) | copy-done | bytes 1048
  23.2 0.0 copy-done.6
  23.2 0.0 copy-done.7
  23.2 0.1 copy.25
  23.3 18.3 %all-to-all-done.recv_ref = bf16[16,224,128]{2,1,0:T(8,128)(2,1)S(1)} async-done(((bf16[16,224,128]{2,1,0:T(8,128)(2,1)}), bf16[16,224,128]{2,1,0:T(8,128)(2,1)S(1)}, u32[]{:S(2)}, u32[]{:S(2)}) %all-to-all-start) | async-done | bytes 917536 | tf_op jit(solution)/shard_map/all_to_all | solution.py:461
  41.7 20.1 %stack.5 = f32[16,128]{1,0:T(8,128)} custom-call(bf16[16,224,128]{2,1,0:T(8,128)(2,1)S(1)} %all-to-all-done.recv_ref, bf16[64,144]{1,0:T(8,128)(2,1)S(1)} %copy-done.1, bf16[64,160]{1,0:T(8,128)(2,1)S(1)} %copy.26.side_ref, bf16[4,192,192]{2,1,0:T(8,128)(2,1)S(1)} %reshape.22.kernel_ref, f32[64,6]{1,0:T(8,128)S(1)} %bitcast.15, f32[1,4352]{1,0:T(1,128)S(1)} %reshape.24.mask_ref), custom_call_target="tpu_custom_call" | custom-call | tf_op jit(solution)/shard_map/stack/pallas_call | solution.py:463
  (7 shorter events, 0.1 us)
Async XLA Ops:
  0.0 1.1 %copy-start = (bf16[9,256,128]{2,1,0:T(8,128)(2,1)S(1)}, bf16[9,256,128]{2,1,0:T(8,128)(2,1)}, u32[]{:S(2)}) copy-start(bf16[9,256,128]{2,1,0:T(8,128)(2,1)} %maps_ref.3) | copy-start | bytes 1769476
  1.5 11.3 %collective-permute-start = (bf16[1376,128]{1,0:T(8,128)(2,1)S(1)}, bf16[1376,128]{1,0:T(8,128)(2,1)S(1)}, u32[]{:S(2)}, u32[]{:S(2)}) collective-permute-start(bf16[1376,128]{1,0:T(8,128)(2,1)S(1)} %bitcast.16), channel_id=1, source_target_pairs={{0,1},{1,0},{2,3},{3,2},{4,5},{5,4},{6,7},{7,6},{8,9},{9,8},{10,11... | collective-permute-start | bytes 1056776 | tf_op jit(solution)/shard_map/ppermute | solution.py:429
  14.6 6.3 %copy-start.3 = (s32[4352]{0:T(1024)S(1)}, s32[4352]{0:T(1024)}, u32[]{:S(2)}) copy-start(s32[4352]{0:T(1024)} %constant.27.clone) | copy-start | bytes 52228
  14.6 6.3 %copy-start.4 = (s32[4352]{0:T(1024)S(1)}, s32[4352]{0:T(1024)}, u32[]{:S(2)}) copy-start(s32[4352]{0:T(1024)} %constant.28.clone) | copy-start | bytes 52228
  14.6 6.3 %copy-start.2 = (bf16[2,2,64,64,3,3]{3,2,5,4,1,0:T(8,128)(2,1)S(1)}, bf16[2,2,64,64,3,3]{3,2,5,4,1,0:T(8,128)(2,1)}, u32[]{:S(2)}) copy-start(bf16[2,2,64,64,3,3]{3,2,5,4,1,0:T(8,128)(2,1)} %param.11) | copy-start | bytes 884740
  14.6 27.1 %all-to-all-start = ((bf16[16,224,128]{2,1,0:T(8,128)(2,1)}), bf16[16,224,128]{2,1,0:T(8,128)(2,1)S(1)}, u32[]{:S(2)}, u32[]{:S(2)}) async-start(bf16[16,224,128]{2,1,0:T(8,128)(2,1)} %correct_pack.1), calls=%async_computation | async-start | bytes 1835008 | tf_op jit(solution)/shard_map/all_to_all | solution.py:461
  21.5 0.8 %copy-start.1 = (bf16[64,144]{1,0:T(8,128)(2,1)S(1)}, bf16[64,144]{1,0:T(8,128)(2,1)}, u32[]{:S(2)}) copy-start(bf16[64,144]{1,0:T(8,128)(2,1)} %proj_ref.1) | copy-start | bytes 55300
  22.5 0.7 %copy-start.5 = (f32[2,2,64]{2,1,0:T(2,128)S(1)}, f32[2,2,64]{2,1,0:T(2,128)}, u32[]{:S(2)}) copy-start(f32[2,2,64]{2,1,0:T(2,128)} %param.12) | copy-start | bytes 3076
  22.6 0.7 %copy-start.6 = (f32[64]{0:T(128)S(1)}, f32[64]{0:T(128)}, u32[]{:S(2)}) copy-start(f32[64]{0:T(128)} %param.13) | copy-start | bytes 772
  22.6 0.7 %copy-start.7 = (f32[64]{0:T(128)S(1)}, f32[64]{0:T(128)}, u32[]{:S(2)}) copy-start(f32[64]{0:T(128)} %param.10) | copy-start | bytes 772

commit v2 on v1

--- a/solution.py
+++ b/solution.py
@@ -11,7 +11,7 @@
 
 BF16, F32 = jnp.bfloat16, jnp.float32
 LANES = 128
-VMEM_LIMIT = 40 * 1024 * 1024
+VMEM_LIMIT = 48 * 1024 * 1024
 
 
 def up(value, step):
@@ -261,16 +261,16 @@
 
 
 def shifted(ref, rows, base, offset, size):
-    low = offset // LANES * LANES
-    rest = offset - low
+    begin = base + offset
+    low = begin // LANES * LANES
+    rest = begin - low
     if rest == 0:
-        return ref[rows, pl.ds(pl.multiple_of(base + low, LANES), size)]
-    value = ref[rows, pl.ds(pl.multiple_of(base + low, LANES), size + LANES)]
-    return pltpu.roll(value, size + LANES - rest, 1)[:, :size]
+        return ref[rows, low : low + size]
+    return pltpu.roll(ref[rows, low : low + size + LANES], size + LANES - rest, 1)[:, :size]
 
 
 def stack(
-    plan, recv_ref, proj_ref, side_ref, kernel_ref, vector_ref, mask_ref, out_ref,
+    plan, recv_ref, proj_ref, side_ref, kernel_ref, vector_ref, mask_ref, spots_ref, out_ref,
     maps_ref, sides_ref, field_ref, stream_ref, hidden_ref, taps_ref, logit_ref,
 ):
     count, cols, rows, halo = plan.maps, plan.cols, plan.rows, plan.halo
@@ -298,32 +298,14 @@
                     moved = pltpu.roll(value, ((at - slot) * rows) % cols, 1)
                 parts[slot] = jnp.where(keep, moved, parts[slot])
         stacked = jnp.concatenate(parts, axis=0).astype(BF16)
-        placed.append((first, (dot(side_ref[...], stacked) + bias).astype(BF16)))
-
-    key = lax.broadcasted_iota(jnp.int32, (cols, chunk), 0)
-    at = sum((key >= k * rows).astype(jnp.int32) for k in range(1, slots + 1))
-    base_target = plan.start + (key - at * rows) * stride
-    spots = lax.broadcasted_iota(jnp.int32, (cols, chunk), 1)
+        placed.append((dot(side_ref[...], stacked) + bias).astype(BF16))
+
     chunks = -(-(rows * stride + plan.start) // chunk)
-
-    def place(i, carry):
-        here = spots + i * chunk
-        value = None
-        for first, columns in placed:
-            column = at + first
-            fits = (at < slots) & (column < plan.edges)
-            if plan.sides == 1:
-                target = base_target + column
-                hit = (here == target) | (here == target + halo + cols)
-            else:
-                target = base_target + column + jnp.where(column < halo, 0, cols)
-                hit = here == target
-            one = dot(columns, (hit & fits).astype(F32).astype(BF16))
-            value = one if value is None else value + one
-        field_ref[:, pl.ds(pl.multiple_of(i * chunk, chunk), chunk)] = value
-        return carry
-
-    lax.fori_loop(0, chunks, place, 0)
+    for i in range(chunks):
+        here = slice(i * chunk, (i + 1) * chunk)
+        field_ref[:, here] = sum(
+            dot(columns, spots_ref[k, :, here]) for k, columns in enumerate(placed)
+        )
 
     weight = proj_ref[...]
     spot = lax.broadcasted_iota(jnp.int32, (feat, cols), 1)
@@ -345,12 +327,9 @@
             field_ref[:, low : low + cols] += jnp.where(spot >= rest, value, 0.0)
             field_ref[:, low + cols : low + 2 * cols] += jnp.where(spot < rest, value, 0.0)
 
-    def settle(i, carry):
-        here = pl.ds(pl.multiple_of(i * chunk, chunk), chunk)
+    for i in range(chunks):
+        here = slice(i * chunk, (i + 1) * chunk)
         stream_ref[:, here] = jnp.where(mask_ref[:, here] > 0, field_ref[:, here], 0.0).astype(BF16)
-        return carry
-
-    lax.fori_loop(0, chunks, settle, 0)
 
     everything = slice(None)
     for n in range(plan.convs):
@@ -359,19 +338,14 @@
         steps = -(-(plan.start + (rows - n - 1) * stride - low) // chunk)
         offsets = vector_ref[:, n + 1 : n + 2]
 
-        def multiply(i, carry):
-            base = low + i * chunk
+        def multiply(base):
             window = jnp.concatenate(
                 [shifted(source, everything, base, d * stride, chunk) for d in (-1, 0, 1)], axis=0
             )
-            taps_ref[:, pl.ds(pl.multiple_of(base, LANES), chunk)] = dot(kernel_ref[n], window)
-            return carry
-
-        lax.fori_loop(0, steps, multiply, 0)
-
-        def finish(i, carry):
-            base = low + i * chunk
-            here = pl.ds(pl.multiple_of(base, LANES), chunk)
+            taps_ref[:, base : base + chunk] = dot(kernel_ref[n], window)
+
+        def finish(base):
+            here = slice(base, base + chunk)
             value = taps_ref[feat : 2 * feat, here]
             value = value + shifted(taps_ref, slice(0, feat), base, -1, chunk)
             value = value + shifted(taps_ref, slice(2 * feat, 3 * feat), base, 1, chunk)
@@ -380,16 +354,19 @@
             if n % 2 == 0:
                 value = jnp.where(value > 0, value, jnp.exp(jnp.minimum(value, 0.0)) - 1.0)
                 hidden_ref[:, here] = jnp.where(keep, value, 0.0).astype(BF16)
-                return carry
+                return
             value = (stream_ref[:, here].astype(F32) + value).astype(BF16)
             if n < plan.convs - 1:
                 stream_ref[:, here] = jnp.where(keep, value.astype(F32), 0.0).astype(BF16)
-                return carry
+                return
             readout = vector_ref[:, plan.convs + 1 : plan.convs + 2]
             logit_ref[0:1, here] = jnp.sum(value.astype(F32) * readout, axis=0, keepdims=True)
-            return carry
-
-        lax.fori_loop(0, steps, finish, 0)
+
+        for i in range(steps + 1):
+            if i < steps:
+                multiply(low + i * chunk)
+            if i > 0:
+                finish(low + (i - 1) * chunk)
 
     for r in range(plan.band):
         begin = plan.start + (r + halo) * stride + halo
@@ -446,6 +423,18 @@
     mask = (row >= 0) & (row < width) & (col >= 0) & (col < width)
     mask = mask.astype(F32)[None]
 
+    key = np.arange(cols)
+    member, line = key // plan.rows, key % plan.rows
+    spots = []
+    for first in range(0, plan.edges, plan.slots):
+        column = first + member
+        fits = (member < plan.slots) & (column < plan.edges)
+        places = (0, plan.halo + cols) if plan.sides == 1 else (np.where(column < plan.halo, 0, cols),)
+        target = [np.where(fits, start + line * stride + column + p, -1) for p in places]
+        hit = [jnp.arange(plan.lanes)[None] == jnp.asarray(p, jnp.int32)[:, None] for p in target]
+        spots.append(functools.reduce(jnp.logical_or, hit).astype(BF16))
+    spots = jnp.stack(spots)
+
     packed = pl.pallas_call(
         functools.partial(correct_pack, plan),
         out_shape=jax.ShapeDtypeStruct((heads, plan.block_rows, cols), BF16),
@@ -463,7 +452,7 @@
     return pl.pallas_call(
         functools.partial(stack, plan),
         out_shape=jax.ShapeDtypeStruct((plan.band, cols), F32),
-        in_specs=[whole()] * 6,
+        in_specs=[whole()] * 7,
         out_specs=whole(),
         scratch_shapes=[
             pltpu.VMEM((heads * maps * plan.rows, cols), F32),
@@ -476,7 +465,7 @@
         ],
         compiler_params=params,
         name="stack",
-    )(grouped, proj_weight, side_weight, kernels, vectors, mask)
+    )(grouped, proj_weight, side_weight, kernels, vectors, mask, spots)
 
 
 def solution(mesh):

time: 62.7 us -> 52.5 us (0.84)
  Pallas kernels: 22.4 us -> 12.1 us
  local copies, waits for them, and re-layouts: 3.39 us -> 2.46 us
  other arithmetic: 0.02 us -> 0.68 us
    pallas_call x1, Pallas kernels: 20.1 us -> 9.9 us  [on_device(): pl.pallas_call(functools.partial(stack, plan), out_shape=jax.ShapeDtypeSt...]
    unnamed x18 -> x22, local copies, waits for them, and re-layouts: 2.16 us -> 1.23 us
    convert_element_type x0 -> x1, other arithmetic: none -> 0.66 us  [on_device(): spots.append(functools.reduce(jnp.logical_or, hit).astype(BF16))]
  transfers between devices with their start and end apart: 2 -> 2, of which waited for: 2 -> 2; matrix products, arithmetic and copies ran while one was open for 2% -> 4% of each run, Pallas kernels for 0% -> 0%
where the time goes in v2:
time: 52.5 us; the launch traced here: 51.6 us
  waiting for transfers between devices  26.8 us (51%)
  Pallas kernels  12.1 us (23%)
  starting transfers between devices  9.31 us (18%)
  local copies, waits for them, and re-layouts  2.46 us (5%)
  other arithmetic  0.68 us (1%)
    all_to_all x1, waiting for transfers between devices, on_device(): lax.all_to_all(packed, 'head', split_axis=0, concat_axis=0, tiled=True)  18.6 us
    pallas_call x1, Pallas kernels, on_device(): pl.pallas_call(functools.partial(stack, plan), out_shape=jax.ShapeDtypeSt...  9.9 us
    ppermute x1, waiting for transfers between devices, on_device(): lax.ppermute(payload[s - 1], 'tile', [(i, (i + s) % tiles) for i in range...  8.23 us
    all_to_all x1, starting transfers between devices, on_device(): lax.all_to_all(packed, 'head', split_axis=0, concat_axis=0, tiled=True)  6.27 us
    ppermute x1, starting transfers between devices, on_device(): lax.ppermute(payload[s - 1], 'tile', [(i, (i + s) % tiles) for i in range...  3.03 us
    pallas_call x1, Pallas kernels, on_device(): pl.pallas_call(functools.partial(correct_pack, plan), out_shape=jax.Shape...  1.78 us
    unnamed x22, local copies, waits for them, and re-layouts  1.23 us
  transfers between devices with their start and end apart: 2, of which 2 were waited for; matrix products, arithmetic and copies ran while one was open for 4% of the time, Pallas kernels for 0%

profile of v2, /device:TPU:0, one launch (start us, length us, event | category | flops | bytes accessed | tf_op | source)
XLA Modules:
  0.0 51.6 jit_solution(2563503836113865698)
XLA Ops:
  0.0 0.0 copy-start
  0.0 1.1 %copy-done = bf16[9,256,128]{2,1,0:T(8,128)(2,1)S(1)} copy-done((bf16[9,256,128]{2,1,0:T(8,128)(2,1)S(1)}, bf16[9,256,128]{2,1,0:T(8,128)(2,1)}, u32[]{:S(2)}) %copy-start) | copy-done | bytes 589848
  1.1 0.5 mirror_pack.1
  1.5 3.0 %collective-permute-start = (bf16[1376,128]{1,0:T(8,128)(2,1)S(1)}, bf16[1376,128]{1,0:T(8,128)(2,1)S(1)}, u32[]{:S(2)}, u32[]{:S(2)}) collective-permute-start(bf16[1376,128]{1,0:T(8,128)(2,1)S(1)} %bitcast.16), channel_id=1, source_target_pairs={{0,1},{1,0},{2,3},{3,2},{4,5},{5,4},{6,7},{7,6},{8,9},{9,8},{10,11... | collective-permute-start | bytes 1056776 | tf_op jit(solution)/shard_map/ppermute | solution.py:406
  4.6 8.2 %collective-permute-done = bf16[1376,128]{1,0:T(8,128)(2,1)S(1)} collective-permute-done((bf16[1376,128]{1,0:T(8,128)(2,1)S(1)}, bf16[1376,128]{1,0:T(8,128)(2,1)S(1)}, u32[]{:S(2)}, u32[]{:S(2)}) %collective-permute-start) | collective-permute-done | bytes 352288 | tf_op jit(solution)/shard_map/ppermute | solution.py:406
  12.8 1.8 %correct_pack.1 = bf16[16,224,128]{2,1,0:T(8,128)(2,1)} custom-call(s32[1]{0:T(128)} %bitcast.tile_ref, bf16[9,256,128]{2,1,0:T(8,128)(2,1)S(1)} %copy-done, bf16[1,1376,128]{2,1,0:T(8,128)(2,1)S(1)} %bitcast.14, f32[16,256]{1,0:T(8,128)S(1)} %get-tuple-element.9.sums_ref, f32[40,128]{1,0:T(8,128)S(1)} %get-tuple-element.10.edge_ref), custom_call_target="tpu_custom_call" | custom-call | tf_op jit(solution)/shard_map/correct_pack/pallas_call | solution.py:438
  14.6 0.0 copy-start.3
  14.6 0.0 copy-start.4
  14.6 0.0 copy-start.5
  14.6 0.0 copy-start.9
  14.6 0.0 copy-start.1
  14.6 0.0 copy-start.2
  14.6 6.3 %all-to-all-start = ((bf16[16,224,128]{2,1,0:T(8,128)(2,1)}), bf16[16,224,128]{2,1,0:T(8,128)(2,1)S(1)}, u32[]{:S(2)}, u32[]{:S(2)}) async-start(bf16[16,224,128]{2,1,0:T(8,128)(2,1)} %correct_pack.1), calls=%async_computation | async-start | bytes 1835008 | tf_op jit(solution)/shard_map/all_to_all | solution.py:450
  20.9 0.0 copy-done.3
  20.9 0.0 copy-done.4
  21.0 0.0 copy-done.5
  21.0 0.0 copy-done.8
  21.0 0.0 copy-done.9
  21.0 0.1 copy.27
  21.1 0.0 copy-done.1
  21.1 0.1 copy.23
  21.4 0.1 copy.28.side_ref
  21.4 0.0 copy-done.2
  21.5 0.0 copy-start.6
  21.5 0.0 copy-start.7
  21.5 0.5 copy.26
  22.0 0.4 reshape.84.kernel_ref
  22.5 0.0 copy-done.6
  22.5 0.0 copy-done.7
  22.5 0.7 %fusion.1.spots_ref = bf16[1,128,4352]{2,1,0:T(8,128)(2,1)S(1)} fusion(s32[128]{0:T(128)S(1)} %copy-done.6, s32[128]{0:T(128)S(1)} %copy-done.7), kind=kLoop, calls=%fused_computation.3 | loop fusion | flops 2228224 | bytes 1115136 | tf_op jit(solution)/shard_map/convert_element_type | solution.py:435
  23.1 18.6 %all-to-all-done.recv_ref = bf16[16,224,128]{2,1,0:T(8,128)(2,1)S(1)} async-done(((bf16[16,224,128]{2,1,0:T(8,128)(2,1)}), bf16[16,224,128]{2,1,0:T(8,128)(2,1)S(1)}, u32[]{:S(2)}, u32[]{:S(2)}) %all-to-all-start) | async-done | bytes 917536 | tf_op jit(solution)/shard_map/all_to_all | solution.py:450
  41.7 9.9 %stack.6 = f32[16,128]{1,0:T(8,128)} custom-call(bf16[16,224,128]{2,1,0:T(8,128)(2,1)S(1)} %all-to-all-done.recv_ref, bf16[64,144]{1,0:T(8,128)(2,1)S(1)} %copy-done.1, bf16[64,160]{1,0:T(8,128)(2,1)S(1)} %copy.28.side_ref, bf16[4,192,192]{2,1,0:T(8,128)(2,1)S(1)} %reshape.84.kernel_ref, f32[64,6]{1,0:T(8,128)S(1)} %bitcast.15, ...), custom_call_target="tpu_custom_call" | custom-call | tf_op jit(solution)/shard_map/stack/pallas_call | solution.py:452
  (8 shorter events, 0.1 us)
Async XLA Ops:
  0.0 1.1 %copy-start = (bf16[9,256,128]{2,1,0:T(8,128)(2,1)S(1)}, bf16[9,256,128]{2,1,0:T(8,128)(2,1)}, u32[]{:S(2)}) copy-start(bf16[9,256,128]{2,1,0:T(8,128)(2,1)} %maps_ref.3) | copy-start | bytes 1769476
  1.5 11.3 %collective-permute-start = (bf16[1376,128]{1,0:T(8,128)(2,1)S(1)}, bf16[1376,128]{1,0:T(8,128)(2,1)S(1)}, u32[]{:S(2)}, u32[]{:S(2)}) collective-permute-start(bf16[1376,128]{1,0:T(8,128)(2,1)S(1)} %bitcast.16), channel_id=1, source_target_pairs={{0,1},{1,0},{2,3},{3,2},{4,5},{5,4},{6,7},{7,6},{8,9},{9,8},{10,11... | collective-permute-start | bytes 1056776 | tf_op jit(solution)/shard_map/ppermute | solution.py:406
  14.6 6.3 %copy-start.3 = (s32[4352]{0:T(1024)S(1)}, s32[4352]{0:T(1024)}, u32[]{:S(2)}) copy-start(s32[4352]{0:T(1024)} %constant.32.clone) | copy-start | bytes 52228
  14.6 6.3 %copy-start.4 = (s32[4352]{0:T(1024)S(1)}, s32[4352]{0:T(1024)}, u32[]{:S(2)}) copy-start(s32[4352]{0:T(1024)} %constant.31.clone) | copy-start | bytes 52228
  14.6 6.4 %copy-start.5 = (f32[2,2,64]{2,1,0:T(2,128)S(1)}, f32[2,2,64]{2,1,0:T(2,128)}, u32[]{:S(2)}) copy-start(f32[2,2,64]{2,1,0:T(2,128)} %param.14) | copy-start | bytes 3076
  14.6 6.4 %copy-start.8 = (f32[64]{0:T(128)S(1)}, f32[64]{0:T(128)}, u32[]{:S(2)}) copy-start(f32[64]{0:T(128)} %param.15) | copy-start | bytes 772
  14.6 6.4 %copy-start.9 = (f32[64]{0:T(128)S(1)}, f32[64]{0:T(128)}, u32[]{:S(2)}) copy-start(f32[64]{0:T(128)} %param.12) | copy-start | bytes 772
  14.6 6.5 %copy-start.1 = (bf16[64,144]{1,0:T(8,128)(2,1)S(1)}, bf16[64,144]{1,0:T(8,128)(2,1)}, u32[]{:S(2)}) copy-start(bf16[64,144]{1,0:T(8,128)(2,1)} %proj_ref.1) | copy-start | bytes 55300
  14.6 6.8 %copy-start.2 = (bf16[2,2,64,64,3,3]{3,2,5,4,1,0:T(8,128)(2,1)S(1)}, bf16[2,2,64,64,3,3]{3,2,5,4,1,0:T(8,128)(2,1)}, u32[]{:S(2)}) copy-start(bf16[2,2,64,64,3,3]{3,2,5,4,1,0:T(8,128)(2,1)} %param.13) | copy-start | bytes 884740
  14.6 27.1 %all-to-all-start = ((bf16[16,224,128]{2,1,0:T(8,128)(2,1)}), bf16[16,224,128]{2,1,0:T(8,128)(2,1)S(1)}, u32[]{:S(2)}, u32[]{:S(2)}) async-start(bf16[16,224,128]{2,1,0:T(8,128)(2,1)} %correct_pack.1), calls=%async_computation | async-start | bytes 1835008 | tf_op jit(solution)/shard_map/all_to_all | solution.py:450
  21.5 1.0 %copy-start.6 = (s32[128]{0:T(128)S(1)}, s32[128]{0:T(128)}, u32[]{:S(2)}) copy-start(s32[128]{0:T(128)} %constant.34.clone) | copy-start | bytes 1540
  21.5 1.0 %copy-start.7 = (s32[128]{0:T(128)S(1)}, s32[128]{0:T(128)}, u32[]{:S(2)}) copy-start(s32[128]{0:T(128)} %constant.33.clone) | copy-start | bytes 1540

commit v3 on v2

--- a/solution.py
+++ b/solution.py
@@ -90,6 +90,12 @@
     @property
     def lanes(self):
         return up(self.start + self.rows * self.stride, LANES) + 2 * self.chunk + 3 * LANES
+
+
+def partner(mine, step, count, back=False):
+    if count & (count - 1) == 0:
+        return mine ^ step
+    return (mine - step if back else mine + step) % count
 
 
 def edge_start(plan, tile, side):
@@ -166,10 +172,9 @@
         out_ref[shift - 1, count * cols :, :] = jnp.concatenate(pieces, axis=0).astype(BF16)
 
 
-def correct_pack(
-    plan, tile_ref, maps_ref, recv_ref, sums_ref, edge_ref, out_ref, field_ref, turned_ref
-):
-    me = tile_ref[0]
+def correct_pack(plan, tile_ref, maps_ref, recv_ref, sums_ref, edge_ref, *refs):
+    *out_refs, field_ref, turned_ref = refs
+    me, band_index = tile_ref[0], tile_ref[1]
     count, cols, width, tiles = plan.maps, plan.cols, plan.width, plan.tiles
     head, edge, halo = plan.map_rows, plan.edge_rows, plan.halo
     tails = [recv_ref[k, count * cols :, :].astype(F32) for k in range(tiles - 1)]
@@ -199,10 +204,10 @@
         lax.broadcasted_iota(jnp.int32, (cols, cols), 0)
         == lax.broadcasted_iota(jnp.int32, (cols, cols), 1)
     ).astype(F32).astype(BF16)
-    margin = 8
+    margin = 8 + halo
     for index in range(count):
-        field_ref[index, :margin, :] = jnp.zeros((margin, cols), F32)
-        field_ref[index, margin + width :, :] = jnp.zeros((margin, cols), F32)
+        field_ref[index, :16, :] = jnp.zeros((16, cols), F32)
+        field_ref[index, width + 8 :, :] = jnp.zeros((16, cols), F32)
         for b in range(tiles):
             shift = lax.rem(b - me + tiles, tiles)
             other = recv_ref[
@@ -247,17 +252,18 @@
         stacks.append(jnp.concatenate(members, axis=0))
     lane = lax.broadcasted_iota(jnp.int32, (plan.side_rows, cols), 1)
     spare = plan.block_rows - count * rows - plan.side_rows
-    for h in range(plan.heads):
-        first = h * plan.band - halo
-        pieces = [field_ref[k, margin + first : margin + first + rows, :] for k in range(count)]
+    for step, out_ref in enumerate(out_refs):
+        first = partner(band_index, step, plan.heads) * plan.band
+        pieces = [field_ref[k, pl.ds(pl.multiple_of(first + 8, 8), rows), :] for k in range(count)]
         side = jnp.zeros((plan.side_rows, cols), F32)
         for slot in range(slots):
-            moved = pltpu.roll(stacks[slot], (slot * rows - first) % width, 1)[:, :cols]
+            amount = lax.rem(slot * rows + halo + width - first, width)
+            moved = pltpu.roll(stacks[slot], amount, 1)[:, :cols]
             side = jnp.where((lane >= slot * rows) & (lane < (slot + 1) * rows), moved, side)
         pieces.append(side)
         if spare:
             pieces.append(jnp.zeros((spare, cols), F32))
-        out_ref[h] = jnp.concatenate(pieces, axis=0).astype(BF16)
+        out_ref[...] = jnp.concatenate(pieces, axis=0).astype(BF16)
 
 
 def shifted(ref, rows, base, offset, size):
@@ -269,17 +275,18 @@
     return pltpu.roll(ref[rows, low : low + size + LANES], size + LANES - rest, 1)[:, :size]
 
 
-def stack(
-    plan, recv_ref, proj_ref, side_ref, kernel_ref, vector_ref, mask_ref, spots_ref, out_ref,
-    maps_ref, sides_ref, field_ref, stream_ref, hidden_ref, taps_ref, logit_ref,
-):
+def stack(plan, tile_ref, *refs):
+    recv_refs, refs = refs[: plan.heads], refs[plan.heads :]
+    proj_ref, side_ref, kernel_ref, vector_ref, mask_ref, spots_ref, out_ref = refs[:7]
+    maps_ref, sides_ref, field_ref, stream_ref, hidden_ref, taps_ref, logit_ref = refs[7:]
     count, cols, rows, halo = plan.maps, plan.cols, plan.rows, plan.halo
     heads, feat, chunk, stride = plan.heads, plan.feat, plan.chunk, plan.stride
     body = count * rows
-    for s in range(heads):
-        block = recv_ref[s].astype(F32)
-        maps_ref[s * body : (s + 1) * body, :] = block[:body]
-        sides_ref[s * plan.side_rows : (s + 1) * plan.side_rows, :] = block[
+    for step, recv_ref in enumerate(recv_refs):
+        block = recv_ref[...].astype(F32)
+        s = partner(tile_ref[1], step, heads, back=True)
+        maps_ref[pl.ds(pl.multiple_of(s * body, 8), body), :] = block[:body]
+        sides_ref[pl.ds(pl.multiple_of(s * plan.side_rows, 8), plan.side_rows), :] = block[
             body : body + plan.side_rows
         ]
     bias = vector_ref[:, 0:1]
@@ -385,7 +392,8 @@
     tiles, heads = lax.axis_size("tile"), lax.axis_size("head")
     plan = Plan(maps, width, cols, tiles, heads, feat, blocks * convs)
     me = lax.axis_index("tile").astype(jnp.int32)
-    tile = me.reshape(1)
+    band_index = lax.axis_index("head").astype(jnp.int32)
+    tile = jnp.stack([me, band_index])
     params = pltpu.CompilerParams(vmem_limit_bytes=VMEM_LIMIT)
 
     payload_rows = maps * cols + plan.tail_rows
@@ -418,7 +426,7 @@
         [proj_bias[None], conv_bias.reshape(-1, feat), out_weight[None]], axis=0
     ).T
     spot = np.arange(plan.lanes) - start
-    row = lax.axis_index("head") * plan.band - plan.halo + (spot // stride).astype(np.int32)
+    row = band_index * plan.band - plan.halo + (spot // stride).astype(np.int32)
     col = me * cols - plan.halo + (spot % stride).astype(np.int32)
     mask = (row >= 0) & (row < width) & (col >= 0) & (col < width)
     mask = mask.astype(F32)[None]
@@ -435,24 +443,27 @@
         spots.append(functools.reduce(jnp.logical_or, hit).astype(BF16))
     spots = jnp.stack(spots)
 
-    packed = pl.pallas_call(
+    blocks = pl.pallas_call(
         functools.partial(correct_pack, plan),
-        out_shape=jax.ShapeDtypeStruct((heads, plan.block_rows, cols), BF16),
+        out_shape=[jax.ShapeDtypeStruct((plan.block_rows, cols), BF16)] * heads,
         in_specs=[whole(pltpu.SMEM)] + [whole()] * 4,
-        out_specs=whole(),
+        out_specs=[whole()] * heads,
         scratch_shapes=[
-            pltpu.VMEM((maps, width + 16, cols), F32),
+            pltpu.VMEM((maps, width + 24, cols), F32),
             pltpu.VMEM((width, LANES), F32),
         ],
         compiler_params=params,
         name="correct_pack",
     )(tile, attention, received, sums, edge)
-    grouped = lax.all_to_all(packed, "head", split_axis=0, concat_axis=0, tiled=True)
+    grouped = list(blocks)
+    for step in sorted(range(1, heads), key=lambda k: -k):
+        pairs = [(i, partner(i, step, heads)) for i in range(heads)]
+        grouped[step] = lax.ppermute(blocks[step], "head", pairs)
 
     return pl.pallas_call(
         functools.partial(stack, plan),
         out_shape=jax.ShapeDtypeStruct((plan.band, cols), F32),
-        in_specs=[whole()] * 7,
+        in_specs=[whole(pltpu.SMEM)] + [whole()] * (heads + 6),
         out_specs=whole(),
         scratch_shapes=[
             pltpu.VMEM((heads * maps * plan.rows, cols), F32),
@@ -465,7 +476,7 @@
         ],
         compiler_params=params,
         name="stack",
-    )(grouped, proj_weight, side_weight, kernels, vectors, mask, spots)
+    )(tile, *grouped, proj_weight, side_weight, kernels, vectors, mask, spots)
 
 
 def solution(mesh):

time: 52.5 us -> 56.2 us (1.070)
  starting transfers between devices: 9.31 us -> 27.8 us
  waiting for transfers between devices: 26.8 us -> 8.82 us
  local copies, waits for them, and re-layouts: 2.46 us -> 4.58 us
  Pallas kernels: 12.1 us -> 13.1 us
    ppermute x0 -> x15, starting transfers between devices: none -> 24.7 us  [on_device(): grouped[step] = lax.ppermute(blocks[step], 'head', pairs)]
    all_to_all x1 -> x0, waiting for transfers between devices: 18.6 us -> none  [on_device(): lax.all_to_all(packed, 'head', split_axis=0, concat_axis=0, tiled=True)]
    all_to_all x1 -> x0, starting transfers between devices: 6.27 us -> none  [on_device(): lax.all_to_all(packed, 'head', split_axis=0, concat_axis=0, tiled=True)]
    reshape x1, local copies, waits for them, and re-layouts: 0.45 us -> 1.69 us  [on_device(): conv_weight.transpose(0, 1, 5, 2, 4, 3)]
    transpose x1, local copies, waits for them, and re-layouts: 0.51 us -> 1.4 us  [on_device(): conv_weight.transpose(0, 1, 5, 2, 4, 3)]
    ppermute x0 -> x15, waiting for transfers between devices: none -> 0.58 us  [on_device(): grouped[step] = lax.ppermute(blocks[step], 'head', pairs)]
    pallas_call x1, Pallas kernels: 9.9 us -> 10.5 us  [on_device(): pl.pallas_call(functools.partial(stack, plan), out_shape=jax.ShapeDtypeSt...]
  transfers between devices with their start and end apart: 2 -> 16, of which waited for: 2 -> 3; matrix products, arithmetic and copies ran while one was open for 4% -> 8% of each run, Pallas kernels for 0% -> 0%
where the time goes in v3:
time: 56.2 us; the launch traced here: 55.2 us
  starting transfers between devices  27.8 us (49%)
  Pallas kernels  13.1 us (23%)
  waiting for transfers between devices  8.82 us (16%)
  local copies, waits for them, and re-layouts  4.58 us (8%)
  other arithmetic  0.75 us (1%)
    ppermute x15, starting transfers between devices, on_device(): grouped[step] = lax.ppermute(blocks[step], 'head', pairs)  24.7 us
    pallas_call x1, Pallas kernels, on_device(): pl.pallas_call(functools.partial(stack, plan), out_shape=jax.ShapeDtypeSt...  10.5 us
    ppermute x1, waiting for transfers between devices, on_device(): lax.ppermute(payload[s - 1], 'tile', [(i, (i + s) % tiles) for i in range...  8.24 us
    ppermute x1, starting transfers between devices, on_device(): lax.ppermute(payload[s - 1], 'tile', [(i, (i + s) % tiles) for i in range...  3.03 us
    reshape x1, local copies, waits for them, and re-layouts, on_device(): conv_weight.transpose(0, 1, 5, 2, 4, 3)  1.69 us
    pallas_call x1, Pallas kernels, on_device(): pl.pallas_call(functools.partial(correct_pack, plan), out_shape=[jax.Shap...  1.61 us
    transpose x1, local copies, waits for them, and re-layouts, on_device(): conv_weight.transpose(0, 1, 5, 2, 4, 3)  1.4 us
    unnamed x22, local copies, waits for them, and re-layouts  1.22 us
  transfers between devices with their start and end apart: 16, of which 3 were waited for; matrix products, arithmetic and copies ran while one was open for 8% of the time, Pallas kernels for 0%

profile of v3, /device:TPU:0, one launch (start us, length us, event | category | flops | bytes accessed | tf_op | source)
XLA Modules:
  0.0 55.2 jit_solution(7497825520891188939)
XLA Ops:
  0.0 0.1 pad_add_fusion.tile_ref
  0.1 1.1 %copy-done = bf16[9,256,128]{2,1,0:T(8,128)(2,1)S(1)} copy-done((bf16[9,256,128]{2,1,0:T(8,128)(2,1)S(1)}, bf16[9,256,128]{2,1,0:T(8,128)(2,1)}, u32[]{:S(2)}) %copy-start) | copy-done | bytes 589848
  1.1 1.0 %mirror_pack.1 = (bf16[1,1376,128]{2,1,0:T(8,128)(2,1)S(1)}, f32[16,256]{1,0:T(8,128)S(1)}, f32[40,128]{1,0:T(8,128)S(1)}) custom-call(s32[2]{0:T(128)S(1)} %pad_add_fusion.tile_ref, bf16[9,256,128]{2,1,0:T(8,128)(2,1)S(1)} %copy-done), custom_call_target="tpu_custom_call" | custom-call | tf_op jit(solution)/shard_map/mirror_pack/pallas_call | solution.py:400
  2.1 0.0 copy-start.3
  2.2 0.0 copy-start.4
  2.2 3.0 %collective-permute-start = (bf16[1376,128]{1,0:T(8,128)(2,1)S(1)}, bf16[1376,128]{1,0:T(8,128)(2,1)S(1)}, u32[]{:S(2)}, u32[]{:S(2)}) collective-permute-start(bf16[1376,128]{1,0:T(8,128)(2,1)S(1)} %bitcast.17), channel_id=1, source_target_pairs={{0,1},{1,0},{2,3},{3,2},{4,5},{5,4},{6,7},{7,6},{8,9},{9,8},{10,11... | collective-permute-start | bytes 1056776 | tf_op jit(solution)/shard_map/ppermute | solution.py:414
  5.2 8.2 %collective-permute-done = bf16[1376,128]{1,0:T(8,128)(2,1)S(1)} collective-permute-done((bf16[1376,128]{1,0:T(8,128)(2,1)S(1)}, bf16[1376,128]{1,0:T(8,128)(2,1)S(1)}, u32[]{:S(2)}, u32[]{:S(2)}) %collective-permute-start) | collective-permute-done | bytes 352288 | tf_op jit(solution)/shard_map/ppermute | solution.py:414
  13.5 1.6 %correct_pack.1 = (bf16[224,128]{1,0:T(8,128)(2,1)S(1)}, bf16[224,128]{1,0:T(8,128)(2,1)S(1)}, bf16[224,128]{1,0:T(8,128)(2,1)S(1)}, bf16[224,128]{1,0:T(8,128)(...) custom-call(s32[2]{0:T(128)S(1)} %pad_add_fusion.tile_ref, ...), custom_call_target="tpu_custom_call" | custom-call | tf_op jit(solution)/shard_map/correct_pack/pallas_call | solution.py:446
  15.1 0.0 copy-start.2
  15.1 0.1 collective-permute-start.1
  15.2 1.8 %collective-permute-start.2 = (bf16[224,128]{1,0:T(8,128)(2,1)S(1)}, bf16[224,128]{1,0:T(8,128)(2,1)S(1)}, u32[]{:S(2)}, u32[]{:S(2)}) collective-permute-start(bf16[224,128]{1,0:T(8,128)(2,1)S(1)} %get-tuple-element.29), channel_id=1, source_target_pairs={{0,4},{2,6},{4,0},{6,2},{8,12},{10,14},{12,8},{14,10},{16,20},{18,... | collective-permute-start | bytes 172040 | tf_op jit(solution)/shard_map/ppermute | solution.py:461
  16.9 0.1 collective-permute-start.3
  17.0 1.8 %collective-permute-start.4 = (bf16[224,128]{1,0:T(8,128)(2,1)S(1)}, bf16[224,128]{1,0:T(8,128)(2,1)S(1)}, u32[]{:S(2)}, u32[]{:S(2)}) collective-permute-start(bf16[224,128]{1,0:T(8,128)(2,1)S(1)} %get-tuple-element.31), channel_id=1, source_target_pairs={{0,8},{2,10},{4,12},{6,14},{8,0},{10,2},{12,4},{14,6},{16,24},{18,... | collective-permute-start | bytes 172040 | tf_op jit(solution)/shard_map/ppermute | solution.py:461
  18.8 0.7 %fusion.1.refs_21_ = bf16[1,128,4352]{2,1,0:T(8,128)(2,1)S(1)} fusion(s32[128]{0:T(128)S(1)} %copy-done.6, s32[128]{0:T(128)S(1)} %copy-done.7), kind=kLoop, calls=%fused_computation.3 | loop fusion | flops 2228224 | bytes 1115136 | tf_op jit(solution)/shard_map/convert_element_type | solution.py:443
  19.5 2.7 %collective-permute-start.6 = (bf16[224,128]{1,0:T(8,128)(2,1)S(1)}, bf16[224,128]{1,0:T(8,128)(2,1)S(1)}, u32[]{:S(2)}, u32[]{:S(2)}) collective-permute-start(bf16[224,128]{1,0:T(8,128)(2,1)S(1)} %get-tuple-element.33), channel_id=1, source_target_pairs={{0,12},{2,14},{4,8},{6,10},{8,4},{10,6},{12,0},{14,2},{16,28},{18,... | collective-permute-start | bytes 172040 | tf_op jit(solution)/shard_map/ppermute | solution.py:461
  22.2 0.1 collective-permute-start.7
  22.3 2.7 %collective-permute-start.8 = (bf16[224,128]{1,0:T(8,128)(2,1)S(1)}, bf16[224,128]{1,0:T(8,128)(2,1)S(1)}, u32[]{:S(2)}, u32[]{:S(2)}) collective-permute-start(bf16[224,128]{1,0:T(8,128)(2,1)S(1)} %get-tuple-element.35), channel_id=1, source_target_pairs={{0,16},{2,18},{4,20},{6,22},{8,24},{10,26},{12,28},{14,30},{16,0},... | collective-permute-start | bytes 172040 | tf_op jit(solution)/shard_map/ppermute | solution.py:461
  25.0 0.0 collective-permute-start.9
  25.1 3.5 %collective-permute-start.10 = (bf16[224,128]{1,0:T(8,128)(2,1)S(1)}, bf16[224,128]{1,0:T(8,128)(2,1)S(1)}, u32[]{:S(2)}, u32[]{:S(2)}) collective-permute-start(bf16[224,128]{1,0:T(8,128)(2,1)S(1)} %get-tuple-element.37), channel_id=1, source_target_pairs={{0,20},{2,22},{4,16},{6,18},{8,28},{10,30},{12,24},{14,26},{16,4},... | collective-permute-start | bytes 172040 | tf_op jit(solution)/shard_map/ppermute | solution.py:461
  28.6 0.1 collective-permute-start.11
  28.7 3.6 %collective-permute-start.12 = (bf16[224,128]{1,0:T(8,128)(2,1)S(1)}, bf16[224,128]{1,0:T(8,128)(2,1)S(1)}, u32[]{:S(2)}, u32[]{:S(2)}) collective-permute-start(bf16[224,128]{1,0:T(8,128)(2,1)S(1)} %get-tuple-element.39), channel_id=1, source_target_pairs={{0,24},{2,26},{4,28},{6,30},{8,16},{10,18},{12,20},{14,22},{16,8},... | collective-permute-start | bytes 172040 | tf_op jit(solution)/shard_map/ppermute | solution.py:461
  32.3 0.8 %collective-permute-start.13 = (bf16[224,128]{1,0:T(8,128)(2,1)S(1)}, bf16[224,128]{1,0:T(8,128)(2,1)S(1)}, u32[]{:S(2)}, u32[]{:S(2)}) collective-permute-start(bf16[224,128]{1,0:T(8,128)(2,1)S(1)} %get-tuple-element.40), channel_id=1, source_target_pairs={{0,26},{2,24},{4,30},{6,28},{8,18},{10,16},{12,22},{14,20},{16,10}... | collective-permute-start | bytes 172040 | tf_op jit(solution)/shard_map/ppermute | solution.py:461
  33.1 0.2 collective-permute-done.9.refs_9_
  33.3 4.7 %collective-permute-start.14 = (bf16[224,128]{1,0:T(8,128)(2,1)S(1)}, bf16[224,128]{1,0:T(8,128)(2,1)S(1)}, u32[]{:S(2)}, u32[]{:S(2)}) collective-permute-start(bf16[224,128]{1,0:T(8,128)(2,1)S(1)} %get-tuple-element.41), channel_id=1, source_target_pairs={{0,28},{2,30},{4,24},{6,26},{8,20},{10,22},{12,16},{14,18},{16,12}... | collective-permute-start | bytes 172040 | tf_op jit(solution)/shard_map/ppermute | solution.py:461
  38.0 2.8 %collective-permute-start.15 = (bf16[224,128]{1,0:T(8,128)(2,1)S(1)}, bf16[224,128]{1,0:T(8,128)(2,1)S(1)}, u32[]{:S(2)}, u32[]{:S(2)}) collective-permute-start(bf16[224,128]{1,0:T(8,128)(2,1)S(1)} %get-tuple-element.42), channel_id=1, source_target_pairs={{0,30},{2,28},{4,26},{6,24},{8,22},{10,20},{12,18},{14,16},{16,14}... | collective-permute-start | bytes 172040 | tf_op jit(solution)/shard_map/ppermute | solution.py:461
  40.8 0.1 copy.27
  40.9 0.1 copy.23
  41.1 0.1 copy.28.refs_17_
  41.2 1.4 %copy.26 = bf16[2,2,3,64,3,64]{5,4,3,2,1,0:T(4,128)(2,1)} copy(bf16[2,2,3,64,3,64]{5,3,2,4,1,0:T(8,128)(2,1)S(1)} %bitcast.18) | data formatting | bytes 589824 | tf_op jit(solution)/shard_map/transpose | solution.py:424
  42.6 1.7 %reshape.80.refs_18_ = bf16[4,192,192]{2,1,0:T(8,128)(2,1)S(1)} reshape(bf16[2,2,3,64,3,64]{5,4,3,2,1,0:T(4,128)(2,1)} %copy.26) | data formatting | bytes 589824 | tf_op jit(solution)/shard_map/reshape | solution.py:424
  44.4 0.4 collective-permute-done.15.refs_15_
  44.7 10.5 %stack.18 = f32[16,128]{1,0:T(8,128)} custom-call(s32[2]{0:T(128)S(1)} %pad_add_fusion.tile_ref, bf16[224,128]{1,0:T(8,128)(2,1)S(1)} %get-tuple-element.27.refs_0_, bf16[224,128]{1,0:T(8,128)(2,1)S(1)} %collective-permute-done.1.refs_1_, bf16[224,128]{1,0:T(8,128)(2,1)S(1)} %collective-permute-done.2.refs_2_, ...), custom_call_target="tpu_custom_call" | custom-call | tf_op jit(solution)/shard_map/stack/pallas_call | solution.py:463
  (37 shorter events, 0.2 us)
Async XLA Ops:
  0.0 18.8 %copy-start.6 = (s32[128]{0:T(128)S(1)}, s32[128]{0:T(128)}, u32[]{:S(2)}) copy-start(s32[128]{0:T(128)} %constant.34.clone) | copy-start | bytes 1540
  0.0 18.8 %copy-start.7 = (s32[128]{0:T(128)S(1)}, s32[128]{0:T(128)}, u32[]{:S(2)}) copy-start(s32[128]{0:T(128)} %constant.33.clone) | copy-start | bytes 1540
  0.1 1.1 %copy-start = (bf16[9,256,128]{2,1,0:T(8,128)(2,1)S(1)}, bf16[9,256,128]{2,1,0:T(8,128)(2,1)}, u32[]{:S(2)}) copy-start(bf16[9,256,128]{2,1,0:T(8,128)(2,1)} %maps_ref.3) | copy-start | bytes 1769476
  2.1 26.4 %copy-start.3 = (s32[4352]{0:T(1024)S(1)}, s32[4352]{0:T(1024)}, u32[]{:S(2)}) copy-start(s32[4352]{0:T(1024)} %constant.32.clone) | copy-start | bytes 52228
  2.2 26.4 %copy-start.4 = (s32[4352]{0:T(1024)S(1)}, s32[4352]{0:T(1024)}, u32[]{:S(2)}) copy-start(s32[4352]{0:T(1024)} %constant.31.clone) | copy-start | bytes 52228
  2.2 11.3 %collective-permute-start = (bf16[1376,128]{1,0:T(8,128)(2,1)S(1)}, bf16[1376,128]{1,0:T(8,128)(2,1)S(1)}, u32[]{:S(2)}, u32[]{:S(2)}) collective-permute-start(bf16[1376,128]{1,0:T(8,128)(2,1)S(1)} %bitcast.17), channel_id=1, source_target_pairs={{0,1},{1,0},{2,3},{3,2},{4,5},{5,4},{6,7},{7,6},{8,9},{9,8},{10,11... | collective-permute-start | bytes 1056776 | tf_op jit(solution)/shard_map/ppermute | solution.py:414
  13.4 27.3 %copy-start.5 = (f32[2,2,64]{2,1,0:T(2,128)S(1)}, f32[2,2,64]{2,1,0:T(2,128)}, u32[]{:S(2)}) copy-start(f32[2,2,64]{2,1,0:T(2,128)} %param.14) | copy-start | bytes 3076
  13.4 27.3 %copy-start.8 = (f32[64]{0:T(128)S(1)}, f32[64]{0:T(128)}, u32[]{:S(2)}) copy-start(f32[64]{0:T(128)} %param.15) | copy-start | bytes 772
  13.4 27.3 %copy-start.9 = (f32[64]{0:T(128)S(1)}, f32[64]{0:T(128)}, u32[]{:S(2)}) copy-start(f32[64]{0:T(128)} %param.12) | copy-start | bytes 772
  13.4 27.4 %copy-start.1 = (bf16[64,144]{1,0:T(8,128)(2,1)S(1)}, bf16[64,144]{1,0:T(8,128)(2,1)}, u32[]{:S(2)}) copy-start(bf16[64,144]{1,0:T(8,128)(2,1)} %refs_16_.1) | copy-start | bytes 55300
  15.1 26.1 %copy-start.2 = (bf16[2,2,64,64,3,3]{3,2,5,4,1,0:T(8,128)(2,1)S(1)}, bf16[2,2,64,64,3,3]{3,2,5,4,1,0:T(8,128)(2,1)}, u32[]{:S(2)}) copy-start(bf16[2,2,64,64,3,3]{3,2,5,4,1,0:T(8,128)(2,1)} %param.13) | copy-start | bytes 884740
  15.1 4.4 %collective-permute-start.1 = (bf16[224,128]{1,0:T(8,128)(2,1)S(1)}, bf16[224,128]{1,0:T(8,128)(2,1)S(1)}, u32[]{:S(2)}, u32[]{:S(2)}) collective-permute-start(bf16[224,128]{1,0:T(8,128)(2,1)S(1)} %get-tuple-element.28), channel_id=1, source_target_pairs={{0,2},{2,0},{4,6},{6,4},{8,10},{10,8},{12,14},{14,12},{16,18},{18,... | collective-permute-start | bytes 172040 | tf_op jit(solution)/shard_map/ppermute | solution.py:461
  15.2 7.0 %collective-permute-start.2 = (bf16[224,128]{1,0:T(8,128)(2,1)S(1)}, bf16[224,128]{1,0:T(8,128)(2,1)S(1)}, u32[]{:S(2)}, u32[]{:S(2)}) collective-permute-start(bf16[224,128]{1,0:T(8,128)(2,1)S(1)} %get-tuple-element.29), channel_id=1, source_target_pairs={{0,4},{2,6},{4,0},{6,2},{8,12},{10,14},{12,8},{14,10},{16,20},{18,... | collective-permute-start | bytes 172040 | tf_op jit(solution)/shard_map/ppermute | solution.py:461
  16.9 5.4 %collective-permute-start.3 = (bf16[224,128]{1,0:T(8,128)(2,1)S(1)}, bf16[224,128]{1,0:T(8,128)(2,1)S(1)}, u32[]{:S(2)}, u32[]{:S(2)}) collective-permute-start(bf16[224,128]{1,0:T(8,128)(2,1)S(1)} %get-tuple-element.30), channel_id=1, source_target_pairs={{0,6},{2,4},{4,2},{6,0},{8,14},{10,12},{12,10},{14,8},{16,22},{18,... | collective-permute-start | bytes 172040 | tf_op jit(solution)/shard_map/ppermute | solution.py:461
  17.0 8.0 %collective-permute-start.4 = (bf16[224,128]{1,0:T(8,128)(2,1)S(1)}, bf16[224,128]{1,0:T(8,128)(2,1)S(1)}, u32[]{:S(2)}, u32[]{:S(2)}) collective-permute-start(bf16[224,128]{1,0:T(8,128)(2,1)S(1)} %get-tuple-element.31), channel_id=1, source_target_pairs={{0,8},{2,10},{4,12},{6,14},{8,0},{10,2},{12,4},{14,6},{16,24},{18,... | collective-permute-start | bytes 172040 | tf_op jit(solution)/shard_map/ppermute | solution.py:461
  18.8 6.2 %collective-permute-start.5 = (bf16[224,128]{1,0:T(8,128)(2,1)S(1)}, bf16[224,128]{1,0:T(8,128)(2,1)S(1)}, u32[]{:S(2)}, u32[]{:S(2)}) collective-permute-start(bf16[224,128]{1,0:T(8,128)(2,1)S(1)} %get-tuple-element.32), channel_id=1, source_target_pairs={{0,10},{2,8},{4,14},{6,12},{8,2},{10,0},{12,6},{14,4},{16,26},{18,... | collective-permute-start | bytes 172040 | tf_op jit(solution)/shard_map/ppermute | solution.py:461
  19.5 9.0 %collective-permute-start.6 = (bf16[224,128]{1,0:T(8,128)(2,1)S(1)}, bf16[224,128]{1,0:T(8,128)(2,1)S(1)}, u32[]{:S(2)}, u32[]{:S(2)}) collective-permute-start(bf16[224,128]{1,0:T(8,128)(2,1)S(1)} %get-tuple-element.33), channel_id=1, source_target_pairs={{0,12},{2,14},{4,8},{6,10},{8,4},{10,6},{12,0},{14,2},{16,28},{18,... | collective-permute-start | bytes 172040 | tf_op jit(solution)/shard_map/ppermute | solution.py:461
  22.2 6.5 %collective-permute-start.7 = (bf16[224,128]{1,0:T(8,128)(2,1)S(1)}, bf16[224,128]{1,0:T(8,128)(2,1)S(1)}, u32[]{:S(2)}, u32[]{:S(2)}) collective-permute-start(bf16[224,128]{1,0:T(8,128)(2,1)S(1)} %get-tuple-element.34), channel_id=1, source_target_pairs={{0,14},{2,12},{4,10},{6,8},{8,6},{10,4},{12,2},{14,0},{16,30},{18,... | collective-permute-start | bytes 172040 | tf_op jit(solution)/shard_map/ppermute | solution.py:461
  22.3 10.0 %collective-permute-start.8 = (bf16[224,128]{1,0:T(8,128)(2,1)S(1)}, bf16[224,128]{1,0:T(8,128)(2,1)S(1)}, u32[]{:S(2)}, u32[]{:S(2)}) collective-permute-start(bf16[224,128]{1,0:T(8,128)(2,1)S(1)} %get-tuple-element.35), channel_id=1, source_target_pairs={{0,16},{2,18},{4,20},{6,22},{8,24},{10,26},{12,28},{14,30},{16,0},... | collective-permute-start | bytes 172040 | tf_op jit(solution)/shard_map/ppermute | solution.py:461
  25.0 8.3 %collective-permute-start.9 = (bf16[224,128]{1,0:T(8,128)(2,1)S(1)}, bf16[224,128]{1,0:T(8,128)(2,1)S(1)}, u32[]{:S(2)}, u32[]{:S(2)}) collective-permute-start(bf16[224,128]{1,0:T(8,128)(2,1)S(1)} %get-tuple-element.36), channel_id=1, source_target_pairs={{0,18},{2,16},{4,22},{6,20},{8,26},{10,24},{12,30},{14,28},{16,2},... | collective-permute-start | bytes 172040 | tf_op jit(solution)/shard_map/ppermute | solution.py:461
  25.1 12.9 %collective-permute-start.10 = (bf16[224,128]{1,0:T(8,128)(2,1)S(1)}, bf16[224,128]{1,0:T(8,128)(2,1)S(1)}, u32[]{:S(2)}, u32[]{:S(2)}) collective-permute-start(bf16[224,128]{1,0:T(8,128)(2,1)S(1)} %get-tuple-element.37), channel_id=1, source_target_pairs={{0,20},{2,22},{4,16},{6,18},{8,28},{10,30},{12,24},{14,26},{16,4},... | collective-permute-start | bytes 172040 | tf_op jit(solution)/shard_map/ppermute | solution.py:461
  28.6 15.8 %collective-permute-start.11 = (bf16[224,128]{1,0:T(8,128)(2,1)S(1)}, bf16[224,128]{1,0:T(8,128)(2,1)S(1)}, u32[]{:S(2)}, u32[]{:S(2)}) collective-permute-start(bf16[224,128]{1,0:T(8,128)(2,1)S(1)} %get-tuple-element.38), channel_id=1, source_target_pairs={{0,22},{2,20},{4,18},{6,16},{8,30},{10,28},{12,26},{14,24},{16,6},... | collective-permute-start | bytes 172040 | tf_op jit(solution)/shard_map/ppermute | solution.py:461
  28.7 15.6 %collective-permute-start.12 = (bf16[224,128]{1,0:T(8,128)(2,1)S(1)}, bf16[224,128]{1,0:T(8,128)(2,1)S(1)}, u32[]{:S(2)}, u32[]{:S(2)}) collective-permute-start(bf16[224,128]{1,0:T(8,128)(2,1)S(1)} %get-tuple-element.39), channel_id=1, source_target_pairs={{0,24},{2,26},{4,28},{6,30},{8,16},{10,18},{12,20},{14,22},{16,8},... | collective-permute-start | bytes 172040 | tf_op jit(solution)/shard_map/ppermute | solution.py:461
  32.3 12.0 %collective-permute-start.13 = (bf16[224,128]{1,0:T(8,128)(2,1)S(1)}, bf16[224,128]{1,0:T(8,128)(2,1)S(1)}, u32[]{:S(2)}, u32[]{:S(2)}) collective-permute-start(bf16[224,128]{1,0:T(8,128)(2,1)S(1)} %get-tuple-element.40), channel_id=1, source_target_pairs={{0,26},{2,24},{4,30},{6,28},{8,18},{10,16},{12,22},{14,20},{16,10}... | collective-permute-start | bytes 172040 | tf_op jit(solution)/shard_map/ppermute | solution.py:461
  33.3 11.0 %collective-permute-start.14 = (bf16[224,128]{1,0:T(8,128)(2,1)S(1)}, bf16[224,128]{1,0:T(8,128)(2,1)S(1)}, u32[]{:S(2)}, u32[]{:S(2)}) collective-permute-start(bf16[224,128]{1,0:T(8,128)(2,1)S(1)} %get-tuple-element.41), channel_id=1, source_target_pairs={{0,28},{2,30},{4,24},{6,26},{8,20},{10,22},{12,16},{14,18},{16,12}... | collective-permute-start | bytes 172040 | tf_op jit(solution)/shard_map/ppermute | solution.py:461
  38.0 6.8 %collective-permute-start.15 = (bf16[224,128]{1,0:T(8,128)(2,1)S(1)}, bf16[224,128]{1,0:T(8,128)(2,1)S(1)}, u32[]{:S(2)}, u32[]{:S(2)}) collective-permute-start(bf16[224,128]{1,0:T(8,128)(2,1)S(1)} %get-tuple-element.42), channel_id=1, source_target_pairs={{0,30},{2,28},{4,26},{6,24},{8,22},{10,20},{12,18},{14,16},{16,14}... | collective-permute-start | bytes 172040 | tf_op jit(solution)/shard_map/ppermute | solution.py:461

commit v4 on v2

--- a/solution.py
+++ b/solution.py
@@ -19,7 +19,9 @@
 
 
 class Plan(NamedTuple):
+    first: int
     maps: int
+    total: int
     width: int
     cols: int
     tiles: int
@@ -40,6 +42,10 @@
         return self.sides * self.halo
 
     @property
+    def last(self):
+        return self.first + self.maps == self.total
+
+    @property
     def edge_rows(self):
         return up(self.maps * self.edges, 8)
 
@@ -65,7 +71,7 @@
 
     @property
     def groups(self):
-        return -(-self.maps // self.slots)
+        return -(-self.total // self.slots)
 
     @property
     def side_rows(self):
@@ -73,7 +79,7 @@
 
     @property
     def block_rows(self):
-        return up(self.maps * self.rows + self.side_rows, 16)
+        return up(self.maps * self.rows + (self.side_rows if self.last else 0), 16)
 
     @property
     def stride(self):
@@ -134,9 +140,9 @@
         dest = lax.rem(me + shift, tiles)
         by_col = by_row = None
         for index in range(count):
-            block = maps_ref[index]
+            block = maps_ref[plan.first + index]
             out_ref[shift - 1, index * cols : (index + 1) * cols, :] = maps_ref[
-                index, pl.ds(pl.multiple_of(dest * cols, cols), cols), :
+                plan.first + index, pl.ds(pl.multiple_of(dest * cols, cols), cols), :
             ]
             left = [pick(edge, cols, me * cols, dest, index)]
             upper = [pick(edge, width, 0, dest, index)]
@@ -166,9 +172,8 @@
         out_ref[shift - 1, count * cols :, :] = jnp.concatenate(pieces, axis=0).astype(BF16)
 
 
-def correct_pack(
-    plan, tile_ref, maps_ref, recv_ref, sums_ref, edge_ref, out_ref, field_ref, turned_ref
-):
+def correct_pack(plan, tile_ref, maps_ref, recv_ref, sums_ref, edge_ref, *refs):
+    *line_refs, out_ref, field_ref, turned_ref = refs
     me = tile_ref[0]
     count, cols, width, tiles = plan.maps, plan.cols, plan.width, plan.tiles
     head, edge, halo = plan.map_rows, plan.edge_rows, plan.halo
@@ -208,7 +213,7 @@
             other = recv_ref[
                 jnp.maximum(shift - 1, 0), index * cols : (index + 1) * cols, :
             ]
-            own = maps_ref[index, b * cols : (b + 1) * cols, :]
+            own = maps_ref[plan.first + index, b * cols : (b + 1) * cols, :]
             mirror = across(eye, jnp.where(shift == 0, own, other))
             column = turned_ref[b * cols : (b + 1) * cols, index : index + 1]
             field_ref[index, margin + b * cols : margin + (b + 1) * cols, :] = (
@@ -238,12 +243,31 @@
         for k in range(count)
     ]
     rows, slots = plan.rows, plan.slots
+    if not plan.last:
+        line_ref, out_ref = line_refs[-1], out_ref
+        filler = plan.edge_rows - count * plan.edges
+        if filler:
+            lines = lines + [jnp.zeros((filler, width), F32)]
+        line_ref[...] = jnp.concatenate(lines, axis=0)
+        for h in range(plan.heads):
+            first = h * plan.band - halo
+            pieces = [field_ref[k, margin + first : margin + first + rows, :] for k in range(count)]
+            spare = plan.block_rows - count * rows
+            if spare:
+                pieces.append(jnp.zeros((spare, cols), F32))
+            out_ref[h] = jnp.concatenate(pieces, axis=0).astype(BF16)
+        return
+    earlier = []
+    for line_ref in line_refs:
+        value = line_ref[...]
+        earlier += [value[k : k + plan.edges] for k in range(0, value.shape[0], plan.edges)]
+    lines = earlier[: plan.first] + lines
     stacks = []
     for slot in range(slots):
         members = []
         for group in range(plan.groups):
             k = group * slots + slot
-            members.append(lines[k] if k < count else jnp.zeros((plan.edges, width), F32))
+            members.append(lines[k] if k < plan.total else jnp.zeros((plan.edges, width), F32))
         stacks.append(jnp.concatenate(members, axis=0))
     lane = lax.broadcasted_iota(jnp.int32, (plan.side_rows, cols), 1)
     spare = plan.block_rows - count * rows - plan.side_rows
@@ -269,9 +293,22 @@
     return pltpu.roll(ref[rows, low : low + size + LANES], size + LANES - rest, 1)[:, :size]
 
 
+def project(plan, recv_ref, proj_ref, out_ref, maps_ref):
+    body, cols, rows = plan.maps * plan.rows, plan.cols, plan.rows
+    for s in range(plan.heads):
+        maps_ref[s * body : (s + 1) * body, :] = recv_ref[s].astype(F32)[:body]
+    weight = proj_ref[...]
+    for r in range(0, rows, 2):
+        pair = [
+            maps_ref[pl.ds(r + k, plan.heads * plan.maps, stride=rows), :].astype(BF16)
+            for k in range(2)
+        ]
+        out_ref[:, r * cols : (r + 2) * cols] = dot(weight, jnp.concatenate(pair, axis=1))
+
+
 def stack(
-    plan, recv_ref, proj_ref, side_ref, kernel_ref, vector_ref, mask_ref, spots_ref, out_ref,
-    maps_ref, sides_ref, field_ref, stream_ref, hidden_ref, taps_ref, logit_ref,
+    plan, recv_ref, part_ref, proj_ref, side_ref, kernel_ref, vector_ref, mask_ref, spots_ref,
+    out_ref, maps_ref, sides_ref, field_ref, stream_ref, hidden_ref, taps_ref, logit_ref,
 ):
     count, cols, rows, halo = plan.maps, plan.cols, plan.rows, plan.halo
     heads, feat, chunk, stride = plan.heads, plan.feat, plan.chunk, plan.stride
@@ -316,6 +353,7 @@
             for k in range(per)
         ]
         pair = dot(weight, jnp.concatenate(blocks, axis=1)) + bias
+        pair = pair + part_ref[:, r * cols : (r + per) * cols]
         for k in range(per):
             begin = plan.start + (r + k) * stride + halo
             low, rest = begin // LANES * LANES, begin % LANES
@@ -383,30 +421,56 @@
     feat = proj_weight.shape[0]
     blocks, convs = conv_weight.shape[:2]
     tiles, heads = lax.axis_size("tile"), lax.axis_size("head")
-    plan = Plan(maps, width, cols, tiles, heads, feat, blocks * convs)
+    plans = [
+        Plan(first, count, maps, width, cols, tiles, heads, feat, blocks * convs)
+        for first, count in ((0, maps // 2), (maps // 2, maps - maps // 2))
+    ]
+    plan = plans[-1]
     me = lax.axis_index("tile").astype(jnp.int32)
     tile = me.reshape(1)
     params = pltpu.CompilerParams(vmem_limit_bytes=VMEM_LIMIT)
 
-    payload_rows = maps * cols + plan.tail_rows
-    payload, sums, edge = pl.pallas_call(
-        functools.partial(mirror_pack, plan),
-        out_shape=[
-            jax.ShapeDtypeStruct((tiles - 1, payload_rows, cols), BF16),
-            jax.ShapeDtypeStruct((plan.map_rows, width), F32),
-            jax.ShapeDtypeStruct((plan.edge_rows, cols), F32),
-        ],
-        in_specs=[whole(pltpu.SMEM), whole()],
-        out_specs=[whole()] * 3,
-        compiler_params=params,
-        name="mirror_pack",
-    )(tile, attention)
-    received = jnp.stack(
-        [
-            lax.ppermute(payload[s - 1], "tile", [(i, (i + s) % tiles) for i in range(tiles)])
-            for s in range(tiles - 1, 0, -1)
-        ]
-    )
+    mirrored = []
+    for part in plans:
+        payload, sums, edge = pl.pallas_call(
+            functools.partial(mirror_pack, part),
+            out_shape=[
+                jax.ShapeDtypeStruct((tiles - 1, part.maps * cols + part.tail_rows, cols), BF16),
+                jax.ShapeDtypeStruct((part.map_rows, width), F32),
+                jax.ShapeDtypeStruct((part.edge_rows, cols), F32),
+            ],
+            in_specs=[whole(pltpu.SMEM), whole()],
+            out_specs=[whole()] * 3,
+            compiler_params=params,
+            name="mirror_pack",
+        )(tile, attention)
+        received = jnp.stack(
+            [
+                lax.ppermute(payload[s - 1], "tile", [(i, (i + s) % tiles) for i in range(tiles)])
+                for s in range(tiles - 1, 0, -1)
+            ]
+        )
+        mirrored.append((received, sums, edge))
+
+    grouped, lines = [], []
+    for part, arrays in zip(plans, mirrored):
+        shapes = [jax.ShapeDtypeStruct((heads, part.block_rows, cols), BF16)]
+        if not part.last:
+            shapes.insert(0, jax.ShapeDtypeStruct((part.edge_rows, width), F32))
+        *line, packed = pl.pallas_call(
+            functools.partial(correct_pack, part),
+            out_shape=shapes,
+            in_specs=[whole(pltpu.SMEM)] + [whole()] * (4 + len(lines)),
+            out_specs=[whole()] * len(shapes),
+            scratch_shapes=[
+                pltpu.VMEM((part.maps, width + 16, cols), F32),
+                pltpu.VMEM((width, LANES), F32),
+            ],
+            compiler_params=params,
+            name="correct_pack",
+        )(tile, attention, *arrays, *lines)
+        lines += line
+        grouped.append(lax.all_to_all(packed, "head", split_axis=0, concat_axis=0, tiled=True))
 
     stride, start = plan.stride, plan.start
     side_weight = proj_weight.reshape(feat, heads, maps)
@@ -435,27 +499,27 @@
         spots.append(functools.reduce(jnp.logical_or, hit).astype(BF16))
     spots = jnp.stack(spots)
 
-    packed = pl.pallas_call(
-        functools.partial(correct_pack, plan),
-        out_shape=jax.ShapeDtypeStruct((heads, plan.block_rows, cols), BF16),
-        in_specs=[whole(pltpu.SMEM)] + [whole()] * 4,
+    by_map = proj_weight.reshape(feat, heads, maps)
+    weights = [
+        by_map[:, :, part.first : part.first + part.maps].reshape(feat, -1) for part in plans
+    ]
+    partial = pl.pallas_call(
+        functools.partial(project, plans[0]),
+        out_shape=jax.ShapeDtypeStruct((feat, plan.rows * cols), F32),
+        in_specs=[whole()] * 2,
         out_specs=whole(),
-        scratch_shapes=[
-            pltpu.VMEM((maps, width + 16, cols), F32),
-            pltpu.VMEM((width, LANES), F32),
-        ],
+        scratch_shapes=[pltpu.VMEM((heads * plans[0].maps * plan.rows, cols), F32)],
         compiler_params=params,
-        name="correct_pack",
-    )(tile, attention, received, sums, edge)
-    grouped = lax.all_to_all(packed, "head", split_axis=0, concat_axis=0, tiled=True)
+        name="project",
+    )(grouped[0], weights[0])
 
     return pl.pallas_call(
         functools.partial(stack, plan),
         out_shape=jax.ShapeDtypeStruct((plan.band, cols), F32),
-        in_specs=[whole()] * 7,
+        in_specs=[whole()] * 8,
         out_specs=whole(),
         scratch_shapes=[
-            pltpu.VMEM((heads * maps * plan.rows, cols), F32),
+            pltpu.VMEM((heads * plan.maps * plan.rows, cols), F32),
             pltpu.VMEM((heads * plan.side_rows, cols), F32),
             pltpu.VMEM((feat, plan.lanes), F32),
             pltpu.VMEM((feat, plan.lanes), BF16),
@@ -465,7 +529,7 @@
         ],
         compiler_params=params,
         name="stack",
-    )(grouped, proj_weight, side_weight, kernels, vectors, mask, spots)
+    )(grouped[1], partial, weights[1], side_weight, kernels, vectors, mask, spots)
 
 
 def solution(mesh):

time: 52.5 us -> 56.5 us (1.076)
  starting transfers between devices: 9.31 us -> 14.4 us
  waiting for transfers between devices: 26.8 us -> 23.8 us
  local copies, waits for them, and re-layouts: 2.46 us -> 3.76 us
  Pallas kernels: 12.1 us -> 13.2 us
    all_to_all x1 -> x2, starting transfers between devices: 6.27 us -> 9.83 us  [on_device(): lax.all_to_all(packed, 'head', split_axis=0, concat_axis=0, tiled=True)]
    all_to_all x1 -> x2, waiting for transfers between devices: 18.6 us -> 16.3 us  [on_device(): lax.all_to_all(packed, 'head', split_axis=0, concat_axis=0, tiled=True)]
    ppermute x1 -> x2, starting transfers between devices: 3.03 us -> 4.62 us  [on_device(): lax.ppermute(payload[s - 1], 'tile', [(i, (i + s) % tiles) for i in range...]
    pallas_call x2 -> x5, Pallas kernels: 2.24 us -> 3.44 us  [the longest x2 2.58 us: on_device(): pl.pallas_call(functools.partial(correct_pack, part), out_shape=shapes, i...]
    transpose x1, local copies, waits for them, and re-layouts: 0.51 us -> 1.58 us  [on_device(): conv_weight.transpose(0, 1, 5, 2, 4, 3)]
    ppermute x1 -> x2, waiting for transfers between devices: 8.23 us -> 7.44 us  [on_device(): lax.ppermute(payload[s - 1], 'tile', [(i, (i + s) % tiles) for i in range...]
  transfers between devices with their start and end apart: 2 -> 4, of which waited for: 2 -> 4; matrix products, arithmetic and copies ran while one was open for 4% -> 6% of each run, Pallas kernels for 0% -> 4%
where the time goes in v4:
time: 56.5 us; the launch traced here: 56.1 us
  waiting for transfers between devices  23.8 us (42%)
  starting transfers between devices  14.4 us (25%)
  Pallas kernels  13.2 us (23%)
  local copies, waits for them, and re-layouts  3.76 us (7%)
  other arithmetic  0.68 us (1%)
    all_to_all x2, waiting for transfers between devices, on_device(): lax.all_to_all(packed, 'head', split_axis=0, concat_axis=0, tiled=True)  16.3 us
    all_to_all x2, starting transfers between devices, on_device(): lax.all_to_all(packed, 'head', split_axis=0, concat_axis=0, tiled=True)  9.83 us
    pallas_call x1, Pallas kernels, on_device(): pl.pallas_call(functools.partial(stack, plan), out_shape=jax.ShapeDtypeSt...  9.74 us
    ppermute x2, waiting for transfers between devices, on_device(): lax.ppermute(payload[s - 1], 'tile', [(i, (i + s) % tiles) for i in range...  7.44 us
    ppermute x2, starting transfers between devices, on_device(): lax.ppermute(payload[s - 1], 'tile', [(i, (i + s) % tiles) for i in range...  4.62 us
    pallas_call x2, Pallas kernels, on_device(): pl.pallas_call(functools.partial(correct_pack, part), out_shape=shapes, i...  2.58 us
    transpose x1, local copies, waits for them, and re-layouts, on_device(): conv_weight.transpose(0, 1, 5, 2, 4, 3)  1.58 us
    unnamed x22, local copies, waits for them, and re-layouts  1.22 us
  transfers between devices with their start and end apart: 4, of which 4 were waited for; matrix products, arithmetic and copies ran while one was open for 6% of the time, Pallas kernels for 4%

profile of v4, /device:TPU:0, one launch (start us, length us, event | category | flops | bytes accessed | tf_op | source)
XLA Modules:
  0.0 56.1 jit_solution(17747560077215438688)
XLA Ops:
  0.0 1.1 %copy-done = bf16[9,256,128]{2,1,0:T(8,128)(2,1)S(1)} copy-done((bf16[9,256,128]{2,1,0:T(8,128)(2,1)S(1)}, bf16[9,256,128]{2,1,0:T(8,128)(2,1)}, u32[]{:S(2)}) %copy-start) | copy-done | bytes 589848
  1.1 0.2 mirror_pack.3
  1.3 0.0 copy-start.3
  1.3 0.0 copy-start.4
  1.3 3.0 %collective-permute-start.1 = (bf16[656,128]{1,0:T(8,128)(2,1)S(1)}, bf16[656,128]{1,0:T(8,128)(2,1)S(1)}, u32[]{:S(2)}, u32[]{:S(2)}) collective-permute-start(bf16[656,128]{1,0:T(8,128)(2,1)S(1)} %bitcast.23), channel_id=1, source_target_pairs={{0,1},{1,0},{2,3},{3,2},{4,5},{5,4},{6,7},{7,6},{8,9},{9,8},{10,11... | collective-permute-start | bytes 503816 | tf_op jit(solution)/shard_map/ppermute | solution.py:449
  4.4 4.3 %collective-permute-done.1 = bf16[656,128]{1,0:T(8,128)(2,1)S(1)} collective-permute-done((bf16[656,128]{1,0:T(8,128)(2,1)S(1)}, bf16[656,128]{1,0:T(8,128)(2,1)S(1)}, u32[]{:S(2)}, u32[]{:S(2)}) %collective-permute-start.1) | collective-permute-done | bytes 167968 | tf_op jit(solution)/shard_map/ppermute | solution.py:449
  8.7 1.2 %correct_pack.2 = (f32[16,256]{1,0:T(8,128)S(1)}, bf16[16,96,128]{2,1,0:T(8,128)(2,1)}) custom-call(s32[1]{0:T(128)} %bitcast.tile_ref, bf16[9,256,128]{2,1,0:T(8,128)(2,1)S(1)} %copy-done, bf16[1,656,128]{2,1,0:T(8,128)(2,1)S(1)} %bitcast.20, f32[16,256]{1,0:T(8,128)S(1)} %get-tuple-element.17.sums_ref, f32[16,128]{1,0:T(8,128)S(1)} %get-tuple-element.18.edge_ref), custom_call_target="tpu_custom_call" | custom-call | tf_op jit(solution)/shard_map/correct_pack/pallas_call | solution.py:460
  9.8 6.3 %all-to-all-start.1 = ((bf16[16,96,128]{2,1,0:T(8,128)(2,1)}), bf16[16,96,128]{2,1,0:T(8,128)(2,1)S(1)}, u32[]{:S(2)}, u32[]{:S(2)}) async-start(bf16[16,96,128]{2,1,0:T(8,128)(2,1)} %get-tuple-element.20), calls=%async_computation.1 | async-start | bytes 786432 | tf_op jit(solution)/shard_map/all_to_all | solution.py:473
  16.1 0.0 copy-done.1
  16.1 0.3 mirror_pack.2
  16.4 1.6 %collective-permute-start = (bf16[816,128]{1,0:T(8,128)(2,1)S(1)}, bf16[816,128]{1,0:T(8,128)(2,1)S(1)}, u32[]{:S(2)}, u32[]{:S(2)}) collective-permute-start(bf16[816,128]{1,0:T(8,128)(2,1)S(1)} %bitcast.22), channel_id=1, source_target_pairs={{0,1},{1,0},{2,3},{3,2},{4,5},{5,4},{6,7},{7,6},{8,9},{9,8},{10,11... | collective-permute-start | bytes 626696 | tf_op jit(solution)/shard_map/ppermute | solution.py:449
  18.0 0.0 copy-done.3
  18.0 0.0 copy-done.4
  18.0 0.0 copy-done.2
  18.0 0.1 copy.25
  18.3 0.0 copy-done.5
  18.3 0.0 copy-done.8
  18.3 0.0 copy-done.9
  18.3 0.1 copy.30
  18.4 0.1 copy.26.proj_ref
  18.5 0.1 copy.31.proj_ref
  18.7 0.1 copy.32.side_ref
  18.8 1.6 %copy.29 = bf16[2,2,3,64,3,64]{5,4,3,2,1,0:T(4,128)(2,1)S(1)} copy(bf16[2,2,3,64,3,64]{5,3,2,4,1,0:T(8,128)(2,1)} %bitcast.24) | data formatting | bytes 589824 | tf_op jit(solution)/shard_map/transpose | solution.py:480
  20.4 0.5 reshape.93.kernel_ref
  20.8 3.2 %collective-permute-done = bf16[816,128]{1,0:T(8,128)(2,1)S(1)} collective-permute-done((bf16[816,128]{1,0:T(8,128)(2,1)S(1)}, bf16[816,128]{1,0:T(8,128)(2,1)S(1)}, u32[]{:S(2)}, u32[]{:S(2)}) %collective-permute-start) | collective-permute-done | bytes 208928 | tf_op jit(solution)/shard_map/ppermute | solution.py:449
  24.0 1.4 %correct_pack.3 = bf16[16,128,128]{2,1,0:T(8,128)(2,1)} custom-call(s32[1]{0:T(128)} %bitcast.tile_ref, bf16[9,256,128]{2,1,0:T(8,128)(2,1)S(1)} %copy-done.1, bf16[1,816,128]{2,1,0:T(8,128)(2,1)S(1)} %bitcast.19, f32[16,256]{1,0:T(8,128)S(1)} %get-tuple-element.14.sums_ref, f32[24,128]{1,0:T(8,128)S(1)} %get-tuple-element.15.edge_ref, ...), custom_call_target="tpu_custom_call" | custom-call | tf_op jit(solution)/shard_map/correct_pack/pallas_call | solution.py:460
  25.4 2.9 %all-to-all-done.1.recv_ref = bf16[16,96,128]{2,1,0:T(8,128)(2,1)S(1)} async-done(((bf16[16,96,128]{2,1,0:T(8,128)(2,1)}), bf16[16,96,128]{2,1,0:T(8,128)(2,1)S(1)}, u32[]{:S(2)}, u32[]{:S(2)}) %all-to-all-start.1) | async-done | bytes 393248 | tf_op jit(solution)/shard_map/all_to_all | solution.py:473
  28.3 3.6 %all-to-all-start = ((bf16[16,128,128]{2,1,0:T(8,128)(2,1)}), bf16[16,128,128]{2,1,0:T(8,128)(2,1)S(1)}, u32[]{:S(2)}, u32[]{:S(2)}) async-start(bf16[16,128,128]{2,1,0:T(8,128)(2,1)} %correct_pack.3), calls=%async_computation | async-start | bytes 1048576 | tf_op jit(solution)/shard_map/all_to_all | solution.py:473
  31.9 0.7 %fusion.1.spots_ref = bf16[1,128,4352]{2,1,0:T(8,128)(2,1)S(1)} fusion(s32[128]{0:T(128)S(1)} %copy-done.6, s32[128]{0:T(128)S(1)} %copy-done.7), kind=kLoop, calls=%fused_computation.3 | loop fusion | flops 2228224 | bytes 1115136 | tf_op jit(solution)/shard_map/convert_element_type | solution.py:499
  32.6 0.3 project.1.part_ref
  32.9 13.4 %all-to-all-done.recv_ref = bf16[16,128,128]{2,1,0:T(8,128)(2,1)S(1)} async-done(((bf16[16,128,128]{2,1,0:T(8,128)(2,1)}), bf16[16,128,128]{2,1,0:T(8,128)(2,1)S(1)}, u32[]{:S(2)}, u32[]{:S(2)}) %all-to-all-start) | async-done | bytes 524320 | tf_op jit(solution)/shard_map/all_to_all | solution.py:473
  46.3 9.7 %stack.10 = f32[16,128]{1,0:T(8,128)} custom-call(bf16[16,128,128]{2,1,0:T(8,128)(2,1)S(1)} %all-to-all-done.recv_ref, f32[64,3072]{1,0:T(8,128)S(1)} %project.1.part_ref, bf16[64,80]{1,0:T(8,128)(2,1)S(1)} %copy.31.proj_ref, bf16[64,160]{1,0:T(8,128)(2,1)S(1)} %copy.32.side_ref, bf16[4,192,192]{2,1,0:T(8,128)(2,1)S(1)} %reshape.93.kernel_ref, ...), custom_call_target="tpu_custom_call" | custom-call | tf_op jit(solution)/shard_map/stack/pallas_call | solution.py:516
  (20 shorter events, 0.2 us)
Async XLA Ops:
  0.0 1.1 %copy-start = (bf16[9,256,128]{2,1,0:T(8,128)(2,1)S(1)}, bf16[9,256,128]{2,1,0:T(8,128)(2,1)}, u32[]{:S(2)}) copy-start(bf16[9,256,128]{2,1,0:T(8,128)(2,1)} %maps_ref.7) | copy-start | bytes 1769476
  1.1 15.1 %copy-start.1 = (bf16[9,256,128]{2,1,0:T(8,128)(2,1)S(1)}, bf16[9,256,128]{2,1,0:T(8,128)(2,1)}, u32[]{:S(2)}) copy-start(bf16[9,256,128]{2,1,0:T(8,128)(2,1)} %maps_ref.7) | copy-start | bytes 1769476
  1.3 16.7 %copy-start.3 = (s32[4352]{0:T(1024)S(1)}, s32[4352]{0:T(1024)}, u32[]{:S(2)}) copy-start(s32[4352]{0:T(1024)} %constant.32.clone) | copy-start | bytes 52228
  1.3 16.7 %copy-start.4 = (s32[4352]{0:T(1024)S(1)}, s32[4352]{0:T(1024)}, u32[]{:S(2)}) copy-start(s32[4352]{0:T(1024)} %constant.31.clone) | copy-start | bytes 52228
  1.3 7.3 %collective-permute-start.1 = (bf16[656,128]{1,0:T(8,128)(2,1)S(1)}, bf16[656,128]{1,0:T(8,128)(2,1)S(1)}, u32[]{:S(2)}, u32[]{:S(2)}) collective-permute-start(bf16[656,128]{1,0:T(8,128)(2,1)S(1)} %bitcast.23), channel_id=1, source_target_pairs={{0,1},{1,0},{2,3},{3,2},{4,5},{5,4},{6,7},{7,6},{8,9},{9,8},{10,11... | collective-permute-start | bytes 503816 | tf_op jit(solution)/shard_map/ppermute | solution.py:449
  8.7 9.4 %copy-start.2 = (bf16[64,144]{1,0:T(8,128)(2,1)S(1)}, bf16[64,144]{1,0:T(8,128)(2,1)}, u32[]{:S(2)}) copy-start(bf16[64,144]{1,0:T(8,128)(2,1)} %param.11) | copy-start | bytes 55300
  9.8 8.4 %copy-start.5 = (f32[2,2,64]{2,1,0:T(2,128)S(1)}, f32[2,2,64]{2,1,0:T(2,128)}, u32[]{:S(2)}) copy-start(f32[2,2,64]{2,1,0:T(2,128)} %param.14) | copy-start | bytes 3076
  9.8 8.4 %copy-start.8 = (f32[64]{0:T(128)S(1)}, f32[64]{0:T(128)}, u32[]{:S(2)}) copy-start(f32[64]{0:T(128)} %param.15) | copy-start | bytes 772
  9.8 8.4 %copy-start.9 = (f32[64]{0:T(128)S(1)}, f32[64]{0:T(128)}, u32[]{:S(2)}) copy-start(f32[64]{0:T(128)} %param.12) | copy-start | bytes 772
  9.8 18.5 %all-to-all-start.1 = ((bf16[16,96,128]{2,1,0:T(8,128)(2,1)}), bf16[16,96,128]{2,1,0:T(8,128)(2,1)S(1)}, u32[]{:S(2)}, u32[]{:S(2)}) async-start(bf16[16,96,128]{2,1,0:T(8,128)(2,1)} %get-tuple-element.20), calls=%async_computation.1 | async-start | bytes 786432 | tf_op jit(solution)/shard_map/all_to_all | solution.py:473
  16.4 7.6 %collective-permute-start = (bf16[816,128]{1,0:T(8,128)(2,1)S(1)}, bf16[816,128]{1,0:T(8,128)(2,1)S(1)}, u32[]{:S(2)}, u32[]{:S(2)}) collective-permute-start(bf16[816,128]{1,0:T(8,128)(2,1)S(1)} %bitcast.22), channel_id=1, source_target_pairs={{0,1},{1,0},{2,3},{3,2},{4,5},{5,4},{6,7},{7,6},{8,9},{9,8},{10,11... | collective-permute-start | bytes 626696 | tf_op jit(solution)/shard_map/ppermute | solution.py:449
  24.0 7.9 %copy-start.6 = (s32[128]{0:T(128)S(1)}, s32[128]{0:T(128)}, u32[]{:S(2)}) copy-start(s32[128]{0:T(128)} %constant.34.clone) | copy-start | bytes 1540
  24.0 7.9 %copy-start.7 = (s32[128]{0:T(128)S(1)}, s32[128]{0:T(128)}, u32[]{:S(2)}) copy-start(s32[128]{0:T(128)} %constant.33.clone) | copy-start | bytes 1540
  28.3 18.0 %all-to-all-start = ((bf16[16,128,128]{2,1,0:T(8,128)(2,1)}), bf16[16,128,128]{2,1,0:T(8,128)(2,1)S(1)}, u32[]{:S(2)}, u32[]{:S(2)}) async-start(bf16[16,128,128]{2,1,0:T(8,128)(2,1)} %correct_pack.3), calls=%async_computation | async-start | bytes 1048576 | tf_op jit(solution)/shard_map/all_to_all | solution.py:473

commit v5 on v3

--- a/solution.py
+++ b/solution.py
@@ -72,8 +72,32 @@
         return self.groups * self.edges
 
     @property
+    def chips(self):
+        return self.heads // 2
+
+    @property
+    def lone(self):
+        return self.band // 8
+
+    @property
+    def shared(self):
+        return 2 * self.halo // 8
+
+    @property
+    def group_rows(self):
+        return 8 * self.maps
+
+    @property
+    def lead(self):
+        return self.lone * self.group_rows + self.side_rows
+
+    @property
+    def half_rows(self):
+        return self.lead + self.shared * self.group_rows
+
+    @property
     def block_rows(self):
-        return up(self.maps * self.rows + self.side_rows, 16)
+        return up(self.lead + self.half_rows, 16)
 
     @property
     def stride(self):
@@ -96,6 +120,12 @@
     if count & (count - 1) == 0:
         return mine ^ step
     return (mine - step if back else mine + step) % count
+
+
+def half(plan, block, core):
+    return jnp.where(
+        core == 0, block[: plan.half_rows], block[plan.lead : plan.lead + plan.half_rows]
+    )
 
 
 def edge_start(plan, tile, side):
@@ -174,7 +204,7 @@
 
 def correct_pack(plan, tile_ref, maps_ref, recv_ref, sums_ref, edge_ref, *refs):
     *out_refs, field_ref, turned_ref = refs
-    me, band_index = tile_ref[0], tile_ref[1]
+    me, chip = tile_ref[0], tile_ref[1] // 2
     count, cols, width, tiles = plan.maps, plan.cols, plan.width, plan.tiles
     head, edge, halo = plan.map_rows, plan.edge_rows, plan.halo
     tails = [recv_ref[k, count * cols :, :].astype(F32) for k in range(tiles - 1)]
@@ -251,19 +281,34 @@
             members.append(lines[k] if k < count else jnp.zeros((plan.edges, width), F32))
         stacks.append(jnp.concatenate(members, axis=0))
     lane = lax.broadcasted_iota(jnp.int32, (plan.side_rows, cols), 1)
-    spare = plan.block_rows - count * rows - plan.side_rows
-    for step, out_ref in enumerate(out_refs):
-        first = partner(band_index, step, plan.heads) * plan.band
-        pieces = [field_ref[k, pl.ds(pl.multiple_of(first + 8, 8), rows), :] for k in range(count)]
-        side = jnp.zeros((plan.side_rows, cols), F32)
-        for slot in range(slots):
-            amount = lax.rem(slot * rows + halo + width - first, width)
-            moved = pltpu.roll(stacks[slot], amount, 1)[:, :cols]
-            side = jnp.where((lane >= slot * rows) & (lane < (slot + 1) * rows), moved, side)
-        pieces.append(side)
+    spare = plan.block_rows - plan.lead - plan.half_rows
+    for step, out_ref in zip(reversed(range(plan.chips)), out_refs):
+        first = partner(chip, step, plan.chips) * 2 * plan.band
+        groups = [
+            field_ref[k, pl.ds(pl.multiple_of(first + 8 + 8 * group, 8), 8), :]
+            for group in range(2 * plan.lone + plan.shared)
+            for k in range(count)
+        ]
+        sides = []
+        for core in range(2):
+            side = jnp.zeros((plan.side_rows, cols), F32)
+            for slot in range(slots):
+                amount = lax.rem(slot * rows + halo + width - core * plan.band - first, width)
+                moved = pltpu.roll(stacks[slot], amount, 1)[:, :cols]
+                side = jnp.where((lane >= slot * rows) & (lane < (slot + 1) * rows), moved, side)
+            sides.append(side)
+        lone = plan.lone * count
+        pieces = groups[:lone] + sides[:1] + groups[lone:] + sides[1:]
         if spare:
             pieces.append(jnp.zeros((spare, cols), F32))
         out_ref[...] = jnp.concatenate(pieces, axis=0).astype(BF16)
+
+
+def core_pack(plan, tile_ref, *refs):
+    *block_refs, out_ref = refs
+    other = 1 - tile_ref[1] % 2
+    for k, block_ref in enumerate(block_refs):
+        out_ref[k] = half(plan, block_ref[...].astype(F32), other).astype(BF16)
 
 
 def shifted(ref, rows, base, offset, size):
@@ -275,20 +320,37 @@
     return pltpu.roll(ref[rows, low : low + size + LANES], size + LANES - rest, 1)[:, :size]
 
 
-def stack(plan, tile_ref, *refs):
-    recv_refs, refs = refs[: plan.heads], refs[plan.heads :]
+def stack(plan, order, tile_ref, *refs):
+    chips = plan.chips
+    own_refs, swap_refs, refs = refs[:chips], refs[chips : chips + len(order)], refs[chips + len(order) :]
     proj_ref, side_ref, kernel_ref, vector_ref, mask_ref, spots_ref, out_ref = refs[:7]
     maps_ref, sides_ref, field_ref, stream_ref, hidden_ref, taps_ref, logit_ref = refs[7:]
     count, cols, rows, halo = plan.maps, plan.cols, plan.rows, plan.halo
     heads, feat, chunk, stride = plan.heads, plan.feat, plan.chunk, plan.stride
-    body = count * rows
-    for step, recv_ref in enumerate(recv_refs):
-        block = recv_ref[...].astype(F32)
-        s = partner(tile_ref[1], step, heads, back=True)
-        maps_ref[pl.ds(pl.multiple_of(s * body, 8), body), :] = block[:body]
-        sides_ref[pl.ds(pl.multiple_of(s * plan.side_rows, 8), plan.side_rows), :] = block[
-            body : body + plan.side_rows
-        ]
+    chip, core = tile_ref[1] // 2, tile_ref[1] % 2
+    group = plan.group_rows
+
+    def spread(block, source):
+        for k in range(plan.lone + plan.shared):
+            value = block[k * group : (k + 1) * group]
+            if k >= plan.lone:
+                late = block[plan.side_rows + k * group : plan.side_rows + (k + 1) * group]
+                value = jnp.where(core == 0, late, value)
+            place = pl.multiple_of((k * heads + source) * group, 8)
+            maps_ref[pl.ds(place, group), :] = value
+        side = jnp.where(
+            core == 0,
+            block[plan.lone * group : plan.lead],
+            block[plan.half_rows - plan.side_rows : plan.half_rows],
+        )
+        place = pl.multiple_of(source * plan.side_rows, 8)
+        sides_ref[pl.ds(place, plan.side_rows), :] = side
+
+    for steps, swap_ref in zip(order, swap_refs):
+        for k, step in enumerate(steps):
+            source = 2 * partner(chip, step, chips, back=True)
+            spread(half(plan, own_refs[chips - 1 - step][...].astype(F32), core), source + core)
+            spread(swap_ref[k].astype(F32), source + 1 - core)
     bias = vector_ref[:, 0:1]
 
     slots, members = plan.slots, heads * plan.groups
@@ -319,7 +381,9 @@
     per = 2
     for r in range(0, rows, per):
         blocks = [
-            maps_ref[pl.ds(r + k, heads * count, stride=rows), :].astype(BF16)
+            maps_ref[
+                pl.ds((r + k) // 8 * heads * group + (r + k) % 8, heads * count, stride=8), :
+            ].astype(BF16)
             for k in range(per)
         ]
         pair = dot(weight, jnp.concatenate(blocks, axis=1)) + bias
@@ -443,11 +507,12 @@
         spots.append(functools.reduce(jnp.logical_or, hit).astype(BF16))
     spots = jnp.stack(spots)
 
+    chips = plan.chips
     blocks = pl.pallas_call(
         functools.partial(correct_pack, plan),
-        out_shape=[jax.ShapeDtypeStruct((plan.block_rows, cols), BF16)] * heads,
+        out_shape=[jax.ShapeDtypeStruct((plan.block_rows, cols), BF16)] * chips,
         in_specs=[whole(pltpu.SMEM)] + [whole()] * 4,
-        out_specs=[whole()] * heads,
+        out_specs=[whole()] * chips,
         scratch_shapes=[
             pltpu.VMEM((maps, width + 24, cols), F32),
             pltpu.VMEM((width, LANES), F32),
@@ -455,15 +520,27 @@
         compiler_params=params,
         name="correct_pack",
     )(tile, attention, received, sums, edge)
-    grouped = list(blocks)
-    for step in sorted(range(1, heads), key=lambda k: -k):
-        pairs = [(i, partner(i, step, heads)) for i in range(heads)]
-        grouped[step] = lax.ppermute(blocks[step], "head", pairs)
+    grouped = list(blocks)[::-1]
+    for step in reversed(range(1, chips)):
+        pairs = [(i, 2 * partner(i // 2, step, chips) + i % 2) for i in range(heads)]
+        grouped[step] = lax.ppermute(grouped[step], "head", pairs)
+    order = [list(range(chips - 1, chips // 2 - 1, -1)), list(range(chips // 2 - 1, -1, -1))]
+    swapped = []
+    for steps in order:
+        packed = pl.pallas_call(
+            functools.partial(core_pack, plan),
+            out_shape=jax.ShapeDtypeStruct((len(steps), plan.half_rows, cols), BF16),
+            in_specs=[whole(pltpu.SMEM)] + [whole()] * len(steps),
+            out_specs=whole(),
+            compiler_params=params,
+            name="core_pack",
+        )(tile, *[grouped[k] for k in steps])
+        swapped.append(lax.ppermute(packed, "head", [(i, i ^ 1) for i in range(heads)]))
 
     return pl.pallas_call(
-        functools.partial(stack, plan),
+        functools.partial(stack, plan, order),
         out_shape=jax.ShapeDtypeStruct((plan.band, cols), F32),
-        in_specs=[whole(pltpu.SMEM)] + [whole()] * (heads + 6),
+        in_specs=[whole(pltpu.SMEM)] + [whole()] * (chips + len(order) + 6),
         out_specs=whole(),
         scratch_shapes=[
             pltpu.VMEM((heads * maps * plan.rows, cols), F32),
@@ -476,7 +553,7 @@
         ],
         compiler_params=params,
         name="stack",
-    )(tile, *grouped, proj_weight, side_weight, kernels, vectors, mask, spots)
+    )(tile, *grouped[::-1], *swapped, proj_weight, side_weight, kernels, vectors, mask, spots)
 
 
 def solution(mesh):

time: 56.2 us -> 53 us (0.943); the launches traced: 55.2 us -> 52.8 us
  starting transfers between devices: 27.8 us -> 20.3 us
  waiting for transfers between devices: 8.82 us -> 11.6 us
  Pallas kernels: 13.1 us -> 14.3 us
  local copies, waits for them, and re-layouts: 4.58 us -> 5.64 us
    ppermute x15 -> x9, starting transfers between devices: 24.7 us -> 17.2 us  [the longest x7 16.8 us: on_device(): grouped[step] = lax.ppermute(grouped[step], 'head', pairs)]
    ppermute x15 -> x9, waiting for transfers between devices: 0.58 us -> 3.4 us  [the longest x7 3.39 us: on_device(): grouped[step] = lax.ppermute(grouped[step], 'head', pairs)]
    pallas_call x1 -> x3, Pallas kernels: 10.5 us -> 11.8 us  [the longest x1 10.6 us: on_device(): pl.pallas_call(functools.partial(stack, plan, order), out_shape=jax.Shape...]
    transpose x1, local copies, waits for them, and re-layouts: 1.4 us -> 2.46 us  [on_device(): conv_weight.transpose(0, 1, 5, 2, 4, 3)]
    unnamed x22 -> x20, local copies, waits for them, and re-layouts: 1.22 us -> 1.22 us
  transfers between devices with their start and end apart: 16 -> 10, of which waited for: 3 -> 4; matrix products, arithmetic and copies ran while one was open for 8% -> 10% of each run, Pallas kernels for 0% -> 2%
where the time goes in v5:
time: 53 us; the launch traced here: 52.8 us
  starting transfers between devices  20.3 us (38%)
  Pallas kernels  14.3 us (27%)
  waiting for transfers between devices  11.6 us (22%)
  local copies, waits for them, and re-layouts  5.64 us (11%)
  other arithmetic  0.75 us (1%)
    ppermute x7, starting transfers between devices, on_device(): grouped[step] = lax.ppermute(grouped[step], 'head', pairs)  16.8 us
    pallas_call x1, Pallas kernels, on_device(): pl.pallas_call(functools.partial(stack, plan, order), out_shape=jax.Shape...  10.6 us
    ppermute x1, waiting for transfers between devices, on_device(): lax.ppermute(payload[s - 1], 'tile', [(i, (i + s) % tiles) for i in range...  8.24 us
    ppermute x7, waiting for transfers between devices, on_device(): grouped[step] = lax.ppermute(grouped[step], 'head', pairs)  3.39 us
    ppermute x1, starting transfers between devices, on_device(): lax.ppermute(payload[s - 1], 'tile', [(i, (i + s) % tiles) for i in range...  3.03 us
    transpose x1, local copies, waits for them, and re-layouts, on_device(): conv_weight.transpose(0, 1, 5, 2, 4, 3)  2.46 us
    reshape x1, local copies, waits for them, and re-layouts, on_device(): conv_weight.transpose(0, 1, 5, 2, 4, 3)  1.69 us
    pallas_call x1, Pallas kernels, on_device(): pl.pallas_call(functools.partial(correct_pack, plan), out_shape=[jax.Shap...  1.57 us
  transfers between devices with their start and end apart: 10, of which 4 were waited for; matrix products, arithmetic and copies ran while one was open for 10% of the time, Pallas kernels for 2%

profile of v5, /device:TPU:0, one launch (start us, length us, event | category | flops | bytes accessed | tf_op | source)
XLA Modules:
  0.0 52.8 jit_solution(3277410477175910284)
XLA Ops:
  0.0 0.1 pad_add_fusion.tile_ref
  0.1 1.1 %copy-done = bf16[9,256,128]{2,1,0:T(8,128)(2,1)S(1)} copy-done((bf16[9,256,128]{2,1,0:T(8,128)(2,1)S(1)}, bf16[9,256,128]{2,1,0:T(8,128)(2,1)}, u32[]{:S(2)}) %copy-start) | copy-done | bytes 589848
  1.1 1.0 %mirror_pack.1 = (bf16[1,1376,128]{2,1,0:T(8,128)(2,1)S(1)}, f32[16,256]{1,0:T(8,128)S(1)}, f32[40,128]{1,0:T(8,128)S(1)}) custom-call(s32[2]{0:T(128)S(1)} %pad_add_fusion.tile_ref, bf16[9,256,128]{2,1,0:T(8,128)(2,1)S(1)} %copy-done), custom_call_target="tpu_custom_call" | custom-call | tf_op jit(solution)/shard_map/mirror_pack/pallas_call | solution.py:464
  2.1 3.0 %collective-permute-start = (bf16[1376,128]{1,0:T(8,128)(2,1)S(1)}, bf16[1376,128]{1,0:T(8,128)(2,1)S(1)}, u32[]{:S(2)}, u32[]{:S(2)}) collective-permute-start(bf16[1376,128]{1,0:T(8,128)(2,1)S(1)} %bitcast.17), channel_id=1, source_target_pairs={{0,1},{1,0},{2,3},{3,2},{4,5},{5,4},{6,7},{7,6},{8,9},{9,8},{10,11... | collective-permute-start | bytes 1056776 | tf_op jit(solution)/shard_map/ppermute | solution.py:478
  5.2 8.2 %collective-permute-done = bf16[1376,128]{1,0:T(8,128)(2,1)S(1)} collective-permute-done((bf16[1376,128]{1,0:T(8,128)(2,1)S(1)}, bf16[1376,128]{1,0:T(8,128)(2,1)S(1)}, u32[]{:S(2)}, u32[]{:S(2)}) %collective-permute-start) | collective-permute-done | bytes 352288 | tf_op jit(solution)/shard_map/ppermute | solution.py:478
  13.4 1.6 %correct_pack.1 = (bf16[384,128]{1,0:T(8,128)(2,1)S(1)}, bf16[384,128]{1,0:T(8,128)(2,1)S(1)}, bf16[384,128]{1,0:T(8,128)(2,1)S(1)}, bf16[384,128]{1,0:T(8,128)(...) custom-call(s32[2]{0:T(128)S(1)} %pad_add_fusion.tile_ref, ...), custom_call_target="tpu_custom_call" | custom-call | tf_op jit(solution)/shard_map/correct_pack/pallas_call | solution.py:511
  15.0 4.8 %collective-permute-start.1 = (bf16[384,128]{1,0:T(8,128)(2,1)S(1)}, bf16[384,128]{1,0:T(8,128)(2,1)S(1)}, u32[]{:S(2)}, u32[]{:S(2)}) collective-permute-start(bf16[384,128]{1,0:T(8,128)(2,1)S(1)} %get-tuple-element.19), channel_id=1, source_target_pairs={{0,28},{2,30},{4,24},{6,26},{8,20},{10,22},{12,16},{14,18},{16,12}... | collective-permute-start | bytes 294920 | tf_op jit(solution)/shard_map/ppermute | solution.py:526
  19.8 0.2 collective-permute-start.2
  20.0 0.8 %collective-permute-start.3 = (bf16[384,128]{1,0:T(8,128)(2,1)S(1)}, bf16[384,128]{1,0:T(8,128)(2,1)S(1)}, u32[]{:S(2)}, u32[]{:S(2)}) collective-permute-start(bf16[384,128]{1,0:T(8,128)(2,1)S(1)} %get-tuple-element.21), channel_id=1, source_target_pairs={{0,20},{2,22},{4,16},{6,18},{8,28},{10,30},{12,24},{14,26},{16,4},... | collective-permute-start | bytes 294920 | tf_op jit(solution)/shard_map/ppermute | solution.py:526
  20.8 2.0 %collective-permute-start.4 = (bf16[384,128]{1,0:T(8,128)(2,1)S(1)}, bf16[384,128]{1,0:T(8,128)(2,1)S(1)}, u32[]{:S(2)}, u32[]{:S(2)}) collective-permute-start(bf16[384,128]{1,0:T(8,128)(2,1)S(1)} %get-tuple-element.22), channel_id=1, source_target_pairs={{0,16},{2,18},{4,20},{6,22},{8,24},{10,26},{12,28},{14,30},{16,0},... | collective-permute-start | bytes 294920 | tf_op jit(solution)/shard_map/ppermute | solution.py:526
  22.8 2.3 %collective-permute-start.5 = (bf16[384,128]{1,0:T(8,128)(2,1)S(1)}, bf16[384,128]{1,0:T(8,128)(2,1)S(1)}, u32[]{:S(2)}, u32[]{:S(2)}) collective-permute-start(bf16[384,128]{1,0:T(8,128)(2,1)S(1)} %get-tuple-element.23), channel_id=1, source_target_pairs={{0,12},{2,14},{4,8},{6,10},{8,4},{10,6},{12,0},{14,2},{16,28},{18,... | collective-permute-start | bytes 294920 | tf_op jit(solution)/shard_map/ppermute | solution.py:526
  25.1 0.0 collective-permute-done.1.refs_0_
  25.1 5.6 %collective-permute-start.6 = (bf16[384,128]{1,0:T(8,128)(2,1)S(1)}, bf16[384,128]{1,0:T(8,128)(2,1)S(1)}, u32[]{:S(2)}, u32[]{:S(2)}) collective-permute-start(bf16[384,128]{1,0:T(8,128)(2,1)S(1)} %get-tuple-element.24), channel_id=1, source_target_pairs={{0,8},{2,10},{4,12},{6,14},{8,0},{10,2},{12,4},{14,6},{16,24},{18,... | collective-permute-start | bytes 294920 | tf_op jit(solution)/shard_map/ppermute | solution.py:526
  30.7 0.0 collective-permute-done.2.refs_1_
  30.7 0.0 copy-start.7
  30.7 0.0 copy-start.8
  30.7 0.0 copy-start.1
  30.7 1.1 %collective-permute-start.7 = (bf16[384,128]{1,0:T(8,128)(2,1)S(1)}, bf16[384,128]{1,0:T(8,128)(2,1)S(1)}, u32[]{:S(2)}, u32[]{:S(2)}) collective-permute-start(bf16[384,128]{1,0:T(8,128)(2,1)S(1)} %get-tuple-element.25), channel_id=1, source_target_pairs={{0,4},{2,6},{4,0},{6,2},{8,12},{10,14},{12,8},{14,10},{16,20},{18,... | collective-permute-start | bytes 294920 | tf_op jit(solution)/shard_map/ppermute | solution.py:526
  31.8 0.7 %fusion.1.refs_15_ = bf16[1,128,4352]{2,1,0:T(8,128)(2,1)S(1)} fusion(s32[128]{0:T(128)S(1)} %copy-done.5, s32[128]{0:T(128)S(1)} %copy-done.6), kind=kLoop, calls=%fused_computation.3 | loop fusion | flops 2228224 | bytes 1115136 | tf_op jit(solution)/shard_map/convert_element_type | solution.py:507
  32.5 2.1 %collective-permute-done.3.refs_2_ = bf16[384,128]{1,0:T(8,128)(2,1)S(1)} collective-permute-done((bf16[384,128]{1,0:T(8,128)(2,1)S(1)}, bf16[384,128]{1,0:T(8,128)(2,1)S(1)}, u32[]{:S(2)}, u32[]{:S(2)}) %collective-permute-start.3) | collective-permute-done | bytes 98336 | tf_op jit(solution)/shard_map/ppermute | solution.py:526
  34.6 1.1 %collective-permute-done.4.refs_3_ = bf16[384,128]{1,0:T(8,128)(2,1)S(1)} collective-permute-done((bf16[384,128]{1,0:T(8,128)(2,1)S(1)}, bf16[384,128]{1,0:T(8,128)(2,1)S(1)}, u32[]{:S(2)}, u32[]{:S(2)}) %collective-permute-start.4) | collective-permute-done | bytes 98336 | tf_op jit(solution)/shard_map/ppermute | solution.py:526
  35.7 0.6 %core_pack.2 = bf16[4,224,128]{2,1,0:T(8,128)(2,1)S(1)} custom-call(s32[2]{0:T(128)S(1)} %pad_add_fusion.tile_ref, bf16[384,128]{1,0:T(8,128)(2,1)S(1)} %collective-permute-done.1.refs_0_, bf16[384,128]{1,0:T(8,128)(2,1)S(1)} %collective-permute-done.2.refs_1_, bf16[384,128]{1,0:T(8,128)(2,1)S(1)} %collective-permute-done.3.refs_2_, ...), custom_call_target="tpu_custom_call" | custom-call | tf_op jit(solution)/shard_map/core_pack/pallas_call | solution.py:530
  36.3 0.1 collective-permute-start.8
  36.4 0.2 collective-permute-done.6.refs_1_.refs_5_
  36.6 0.6 %core_pack.3 = bf16[4,224,128]{2,1,0:T(8,128)(2,1)S(1)} custom-call(s32[2]{0:T(128)S(1)} %pad_add_fusion.tile_ref, bf16[384,128]{1,0:T(8,128)(2,1)S(1)} %collective-permute-done.5.refs_0_.refs_4_, bf16[384,128]{1,0:T(8,128)(2,1)S(1)} %collective-permute-done.6.refs_1_.refs_5_, bf16[384,128]{1,0:T(8,128)(2,1)S(1)} %collective-permute-done.7.refs_2_.refs_6_, ...), custom_call_target="tpu_custom_call" | custom-call | tf_op jit(solution)/shard_map/core_pack/pallas_call | solution.py:530
  37.2 0.4 collective-permute-start.9
  37.7 0.1 copy.27
  37.8 0.1 copy.23
  38.0 0.1 copy.28.refs_11_
  38.1 2.5 %copy.26 = bf16[2,2,3,64,3,64]{5,4,3,2,1,0:T(4,128)(2,1)} copy(bf16[2,2,3,64,3,64]{5,3,2,4,1,0:T(8,128)(2,1)} %bitcast.18) | data formatting | bytes 589824 | tf_op jit(solution)/shard_map/transpose | solution.py:488
  40.6 1.7 %reshape.80.refs_12_ = bf16[4,192,192]{2,1,0:T(8,128)(2,1)S(1)} reshape(bf16[2,2,3,64,3,64]{5,4,3,2,1,0:T(4,128)(2,1)} %copy.26) | data formatting | bytes 589824 | tf_op jit(solution)/shard_map/reshape | solution.py:488
  42.3 10.6 %stack.18 = f32[16,128]{1,0:T(8,128)} custom-call(s32[2]{0:T(128)S(1)} %pad_add_fusion.tile_ref, bf16[384,128]{1,0:T(8,128)(2,1)S(1)} %collective-permute-done.1.refs_0_, bf16[384,128]{1,0:T(8,128)(2,1)S(1)} %collective-permute-done.2.refs_1_, bf16[384,128]{1,0:T(8,128)(2,1)S(1)} %collective-permute-done.3.refs_2_, ...), custom_call_target="tpu_custom_call" | custom-call | tf_op jit(solution)/shard_map/stack/pallas_call | solution.py:540
  (25 shorter events, 0.2 us)
Async XLA Ops:
  0.0 31.8 %copy-start.5 = (s32[128]{0:T(128)S(1)}, s32[128]{0:T(128)}, u32[]{:S(2)}) copy-start(s32[128]{0:T(128)} %constant.34.clone) | copy-start | bytes 1540
  0.0 31.8 %copy-start.6 = (s32[128]{0:T(128)S(1)}, s32[128]{0:T(128)}, u32[]{:S(2)}) copy-start(s32[128]{0:T(128)} %constant.33.clone) | copy-start | bytes 1540
  0.1 1.1 %copy-start = (bf16[9,256,128]{2,1,0:T(8,128)(2,1)S(1)}, bf16[9,256,128]{2,1,0:T(8,128)(2,1)}, u32[]{:S(2)}) copy-start(bf16[9,256,128]{2,1,0:T(8,128)(2,1)} %maps_ref.3) | copy-start | bytes 1769476
  2.1 11.3 %collective-permute-start = (bf16[1376,128]{1,0:T(8,128)(2,1)S(1)}, bf16[1376,128]{1,0:T(8,128)(2,1)S(1)}, u32[]{:S(2)}, u32[]{:S(2)}) collective-permute-start(bf16[1376,128]{1,0:T(8,128)(2,1)S(1)} %bitcast.17), channel_id=1, source_target_pairs={{0,1},{1,0},{2,3},{3,2},{4,5},{5,4},{6,7},{7,6},{8,9},{9,8},{10,11... | collective-permute-start | bytes 1056776 | tf_op jit(solution)/shard_map/ppermute | solution.py:478
  15.0 10.1 %collective-permute-start.1 = (bf16[384,128]{1,0:T(8,128)(2,1)S(1)}, bf16[384,128]{1,0:T(8,128)(2,1)S(1)}, u32[]{:S(2)}, u32[]{:S(2)}) collective-permute-start(bf16[384,128]{1,0:T(8,128)(2,1)S(1)} %get-tuple-element.19), channel_id=1, source_target_pairs={{0,28},{2,30},{4,24},{6,26},{8,20},{10,22},{12,16},{14,18},{16,12}... | collective-permute-start | bytes 294920 | tf_op jit(solution)/shard_map/ppermute | solution.py:526
  19.8 10.9 %collective-permute-start.2 = (bf16[384,128]{1,0:T(8,128)(2,1)S(1)}, bf16[384,128]{1,0:T(8,128)(2,1)S(1)}, u32[]{:S(2)}, u32[]{:S(2)}) collective-permute-start(bf16[384,128]{1,0:T(8,128)(2,1)S(1)} %get-tuple-element.20), channel_id=1, source_target_pairs={{0,24},{2,26},{4,28},{6,30},{8,16},{10,18},{12,20},{14,22},{16,8},... | collective-permute-start | bytes 294920 | tf_op jit(solution)/shard_map/ppermute | solution.py:526
  20.0 14.6 %collective-permute-start.3 = (bf16[384,128]{1,0:T(8,128)(2,1)S(1)}, bf16[384,128]{1,0:T(8,128)(2,1)S(1)}, u32[]{:S(2)}, u32[]{:S(2)}) collective-permute-start(bf16[384,128]{1,0:T(8,128)(2,1)S(1)} %get-tuple-element.21), channel_id=1, source_target_pairs={{0,20},{2,22},{4,16},{6,18},{8,28},{10,30},{12,24},{14,26},{16,4},... | collective-permute-start | bytes 294920 | tf_op jit(solution)/shard_map/ppermute | solution.py:526
  20.8 14.9 %collective-permute-start.4 = (bf16[384,128]{1,0:T(8,128)(2,1)S(1)}, bf16[384,128]{1,0:T(8,128)(2,1)S(1)}, u32[]{:S(2)}, u32[]{:S(2)}) collective-permute-start(bf16[384,128]{1,0:T(8,128)(2,1)S(1)} %get-tuple-element.22), channel_id=1, source_target_pairs={{0,16},{2,18},{4,20},{6,22},{8,24},{10,26},{12,28},{14,30},{16,0},... | collective-permute-start | bytes 294920 | tf_op jit(solution)/shard_map/ppermute | solution.py:526
  22.8 13.6 %collective-permute-start.5 = (bf16[384,128]{1,0:T(8,128)(2,1)S(1)}, bf16[384,128]{1,0:T(8,128)(2,1)S(1)}, u32[]{:S(2)}, u32[]{:S(2)}) collective-permute-start(bf16[384,128]{1,0:T(8,128)(2,1)S(1)} %get-tuple-element.23), channel_id=1, source_target_pairs={{0,12},{2,14},{4,8},{6,10},{8,4},{10,6},{12,0},{14,2},{16,28},{18,... | collective-permute-start | bytes 294920 | tf_op jit(solution)/shard_map/ppermute | solution.py:526
  25.1 11.5 %collective-permute-start.6 = (bf16[384,128]{1,0:T(8,128)(2,1)S(1)}, bf16[384,128]{1,0:T(8,128)(2,1)S(1)}, u32[]{:S(2)}, u32[]{:S(2)}) collective-permute-start(bf16[384,128]{1,0:T(8,128)(2,1)S(1)} %get-tuple-element.24), channel_id=1, source_target_pairs={{0,8},{2,10},{4,12},{6,14},{8,0},{10,2},{12,4},{14,6},{16,24},{18,... | collective-permute-start | bytes 294920 | tf_op jit(solution)/shard_map/ppermute | solution.py:526
  30.7 6.9 %copy-start.2 = (s32[4352]{0:T(1024)S(1)}, s32[4352]{0:T(1024)}, u32[]{:S(2)}) copy-start(s32[4352]{0:T(1024)} %constant.32.clone) | copy-start | bytes 52228
  30.7 6.9 %copy-start.3 = (s32[4352]{0:T(1024)S(1)}, s32[4352]{0:T(1024)}, u32[]{:S(2)}) copy-start(s32[4352]{0:T(1024)} %constant.31.clone) | copy-start | bytes 52228
  30.7 6.9 %copy-start.4 = (f32[2,2,64]{2,1,0:T(2,128)S(1)}, f32[2,2,64]{2,1,0:T(2,128)}, u32[]{:S(2)}) copy-start(f32[2,2,64]{2,1,0:T(2,128)} %param.14) | copy-start | bytes 3076
  30.7 6.9 %copy-start.7 = (f32[64]{0:T(128)S(1)}, f32[64]{0:T(128)}, u32[]{:S(2)}) copy-start(f32[64]{0:T(128)} %param.15) | copy-start | bytes 772
  30.7 6.9 %copy-start.8 = (f32[64]{0:T(128)S(1)}, f32[64]{0:T(128)}, u32[]{:S(2)}) copy-start(f32[64]{0:T(128)} %param.12) | copy-start | bytes 772
  30.7 7.0 %copy-start.1 = (bf16[64,144]{1,0:T(8,128)(2,1)S(1)}, bf16[64,144]{1,0:T(8,128)(2,1)}, u32[]{:S(2)}) copy-start(bf16[64,144]{1,0:T(8,128)(2,1)} %refs_10_.1) | copy-start | bytes 55300
  30.7 5.8 %collective-permute-start.7 = (bf16[384,128]{1,0:T(8,128)(2,1)S(1)}, bf16[384,128]{1,0:T(8,128)(2,1)S(1)}, u32[]{:S(2)}, u32[]{:S(2)}) collective-permute-start(bf16[384,128]{1,0:T(8,128)(2,1)S(1)} %get-tuple-element.25), channel_id=1, source_target_pairs={{0,4},{2,6},{4,0},{6,2},{8,12},{10,14},{12,8},{14,10},{16,20},{18,... | collective-permute-start | bytes 294920 | tf_op jit(solution)/shard_map/ppermute | solution.py:526
  36.3 5.9 %collective-permute-start.8 = (bf16[4,224,128]{2,1,0:T(8,128)(2,1)S(1)}, bf16[4,224,128]{2,1,0:T(8,128)(2,1)S(1)}, u32[]{:S(2)}, u32[]{:S(2)}) collective-permute-start(bf16[4,224,128]{2,1,0:T(8,128)(2,1)S(1)} %core_pack.2), channel_id=1, source_target_pairs={{0,2},{2,0},{4,6},{6,4},{8,10},{10,8},{12,14},{14,12},{16,18},{18,... | collective-permute-start | bytes 688136 | tf_op jit(solution)/shard_map/ppermute | solution.py:538
  37.2 5.1 %collective-permute-start.9 = (bf16[4,224,128]{2,1,0:T(8,128)(2,1)S(1)}, bf16[4,224,128]{2,1,0:T(8,128)(2,1)S(1)}, u32[]{:S(2)}, u32[]{:S(2)}) collective-permute-start(bf16[4,224,128]{2,1,0:T(8,128)(2,1)S(1)} %core_pack.3), channel_id=1, source_target_pairs={{0,2},{2,0},{4,6},{6,4},{8,10},{10,8},{12,14},{14,12},{16,18},{18,... | collective-permute-start | bytes 688136 | tf_op jit(solution)/shard_map/ppermute | solution.py:538

commit v6 on v5

--- a/solution.py
+++ b/solution.py
@@ -1,4 +1,5 @@
 import functools
+import math
 from typing import NamedTuple
 
 import jax
@@ -11,7 +12,6 @@
 
 BF16, F32 = jnp.bfloat16, jnp.float32
 LANES = 128
-VMEM_LIMIT = 48 * 1024 * 1024
 
 
 def up(value, step):
@@ -445,8 +445,22 @@
         out_ref[r : r + 1, :] = shifted(logit_ref, slice(0, 1), low, begin - low, cols)
 
 
-def whole(space=pltpu.VMEM):
-    return pl.BlockSpec(memory_space=space)
+def call(kernel, name, args, outs, scratch=()):
+    held = sum(math.prod(x.shape) * jnp.dtype(x.dtype).itemsize for x in [*args, *outs, *scratch])
+    vmem = pl.BlockSpec(memory_space=pltpu.VMEM)
+    return pl.pallas_call(
+        kernel,
+        out_shape=list(outs),
+        in_specs=[pl.BlockSpec(memory_space=pltpu.SMEM)] + [vmem] * (len(args) - 1),
+        out_specs=[vmem] * len(outs),
+        scratch_shapes=list(scratch),
+        compiler_params=pltpu.CompilerParams(vmem_limit_bytes=held * 5 // 4 + 4 * 1024 * 1024),
+        name=name,
+    )(*args)
+
+
+def array(dtype, *shape):
+    return jax.ShapeDtypeStruct(shape, dtype)
 
 
 def on_device(attention, proj_weight, proj_bias, conv_weight, conv_bias, out_weight):
@@ -458,21 +472,17 @@
     me = lax.axis_index("tile").astype(jnp.int32)
     band_index = lax.axis_index("head").astype(jnp.int32)
     tile = jnp.stack([me, band_index])
-    params = pltpu.CompilerParams(vmem_limit_bytes=VMEM_LIMIT)
-
-    payload_rows = maps * cols + plan.tail_rows
-    payload, sums, edge = pl.pallas_call(
+
+    payload, sums, edge = call(
         functools.partial(mirror_pack, plan),
-        out_shape=[
-            jax.ShapeDtypeStruct((tiles - 1, payload_rows, cols), BF16),
-            jax.ShapeDtypeStruct((plan.map_rows, width), F32),
-            jax.ShapeDtypeStruct((plan.edge_rows, cols), F32),
+        "mirror_pack",
+        [tile, attention],
+        [
+            array(BF16, tiles - 1, maps * cols + plan.tail_rows, cols),
+            array(F32, plan.map_rows, width),
+            array(F32, plan.edge_rows, cols),
         ],
-        in_specs=[whole(pltpu.SMEM), whole()],
-        out_specs=[whole()] * 3,
-        compiler_params=params,
-        name="mirror_pack",
-    )(tile, attention)
+    )
     received = jnp.stack(
         [
             lax.ppermute(payload[s - 1], "tile", [(i, (i + s) % tiles) for i in range(tiles)])
@@ -507,19 +517,17 @@
         spots.append(functools.reduce(jnp.logical_or, hit).astype(BF16))
     spots = jnp.stack(spots)
 
+    weights = (side_weight, kernels, vectors, mask, spots)
+    received, weights = lax.optimization_barrier((received, weights))
+
     chips = plan.chips
-    blocks = pl.pallas_call(
+    blocks = call(
         functools.partial(correct_pack, plan),
-        out_shape=[jax.ShapeDtypeStruct((plan.block_rows, cols), BF16)] * chips,
-        in_specs=[whole(pltpu.SMEM)] + [whole()] * 4,
-        out_specs=[whole()] * chips,
-        scratch_shapes=[
-            pltpu.VMEM((maps, width + 24, cols), F32),
-            pltpu.VMEM((width, LANES), F32),
-        ],
-        compiler_params=params,
-        name="correct_pack",
-    )(tile, attention, received, sums, edge)
+        "correct_pack",
+        [tile, attention, received, sums, edge],
+        [array(BF16, plan.block_rows, cols)] * chips,
+        [pltpu.VMEM((maps, width + 24, cols), F32), pltpu.VMEM((width, LANES), F32)],
+    )
     grouped = list(blocks)[::-1]
     for step in reversed(range(1, chips)):
         pairs = [(i, 2 * partner(i // 2, step, chips) + i % 2) for i in range(heads)]
@@ -527,22 +535,20 @@
     order = [list(range(chips - 1, chips // 2 - 1, -1)), list(range(chips // 2 - 1, -1, -1))]
     swapped = []
     for steps in order:
-        packed = pl.pallas_call(
+        (packed,) = call(
             functools.partial(core_pack, plan),
-            out_shape=jax.ShapeDtypeStruct((len(steps), plan.half_rows, cols), BF16),
-            in_specs=[whole(pltpu.SMEM)] + [whole()] * len(steps),
-            out_specs=whole(),
-            compiler_params=params,
-            name="core_pack",
-        )(tile, *[grouped[k] for k in steps])
+            "core_pack",
+            [tile] + [grouped[k] for k in steps],
+            [array(BF16, len(steps), plan.half_rows, cols)],
+        )
         swapped.append(lax.ppermute(packed, "head", [(i, i ^ 1) for i in range(heads)]))
 
-    return pl.pallas_call(
+    (logits,) = call(
         functools.partial(stack, plan, order),
-        out_shape=jax.ShapeDtypeStruct((plan.band, cols), F32),
-        in_specs=[whole(pltpu.SMEM)] + [whole()] * (chips + len(order) + 6),
-        out_specs=whole(),
-        scratch_shapes=[
+        "stack",
+        [tile, *grouped[::-1], *swapped, proj_weight, *weights],
+        [array(F32, plan.band, cols)],
+        [
             pltpu.VMEM((heads * maps * plan.rows, cols), F32),
             pltpu.VMEM((heads * plan.side_rows, cols), F32),
             pltpu.VMEM((feat, plan.lanes), F32),
@@ -551,9 +557,8 @@
             pltpu.VMEM((3 * feat, plan.lanes), F32),
             pltpu.VMEM((8, plan.lanes), F32),
         ],
-        compiler_params=params,
-        name="stack",
-    )(tile, *grouped[::-1], *swapped, proj_weight, side_weight, kernels, vectors, mask, spots)
+    )
+    return logits
 
 
 def solution(mesh):

time: 53 us -> 49.5 us (0.934)
  waiting for transfers between devices: 11.6 us -> 7.46 us
  other arithmetic: 0.75 us -> 1.42 us
    ppermute x1, waiting for transfers between devices: 8.24 us -> 2.22 us  [on_device(): lax.ppermute(payload[s - 1], 'tile', [(i, (i + s) % tiles) for i in range...]
    ppermute x2, waiting for transfers between devices: 0.01 us -> 1.06 us  [on_device(): lax.ppermute(packed, 'head', [(i, i ^ 1) for i in range(heads)])]
    ppermute x7, waiting for transfers between devices: 3.39 us -> 4.18 us  [on_device(): grouped[step] = lax.ppermute(grouped[step], 'head', pairs)]
    convert_element_type x1, other arithmetic: 0.66 us -> 1.33 us  [on_device(): spots.append(functools.reduce(jnp.logical_or, hit).astype(BF16))]
    unnamed x20 -> x18, local copies, waits for them, and re-layouts: 1.22 us -> 1.21 us
  transfers between devices with their start and end apart: 10 -> 10, of which waited for: 4 -> 6; matrix products, arithmetic and copies ran while one was open for 10% -> 12% of each run, Pallas kernels for 2% -> 2%
where the time goes in v6:
time: 49.5 us; the launch traced here: 49.3 us
  starting transfers between devices  20.2 us (41%)
  Pallas kernels  14.3 us (29%)
  waiting for transfers between devices  7.46 us (15%)
  local copies, waits for them, and re-layouts  5.69 us (11%)
  other arithmetic  1.42 us (3%)
    ppermute x7, starting transfers between devices, on_device(): grouped[step] = lax.ppermute(grouped[step], 'head', pairs)  16.7 us
    pallas_call x5, Pallas kernels, call(): pl.pallas_call(kernel, out_shape=list(outs), in_specs=[pl.BlockSpec(memor...  14.3 us
    ppermute x7, waiting for transfers between devices, on_device(): grouped[step] = lax.ppermute(grouped[step], 'head', pairs)  4.18 us
    ppermute x1, starting transfers between devices, on_device(): lax.ppermute(payload[s - 1], 'tile', [(i, (i + s) % tiles) for i in range...  3.03 us
    transpose x1, local copies, waits for them, and re-layouts, on_device(): conv_weight.transpose(0, 1, 5, 2, 4, 3)  2.53 us
    ppermute x1, waiting for transfers between devices, on_device(): lax.ppermute(payload[s - 1], 'tile', [(i, (i + s) % tiles) for i in range...  2.22 us
    reshape x1, local copies, waits for them, and re-layouts, on_device(): conv_weight.transpose(0, 1, 5, 2, 4, 3)  1.69 us
    convert_element_type x1, other arithmetic, on_device(): spots.append(functools.reduce(jnp.logical_or, hit).astype(BF16))  1.33 us
  transfers between devices with their start and end apart: 10, of which 6 were waited for; matrix products, arithmetic and copies ran while one was open for 12% of the time, Pallas kernels for 2%

profile of v6, /device:TPU:0, one launch (start us, length us, event | category | flops | bytes accessed | tf_op | source)
XLA Modules:
  0.0 49.3 jit_solution(8599053534361136292)
XLA Ops:
  0.0 0.1 pad_add_fusion.tile_ref
  0.1 1.1 %copy-done = bf16[9,256,128]{2,1,0:T(8,128)(2,1)S(1)} copy-done((bf16[9,256,128]{2,1,0:T(8,128)(2,1)S(1)}, bf16[9,256,128]{2,1,0:T(8,128)(2,1)}, u32[]{:S(2)}) %copy-start) | copy-done | bytes 589848
  1.2 1.0 %mirror_pack.1 = (bf16[1,1376,128]{2,1,0:T(8,128)(2,1)S(1)}, f32[16,256]{1,0:T(8,128)S(1)}, f32[40,128]{1,0:T(8,128)S(1)}) custom-call(s32[2]{0:T(128)S(1)} %pad_add_fusion.tile_ref, bf16[9,256,128]{2,1,0:T(8,128)(2,1)S(1)} %copy-done), custom_call_target="tpu_custom_call" | custom-call | tf_op jit(solution)/shard_map/mirror_pack/pallas_call | solution.py:451
  2.2 3.0 %collective-permute-start = (bf16[1376,128]{1,0:T(8,128)(2,1)S(1)}, bf16[1376,128]{1,0:T(8,128)(2,1)S(1)}, u32[]{:S(2)}, u32[]{:S(2)}) collective-permute-start(bf16[1376,128]{1,0:T(8,128)(2,1)S(1)} %bitcast.17), channel_id=1, source_target_pairs={{0,1},{1,0},{2,3},{3,2},{4,5},{5,4},{6,7},{7,6},{8,9},{9,8},{10,11... | collective-permute-start | bytes 1056776 | tf_op jit(solution)/shard_map/ppermute | solution.py:488
  5.2 1.3 %fusion.1.refs_15_ = bf16[1,128,4352]{2,1,0:T(8,128)(2,1)S(1)} fusion(s32[128]{0:T(128)} %constant.34.clone, s32[128]{0:T(128)} %constant.33.clone), kind=kLoop, calls=%fused_computation.3 | loop fusion | flops 2228224 | bytes 1115136 | tf_op jit(solution)/shard_map/convert_element_type | solution.py:517
  6.6 0.1 copy.27
  6.7 0.1 copy.23
  7.0 0.0 copy-start.1
  7.0 2.5 %copy.26 = bf16[2,2,3,64,3,64]{5,4,3,2,1,0:T(4,128)(2,1)} copy(bf16[2,2,3,64,3,64]{5,3,2,4,1,0:T(8,128)(2,1)} %bitcast.18) | data formatting | bytes 589824 | tf_op jit(solution)/shard_map/transpose | solution.py:498
  9.5 1.7 %reshape.80.refs_12_ = bf16[4,192,192]{2,1,0:T(8,128)(2,1)S(1)} reshape(bf16[2,2,3,64,3,64]{5,4,3,2,1,0:T(4,128)(2,1)} %copy.26) | data formatting | bytes 589824 | tf_op jit(solution)/shard_map/reshape | solution.py:498
  11.2 2.2 %collective-permute-done = bf16[1376,128]{1,0:T(8,128)(2,1)S(1)} collective-permute-done((bf16[1376,128]{1,0:T(8,128)(2,1)S(1)}, bf16[1376,128]{1,0:T(8,128)(2,1)S(1)}, u32[]{:S(2)}, u32[]{:S(2)}) %collective-permute-start) | collective-permute-done | bytes 352288 | tf_op jit(solution)/shard_map/ppermute | solution.py:488
  13.4 1.6 %correct_pack.1 = (bf16[384,128]{1,0:T(8,128)(2,1)S(1)}, bf16[384,128]{1,0:T(8,128)(2,1)S(1)}, bf16[384,128]{1,0:T(8,128)(2,1)S(1)}, bf16[384,128]{1,0:T(8,128)(...) custom-call(s32[2]{0:T(128)S(1)} %pad_add_fusion.tile_ref, ...), custom_call_target="tpu_custom_call" | custom-call | tf_op jit(solution)/shard_map/correct_pack/pallas_call | solution.py:451
  15.0 4.8 %collective-permute-start.1 = (bf16[384,128]{1,0:T(8,128)(2,1)S(1)}, bf16[384,128]{1,0:T(8,128)(2,1)S(1)}, u32[]{:S(2)}, u32[]{:S(2)}) collective-permute-start(bf16[384,128]{1,0:T(8,128)(2,1)S(1)} %get-tuple-element.26), channel_id=1, source_target_pairs={{0,28},{2,30},{4,24},{6,26},{8,20},{10,22},{12,16},{14,18},{16,12}... | collective-permute-start | bytes 294920 | tf_op jit(solution)/shard_map/ppermute | solution.py:534
  19.8 0.2 collective-permute-start.2
  20.0 0.8 %collective-permute-start.3 = (bf16[384,128]{1,0:T(8,128)(2,1)S(1)}, bf16[384,128]{1,0:T(8,128)(2,1)S(1)}, u32[]{:S(2)}, u32[]{:S(2)}) collective-permute-start(bf16[384,128]{1,0:T(8,128)(2,1)S(1)} %get-tuple-element.28), channel_id=1, source_target_pairs={{0,20},{2,22},{4,16},{6,18},{8,28},{10,30},{12,24},{14,26},{16,4},... | collective-permute-start | bytes 294920 | tf_op jit(solution)/shard_map/ppermute | solution.py:534
  20.8 2.0 %collective-permute-start.4 = (bf16[384,128]{1,0:T(8,128)(2,1)S(1)}, bf16[384,128]{1,0:T(8,128)(2,1)S(1)}, u32[]{:S(2)}, u32[]{:S(2)}) collective-permute-start(bf16[384,128]{1,0:T(8,128)(2,1)S(1)} %get-tuple-element.29), channel_id=1, source_target_pairs={{0,16},{2,18},{4,20},{6,22},{8,24},{10,26},{12,28},{14,30},{16,0},... | collective-permute-start | bytes 294920 | tf_op jit(solution)/shard_map/ppermute | solution.py:534
  22.8 2.3 %collective-permute-start.5 = (bf16[384,128]{1,0:T(8,128)(2,1)S(1)}, bf16[384,128]{1,0:T(8,128)(2,1)S(1)}, u32[]{:S(2)}, u32[]{:S(2)}) collective-permute-start(bf16[384,128]{1,0:T(8,128)(2,1)S(1)} %get-tuple-element.30), channel_id=1, source_target_pairs={{0,12},{2,14},{4,8},{6,10},{8,4},{10,6},{12,0},{14,2},{16,28},{18,... | collective-permute-start | bytes 294920 | tf_op jit(solution)/shard_map/ppermute | solution.py:534
  25.1 0.0 collective-permute-done.1.refs_0_
  25.1 5.6 %collective-permute-start.6 = (bf16[384,128]{1,0:T(8,128)(2,1)S(1)}, bf16[384,128]{1,0:T(8,128)(2,1)S(1)}, u32[]{:S(2)}, u32[]{:S(2)}) collective-permute-start(bf16[384,128]{1,0:T(8,128)(2,1)S(1)} %get-tuple-element.31), channel_id=1, source_target_pairs={{0,8},{2,10},{4,12},{6,14},{8,0},{10,2},{12,4},{14,6},{16,24},{18,... | collective-permute-start | bytes 294920 | tf_op jit(solution)/shard_map/ppermute | solution.py:534
  30.7 0.0 collective-permute-done.2.refs_1_
  30.7 1.0 %collective-permute-start.7 = (bf16[384,128]{1,0:T(8,128)(2,1)S(1)}, bf16[384,128]{1,0:T(8,128)(2,1)S(1)}, u32[]{:S(2)}, u32[]{:S(2)}) collective-permute-start(bf16[384,128]{1,0:T(8,128)(2,1)S(1)} %get-tuple-element.32), channel_id=1, source_target_pairs={{0,4},{2,6},{4,0},{6,2},{8,12},{10,14},{12,8},{14,10},{16,20},{18,... | collective-permute-start | bytes 294920 | tf_op jit(solution)/shard_map/ppermute | solution.py:534
  31.7 2.9 %collective-permute-done.3.refs_2_ = bf16[384,128]{1,0:T(8,128)(2,1)S(1)} collective-permute-done((bf16[384,128]{1,0:T(8,128)(2,1)S(1)}, bf16[384,128]{1,0:T(8,128)(2,1)S(1)}, u32[]{:S(2)}, u32[]{:S(2)}) %collective-permute-start.3) | collective-permute-done | bytes 98336 | tf_op jit(solution)/shard_map/ppermute | solution.py:534
  34.6 1.1 %collective-permute-done.4.refs_3_ = bf16[384,128]{1,0:T(8,128)(2,1)S(1)} collective-permute-done((bf16[384,128]{1,0:T(8,128)(2,1)S(1)}, bf16[384,128]{1,0:T(8,128)(2,1)S(1)}, u32[]{:S(2)}, u32[]{:S(2)}) %collective-permute-start.4) | collective-permute-done | bytes 98336 | tf_op jit(solution)/shard_map/ppermute | solution.py:534
  35.7 0.6 %core_pack.2 = bf16[4,224,128]{2,1,0:T(8,128)(2,1)S(1)} custom-call(s32[2]{0:T(128)S(1)} %pad_add_fusion.tile_ref, bf16[384,128]{1,0:T(8,128)(2,1)S(1)} %collective-permute-done.1.refs_0_, bf16[384,128]{1,0:T(8,128)(2,1)S(1)} %collective-permute-done.2.refs_1_, bf16[384,128]{1,0:T(8,128)(2,1)S(1)} %collective-permute-done.3.refs_2_, ...), custom_call_target="tpu_custom_call" | custom-call | tf_op jit(solution)/shard_map/core_pack/pallas_call | solution.py:451
  36.3 0.1 collective-permute-start.8
  36.4 0.2 collective-permute-done.6.refs_1_.refs_5_
  36.6 0.6 %core_pack.3 = bf16[4,224,128]{2,1,0:T(8,128)(2,1)S(1)} custom-call(s32[2]{0:T(128)S(1)} %pad_add_fusion.tile_ref, bf16[384,128]{1,0:T(8,128)(2,1)S(1)} %collective-permute-done.5.refs_0_.refs_4_, bf16[384,128]{1,0:T(8,128)(2,1)S(1)} %collective-permute-done.6.refs_1_.refs_5_, bf16[384,128]{1,0:T(8,128)(2,1)S(1)} %collective-permute-done.7.refs_2_.refs_6_, ...), custom_call_target="tpu_custom_call" | custom-call | tf_op jit(solution)/shard_map/core_pack/pallas_call | solution.py:451
  37.2 0.4 collective-permute-start.9
  37.6 0.1 copy.28.refs_11_
  37.7 0.2 collective-permute-done.8.refs_8_
  37.9 0.9 %collective-permute-done.9.refs_9_ = bf16[4,224,128]{2,1,0:T(8,128)(2,1)S(1)} collective-permute-done((bf16[4,224,128]{2,1,0:T(8,128)(2,1)S(1)}, bf16[4,224,128]{2,1,0:T(8,128)(2,1)S(1)}, u32[]{:S(2)}, u32[]{:S(2)}) %collective-permute-start.9) | collective-permute-done | bytes 229408 | tf_op jit(solution)/shard_map/ppermute | solution.py:544
  38.8 10.5 %stack.18 = f32[16,128]{1,0:T(8,128)} custom-call(s32[2]{0:T(128)S(1)} %pad_add_fusion.tile_ref, bf16[384,128]{1,0:T(8,128)(2,1)S(1)} %collective-permute-done.1.refs_0_, bf16[384,128]{1,0:T(8,128)(2,1)S(1)} %collective-permute-done.2.refs_1_, bf16[384,128]{1,0:T(8,128)(2,1)S(1)} %collective-permute-done.3.refs_2_, ...), custom_call_target="tpu_custom_call" | custom-call | tf_op jit(solution)/shard_map/stack/pallas_call | solution.py:451
  (23 shorter events, 0.2 us)
Async XLA Ops:
  0.0 6.5 %copy-start.3 = (s32[4352]{0:T(1024)S(1)}, s32[4352]{0:T(1024)}, u32[]{:S(2)}) copy-start(s32[4352]{0:T(1024)} %constant.32.clone) | copy-start | bytes 52228
  0.0 6.6 %copy-start.6 = (f32[64]{0:T(128)S(1)}, f32[64]{0:T(128)}, u32[]{:S(2)}) copy-start(f32[64]{0:T(128)} %param.15) | copy-start | bytes 772
  0.1 1.1 %copy-start = (bf16[9,256,128]{2,1,0:T(8,128)(2,1)S(1)}, bf16[9,256,128]{2,1,0:T(8,128)(2,1)}, u32[]{:S(2)}) copy-start(bf16[9,256,128]{2,1,0:T(8,128)(2,1)} %maps_ref.3) | copy-start | bytes 1769476
  1.1 5.4 %copy-start.4 = (s32[4352]{0:T(1024)S(1)}, s32[4352]{0:T(1024)}, u32[]{:S(2)}) copy-start(s32[4352]{0:T(1024)} %constant.31.clone) | copy-start | bytes 52228
  1.1 5.5 %copy-start.5 = (f32[2,2,64]{2,1,0:T(2,128)S(1)}, f32[2,2,64]{2,1,0:T(2,128)}, u32[]{:S(2)}) copy-start(f32[2,2,64]{2,1,0:T(2,128)} %param.14) | copy-start | bytes 3076
  1.1 5.5 %copy-start.7 = (f32[64]{0:T(128)S(1)}, f32[64]{0:T(128)}, u32[]{:S(2)}) copy-start(f32[64]{0:T(128)} %param.12) | copy-start | bytes 772
  1.2 5.6 %copy-start.2 = (bf16[64,144]{1,0:T(8,128)(2,1)S(1)}, bf16[64,144]{1,0:T(8,128)(2,1)}, u32[]{:S(2)}) copy-start(bf16[64,144]{1,0:T(8,128)(2,1)} %refs_10_.1) | copy-start | bytes 55300
  2.2 11.3 %collective-permute-start = (bf16[1376,128]{1,0:T(8,128)(2,1)S(1)}, bf16[1376,128]{1,0:T(8,128)(2,1)S(1)}, u32[]{:S(2)}, u32[]{:S(2)}) collective-permute-start(bf16[1376,128]{1,0:T(8,128)(2,1)S(1)} %bitcast.17), channel_id=1, source_target_pairs={{0,1},{1,0},{2,3},{3,2},{4,5},{5,4},{6,7},{7,6},{8,9},{9,8},{10,11... | collective-permute-start | bytes 1056776 | tf_op jit(solution)/shard_map/ppermute | solution.py:488
  7.0 6.5 %copy-start.1 = (bf16[9,256,128]{2,1,0:T(8,128)(2,1)S(1)}, bf16[9,256,128]{2,1,0:T(8,128)(2,1)}, u32[]{:S(2)}) copy-start(bf16[9,256,128]{2,1,0:T(8,128)(2,1)} %maps_ref.3) | copy-start | bytes 1769476
  15.0 10.1 %collective-permute-start.1 = (bf16[384,128]{1,0:T(8,128)(2,1)S(1)}, bf16[384,128]{1,0:T(8,128)(2,1)S(1)}, u32[]{:S(2)}, u32[]{:S(2)}) collective-permute-start(bf16[384,128]{1,0:T(8,128)(2,1)S(1)} %get-tuple-element.26), channel_id=1, source_target_pairs={{0,28},{2,30},{4,24},{6,26},{8,20},{10,22},{12,16},{14,18},{16,12}... | collective-permute-start | bytes 294920 | tf_op jit(solution)/shard_map/ppermute | solution.py:534
  19.8 10.9 %collective-permute-start.2 = (bf16[384,128]{1,0:T(8,128)(2,1)S(1)}, bf16[384,128]{1,0:T(8,128)(2,1)S(1)}, u32[]{:S(2)}, u32[]{:S(2)}) collective-permute-start(bf16[384,128]{1,0:T(8,128)(2,1)S(1)} %get-tuple-element.27), channel_id=1, source_target_pairs={{0,24},{2,26},{4,28},{6,30},{8,16},{10,18},{12,20},{14,22},{16,8},... | collective-permute-start | bytes 294920 | tf_op jit(solution)/shard_map/ppermute | solution.py:534
  20.0 14.6 %collective-permute-start.3 = (bf16[384,128]{1,0:T(8,128)(2,1)S(1)}, bf16[384,128]{1,0:T(8,128)(2,1)S(1)}, u32[]{:S(2)}, u32[]{:S(2)}) collective-permute-start(bf16[384,128]{1,0:T(8,128)(2,1)S(1)} %get-tuple-element.28), channel_id=1, source_target_pairs={{0,20},{2,22},{4,16},{6,18},{8,28},{10,30},{12,24},{14,26},{16,4},... | collective-permute-start | bytes 294920 | tf_op jit(solution)/shard_map/ppermute | solution.py:534
  20.8 14.9 %collective-permute-start.4 = (bf16[384,128]{1,0:T(8,128)(2,1)S(1)}, bf16[384,128]{1,0:T(8,128)(2,1)S(1)}, u32[]{:S(2)}, u32[]{:S(2)}) collective-permute-start(bf16[384,128]{1,0:T(8,128)(2,1)S(1)} %get-tuple-element.29), channel_id=1, source_target_pairs={{0,16},{2,18},{4,20},{6,22},{8,24},{10,26},{12,28},{14,30},{16,0},... | collective-permute-start | bytes 294920 | tf_op jit(solution)/shard_map/ppermute | solution.py:534
  22.8 13.6 %collective-permute-start.5 = (bf16[384,128]{1,0:T(8,128)(2,1)S(1)}, bf16[384,128]{1,0:T(8,128)(2,1)S(1)}, u32[]{:S(2)}, u32[]{:S(2)}) collective-permute-start(bf16[384,128]{1,0:T(8,128)(2,1)S(1)} %get-tuple-element.30), channel_id=1, source_target_pairs={{0,12},{2,14},{4,8},{6,10},{8,4},{10,6},{12,0},{14,2},{16,28},{18,... | collective-permute-start | bytes 294920 | tf_op jit(solution)/shard_map/ppermute | solution.py:534
  25.1 11.5 %collective-permute-start.6 = (bf16[384,128]{1,0:T(8,128)(2,1)S(1)}, bf16[384,128]{1,0:T(8,128)(2,1)S(1)}, u32[]{:S(2)}, u32[]{:S(2)}) collective-permute-start(bf16[384,128]{1,0:T(8,128)(2,1)S(1)} %get-tuple-element.31), channel_id=1, source_target_pairs={{0,8},{2,10},{4,12},{6,14},{8,0},{10,2},{12,4},{14,6},{16,24},{18,... | collective-permute-start | bytes 294920 | tf_op jit(solution)/shard_map/ppermute | solution.py:534
  30.7 5.9 %collective-permute-start.7 = (bf16[384,128]{1,0:T(8,128)(2,1)S(1)}, bf16[384,128]{1,0:T(8,128)(2,1)S(1)}, u32[]{:S(2)}, u32[]{:S(2)}) collective-permute-start(bf16[384,128]{1,0:T(8,128)(2,1)S(1)} %get-tuple-element.32), channel_id=1, source_target_pairs={{0,4},{2,6},{4,0},{6,2},{8,12},{10,14},{12,8},{14,10},{16,20},{18,... | collective-permute-start | bytes 294920 | tf_op jit(solution)/shard_map/ppermute | solution.py:534
  36.3 1.6 %collective-permute-start.8 = (bf16[4,224,128]{2,1,0:T(8,128)(2,1)S(1)}, bf16[4,224,128]{2,1,0:T(8,128)(2,1)S(1)}, u32[]{:S(2)}, u32[]{:S(2)}) collective-permute-start(bf16[4,224,128]{2,1,0:T(8,128)(2,1)S(1)} %core_pack.2), channel_id=1, source_target_pairs={{0,2},{2,0},{4,6},{6,4},{8,10},{10,8},{12,14},{14,12},{16,18},{18,... | collective-permute-start | bytes 688136 | tf_op jit(solution)/shard_map/ppermute | solution.py:544
  37.2 1.6 %collective-permute-start.9 = (bf16[4,224,128]{2,1,0:T(8,128)(2,1)S(1)}, bf16[4,224,128]{2,1,0:T(8,128)(2,1)S(1)}, u32[]{:S(2)}, u32[]{:S(2)}) collective-permute-start(bf16[4,224,128]{2,1,0:T(8,128)(2,1)S(1)} %core_pack.3), channel_id=1, source_target_pairs={{0,2},{2,0},{4,6},{6,4},{8,10},{10,8},{12,14},{14,12},{16,18},{18,... | collective-permute-start | bytes 688136 | tf_op jit(solution)/shard_map/ppermute | solution.py:544

commit v7 on v6

--- a/solution.py
+++ b/solution.py
@@ -19,7 +19,9 @@
 
 
 class Plan(NamedTuple):
+    first: int
     maps: int
+    total: int
     width: int
     cols: int
     tiles: int
@@ -40,6 +42,10 @@
         return self.sides * self.halo
 
     @property
+    def last(self):
+        return self.first + self.maps == self.total
+
+    @property
     def edge_rows(self):
         return up(self.maps * self.edges, 8)
 
@@ -65,7 +71,7 @@
 
     @property
     def groups(self):
-        return -(-self.maps // self.slots)
+        return -(-self.total // self.slots)
 
     @property
     def side_rows(self):
@@ -89,7 +95,7 @@
 
     @property
     def lead(self):
-        return self.lone * self.group_rows + self.side_rows
+        return self.lone * self.group_rows + (self.side_rows if self.last else 0)
 
     @property
     def half_rows(self):
@@ -122,10 +128,19 @@
     return (mine - step if back else mine + step) % count
 
 
-def half(plan, block, core):
-    return jnp.where(
-        core == 0, block[: plan.half_rows], block[plan.lead : plan.lead + plan.half_rows]
-    )
+def half(parts, block, core):
+    pieces, base = [], 0
+    for plan in parts:
+        early = block[base : base + plan.half_rows]
+        late = block[base + plan.lead : base + plan.lead + plan.half_rows]
+        pieces.append(jnp.where(core == 0, early, late))
+        base += plan.block_rows
+    return jnp.concatenate(pieces, axis=0)
+
+
+def far_near(plan):
+    steps = list(reversed(range(plan.chips)))
+    return steps[: plan.chips // 2], steps[plan.chips // 2 :]
 
 
 def edge_start(plan, tile, side):
@@ -153,8 +168,13 @@
     return jnp.dot(a, b, preferred_element_type=F32)
 
 
-def mirror_pack(plan, tile_ref, maps_ref, out_ref, sums_ref, edge_ref):
-    me = tile_ref[0]
+def mirror_pack(parts, maps_ref, *refs):
+    for k, plan in enumerate(parts):
+        mirror_pack_part(plan, maps_ref, *refs[3 * k : 3 * k + 3])
+
+
+def mirror_pack_part(plan, maps_ref, out_ref, sums_ref, edge_ref):
+    me = lax.axis_index("tile")
     count, cols, width, tiles = plan.maps, plan.cols, plan.width, plan.tiles
     head, edge = plan.map_rows, plan.edge_rows
 
@@ -170,9 +190,9 @@
         dest = lax.rem(me + shift, tiles)
         by_col = by_row = None
         for index in range(count):
-            block = maps_ref[index]
+            block = maps_ref[plan.first + index]
             out_ref[shift - 1, index * cols : (index + 1) * cols, :] = maps_ref[
-                index, pl.ds(pl.multiple_of(dest * cols, cols), cols), :
+                plan.first + index, pl.ds(pl.multiple_of(dest * cols, cols), cols), :
             ]
             left = [pick(edge, cols, me * cols, dest, index)]
             upper = [pick(edge, width, 0, dest, index)]
@@ -202,9 +222,12 @@
         out_ref[shift - 1, count * cols :, :] = jnp.concatenate(pieces, axis=0).astype(BF16)
 
 
-def correct_pack(plan, tile_ref, maps_ref, recv_ref, sums_ref, edge_ref, *refs):
-    *out_refs, field_ref, turned_ref = refs
-    me, chip = tile_ref[0], tile_ref[1] // 2
+def correct_pack(plan, maps_ref, recv_ref, sums_ref, edge_ref, *refs):
+    *refs, field_ref, turned_ref = refs
+    far, near = far_near(plan)
+    refs, out_refs = refs[: -plan.chips], refs[-plan.chips :]
+    (line_ref,) = refs
+    me, chip = lax.axis_index("tile"), lax.axis_index("head") // 2
     count, cols, width, tiles = plan.maps, plan.cols, plan.width, plan.tiles
     head, edge, halo = plan.map_rows, plan.edge_rows, plan.halo
     tails = [recv_ref[k, count * cols :, :].astype(F32) for k in range(tiles - 1)]
@@ -243,7 +266,7 @@
             other = recv_ref[
                 jnp.maximum(shift - 1, 0), index * cols : (index + 1) * cols, :
             ]
-            own = maps_ref[index, b * cols : (b + 1) * cols, :]
+            own = maps_ref[plan.first + index, b * cols : (b + 1) * cols, :]
             mirror = across(eye, jnp.where(shift == 0, own, other))
             column = turned_ref[b * cols : (b + 1) * cols, index : index + 1]
             field_ref[index, margin + b * cols : margin + (b + 1) * cols, :] = (
@@ -273,16 +296,26 @@
         for k in range(count)
     ]
     rows, slots = plan.rows, plan.slots
+    if plan.last:
+        earlier = line_ref[...]
+        lines = [
+            earlier[k * plan.edges : (k + 1) * plan.edges] for k in range(plan.first)
+        ] + lines
+    else:
+        filler = plan.edge_rows - count * plan.edges
+        if filler:
+            lines = lines + [jnp.zeros((filler, width), F32)]
+        line_ref[...] = jnp.concatenate(lines, axis=0)
     stacks = []
-    for slot in range(slots):
+    for slot in range(slots if plan.last else 0):
         members = []
         for group in range(plan.groups):
             k = group * slots + slot
-            members.append(lines[k] if k < count else jnp.zeros((plan.edges, width), F32))
+            members.append(lines[k] if k < plan.total else jnp.zeros((plan.edges, width), F32))
         stacks.append(jnp.concatenate(members, axis=0))
     lane = lax.broadcasted_iota(jnp.int32, (plan.side_rows, cols), 1)
     spare = plan.block_rows - plan.lead - plan.half_rows
-    for step, out_ref in zip(reversed(range(plan.chips)), out_refs):
+    for step, out_ref in zip(far + near, out_refs):
         first = partner(chip, step, plan.chips) * 2 * plan.band
         groups = [
             field_ref[k, pl.ds(pl.multiple_of(first + 8 + 8 * group, 8), 8), :]
@@ -290,7 +323,7 @@
             for k in range(count)
         ]
         sides = []
-        for core in range(2):
+        for core in range(2 if plan.last else 0):
             side = jnp.zeros((plan.side_rows, cols), F32)
             for slot in range(slots):
                 amount = lax.rem(slot * rows + halo + width - core * plan.band - first, width)
@@ -304,11 +337,26 @@
         out_ref[...] = jnp.concatenate(pieces, axis=0).astype(BF16)
 
 
-def core_pack(plan, tile_ref, *refs):
+def core_pack(parts, *refs):
     *block_refs, out_ref = refs
-    other = 1 - tile_ref[1] % 2
+    other = 1 - lax.axis_index("head") % 2
     for k, block_ref in enumerate(block_refs):
-        out_ref[k] = half(plan, block_ref[...].astype(F32), other).astype(BF16)
+        out_ref[k] = half(parts, block_ref[...].astype(F32), other).astype(BF16)
+
+
+def kernel_pack(blocks_ref, out_ref):
+    layers, convs, height, breadth = blocks_ref.shape[:4]
+    for b in range(layers):
+        for m in range(convs):
+            out_ref[b * convs + m] = jnp.concatenate(
+                [
+                    jnp.concatenate(
+                        [blocks_ref[b, m, dy, dx].astype(F32) for dy in range(height)], axis=1
+                    )
+                    for dx in range(breadth)
+                ],
+                axis=0,
+            ).astype(BF16)
 
 
 def shifted(ref, rows, base, offset, size):
@@ -320,37 +368,44 @@
     return pltpu.roll(ref[rows, low : low + size + LANES], size + LANES - rest, 1)[:, :size]
 
 
-def stack(plan, order, tile_ref, *refs):
+def stack(plan, parcels, *refs):
+    own_refs, swap_refs = [], []
+    for steps, _ in parcels:
+        own_refs.append(refs[: len(steps)])
+        swap_refs.append(refs[len(steps)])
+        refs = refs[len(steps) + 1 :]
     chips = plan.chips
-    own_refs, swap_refs, refs = refs[:chips], refs[chips : chips + len(order)], refs[chips + len(order) :]
     proj_ref, side_ref, kernel_ref, vector_ref, mask_ref, spots_ref, out_ref = refs[:7]
     maps_ref, sides_ref, field_ref, stream_ref, hidden_ref, taps_ref, logit_ref = refs[7:]
-    count, cols, rows, halo = plan.maps, plan.cols, plan.rows, plan.halo
+    count, cols, rows, halo = plan.total, plan.cols, plan.rows, plan.halo
     heads, feat, chunk, stride = plan.heads, plan.feat, plan.chunk, plan.stride
-    chip, core = tile_ref[1] // 2, tile_ref[1] % 2
-    group = plan.group_rows
-
-    def spread(block, source):
-        for k in range(plan.lone + plan.shared):
-            value = block[k * group : (k + 1) * group]
-            if k >= plan.lone:
-                late = block[plan.side_rows + k * group : plan.side_rows + (k + 1) * group]
-                value = jnp.where(core == 0, late, value)
-            place = pl.multiple_of((k * heads + source) * group, 8)
-            maps_ref[pl.ds(place, group), :] = value
-        side = jnp.where(
-            core == 0,
-            block[plan.lone * group : plan.lead],
-            block[plan.half_rows - plan.side_rows : plan.half_rows],
-        )
-        place = pl.multiple_of(source * plan.side_rows, 8)
-        sides_ref[pl.ds(place, plan.side_rows), :] = side
-
-    for steps, swap_ref in zip(order, swap_refs):
+    head = lax.axis_index("head")
+    chip, core = head // 2, head % 2
+
+    def spread(parts, halves, source):
+        base = 0
+        for part in parts:
+            block = halves[base : base + part.half_rows]
+            base += part.half_rows
+            group, skip = part.group_rows, part.side_rows if part.last else 0
+            for k in range(part.lone + part.shared):
+                value = block[k * group : (k + 1) * group]
+                if k >= part.lone and skip:
+                    late = block[skip + k * group : skip + (k + 1) * group]
+                    value = jnp.where(core == 0, late, value)
+                place = ((k * heads + source) * count + part.first) * 8
+                maps_ref[pl.ds(pl.multiple_of(place, 8), group), :] = value
+            if skip:
+                early = block[part.lone * group : part.lead]
+                late = block[part.half_rows - skip : part.half_rows]
+                place = pl.multiple_of(source * skip, 8)
+                sides_ref[pl.ds(place, skip), :] = jnp.where(core == 0, early, late)
+
+    for (steps, parts), blocks, swap_ref in zip(parcels, own_refs, swap_refs):
         for k, step in enumerate(steps):
             source = 2 * partner(chip, step, chips, back=True)
-            spread(half(plan, own_refs[chips - 1 - step][...].astype(F32), core), source + core)
-            spread(swap_ref[k].astype(F32), source + 1 - core)
+            spread(parts, half(parts, blocks[k][...].astype(F32), core), source + core)
+            spread(parts, swap_ref[k].astype(F32), source + 1 - core)
     bias = vector_ref[:, 0:1]
 
     slots, members = plan.slots, heads * plan.groups
@@ -382,7 +437,7 @@
     for r in range(0, rows, per):
         blocks = [
             maps_ref[
-                pl.ds((r + k) // 8 * heads * group + (r + k) % 8, heads * count, stride=8), :
+                pl.ds((r + k) // 8 * heads * count * 8 + (r + k) % 8, heads * count, stride=8), :
             ].astype(BF16)
             for k in range(per)
         ]
@@ -451,7 +506,7 @@
     return pl.pallas_call(
         kernel,
         out_shape=list(outs),
-        in_specs=[pl.BlockSpec(memory_space=pltpu.SMEM)] + [vmem] * (len(args) - 1),
+        in_specs=[vmem] * len(args),
         out_specs=[vmem] * len(outs),
         scratch_shapes=list(scratch),
         compiler_params=pltpu.CompilerParams(vmem_limit_bytes=held * 5 // 4 + 4 * 1024 * 1024),
@@ -468,34 +523,44 @@
     feat = proj_weight.shape[0]
     blocks, convs = conv_weight.shape[:2]
     tiles, heads = lax.axis_size("tile"), lax.axis_size("head")
-    plan = Plan(maps, width, cols, tiles, heads, feat, blocks * convs)
-    me = lax.axis_index("tile").astype(jnp.int32)
-    band_index = lax.axis_index("head").astype(jnp.int32)
-    tile = jnp.stack([me, band_index])
-
-    payload, sums, edge = call(
-        functools.partial(mirror_pack, plan),
-        "mirror_pack",
-        [tile, attention],
-        [
-            array(BF16, tiles - 1, maps * cols + plan.tail_rows, cols),
-            array(F32, plan.map_rows, width),
-            array(F32, plan.edge_rows, cols),
-        ],
-    )
-    received = jnp.stack(
-        [
-            lax.ppermute(payload[s - 1], "tile", [(i, (i + s) % tiles) for i in range(tiles)])
-            for s in range(tiles - 1, 0, -1)
+    parts = [
+        Plan(first, count, maps, width, cols, tiles, heads, feat, blocks * convs)
+        for first, count in ((0, maps // 2), (maps // 2, maps - maps // 2))
+    ]
+    plan = parts[-1]
+    me, band_index = lax.axis_index("tile"), lax.axis_index("head")
+
+    def mirror(payload):
+        return jnp.stack(
+            [
+                lax.ppermute(payload[s - 1], "tile", [(i, (i + s) % tiles) for i in range(tiles)])
+                for s in range(tiles - 1, 0, -1)
+            ]
+        )
+
+    outs = []
+    for part in parts:
+        outs += [
+            array(BF16, tiles - 1, part.maps * cols + part.tail_rows, cols),
+            array(F32, part.map_rows, width),
+            array(F32, part.edge_rows, cols),
         ]
-    )
+    packed = call(functools.partial(mirror_pack, parts), "mirror_pack", [attention], outs)
+    received = mirror(packed[0])
+    payload, received = lax.optimization_barrier((packed[3], received))
+    mirrored = [received, mirror(payload)]
 
     stride, start = plan.stride, plan.start
     side_weight = proj_weight.reshape(feat, heads, maps)
     side_weight = jnp.pad(side_weight, ((0, 0), (0, 0), (0, plan.groups * plan.slots - maps)))
     side_weight = side_weight.reshape(feat, heads, plan.groups, plan.slots)
     side_weight = side_weight.transpose(0, 3, 1, 2).reshape(feat, -1)
-    kernels = conv_weight.transpose(0, 1, 5, 2, 4, 3).reshape(plan.convs, 3 * feat, 3 * feat)
+    (kernels,) = call(
+        kernel_pack,
+        "kernel_pack",
+        [conv_weight.transpose(0, 1, 4, 5, 2, 3)],
+        [array(BF16, plan.convs, 3 * feat, 3 * feat)],
+    )
     vectors = jnp.concatenate(
         [proj_bias[None], conv_bias.reshape(-1, feat), out_weight[None]], axis=0
     ).T
@@ -518,35 +583,57 @@
     spots = jnp.stack(spots)
 
     weights = (side_weight, kernels, vectors, mask, spots)
-    received, weights = lax.optimization_barrier((received, weights))
+    mirrored[-1], weights = lax.optimization_barrier((mirrored[-1], weights))
 
     chips = plan.chips
-    blocks = call(
-        functools.partial(correct_pack, plan),
-        "correct_pack",
-        [tile, attention, received, sums, edge],
-        [array(BF16, plan.block_rows, cols)] * chips,
-        [pltpu.VMEM((maps, width + 24, cols), F32), pltpu.VMEM((width, LANES), F32)],
-    )
-    grouped = list(blocks)[::-1]
-    for step in reversed(range(1, chips)):
-        pairs = [(i, 2 * partner(i // 2, step, chips) + i % 2) for i in range(heads)]
-        grouped[step] = lax.ppermute(grouped[step], "head", pairs)
-    order = [list(range(chips - 1, chips // 2 - 1, -1)), list(range(chips // 2 - 1, -1, -1))]
-    swapped = []
-    for steps in order:
-        (packed,) = call(
-            functools.partial(core_pack, plan),
+    far, near = far_near(plan)
+    parcels, arrived = [], []
+
+    def travel(steps, blocks):
+        own = []
+        for step, block in zip(steps, blocks):
+            pairs = [(i, 2 * partner(i // 2, step, chips) + i % 2) for i in range(heads)]
+            own.append(lax.ppermute(block, "head", pairs) if step else block)
+        return own
+
+    def halve(steps, members, own):
+        (halves,) = call(
+            functools.partial(core_pack, members),
             "core_pack",
-            [tile] + [grouped[k] for k in steps],
-            [array(BF16, len(steps), plan.half_rows, cols)],
+            own,
+            [array(BF16, len(steps), sum(part.half_rows for part in members), cols)],
         )
-        swapped.append(lax.ppermute(packed, "head", [(i, i ^ 1) for i in range(heads)]))
+        return steps, members, own, halves
+
+    def swap(steps, members, own, halves):
+        parcels.append((steps, members))
+        arrived.extend([*own, lax.ppermute(halves, "head", [(i, i ^ 1) for i in range(heads)])])
+
+    line = []
+    for k, part in enumerate(parts):
+        outs = [array(BF16, part.block_rows, cols)] * chips
+        if not part.last:
+            outs.insert(0, array(F32, part.edge_rows, width))
+        result = call(
+            functools.partial(correct_pack, part),
+            "correct_pack",
+            [attention, mirrored[k], *packed[3 * k + 1 : 3 * k + 3], *line],
+            outs,
+            [pltpu.VMEM((part.maps, width + 24, cols), F32), pltpu.VMEM((width, LANES), F32)],
+        )
+        line, result = result[:-chips], result[-chips:]
+        own = travel(far + near, result)
+        if part.last:
+            swap(*halve(far, [part], own[: len(far)]))
+            swap(*halve(near, [part], own[len(far) :]))
+        else:
+            ahead, mirrored[k + 1] = lax.optimization_barrier((own[: len(far)], mirrored[k + 1]))
+            swap(*halve(far + near, [part], ahead + own[len(far) :]))
 
     (logits,) = call(
-        functools.partial(stack, plan, order),
+        functools.partial(stack, plan, parcels),
         "stack",
-        [tile, *grouped[::-1], *swapped, proj_weight, *weights],
+        [*arrived, proj_weight, *weights],
         [array(F32, plan.band, cols)],
         [
             pltpu.VMEM((heads * maps * plan.rows, cols), F32),

time: 49.5 us -> 55.5 us (1.12)
  starting transfers between devices: 20.2 us -> 27.8 us
  waiting for transfers between devices: 7.46 us -> 10.7 us
  local copies, waits for them, and re-layouts: 5.69 us -> 2.89 us
  Pallas kernels: 14.3 us -> 12.4 us
    ppermute x10 -> x19, starting transfers between devices: 20.2 us -> 27.8 us  [the longest x14 22.8 us: travel(): own.append(lax.ppermute(block, 'head', pairs) if step else block)]
    ppermute x10 -> x19, waiting for transfers between devices: 7.46 us -> 10.7 us  [the longest x14 7.25 us: travel(): own.append(lax.ppermute(block, 'head', pairs) if step else block)]
    transpose x1 -> x0, local copies, waits for them, and re-layouts: 2.53 us -> none  [on_device(): conv_weight.transpose(0, 1, 5, 2, 4, 3)]
    pallas_call x5 -> x8, Pallas kernels: 14.3 us -> 12.4 us  [call(): pl.pallas_call(kernel, out_shape=list(outs), in_specs=[vmem] * len(args),...]
    reshape x1 -> x0, local copies, waits for them, and re-layouts: 1.69 us -> none  [on_device(): conv_weight.transpose(0, 1, 5, 2, 4, 3)]
    optimization_barrier x1, local copies, waits for them, and re-layouts: 0.09 us -> 0.86 us  [on_device(): mirrored[-1], weights = lax.optimization_barrier((mirrored[-1], weights))]
    transpose x1, local copies, waits for them, and re-layouts: 0.03 us -> 0.65 us  [on_device(): side_weight = side_weight.transpose(0, 3, 1, 2).reshape(feat, -1)]
    unnamed x18 -> x20, local copies, waits for them, and re-layouts: 1.21 us -> 1.23 us
  transfers between devices with their start and end apart: 10 -> 19, of which waited for: 6 -> 8; matrix products, arithmetic and copies ran while one was open for 12% -> 6% of each run, Pallas kernels for 2% -> 4%
where the time goes in v7:
time: 55.5 us; the launch traced here: 55.3 us
  starting transfers between devices  27.8 us (50%)
  Pallas kernels  12.4 us (22%)
  waiting for transfers between devices  10.7 us (19%)
  local copies, waits for them, and re-layouts  2.89 us (5%)
  other arithmetic  1.35 us (2%)
    ppermute x14, starting transfers between devices, travel(): own.append(lax.ppermute(block, 'head', pairs) if step else block)  22.8 us
    pallas_call x8, Pallas kernels, call(): pl.pallas_call(kernel, out_shape=list(outs), in_specs=[vmem] * len(args),...  12.4 us
    ppermute x14, waiting for transfers between devices, travel(): own.append(lax.ppermute(block, 'head', pairs) if step else block)  7.25 us
    ppermute x2, starting transfers between devices, mirror(): lax.ppermute(payload[s - 1], 'tile', [(i, (i + s) % tiles) for i in range...  4.77 us
    ppermute x2, waiting for transfers between devices, mirror(): lax.ppermute(payload[s - 1], 'tile', [(i, (i + s) % tiles) for i in range...  2.95 us
    convert_element_type x1, other arithmetic, on_device(): spots.append(functools.reduce(jnp.logical_or, hit).astype(BF16))  1.33 us
    unnamed x20, local copies, waits for them, and re-layouts  1.23 us
  transfers between devices with their start and end apart: 19, of which 8 were waited for; matrix products, arithmetic and copies ran while one was open for 6% of the time, Pallas kernels for 4%

profile of v7, /device:TPU:0, one launch (start us, length us, event | category | flops | bytes accessed | tf_op | source)
XLA Modules:
  0.0 55.3 jit_solution(5588493455932822637)
XLA Ops:
  0.0 1.1 %copy-done = bf16[9,256,128]{2,1,0:T(8,128)(2,1)S(1)} copy-done((bf16[9,256,128]{2,1,0:T(8,128)(2,1)S(1)}, bf16[9,256,128]{2,1,0:T(8,128)(2,1)}, u32[]{:S(2)}) %copy-start) | copy-done | bytes 589848
  1.1 0.4 mirror_pack.1
  1.5 3.0 %collective-permute-start = (bf16[656,128]{1,0:T(8,128)(2,1)S(1)}, bf16[656,128]{1,0:T(8,128)(2,1)S(1)}, u32[]{:S(2)}, u32[]{:S(2)}) collective-permute-start(bf16[656,128]{1,0:T(8,128)(2,1)S(1)} %bitcast.20), channel_id=1, source_target_pairs={{0,1},{1,0},{2,3},{3,2},{4,5},{5,4},{6,7},{7,6},{8,9},{9,8},{10,11... | collective-permute-start | bytes 503816 | tf_op jit(solution)/shard_map/ppermute | solution.py:536
  4.6 1.3 %fusion.1.refs_24_ = bf16[1,128,4352]{2,1,0:T(8,128)(2,1)S(1)} fusion(s32[128]{0:T(128)} %constant.34.clone, s32[128]{0:T(128)} %constant.33.clone), kind=kLoop, calls=%fused_computation.3 | loop fusion | flops 2228224 | bytes 1115136 | tf_op jit(solution)/shard_map/convert_element_type | solution.py:582
  5.9 2.9 %collective-permute-done = bf16[656,128]{1,0:T(8,128)(2,1)S(1)} collective-permute-done((bf16[656,128]{1,0:T(8,128)(2,1)S(1)}, bf16[656,128]{1,0:T(8,128)(2,1)S(1)}, u32[]{:S(2)}, u32[]{:S(2)}) %collective-permute-start) | collective-permute-done | bytes 167968 | tf_op jit(solution)/shard_map/ppermute | solution.py:536
  8.9 1.7 %collective-permute-start.5 = (bf16[816,128]{1,0:T(8,128)(2,1)S(1)}, bf16[816,128]{1,0:T(8,128)(2,1)S(1)}, u32[]{:S(2)}, u32[]{:S(2)}) collective-permute-start(bf16[816,128]{1,0:T(8,128)(2,1)S(1)} %bitcast.19), channel_id=1, source_target_pairs={{0,1},{1,0},{2,3},{3,2},{4,5},{5,4},{6,7},{7,6},{8,9},{9,8},{10,11... | collective-permute-start | bytes 626696 | tf_op jit(solution)/shard_map/ppermute | solution.py:536
  10.6 1.0 %correct_pack.2 = (f32[16,256]{1,0:T(8,128)S(1)}, bf16[160,128]{1,0:T(8,128)(2,1)S(1)}, bf16[160,128]{1,0:T(8,128)(2,1)S(1)}, bf16[160,128]{1,0:T(8,128)(2,1)S(1...) custom-call(bf16[9,256,128]{2,1,0:T(8,128)(2,1)S(1)} %copy-done.1, ...), custom_call_target="tpu_custom_call" | custom-call | tf_op jit(solution)/shard_map/correct_pack/pallas_call | solution.py:506
  11.6 4.5 %collective-permute-start.1 = (bf16[160,128]{1,0:T(8,128)(2,1)S(1)}, bf16[160,128]{1,0:T(8,128)(2,1)S(1)}, u32[]{:S(2)}, u32[]{:S(2)}) collective-permute-start(bf16[160,128]{1,0:T(8,128)(2,1)S(1)} %get-tuple-element.46), channel_id=1, source_target_pairs={{0,28},{2,30},{4,24},{6,26},{8,20},{10,22},{12,16},{14,18},{16,12}... | collective-permute-start | bytes 122888 | tf_op jit(solution)/shard_map/ppermute | solution.py:596
  16.2 0.2 collective-permute-start.2
  16.4 0.8 %collective-permute-start.3 = (bf16[160,128]{1,0:T(8,128)(2,1)S(1)}, bf16[160,128]{1,0:T(8,128)(2,1)S(1)}, u32[]{:S(2)}, u32[]{:S(2)}) collective-permute-start(bf16[160,128]{1,0:T(8,128)(2,1)S(1)} %get-tuple-element.48), channel_id=1, source_target_pairs={{0,20},{2,22},{4,16},{6,18},{8,28},{10,30},{12,24},{14,26},{16,4},... | collective-permute-start | bytes 122888 | tf_op jit(solution)/shard_map/ppermute | solution.py:596
  17.2 2.1 %collective-permute-start.4 = (bf16[160,128]{1,0:T(8,128)(2,1)S(1)}, bf16[160,128]{1,0:T(8,128)(2,1)S(1)}, u32[]{:S(2)}, u32[]{:S(2)}) collective-permute-start(bf16[160,128]{1,0:T(8,128)(2,1)S(1)} %get-tuple-element.49), channel_id=1, source_target_pairs={{0,16},{2,18},{4,20},{6,22},{8,24},{10,26},{12,28},{14,30},{16,0},... | collective-permute-start | bytes 122888 | tf_op jit(solution)/shard_map/ppermute | solution.py:596
  19.3 2.2 %collective-permute-start.6 = (bf16[160,128]{1,0:T(8,128)(2,1)}, bf16[160,128]{1,0:T(8,128)(2,1)S(1)}, u32[]{:S(2)}, u32[]{:S(2)}) collective-permute-start(bf16[160,128]{1,0:T(8,128)(2,1)} %get-tuple-element.56), channel_id=1, source_target_pairs={{0,12},{2,14},{4,8},{6,10},{8,4},{10,6},{12,0},{14,2},{16,28},{18,... | collective-permute-start | bytes 122888 | tf_op jit(solution)/shard_map/ppermute | solution.py:596
  21.7 0.7 %copy.23 = bf16[64,5,16,2]{0,3,2,1:T(2,128)(2,1)} copy(bf16[64,5,16,2]{0,2,1,3:T(8,128)(2,1)S(1)} %bitcast.22) | data formatting | bytes 40960 | tf_op jit(solution)/shard_map/transpose | solution.py:557
  22.3 0.1 kernel_pack.1.refs_21_
  22.6 0.6 %collective-permute-done.3.refs_2_ = bf16[160,128]{1,0:T(8,128)(2,1)S(1)} collective-permute-done((bf16[160,128]{1,0:T(8,128)(2,1)S(1)}, bf16[160,128]{1,0:T(8,128)(2,1)S(1)}, u32[]{:S(2)}, u32[]{:S(2)}) %collective-permute-start.3) | collective-permute-done | bytes 40992 | tf_op jit(solution)/shard_map/ppermute | solution.py:596
  23.3 0.8 %correct_pack.3 = (bf16[224,128]{1,0:T(8,128)(2,1)S(1)}, bf16[224,128]{1,0:T(8,128)(2,1)S(1)}, bf16[224,128]{1,0:T(8,128)(2,1)S(1)}, bf16[224,128]{1,0:T(8,128)(...) custom-call(bf16[9,256,128]{2,1,0:T(8,128)(2,1)S(1)} %copy-done.1, ...), custom_call_target="tpu_custom_call" | custom-call | tf_op jit(solution)/shard_map/correct_pack/pallas_call | solution.py:506
  24.0 3.5 %collective-permute-start.10 = (bf16[224,128]{1,0:T(8,128)(2,1)S(1)}, bf16[224,128]{1,0:T(8,128)(2,1)S(1)}, u32[]{:S(2)}, u32[]{:S(2)}) collective-permute-start(bf16[224,128]{1,0:T(8,128)(2,1)S(1)} %get-tuple-element.64), channel_id=1, source_target_pairs={{0,28},{2,30},{4,24},{6,26},{8,20},{10,22},{12,16},{14,18},{16,12}... | collective-permute-start | bytes 172040 | tf_op jit(solution)/shard_map/ppermute | solution.py:596
  27.5 0.8 %collective-permute-start.11 = (bf16[224,128]{1,0:T(8,128)(2,1)S(1)}, bf16[224,128]{1,0:T(8,128)(2,1)S(1)}, u32[]{:S(2)}, u32[]{:S(2)}) collective-permute-start(bf16[224,128]{1,0:T(8,128)(2,1)S(1)} %get-tuple-element.65), channel_id=1, source_target_pairs={{0,24},{2,26},{4,28},{6,30},{8,16},{10,18},{12,20},{14,22},{16,8},... | collective-permute-start | bytes 172040 | tf_op jit(solution)/shard_map/ppermute | solution.py:596
  28.4 1.0 %collective-permute-start.12 = (bf16[224,128]{1,0:T(8,128)(2,1)S(1)}, bf16[224,128]{1,0:T(8,128)(2,1)S(1)}, u32[]{:S(2)}, u32[]{:S(2)}) collective-permute-start(bf16[224,128]{1,0:T(8,128)(2,1)S(1)} %get-tuple-element.66), channel_id=1, source_target_pairs={{0,20},{2,22},{4,16},{6,18},{8,28},{10,30},{12,24},{14,26},{16,4},... | collective-permute-start | bytes 172040 | tf_op jit(solution)/shard_map/ppermute | solution.py:596
  29.3 3.0 %collective-permute-start.7 = (bf16[160,128]{1,0:T(8,128)(2,1)S(1)}, bf16[160,128]{1,0:T(8,128)(2,1)S(1)}, u32[]{:S(2)}, u32[]{:S(2)}) collective-permute-start(bf16[160,128]{1,0:T(8,128)(2,1)S(1)} %get-tuple-element.57), channel_id=1, source_target_pairs={{0,8},{2,10},{4,12},{6,14},{8,0},{10,2},{12,4},{14,6},{16,24},{18,... | collective-permute-start | bytes 122888 | tf_op jit(solution)/shard_map/ppermute | solution.py:596
  32.4 1.0 %collective-permute-start.8 = (bf16[160,128]{1,0:T(8,128)(2,1)S(1)}, bf16[160,128]{1,0:T(8,128)(2,1)S(1)}, u32[]{:S(2)}, u32[]{:S(2)}) collective-permute-start(bf16[160,128]{1,0:T(8,128)(2,1)S(1)} %get-tuple-element.58), channel_id=1, source_target_pairs={{0,4},{2,6},{4,0},{6,2},{8,12},{10,14},{12,8},{14,10},{16,20},{18,... | collective-permute-start | bytes 122888 | tf_op jit(solution)/shard_map/ppermute | solution.py:596
  33.4 1.5 %collective-permute-done.7.refs_5_ = bf16[160,128]{1,0:T(8,128)(2,1)S(1)} collective-permute-done((bf16[160,128]{1,0:T(8,128)(2,1)S(1)}, bf16[160,128]{1,0:T(8,128)(2,1)S(1)}, u32[]{:S(2)}, u32[]{:S(2)}) %collective-permute-start.7) | collective-permute-done | bytes 40992 | tf_op jit(solution)/shard_map/ppermute | solution.py:596
  34.9 1.5 %collective-permute-done.8.refs_6_ = bf16[160,128]{1,0:T(8,128)(2,1)S(1)} collective-permute-done((bf16[160,128]{1,0:T(8,128)(2,1)S(1)}, bf16[160,128]{1,0:T(8,128)(2,1)S(1)}, u32[]{:S(2)}, u32[]{:S(2)}) %collective-permute-start.8) | collective-permute-done | bytes 40992 | tf_op jit(solution)/shard_map/ppermute | solution.py:596
  36.6 2.4 %collective-permute-start.15 = (bf16[224,128]{1,0:T(8,128)(2,1)S(1)}, bf16[224,128]{1,0:T(8,128)(2,1)S(1)}, u32[]{:S(2)}, u32[]{:S(2)}) collective-permute-start(bf16[224,128]{1,0:T(8,128)(2,1)S(1)} %get-tuple-element.68), channel_id=1, source_target_pairs={{0,12},{2,14},{4,8},{6,10},{8,4},{10,6},{12,0},{14,2},{16,28},{18,... | collective-permute-start | bytes 172040 | tf_op jit(solution)/shard_map/ppermute | solution.py:596
  39.0 0.3 collective-permute-start.16
  39.3 0.9 %collective-permute-start.17 = (bf16[224,128]{1,0:T(8,128)(2,1)S(1)}, bf16[224,128]{1,0:T(8,128)(2,1)S(1)}, u32[]{:S(2)}, u32[]{:S(2)}) collective-permute-start(bf16[224,128]{1,0:T(8,128)(2,1)S(1)} %get-tuple-element.70), channel_id=1, source_target_pairs={{0,4},{2,6},{4,0},{6,2},{8,12},{10,14},{12,8},{14,10},{16,20},{18,... | collective-permute-start | bytes 172040 | tf_op jit(solution)/shard_map/ppermute | solution.py:596
  40.2 2.3 %collective-permute-done.13.refs_3_.refs_12_ = bf16[224,128]{1,0:T(8,128)(2,1)S(1)} collective-permute-done((bf16[224,128]{1,0:T(8,128)(2,1)S(1)}, bf16[224,128]{1,0:T(8,128)(2,1)S(1)}, u32[]{:S(2)}, u32[]{:S(2)}) %collective-permute-start.13) | collective-permute-done | bytes 57376 | tf_op jit(solution)/shard_map/ppermute | solution.py:596
  42.7 0.4 collective-permute-done.15.refs_0_.refs_14_
  43.0 0.9 %collective-permute-done.16.refs_1_.refs_15_ = bf16[224,128]{1,0:T(8,128)(2,1)S(1)} collective-permute-done((bf16[224,128]{1,0:T(8,128)(2,1)S(1)}, bf16[224,128]{1,0:T(8,128)(2,1)S(1)}, u32[]{:S(2)}, u32[]{:S(2)}) %collective-permute-start.16) | collective-permute-done | bytes 57376 | tf_op jit(solution)/shard_map/ppermute | solution.py:596
  44.0 0.9 %copy.25.refs_20_ = bf16[64,160]{1,0:T(8,128)(2,1)S(1)} copy(bf16[64,160]{0,1:T(8,128)(2,1)} %bitcast.21) | data formatting | bytes 40960 | tf_op jit(solution)/shard_map/optimization_barrier | solution.py:586
  44.9 0.5 collective-permute-done.18.refs_18_
  45.4 10.0 %stack.10 = f32[16,128]{1,0:T(8,128)} custom-call(bf16[160,128]{1,0:T(8,128)(2,1)S(1)} %collective-permute-done.1.refs_0_, bf16[160,128]{1,0:T(8,128)(2,1)S(1)} %collective-permute-done.2.refs_1_, bf16[160,128]{1,0:T(8,128)(2,1)S(1)} %collective-permute-done.3.refs_2_, bf16[160,128]{1,0:T(8,128)(2,1)S(1)} %collective-permute-done.4.refs_3_, ...), custom_call_target="tpu_custom_call" | custom-call | tf_op jit(solution)/shard_map/stack/pallas_call | solution.py:506
  (43 shorter events, 0.8 us)
Async XLA Ops:
  0.0 1.1 %copy-start = (bf16[9,256,128]{2,1,0:T(8,128)(2,1)S(1)}, bf16[9,256,128]{2,1,0:T(8,128)(2,1)}, u32[]{:S(2)}) copy-start(bf16[9,256,128]{2,1,0:T(8,128)(2,1)} %maps_ref.5) | copy-start | bytes 1769476
  1.1 9.5 %copy-start.4 = (s32[4352]{0:T(1024)S(1)}, s32[4352]{0:T(1024)}, u32[]{:S(2)}) copy-start(s32[4352]{0:T(1024)} %constant.31.clone) | copy-start | bytes 52228
  1.1 9.5 %copy-start.5 = (s32[4352]{0:T(1024)S(1)}, s32[4352]{0:T(1024)}, u32[]{:S(2)}) copy-start(s32[4352]{0:T(1024)} %constant.32.clone) | copy-start | bytes 52228
  1.1 9.6 %copy-start.1 = (bf16[9,256,128]{2,1,0:T(8,128)(2,1)S(1)}, bf16[9,256,128]{2,1,0:T(8,128)(2,1)}, u32[]{:S(2)}) copy-start(bf16[9,256,128]{2,1,0:T(8,128)(2,1)} %maps_ref.5) | copy-start | bytes 1769476
  1.5 20.0 %copy-start.6 = (f32[2,2,64]{2,1,0:T(2,128)S(1)}, f32[2,2,64]{2,1,0:T(2,128)}, u32[]{:S(2)}) copy-start(f32[2,2,64]{2,1,0:T(2,128)} %param.14) | copy-start | bytes 3076
  1.5 20.0 %copy-start.7 = (f32[64]{0:T(128)S(1)}, f32[64]{0:T(128)}, u32[]{:S(2)}) copy-start(f32[64]{0:T(128)} %param.15) | copy-start | bytes 772
  1.5 20.0 %copy-start.8 = (f32[64]{0:T(128)S(1)}, f32[64]{0:T(128)}, u32[]{:S(2)}) copy-start(f32[64]{0:T(128)} %param.12) | copy-start | bytes 772
  1.5 20.0 %copy-start.3 = (bf16[64,144]{1,0:T(8,128)(2,1)S(1)}, bf16[64,144]{1,0:T(8,128)(2,1)}, u32[]{:S(2)}) copy-start(bf16[64,144]{1,0:T(8,128)(2,1)} %refs_19_.1) | copy-start | bytes 55300
  1.5 20.8 %copy-start.2 = (bf16[2,2,64,64,3,3]{3,2,5,4,1,0:T(8,128)(2,1)S(1)}, bf16[2,2,64,64,3,3]{3,2,5,4,1,0:T(8,128)(2,1)}, u32[]{:S(2)}) copy-start(bf16[2,2,64,64,3,3]{3,2,5,4,1,0:T(8,128)(2,1)} %param.13) | copy-start | bytes 884740
  1.5 7.3 %collective-permute-start = (bf16[656,128]{1,0:T(8,128)(2,1)S(1)}, bf16[656,128]{1,0:T(8,128)(2,1)S(1)}, u32[]{:S(2)}, u32[]{:S(2)}) collective-permute-start(bf16[656,128]{1,0:T(8,128)(2,1)S(1)} %bitcast.20), channel_id=1, source_target_pairs={{0,1},{1,0},{2,3},{3,2},{4,5},{5,4},{6,7},{7,6},{8,9},{9,8},{10,11... | collective-permute-start | bytes 503816 | tf_op jit(solution)/shard_map/ppermute | solution.py:536
  8.9 10.4 %collective-permute-start.5 = (bf16[816,128]{1,0:T(8,128)(2,1)S(1)}, bf16[816,128]{1,0:T(8,128)(2,1)S(1)}, u32[]{:S(2)}, u32[]{:S(2)}) collective-permute-start(bf16[816,128]{1,0:T(8,128)(2,1)S(1)} %bitcast.19), channel_id=1, source_target_pairs={{0,1},{1,0},{2,3},{3,2},{4,5},{5,4},{6,7},{7,6},{8,9},{9,8},{10,11... | collective-permute-start | bytes 626696 | tf_op jit(solution)/shard_map/ppermute | solution.py:536
  11.6 11.0 %collective-permute-start.1 = (bf16[160,128]{1,0:T(8,128)(2,1)S(1)}, bf16[160,128]{1,0:T(8,128)(2,1)S(1)}, u32[]{:S(2)}, u32[]{:S(2)}) collective-permute-start(bf16[160,128]{1,0:T(8,128)(2,1)S(1)} %get-tuple-element.46), channel_id=1, source_target_pairs={{0,28},{2,30},{4,24},{6,26},{8,20},{10,22},{12,16},{14,18},{16,12}... | collective-permute-start | bytes 122888 | tf_op jit(solution)/shard_map/ppermute | solution.py:596
  16.2 6.4 %collective-permute-start.2 = (bf16[160,128]{1,0:T(8,128)(2,1)S(1)}, bf16[160,128]{1,0:T(8,128)(2,1)S(1)}, u32[]{:S(2)}, u32[]{:S(2)}) collective-permute-start(bf16[160,128]{1,0:T(8,128)(2,1)S(1)} %get-tuple-element.47), channel_id=1, source_target_pairs={{0,24},{2,26},{4,28},{6,30},{8,16},{10,18},{12,20},{14,22},{16,8},... | collective-permute-start | bytes 122888 | tf_op jit(solution)/shard_map/ppermute | solution.py:596
  16.4 6.9 %collective-permute-start.3 = (bf16[160,128]{1,0:T(8,128)(2,1)S(1)}, bf16[160,128]{1,0:T(8,128)(2,1)S(1)}, u32[]{:S(2)}, u32[]{:S(2)}) collective-permute-start(bf16[160,128]{1,0:T(8,128)(2,1)S(1)} %get-tuple-element.48), channel_id=1, source_target_pairs={{0,20},{2,22},{4,16},{6,18},{8,28},{10,30},{12,24},{14,26},{16,4},... | collective-permute-start | bytes 122888 | tf_op jit(solution)/shard_map/ppermute | solution.py:596
  17.2 6.1 %collective-permute-start.4 = (bf16[160,128]{1,0:T(8,128)(2,1)S(1)}, bf16[160,128]{1,0:T(8,128)(2,1)S(1)}, u32[]{:S(2)}, u32[]{:S(2)}) collective-permute-start(bf16[160,128]{1,0:T(8,128)(2,1)S(1)} %get-tuple-element.49), channel_id=1, source_target_pairs={{0,16},{2,18},{4,20},{6,22},{8,24},{10,26},{12,28},{14,30},{16,0},... | collective-permute-start | bytes 122888 | tf_op jit(solution)/shard_map/ppermute | solution.py:596
  19.3 13.1 %collective-permute-start.6 = (bf16[160,128]{1,0:T(8,128)(2,1)}, bf16[160,128]{1,0:T(8,128)(2,1)S(1)}, u32[]{:S(2)}, u32[]{:S(2)}) collective-permute-start(bf16[160,128]{1,0:T(8,128)(2,1)} %get-tuple-element.56), channel_id=1, source_target_pairs={{0,12},{2,14},{4,8},{6,10},{8,4},{10,6},{12,0},{14,2},{16,28},{18,... | collective-permute-start | bytes 122888 | tf_op jit(solution)/shard_map/ppermute | solution.py:596
  24.0 12.6 %collective-permute-start.10 = (bf16[224,128]{1,0:T(8,128)(2,1)S(1)}, bf16[224,128]{1,0:T(8,128)(2,1)S(1)}, u32[]{:S(2)}, u32[]{:S(2)}) collective-permute-start(bf16[224,128]{1,0:T(8,128)(2,1)S(1)} %get-tuple-element.64), channel_id=1, source_target_pairs={{0,28},{2,30},{4,24},{6,26},{8,20},{10,22},{12,16},{14,18},{16,12}... | collective-permute-start | bytes 172040 | tf_op jit(solution)/shard_map/ppermute | solution.py:596
  27.5 11.5 %collective-permute-start.11 = (bf16[224,128]{1,0:T(8,128)(2,1)S(1)}, bf16[224,128]{1,0:T(8,128)(2,1)S(1)}, u32[]{:S(2)}, u32[]{:S(2)}) collective-permute-start(bf16[224,128]{1,0:T(8,128)(2,1)S(1)} %get-tuple-element.65), channel_id=1, source_target_pairs={{0,24},{2,26},{4,28},{6,30},{8,16},{10,18},{12,20},{14,22},{16,8},... | collective-permute-start | bytes 172040 | tf_op jit(solution)/shard_map/ppermute | solution.py:596
  28.4 10.9 %collective-permute-start.12 = (bf16[224,128]{1,0:T(8,128)(2,1)S(1)}, bf16[224,128]{1,0:T(8,128)(2,1)S(1)}, u32[]{:S(2)}, u32[]{:S(2)}) collective-permute-start(bf16[224,128]{1,0:T(8,128)(2,1)S(1)} %get-tuple-element.66), channel_id=1, source_target_pairs={{0,20},{2,22},{4,16},{6,18},{8,28},{10,30},{12,24},{14,26},{16,4},... | collective-permute-start | bytes 172040 | tf_op jit(solution)/shard_map/ppermute | solution.py:596
  29.3 5.6 %collective-permute-start.7 = (bf16[160,128]{1,0:T(8,128)(2,1)S(1)}, bf16[160,128]{1,0:T(8,128)(2,1)S(1)}, u32[]{:S(2)}, u32[]{:S(2)}) collective-permute-start(bf16[160,128]{1,0:T(8,128)(2,1)S(1)} %get-tuple-element.57), channel_id=1, source_target_pairs={{0,8},{2,10},{4,12},{6,14},{8,0},{10,2},{12,4},{14,6},{16,24},{18,... | collective-permute-start | bytes 122888 | tf_op jit(solution)/shard_map/ppermute | solution.py:596
  32.4 4.0 %collective-permute-start.8 = (bf16[160,128]{1,0:T(8,128)(2,1)S(1)}, bf16[160,128]{1,0:T(8,128)(2,1)S(1)}, u32[]{:S(2)}, u32[]{:S(2)}) collective-permute-start(bf16[160,128]{1,0:T(8,128)(2,1)S(1)} %get-tuple-element.58), channel_id=1, source_target_pairs={{0,4},{2,6},{4,0},{6,2},{8,12},{10,14},{12,8},{14,10},{16,20},{18,... | collective-permute-start | bytes 122888 | tf_op jit(solution)/shard_map/ppermute | solution.py:596
  36.4 8.9 %collective-permute-start.9 = (bf16[8,96,128]{2,1,0:T(8,128)(2,1)S(1)}, bf16[8,96,128]{2,1,0:T(8,128)(2,1)S(1)}, u32[]{:S(2)}, u32[]{:S(2)}) collective-permute-start(bf16[8,96,128]{2,1,0:T(8,128)(2,1)S(1)} %core_pack.3), channel_id=1, source_target_pairs={{0,2},{2,0},{4,6},{6,4},{8,10},{10,8},{12,14},{14,12},{16,18},{18,... | collective-permute-start | bytes 589832 | tf_op jit(solution)/shard_map/ppermute | solution.py:610
  36.5 6.0 %collective-permute-start.13 = (bf16[224,128]{1,0:T(8,128)(2,1)S(1)}, bf16[224,128]{1,0:T(8,128)(2,1)S(1)}, u32[]{:S(2)}, u32[]{:S(2)}) collective-permute-start(bf16[224,128]{1,0:T(8,128)(2,1)S(1)} %get-tuple-element.67), channel_id=1, source_target_pairs={{0,16},{2,18},{4,20},{6,22},{8,24},{10,26},{12,28},{14,30},{16,0},... | collective-permute-start | bytes 172040 | tf_op jit(solution)/shard_map/ppermute | solution.py:596
  36.6 6.4 %collective-permute-start.15 = (bf16[224,128]{1,0:T(8,128)(2,1)S(1)}, bf16[224,128]{1,0:T(8,128)(2,1)S(1)}, u32[]{:S(2)}, u32[]{:S(2)}) collective-permute-start(bf16[224,128]{1,0:T(8,128)(2,1)S(1)} %get-tuple-element.68), channel_id=1, source_target_pairs={{0,12},{2,14},{4,8},{6,10},{8,4},{10,6},{12,0},{14,2},{16,28},{18,... | collective-permute-start | bytes 172040 | tf_op jit(solution)/shard_map/ppermute | solution.py:596
  39.0 4.9 %collective-permute-start.16 = (bf16[224,128]{1,0:T(8,128)(2,1)S(1)}, bf16[224,128]{1,0:T(8,128)(2,1)S(1)}, u32[]{:S(2)}, u32[]{:S(2)}) collective-permute-start(bf16[224,128]{1,0:T(8,128)(2,1)S(1)} %get-tuple-element.69), channel_id=1, source_target_pairs={{0,8},{2,10},{4,12},{6,14},{8,0},{10,2},{12,4},{14,6},{16,24},{18,... | collective-permute-start | bytes 172040 | tf_op jit(solution)/shard_map/ppermute | solution.py:596
  39.3 4.6 %collective-permute-start.17 = (bf16[224,128]{1,0:T(8,128)(2,1)S(1)}, bf16[224,128]{1,0:T(8,128)(2,1)S(1)}, u32[]{:S(2)}, u32[]{:S(2)}) collective-permute-start(bf16[224,128]{1,0:T(8,128)(2,1)S(1)} %get-tuple-element.70), channel_id=1, source_target_pairs={{0,4},{2,6},{4,0},{6,2},{8,12},{10,14},{12,8},{14,10},{16,20},{18,... | collective-permute-start | bytes 172040 | tf_op jit(solution)/shard_map/ppermute | solution.py:596
  42.6 2.3 %collective-permute-start.14 = (bf16[4,128,128]{2,1,0:T(8,128)(2,1)S(1)}, bf16[4,128,128]{2,1,0:T(8,128)(2,1)S(1)}, u32[]{:S(2)}, u32[]{:S(2)}) collective-permute-start(bf16[4,128,128]{2,1,0:T(8,128)(2,1)S(1)} %core_pack.4), channel_id=1, source_target_pairs={{0,2},{2,0},{4,6},{6,4},{8,10},{10,8},{12,14},{14,12},{16,18},{18,... | collective-permute-start | bytes 393224 | tf_op jit(solution)/shard_map/ppermute | solution.py:610
  43.9 1.4 %collective-permute-start.18 = (bf16[4,128,128]{2,1,0:T(8,128)(2,1)S(1)}, bf16[4,128,128]{2,1,0:T(8,128)(2,1)S(1)}, u32[]{:S(2)}, u32[]{:S(2)}) collective-permute-start(bf16[4,128,128]{2,1,0:T(8,128)(2,1)S(1)} %core_pack.5), channel_id=1, source_target_pairs={{0,2},{2,0},{4,6},{6,4},{8,10},{10,8},{12,14},{14,12},{16,18},{18,... | collective-permute-start | bytes 393224 | tf_op jit(solution)/shard_map/ppermute | solution.py:610

commit v8 on v6

--- a/solution.py
+++ b/solution.py
@@ -122,6 +122,16 @@
     return (mine - step if back else mine + step) % count
 
 
+def far_near(plan):
+    steps = list(range(plan.chips - 1, 0, -1))
+    return steps[: plan.chips // 2], steps[plan.chips // 2 :]
+
+
+def step_order(plan):
+    far, near = far_near(plan)
+    return far + near + [0]
+
+
 def half(plan, block, core):
     return jnp.where(
         core == 0, block[: plan.half_rows], block[plan.lead : plan.lead + plan.half_rows]
@@ -153,8 +163,8 @@
     return jnp.dot(a, b, preferred_element_type=F32)
 
 
-def mirror_pack(plan, tile_ref, maps_ref, out_ref, sums_ref, edge_ref):
-    me = tile_ref[0]
+def mirror_pack(plan, maps_ref, out_ref, sums_ref, edge_ref):
+    me = lax.axis_index("tile")
     count, cols, width, tiles = plan.maps, plan.cols, plan.width, plan.tiles
     head, edge = plan.map_rows, plan.edge_rows
 
@@ -202,9 +212,9 @@
         out_ref[shift - 1, count * cols :, :] = jnp.concatenate(pieces, axis=0).astype(BF16)
 
 
-def correct_pack(plan, tile_ref, maps_ref, recv_ref, sums_ref, edge_ref, *refs):
+def correct_pack(plan, maps_ref, recv_ref, sums_ref, edge_ref, *refs):
     *out_refs, field_ref, turned_ref = refs
-    me, chip = tile_ref[0], tile_ref[1] // 2
+    me, chip = lax.axis_index("tile"), lax.axis_index("head") // 2
     count, cols, width, tiles = plan.maps, plan.cols, plan.width, plan.tiles
     head, edge, halo = plan.map_rows, plan.edge_rows, plan.halo
     tails = [recv_ref[k, count * cols :, :].astype(F32) for k in range(tiles - 1)]
@@ -282,7 +292,7 @@
         stacks.append(jnp.concatenate(members, axis=0))
     lane = lax.broadcasted_iota(jnp.int32, (plan.side_rows, cols), 1)
     spare = plan.block_rows - plan.lead - plan.half_rows
-    for step, out_ref in zip(reversed(range(plan.chips)), out_refs):
+    for step, out_ref in zip(step_order(plan), out_refs):
         first = partner(chip, step, plan.chips) * 2 * plan.band
         groups = [
             field_ref[k, pl.ds(pl.multiple_of(first + 8 + 8 * group, 8), 8), :]
@@ -304,11 +314,26 @@
         out_ref[...] = jnp.concatenate(pieces, axis=0).astype(BF16)
 
 
-def core_pack(plan, tile_ref, *refs):
+def core_pack(plan, *refs):
     *block_refs, out_ref = refs
-    other = 1 - tile_ref[1] % 2
+    other = 1 - lax.axis_index("head") % 2
     for k, block_ref in enumerate(block_refs):
         out_ref[k] = half(plan, block_ref[...].astype(F32), other).astype(BF16)
+
+
+def kernel_pack(blocks_ref, out_ref):
+    layers, convs, height, breadth = blocks_ref.shape[:4]
+    for b in range(layers):
+        for m in range(convs):
+            out_ref[b * convs + m] = jnp.concatenate(
+                [
+                    jnp.concatenate(
+                        [blocks_ref[b, m, dy, dx].astype(F32) for dy in range(height)], axis=1
+                    )
+                    for dx in range(breadth)
+                ],
+                axis=0,
+            ).astype(BF16)
 
 
 def shifted(ref, rows, base, offset, size):
@@ -320,14 +345,16 @@
     return pltpu.roll(ref[rows, low : low + size + LANES], size + LANES - rest, 1)[:, :size]
 
 
-def stack(plan, order, tile_ref, *refs):
+def stack(plan, order, *refs):
     chips = plan.chips
-    own_refs, swap_refs, refs = refs[:chips], refs[chips : chips + len(order)], refs[chips + len(order) :]
+    own_refs, swap_refs = refs[:chips], refs[chips : chips + len(order)]
+    refs = refs[chips + len(order) :]
     proj_ref, side_ref, kernel_ref, vector_ref, mask_ref, spots_ref, out_ref = refs[:7]
     maps_ref, sides_ref, field_ref, stream_ref, hidden_ref, taps_ref, logit_ref = refs[7:]
     count, cols, rows, halo = plan.maps, plan.cols, plan.rows, plan.halo
     heads, feat, chunk, stride = plan.heads, plan.feat, plan.chunk, plan.stride
-    chip, core = tile_ref[1] // 2, tile_ref[1] % 2
+    head = lax.axis_index("head")
+    chip, core = head // 2, head % 2
     group = plan.group_rows
 
     def spread(block, source):
@@ -349,7 +376,7 @@
     for steps, swap_ref in zip(order, swap_refs):
         for k, step in enumerate(steps):
             source = 2 * partner(chip, step, chips, back=True)
-            spread(half(plan, own_refs[chips - 1 - step][...].astype(F32), core), source + core)
+            spread(half(plan, own_refs[step_order(plan).index(step)][...].astype(F32), core), source + core)
             spread(swap_ref[k].astype(F32), source + 1 - core)
     bias = vector_ref[:, 0:1]
 
@@ -451,7 +478,7 @@
     return pl.pallas_call(
         kernel,
         out_shape=list(outs),
-        in_specs=[pl.BlockSpec(memory_space=pltpu.SMEM)] + [vmem] * (len(args) - 1),
+        in_specs=[vmem] * len(args),
         out_specs=[vmem] * len(outs),
         scratch_shapes=list(scratch),
         compiler_params=pltpu.CompilerParams(vmem_limit_bytes=held * 5 // 4 + 4 * 1024 * 1024),
@@ -469,14 +496,12 @@
     blocks, convs = conv_weight.shape[:2]
     tiles, heads = lax.axis_size("tile"), lax.axis_size("head")
     plan = Plan(maps, width, cols, tiles, heads, feat, blocks * convs)
-    me = lax.axis_index("tile").astype(jnp.int32)
-    band_index = lax.axis_index("head").astype(jnp.int32)
-    tile = jnp.stack([me, band_index])
+    me, band_index = lax.axis_index("tile"), lax.axis_index("head")
 
     payload, sums, edge = call(
         functools.partial(mirror_pack, plan),
         "mirror_pack",
-        [tile, attention],
+        [attention],
         [
             array(BF16, tiles - 1, maps * cols + plan.tail_rows, cols),
             array(F32, plan.map_rows, width),
@@ -495,7 +520,12 @@
     side_weight = jnp.pad(side_weight, ((0, 0), (0, 0), (0, plan.groups * plan.slots - maps)))
     side_weight = side_weight.reshape(feat, heads, plan.groups, plan.slots)
     side_weight = side_weight.transpose(0, 3, 1, 2).reshape(feat, -1)
-    kernels = conv_weight.transpose(0, 1, 5, 2, 4, 3).reshape(plan.convs, 3 * feat, 3 * feat)
+    (kernels,) = call(
+        kernel_pack,
+        "kernel_pack",
+        [conv_weight.transpose(0, 1, 4, 5, 2, 3)],
+        [array(BF16, plan.convs, 3 * feat, 3 * feat)],
+    )
     vectors = jnp.concatenate(
         [proj_bias[None], conv_bias.reshape(-1, feat), out_weight[None]], axis=0
     ).T
@@ -524,21 +554,22 @@
     blocks = call(
         functools.partial(correct_pack, plan),
         "correct_pack",
-        [tile, attention, received, sums, edge],
+        [attention, received, sums, edge],
         [array(BF16, plan.block_rows, cols)] * chips,
         [pltpu.VMEM((maps, width + 24, cols), F32), pltpu.VMEM((width, LANES), F32)],
     )
-    grouped = list(blocks)[::-1]
-    for step in reversed(range(1, chips)):
+    arrived = {}
+    for step, block in zip(step_order(plan), blocks):
         pairs = [(i, 2 * partner(i // 2, step, chips) + i % 2) for i in range(heads)]
-        grouped[step] = lax.ppermute(grouped[step], "head", pairs)
-    order = [list(range(chips - 1, chips // 2 - 1, -1)), list(range(chips // 2 - 1, -1, -1))]
+        arrived[step] = lax.ppermute(block, "head", pairs) if step else block
+    far, near = far_near(plan)
+    order = [far, near + [0]]
     swapped = []
     for steps in order:
         (packed,) = call(
             functools.partial(core_pack, plan),
             "core_pack",
-            [tile] + [grouped[k] for k in steps],
+            [arrived[k] for k in steps],
             [array(BF16, len(steps), plan.half_rows, cols)],
         )
         swapped.append(lax.ppermute(packed, "head", [(i, i ^ 1) for i in range(heads)]))
@@ -546,7 +577,7 @@
     (logits,) = call(
         functools.partial(stack, plan, order),
         "stack",
-        [tile, *grouped[::-1], *swapped, proj_weight, *weights],
+        [*arrived.values(), *swapped, proj_weight, *weights],
         [array(F32, plan.band, cols)],
         [
             pltpu.VMEM((heads * maps * plan.rows, cols), F32),

time: 49.5 us -> 48.1 us (0.972)
  waiting for transfers between devices: 7.46 us -> 12.6 us
  local copies, waits for them, and re-layouts: 5.69 us -> 1.48 us
  Pallas kernels: 14.3 us -> 12.4 us
    ppermute x1, waiting for transfers between devices: 2.22 us -> 6.52 us  [on_device(): lax.ppermute(payload[s - 1], 'tile', [(i, (i + s) % tiles) for i in range...]
    transpose x1 -> x0, local copies, waits for them, and re-layouts: 2.53 us -> none  [on_device(): conv_weight.transpose(0, 1, 5, 2, 4, 3)]
    pallas_call x5 -> x6, Pallas kernels: 14.3 us -> 12.4 us  [call(): pl.pallas_call(kernel, out_shape=list(outs), in_specs=[vmem] * len(args),...]
    reshape x1 -> x0, local copies, waits for them, and re-layouts: 1.69 us -> none  [on_device(): conv_weight.transpose(0, 1, 5, 2, 4, 3)]
    ppermute x7, waiting for transfers between devices: 4.18 us -> 4.72 us  [on_device(): arrived[step] = lax.ppermute(block, 'head', pairs) if step else block]
    unnamed x18 -> x20, local copies, waits for them, and re-layouts: 1.21 us -> 1.21 us
  transfers between devices with their start and end apart: 10 -> 10, of which waited for: 6 -> 6; matrix products, arithmetic and copies ran while one was open for 12% -> 4% of each run, Pallas kernels for 2% -> 1%
where the time goes in v8:
time: 48.1 us; the launch traced here: 47.9 us
  starting transfers between devices  19.8 us (41%)
  waiting for transfers between devices  12.6 us (26%)
  Pallas kernels  12.4 us (26%)
  local copies, waits for them, and re-layouts  1.48 us (3%)
  other arithmetic  1.35 us (3%)
    ppermute x7, starting transfers between devices, on_device(): arrived[step] = lax.ppermute(block, 'head', pairs) if step else block  16.7 us
    pallas_call x6, Pallas kernels, call(): pl.pallas_call(kernel, out_shape=list(outs), in_specs=[vmem] * len(args),...  12.4 us
    ppermute x1, waiting for transfers between devices, on_device(): lax.ppermute(payload[s - 1], 'tile', [(i, (i + s) % tiles) for i in range...  6.52 us
    ppermute x7, waiting for transfers between devices, on_device(): arrived[step] = lax.ppermute(block, 'head', pairs) if step else block  4.72 us
    ppermute x1, starting transfers between devices, on_device(): lax.ppermute(payload[s - 1], 'tile', [(i, (i + s) % tiles) for i in range...  2.97 us
    ppermute x2, waiting for transfers between devices, on_device(): lax.ppermute(packed, 'head', [(i, i ^ 1) for i in range(heads)])  1.38 us
    convert_element_type x1, other arithmetic, on_device(): spots.append(functools.reduce(jnp.logical_or, hit).astype(BF16))  1.33 us
    unnamed x20, local copies, waits for them, and re-layouts  1.21 us
  transfers between devices with their start and end apart: 10, of which 6 were waited for; matrix products, arithmetic and copies ran while one was open for 4% of the time, Pallas kernels for 1%

profile of v8, /device:TPU:0, one launch (start us, length us, event | category | flops | bytes accessed | tf_op | source)
XLA Modules:
  0.0 47.9 jit_solution(9417740000726552685)
XLA Ops:
  0.0 1.1 %copy-done = bf16[9,256,128]{2,1,0:T(8,128)(2,1)S(1)} copy-done((bf16[9,256,128]{2,1,0:T(8,128)(2,1)S(1)}, bf16[9,256,128]{2,1,0:T(8,128)(2,1)}, u32[]{:S(2)}) %copy-start) | copy-done | bytes 589848
  1.1 0.0 copy-start.8
  1.1 1.2 %mirror_pack.1 = (bf16[1,1376,128]{2,1,0:T(8,128)(2,1)}, f32[16,256]{1,0:T(8,128)S(1)}, f32[40,128]{1,0:T(8,128)S(1)}) custom-call(bf16[9,256,128]{2,1,0:T(8,128)(2,1)S(1)} %copy-done), custom_call_target="tpu_custom_call" | custom-call | tf_op jit(solution)/shard_map/mirror_pack/pallas_call | solution.py:478
  2.3 3.0 %collective-permute-start = (bf16[1376,128]{1,0:T(8,128)(2,1)}, bf16[1376,128]{1,0:T(8,128)(2,1)S(1)}, u32[]{:S(2)}, u32[]{:S(2)}) collective-permute-start(bf16[1376,128]{1,0:T(8,128)(2,1)} %bitcast), channel_id=1, source_target_pairs={{0,1},{1,0},{2,3},{3,2},{4,5},{5,4},{6,7},{7,6},{8,9},{9,8},{10,11... | collective-permute-start | bytes 1056776 | tf_op jit(solution)/shard_map/ppermute | solution.py:513
  5.3 1.3 %fusion.1.refs_15_ = bf16[1,128,4352]{2,1,0:T(8,128)(2,1)S(1)} fusion(s32[128]{0:T(128)} %constant.34.clone, s32[128]{0:T(128)} %constant.33.clone), kind=kLoop, calls=%fused_computation.3 | loop fusion | flops 2228224 | bytes 1115136 | tf_op jit(solution)/shard_map/convert_element_type | solution.py:547
  6.7 0.1 copy.24
  6.8 0.1 copy.21
  7.1 0.1 kernel_pack.1.refs_12_
  7.2 6.5 %collective-permute-done = bf16[1376,128]{1,0:T(8,128)(2,1)S(1)} collective-permute-done((bf16[1376,128]{1,0:T(8,128)(2,1)}, bf16[1376,128]{1,0:T(8,128)(2,1)S(1)}, u32[]{:S(2)}, u32[]{:S(2)}) %collective-permute-start) | collective-permute-done | bytes 352288 | tf_op jit(solution)/shard_map/ppermute | solution.py:513
  13.7 1.0 %correct_pack.1 = (bf16[384,128]{1,0:T(8,128)(2,1)S(1)}, bf16[384,128]{1,0:T(8,128)(2,1)S(1)}, bf16[384,128]{1,0:T(8,128)(2,1)S(1)}, bf16[384,128]{1,0:T(8,128)(...) custom-call(bf16[9,256,128]{2,1,0:T(8,128)(2,1)S(1)} %copy-done.1, ...), custom_call_target="tpu_custom_call" | custom-call | tf_op jit(solution)/shard_map/correct_pack/pallas_call | solution.py:478
  14.7 4.8 %collective-permute-start.1 = (bf16[384,128]{1,0:T(8,128)(2,1)S(1)}, bf16[384,128]{1,0:T(8,128)(2,1)S(1)}, u32[]{:S(2)}, u32[]{:S(2)}) collective-permute-start(bf16[384,128]{1,0:T(8,128)(2,1)S(1)} %get-tuple-element.26), channel_id=1, source_target_pairs={{0,28},{2,30},{4,24},{6,26},{8,20},{10,22},{12,16},{14,18},{16,12}... | collective-permute-start | bytes 294920 | tf_op jit(solution)/shard_map/ppermute | solution.py:564
  19.5 0.2 collective-permute-start.2
  19.8 0.8 %collective-permute-start.3 = (bf16[384,128]{1,0:T(8,128)(2,1)S(1)}, bf16[384,128]{1,0:T(8,128)(2,1)S(1)}, u32[]{:S(2)}, u32[]{:S(2)}) collective-permute-start(bf16[384,128]{1,0:T(8,128)(2,1)S(1)} %get-tuple-element.28), channel_id=1, source_target_pairs={{0,20},{2,22},{4,16},{6,18},{8,28},{10,30},{12,24},{14,26},{16,4},... | collective-permute-start | bytes 294920 | tf_op jit(solution)/shard_map/ppermute | solution.py:564
  20.5 2.0 %collective-permute-start.4 = (bf16[384,128]{1,0:T(8,128)(2,1)S(1)}, bf16[384,128]{1,0:T(8,128)(2,1)S(1)}, u32[]{:S(2)}, u32[]{:S(2)}) collective-permute-start(bf16[384,128]{1,0:T(8,128)(2,1)S(1)} %get-tuple-element.29), channel_id=1, source_target_pairs={{0,16},{2,18},{4,20},{6,22},{8,24},{10,26},{12,28},{14,30},{16,0},... | collective-permute-start | bytes 294920 | tf_op jit(solution)/shard_map/ppermute | solution.py:564
  22.6 2.3 %collective-permute-start.5 = (bf16[384,128]{1,0:T(8,128)(2,1)S(1)}, bf16[384,128]{1,0:T(8,128)(2,1)S(1)}, u32[]{:S(2)}, u32[]{:S(2)}) collective-permute-start(bf16[384,128]{1,0:T(8,128)(2,1)S(1)} %get-tuple-element.30), channel_id=1, source_target_pairs={{0,12},{2,14},{4,8},{6,10},{8,4},{10,6},{12,0},{14,2},{16,28},{18,... | collective-permute-start | bytes 294920 | tf_op jit(solution)/shard_map/ppermute | solution.py:564
  24.8 0.0 collective-permute-done.1.refs_0_
  24.8 5.6 %collective-permute-start.6 = (bf16[384,128]{1,0:T(8,128)(2,1)S(1)}, bf16[384,128]{1,0:T(8,128)(2,1)S(1)}, u32[]{:S(2)}, u32[]{:S(2)}) collective-permute-start(bf16[384,128]{1,0:T(8,128)(2,1)S(1)} %get-tuple-element.31), channel_id=1, source_target_pairs={{0,8},{2,10},{4,12},{6,14},{8,0},{10,2},{12,4},{14,6},{16,24},{18,... | collective-permute-start | bytes 294920 | tf_op jit(solution)/shard_map/ppermute | solution.py:564
  30.4 0.0 collective-permute-done.2.refs_1_
  30.4 1.0 %collective-permute-start.7 = (bf16[384,128]{1,0:T(8,128)(2,1)S(1)}, bf16[384,128]{1,0:T(8,128)(2,1)S(1)}, u32[]{:S(2)}, u32[]{:S(2)}) collective-permute-start(bf16[384,128]{1,0:T(8,128)(2,1)S(1)} %get-tuple-element.32), channel_id=1, source_target_pairs={{0,4},{2,6},{4,0},{6,2},{8,12},{10,14},{12,8},{14,10},{16,20},{18,... | collective-permute-start | bytes 294920 | tf_op jit(solution)/shard_map/ppermute | solution.py:564
  31.5 2.9 %collective-permute-done.3.refs_2_ = bf16[384,128]{1,0:T(8,128)(2,1)S(1)} collective-permute-done((bf16[384,128]{1,0:T(8,128)(2,1)S(1)}, bf16[384,128]{1,0:T(8,128)(2,1)S(1)}, u32[]{:S(2)}, u32[]{:S(2)}) %collective-permute-start.3) | collective-permute-done | bytes 98336 | tf_op jit(solution)/shard_map/ppermute | solution.py:564
  34.4 1.1 %collective-permute-done.4.refs_3_ = bf16[384,128]{1,0:T(8,128)(2,1)S(1)} collective-permute-done((bf16[384,128]{1,0:T(8,128)(2,1)S(1)}, bf16[384,128]{1,0:T(8,128)(2,1)S(1)}, u32[]{:S(2)}, u32[]{:S(2)}) %collective-permute-start.4) | collective-permute-done | bytes 98336 | tf_op jit(solution)/shard_map/ppermute | solution.py:564
  35.5 0.1 core_pack.2
  35.5 0.1 collective-permute-start.8
  35.6 0.0 collective-permute-done.5.refs_0_.refs_4_
  35.6 0.7 %collective-permute-done.6.refs_1_.refs_5_ = bf16[384,128]{1,0:T(8,128)(2,1)S(1)} collective-permute-done((bf16[384,128]{1,0:T(8,128)(2,1)S(1)}, bf16[384,128]{1,0:T(8,128)(2,1)S(1)}, u32[]{:S(2)}, u32[]{:S(2)}) %collective-permute-start.6) | collective-permute-done | bytes 98336 | tf_op jit(solution)/shard_map/ppermute | solution.py:564
  36.3 0.0 collective-permute-done.7.refs_2_.refs_6_
  36.3 0.1 core_pack.3
  36.4 0.1 collective-permute-start.9
  36.5 0.1 copy.25.refs_11_
  36.6 0.5 %collective-permute-done.8.refs_8_ = bf16[4,224,128]{2,1,0:T(8,128)(2,1)S(1)} collective-permute-done((bf16[4,224,128]{2,1,0:T(8,128)(2,1)S(1)}, bf16[4,224,128]{2,1,0:T(8,128)(2,1)S(1)}, u32[]{:S(2)}, u32[]{:S(2)}) %collective-permute-start.8) | collective-permute-done | bytes 229408 | tf_op jit(solution)/shard_map/ppermute | solution.py:575
  37.1 0.9 %collective-permute-done.9.refs_9_ = bf16[4,224,128]{2,1,0:T(8,128)(2,1)S(1)} collective-permute-done((bf16[4,224,128]{2,1,0:T(8,128)(2,1)S(1)}, bf16[4,224,128]{2,1,0:T(8,128)(2,1)S(1)}, u32[]{:S(2)}, u32[]{:S(2)}) %collective-permute-start.9) | collective-permute-done | bytes 229408 | tf_op jit(solution)/shard_map/ppermute | solution.py:575
  38.0 10.0 %stack.6 = f32[16,128]{1,0:T(8,128)} custom-call(bf16[384,128]{1,0:T(8,128)(2,1)S(1)} %collective-permute-done.1.refs_0_, bf16[384,128]{1,0:T(8,128)(2,1)S(1)} %collective-permute-done.2.refs_1_, bf16[384,128]{1,0:T(8,128)(2,1)S(1)} %collective-permute-done.3.refs_2_, bf16[384,128]{1,0:T(8,128)(2,1)S(1)} %collective-permute-done.4.refs_3_, ...), custom_call_target="tpu_custom_call" | custom-call | tf_op jit(solution)/shard_map/stack/pallas_call | solution.py:478
  (23 shorter events, 0.2 us)
Async XLA Ops:
  0.0 1.1 %copy-start = (bf16[9,256,128]{2,1,0:T(8,128)(2,1)S(1)}, bf16[9,256,128]{2,1,0:T(8,128)(2,1)}, u32[]{:S(2)}) copy-start(bf16[9,256,128]{2,1,0:T(8,128)(2,1)} %maps_ref.3) | copy-start | bytes 1769476
  1.1 5.6 %copy-start.4 = (s32[4352]{0:T(1024)S(1)}, s32[4352]{0:T(1024)}, u32[]{:S(2)}) copy-start(s32[4352]{0:T(1024)} %constant.32.clone) | copy-start | bytes 52228
  1.1 5.6 %copy-start.5 = (s32[4352]{0:T(1024)S(1)}, s32[4352]{0:T(1024)}, u32[]{:S(2)}) copy-start(s32[4352]{0:T(1024)} %constant.31.clone) | copy-start | bytes 52228
  1.1 5.6 %copy-start.6 = (f32[2,2,64]{2,1,0:T(2,128)S(1)}, f32[2,2,64]{2,1,0:T(2,128)}, u32[]{:S(2)}) copy-start(f32[2,2,64]{2,1,0:T(2,128)} %param.14) | copy-start | bytes 3076
  1.1 5.6 %copy-start.7 = (f32[64]{0:T(128)S(1)}, f32[64]{0:T(128)}, u32[]{:S(2)}) copy-start(f32[64]{0:T(128)} %param.15) | copy-start | bytes 772
  1.1 5.6 %copy-start.8 = (f32[64]{0:T(128)S(1)}, f32[64]{0:T(128)}, u32[]{:S(2)}) copy-start(f32[64]{0:T(128)} %param.12) | copy-start | bytes 772
  1.1 5.7 %copy-start.3 = (bf16[64,144]{1,0:T(8,128)(2,1)S(1)}, bf16[64,144]{1,0:T(8,128)(2,1)}, u32[]{:S(2)}) copy-start(bf16[64,144]{1,0:T(8,128)(2,1)} %refs_10_.1) | copy-start | bytes 55300
  1.1 6.0 %copy-start.2 = (bf16[2,2,64,64,3,3]{3,2,5,4,1,0:T(8,128)(2,1)S(1)}, bf16[2,2,64,64,3,3]{3,2,5,4,1,0:T(8,128)(2,1)}, u32[]{:S(2)}) copy-start(bf16[2,2,64,64,3,3]{3,2,5,4,1,0:T(8,128)(2,1)} %param.13) | copy-start | bytes 884740
  2.3 11.4 %copy-start.1 = (bf16[9,256,128]{2,1,0:T(8,128)(2,1)S(1)}, bf16[9,256,128]{2,1,0:T(8,128)(2,1)}, u32[]{:S(2)}) copy-start(bf16[9,256,128]{2,1,0:T(8,128)(2,1)} %maps_ref.3) | copy-start | bytes 1769476
  2.3 11.4 %collective-permute-start = (bf16[1376,128]{1,0:T(8,128)(2,1)}, bf16[1376,128]{1,0:T(8,128)(2,1)S(1)}, u32[]{:S(2)}, u32[]{:S(2)}) collective-permute-start(bf16[1376,128]{1,0:T(8,128)(2,1)} %bitcast), channel_id=1, source_target_pairs={{0,1},{1,0},{2,3},{3,2},{4,5},{5,4},{6,7},{7,6},{8,9},{9,8},{10,11... | collective-permute-start | bytes 1056776 | tf_op jit(solution)/shard_map/ppermute | solution.py:513
  14.7 10.1 %collective-permute-start.1 = (bf16[384,128]{1,0:T(8,128)(2,1)S(1)}, bf16[384,128]{1,0:T(8,128)(2,1)S(1)}, u32[]{:S(2)}, u32[]{:S(2)}) collective-permute-start(bf16[384,128]{1,0:T(8,128)(2,1)S(1)} %get-tuple-element.26), channel_id=1, source_target_pairs={{0,28},{2,30},{4,24},{6,26},{8,20},{10,22},{12,16},{14,18},{16,12}... | collective-permute-start | bytes 294920 | tf_op jit(solution)/shard_map/ppermute | solution.py:564
  19.5 10.9 %collective-permute-start.2 = (bf16[384,128]{1,0:T(8,128)(2,1)S(1)}, bf16[384,128]{1,0:T(8,128)(2,1)S(1)}, u32[]{:S(2)}, u32[]{:S(2)}) collective-permute-start(bf16[384,128]{1,0:T(8,128)(2,1)S(1)} %get-tuple-element.27), channel_id=1, source_target_pairs={{0,24},{2,26},{4,28},{6,30},{8,16},{10,18},{12,20},{14,22},{16,8},... | collective-permute-start | bytes 294920 | tf_op jit(solution)/shard_map/ppermute | solution.py:564
  19.8 14.6 %collective-permute-start.3 = (bf16[384,128]{1,0:T(8,128)(2,1)S(1)}, bf16[384,128]{1,0:T(8,128)(2,1)S(1)}, u32[]{:S(2)}, u32[]{:S(2)}) collective-permute-start(bf16[384,128]{1,0:T(8,128)(2,1)S(1)} %get-tuple-element.28), channel_id=1, source_target_pairs={{0,20},{2,22},{4,16},{6,18},{8,28},{10,30},{12,24},{14,26},{16,4},... | collective-permute-start | bytes 294920 | tf_op jit(solution)/shard_map/ppermute | solution.py:564
  20.5 14.9 %collective-permute-start.4 = (bf16[384,128]{1,0:T(8,128)(2,1)S(1)}, bf16[384,128]{1,0:T(8,128)(2,1)S(1)}, u32[]{:S(2)}, u32[]{:S(2)}) collective-permute-start(bf16[384,128]{1,0:T(8,128)(2,1)S(1)} %get-tuple-element.29), channel_id=1, source_target_pairs={{0,16},{2,18},{4,20},{6,22},{8,24},{10,26},{12,28},{14,30},{16,0},... | collective-permute-start | bytes 294920 | tf_op jit(solution)/shard_map/ppermute | solution.py:564
  22.6 13.1 %collective-permute-start.5 = (bf16[384,128]{1,0:T(8,128)(2,1)S(1)}, bf16[384,128]{1,0:T(8,128)(2,1)S(1)}, u32[]{:S(2)}, u32[]{:S(2)}) collective-permute-start(bf16[384,128]{1,0:T(8,128)(2,1)S(1)} %get-tuple-element.30), channel_id=1, source_target_pairs={{0,12},{2,14},{4,8},{6,10},{8,4},{10,6},{12,0},{14,2},{16,28},{18,... | collective-permute-start | bytes 294920 | tf_op jit(solution)/shard_map/ppermute | solution.py:564
  24.8 11.5 %collective-permute-start.6 = (bf16[384,128]{1,0:T(8,128)(2,1)S(1)}, bf16[384,128]{1,0:T(8,128)(2,1)S(1)}, u32[]{:S(2)}, u32[]{:S(2)}) collective-permute-start(bf16[384,128]{1,0:T(8,128)(2,1)S(1)} %get-tuple-element.31), channel_id=1, source_target_pairs={{0,8},{2,10},{4,12},{6,14},{8,0},{10,2},{12,4},{14,6},{16,24},{18,... | collective-permute-start | bytes 294920 | tf_op jit(solution)/shard_map/ppermute | solution.py:564
  30.4 5.9 %collective-permute-start.7 = (bf16[384,128]{1,0:T(8,128)(2,1)S(1)}, bf16[384,128]{1,0:T(8,128)(2,1)S(1)}, u32[]{:S(2)}, u32[]{:S(2)}) collective-permute-start(bf16[384,128]{1,0:T(8,128)(2,1)S(1)} %get-tuple-element.32), channel_id=1, source_target_pairs={{0,4},{2,6},{4,0},{6,2},{8,12},{10,14},{12,8},{14,10},{16,20},{18,... | collective-permute-start | bytes 294920 | tf_op jit(solution)/shard_map/ppermute | solution.py:564
  35.5 1.6 %collective-permute-start.8 = (bf16[4,224,128]{2,1,0:T(8,128)(2,1)S(1)}, bf16[4,224,128]{2,1,0:T(8,128)(2,1)S(1)}, u32[]{:S(2)}, u32[]{:S(2)}) collective-permute-start(bf16[4,224,128]{2,1,0:T(8,128)(2,1)S(1)} %core_pack.2), channel_id=1, source_target_pairs={{0,2},{2,0},{4,6},{6,4},{8,10},{10,8},{12,14},{14,12},{16,18},{18,... | collective-permute-start | bytes 688136 | tf_op jit(solution)/shard_map/ppermute | solution.py:575
  36.4 1.6 %collective-permute-start.9 = (bf16[4,224,128]{2,1,0:T(8,128)(2,1)S(1)}, bf16[4,224,128]{2,1,0:T(8,128)(2,1)S(1)}, u32[]{:S(2)}, u32[]{:S(2)}) collective-permute-start(bf16[4,224,128]{2,1,0:T(8,128)(2,1)S(1)} %core_pack.3), channel_id=1, source_target_pairs={{0,2},{2,0},{4,6},{6,4},{8,10},{10,8},{12,14},{14,12},{16,18},{18,... | collective-permute-start | bytes 688136 | tf_op jit(solution)/shard_map/ppermute | solution.py:575

commit v9 on v8

--- a/solution.py
+++ b/solution.py
@@ -163,7 +163,7 @@
     return jnp.dot(a, b, preferred_element_type=F32)
 
 
-def mirror_pack(plan, maps_ref, out_ref, sums_ref, edge_ref):
+def mirror_pack(plan, source_ref, out_ref, sums_ref, edge_ref, maps_ref, arrived):
     me = lax.axis_index("tile")
     count, cols, width, tiles = plan.maps, plan.cols, plan.width, plan.tiles
     head, edge = plan.map_rows, plan.edge_rows
@@ -176,10 +176,18 @@
     def total(span, index):
         return (lax.broadcasted_iota(jnp.int32, (head, span), 0) == index).astype(F32)
 
+    copies = [
+        pltpu.make_async_copy(source_ref.at[index], maps_ref.at[index], arrived.at[index])
+        for index in range(count)
+    ]
+    for copy in copies:
+        copy.start()
     for shift in range(1, tiles):
         dest = lax.rem(me + shift, tiles)
         by_col = by_row = None
         for index in range(count):
+            if shift == 1:
+                copies[index].wait()
             block = maps_ref[index]
             out_ref[shift - 1, index * cols : (index + 1) * cols, :] = maps_ref[
                 index, pl.ds(pl.multiple_of(dest * cols, cols), cols), :
@@ -460,11 +468,11 @@
             readout = vector_ref[:, plan.convs + 1 : plan.convs + 2]
             logit_ref[0:1, here] = jnp.sum(value.astype(F32) * readout, axis=0, keepdims=True)
 
-        for i in range(steps + 1):
+        for i in range(steps + 2):
+            if i > 1:
+                finish(low + (i - 2) * chunk)
             if i < steps:
                 multiply(low + i * chunk)
-            if i > 0:
-                finish(low + (i - 1) * chunk)
 
     for r in range(plan.band):
         begin = plan.start + (r + halo) * stride + halo
@@ -472,15 +480,15 @@
         out_ref[r : r + 1, :] = shifted(logit_ref, slice(0, 1), low, begin - low, cols)
 
 
-def call(kernel, name, args, outs, scratch=()):
+def call(kernel, name, args, outs, scratch=(), space=pltpu.VMEM, semaphores=()):
     held = sum(math.prod(x.shape) * jnp.dtype(x.dtype).itemsize for x in [*args, *outs, *scratch])
     vmem = pl.BlockSpec(memory_space=pltpu.VMEM)
     return pl.pallas_call(
         kernel,
         out_shape=list(outs),
-        in_specs=[vmem] * len(args),
+        in_specs=[pl.BlockSpec(memory_space=space)] + [vmem] * (len(args) - 1),
         out_specs=[vmem] * len(outs),
-        scratch_shapes=list(scratch),
+        scratch_shapes=[*scratch, *semaphores],
         compiler_params=pltpu.CompilerParams(vmem_limit_bytes=held * 5 // 4 + 4 * 1024 * 1024),
         name=name,
     )(*args)
@@ -507,6 +515,9 @@
             array(F32, plan.map_rows, width),
             array(F32, plan.edge_rows, cols),
         ],
+        [pltpu.VMEM(attention.shape, BF16)],
+        space=pltpu.HBM,
+        semaphores=[pltpu.SemaphoreType.DMA((maps,))],
     )
     received = jnp.stack(
         [

time: 48.1 us -> 49.9 us (1.037)
  Pallas kernels: 12.4 us -> 14.2 us
    pallas_call x6, Pallas kernels: 12.4 us -> 14.2 us  [call(): pl.pallas_call(kernel, out_shape=list(outs), in_specs=[pl.BlockSpec(memor...]
  transfers between devices with their start and end apart: 10 -> 10, of which waited for: 6 -> 6; matrix products, arithmetic and copies ran while one was open for 4% -> 3% of each run, Pallas kernels for 1% -> 1%
where the time goes in v9:
time: 49.9 us; the launch traced here: 49.8 us
  starting transfers between devices  19.9 us (40%)
  Pallas kernels  14.2 us (28%)
  waiting for transfers between devices  12.6 us (25%)
  local copies, waits for them, and re-layouts  1.49 us (3%)
  other arithmetic  1.35 us (3%)
    ppermute x7, starting transfers between devices, on_device(): arrived[step] = lax.ppermute(block, 'head', pairs) if step else block  16.7 us
    pallas_call x6, Pallas kernels, call(): pl.pallas_call(kernel, out_shape=list(outs), in_specs=[pl.BlockSpec(memor...  14.2 us
    ppermute x1, waiting for transfers between devices, on_device(): lax.ppermute(payload[s - 1], 'tile', [(i, (i + s) % tiles) for i in range...  6.52 us
    ppermute x7, waiting for transfers between devices, on_device(): arrived[step] = lax.ppermute(block, 'head', pairs) if step else block  4.73 us
    ppermute x1, starting transfers between devices, on_device(): lax.ppermute(payload[s - 1], 'tile', [(i, (i + s) % tiles) for i in range...  3.03 us
    ppermute x2, waiting for transfers between devices, on_device(): lax.ppermute(packed, 'head', [(i, i ^ 1) for i in range(heads)])  1.38 us
    convert_element_type x1, other arithmetic, on_device(): spots.append(functools.reduce(jnp.logical_or, hit).astype(BF16))  1.33 us
    unnamed x20, local copies, waits for them, and re-layouts  1.22 us
  transfers between devices with their start and end apart: 10, of which 6 were waited for; matrix products, arithmetic and copies ran while one was open for 3% of the time, Pallas kernels for 1%

profile of v9, /device:TPU:0, one launch (start us, length us, event | category | flops | bytes accessed | tf_op | source)
XLA Modules:
  0.0 49.8 jit_solution(8275351724109501168)
XLA Ops:
  0.0 1.1 %copy-done = bf16[9,256,128]{2,1,0:T(8,128)(2,1)S(1)} copy-done((bf16[9,256,128]{2,1,0:T(8,128)(2,1)S(1)}, bf16[9,256,128]{2,1,0:T(8,128)(2,1)}, u32[]{:S(2)}) %copy-start) | copy-done | bytes 589848
  1.1 3.0 %mirror_pack.1 = (bf16[1,1376,128]{2,1,0:T(8,128)(2,1)}, f32[16,256]{1,0:T(8,128)S(1)}, f32[40,128]{1,0:T(8,128)S(1)}) custom-call(bf16[9,256,128]{2,1,0:T(8,128)(2,1)S(1)} %copy-done), custom_call_target="tpu_custom_call" | custom-call | tf_op jit(solution)/shard_map/mirror_pack/pallas_call | solution.py:486
  4.1 0.0 copy-start.1
  4.1 3.0 %collective-permute-start = (bf16[1376,128]{1,0:T(8,128)(2,1)}, bf16[1376,128]{1,0:T(8,128)(2,1)S(1)}, u32[]{:S(2)}, u32[]{:S(2)}) collective-permute-start(bf16[1376,128]{1,0:T(8,128)(2,1)} %bitcast), channel_id=1, source_target_pairs={{0,1},{1,0},{2,3},{3,2},{4,5},{5,4},{6,7},{7,6},{8,9},{9,8},{10,11... | collective-permute-start | bytes 1056776 | tf_op jit(solution)/shard_map/ppermute | solution.py:524
  7.1 1.3 %fusion.1.refs_15_ = bf16[1,128,4352]{2,1,0:T(8,128)(2,1)S(1)} fusion(s32[128]{0:T(128)} %constant.34.clone, s32[128]{0:T(128)} %constant.33.clone), kind=kLoop, calls=%fused_computation.3 | loop fusion | flops 2228224 | bytes 1115136 | tf_op jit(solution)/shard_map/convert_element_type | solution.py:558
  8.6 0.1 copy.24
  8.7 0.1 copy.21
  8.9 0.1 kernel_pack.1.refs_12_
  9.1 6.5 %collective-permute-done = bf16[1376,128]{1,0:T(8,128)(2,1)S(1)} collective-permute-done((bf16[1376,128]{1,0:T(8,128)(2,1)}, bf16[1376,128]{1,0:T(8,128)(2,1)S(1)}, u32[]{:S(2)}, u32[]{:S(2)}) %collective-permute-start) | collective-permute-done | bytes 352288 | tf_op jit(solution)/shard_map/ppermute | solution.py:524
  15.6 1.0 %correct_pack.1 = (bf16[384,128]{1,0:T(8,128)(2,1)S(1)}, bf16[384,128]{1,0:T(8,128)(2,1)S(1)}, bf16[384,128]{1,0:T(8,128)(2,1)S(1)}, bf16[384,128]{1,0:T(8,128)(...) custom-call(bf16[9,256,128]{2,1,0:T(8,128)(2,1)S(1)} %copy-done.1, ...), custom_call_target="tpu_custom_call" | custom-call | tf_op jit(solution)/shard_map/correct_pack/pallas_call | solution.py:486
  16.6 4.8 %collective-permute-start.1 = (bf16[384,128]{1,0:T(8,128)(2,1)S(1)}, bf16[384,128]{1,0:T(8,128)(2,1)S(1)}, u32[]{:S(2)}, u32[]{:S(2)}) collective-permute-start(bf16[384,128]{1,0:T(8,128)(2,1)S(1)} %get-tuple-element.26), channel_id=1, source_target_pairs={{0,28},{2,30},{4,24},{6,26},{8,20},{10,22},{12,16},{14,18},{16,12}... | collective-permute-start | bytes 294920 | tf_op jit(solution)/shard_map/ppermute | solution.py:575
  21.4 0.2 collective-permute-start.2
  21.6 0.8 %collective-permute-start.3 = (bf16[384,128]{1,0:T(8,128)(2,1)S(1)}, bf16[384,128]{1,0:T(8,128)(2,1)S(1)}, u32[]{:S(2)}, u32[]{:S(2)}) collective-permute-start(bf16[384,128]{1,0:T(8,128)(2,1)S(1)} %get-tuple-element.28), channel_id=1, source_target_pairs={{0,20},{2,22},{4,16},{6,18},{8,28},{10,30},{12,24},{14,26},{16,4},... | collective-permute-start | bytes 294920 | tf_op jit(solution)/shard_map/ppermute | solution.py:575
  22.4 2.0 %collective-permute-start.4 = (bf16[384,128]{1,0:T(8,128)(2,1)S(1)}, bf16[384,128]{1,0:T(8,128)(2,1)S(1)}, u32[]{:S(2)}, u32[]{:S(2)}) collective-permute-start(bf16[384,128]{1,0:T(8,128)(2,1)S(1)} %get-tuple-element.29), channel_id=1, source_target_pairs={{0,16},{2,18},{4,20},{6,22},{8,24},{10,26},{12,28},{14,30},{16,0},... | collective-permute-start | bytes 294920 | tf_op jit(solution)/shard_map/ppermute | solution.py:575
  24.4 2.3 %collective-permute-start.5 = (bf16[384,128]{1,0:T(8,128)(2,1)S(1)}, bf16[384,128]{1,0:T(8,128)(2,1)S(1)}, u32[]{:S(2)}, u32[]{:S(2)}) collective-permute-start(bf16[384,128]{1,0:T(8,128)(2,1)S(1)} %get-tuple-element.30), channel_id=1, source_target_pairs={{0,12},{2,14},{4,8},{6,10},{8,4},{10,6},{12,0},{14,2},{16,28},{18,... | collective-permute-start | bytes 294920 | tf_op jit(solution)/shard_map/ppermute | solution.py:575
  26.7 0.0 collective-permute-done.1.refs_0_
  26.7 5.6 %collective-permute-start.6 = (bf16[384,128]{1,0:T(8,128)(2,1)S(1)}, bf16[384,128]{1,0:T(8,128)(2,1)S(1)}, u32[]{:S(2)}, u32[]{:S(2)}) collective-permute-start(bf16[384,128]{1,0:T(8,128)(2,1)S(1)} %get-tuple-element.31), channel_id=1, source_target_pairs={{0,8},{2,10},{4,12},{6,14},{8,0},{10,2},{12,4},{14,6},{16,24},{18,... | collective-permute-start | bytes 294920 | tf_op jit(solution)/shard_map/ppermute | solution.py:575
  32.3 0.0 collective-permute-done.2.refs_1_
  32.3 1.0 %collective-permute-start.7 = (bf16[384,128]{1,0:T(8,128)(2,1)S(1)}, bf16[384,128]{1,0:T(8,128)(2,1)S(1)}, u32[]{:S(2)}, u32[]{:S(2)}) collective-permute-start(bf16[384,128]{1,0:T(8,128)(2,1)S(1)} %get-tuple-element.32), channel_id=1, source_target_pairs={{0,4},{2,6},{4,0},{6,2},{8,12},{10,14},{12,8},{14,10},{16,20},{18,... | collective-permute-start | bytes 294920 | tf_op jit(solution)/shard_map/ppermute | solution.py:575
  33.3 2.9 %collective-permute-done.3.refs_2_ = bf16[384,128]{1,0:T(8,128)(2,1)S(1)} collective-permute-done((bf16[384,128]{1,0:T(8,128)(2,1)S(1)}, bf16[384,128]{1,0:T(8,128)(2,1)S(1)}, u32[]{:S(2)}, u32[]{:S(2)}) %collective-permute-start.3) | collective-permute-done | bytes 98336 | tf_op jit(solution)/shard_map/ppermute | solution.py:575
  36.2 1.1 %collective-permute-done.4.refs_3_ = bf16[384,128]{1,0:T(8,128)(2,1)S(1)} collective-permute-done((bf16[384,128]{1,0:T(8,128)(2,1)S(1)}, bf16[384,128]{1,0:T(8,128)(2,1)S(1)}, u32[]{:S(2)}, u32[]{:S(2)}) %collective-permute-start.4) | collective-permute-done | bytes 98336 | tf_op jit(solution)/shard_map/ppermute | solution.py:575
  37.3 0.1 core_pack.2
  37.4 0.1 collective-permute-start.8
  37.5 0.0 collective-permute-done.5.refs_0_.refs_4_
  37.5 0.7 %collective-permute-done.6.refs_1_.refs_5_ = bf16[384,128]{1,0:T(8,128)(2,1)S(1)} collective-permute-done((bf16[384,128]{1,0:T(8,128)(2,1)S(1)}, bf16[384,128]{1,0:T(8,128)(2,1)S(1)}, u32[]{:S(2)}, u32[]{:S(2)}) %collective-permute-start.6) | collective-permute-done | bytes 98336 | tf_op jit(solution)/shard_map/ppermute | solution.py:575
  38.2 0.0 collective-permute-done.7.refs_2_.refs_6_
  38.2 0.1 core_pack.3
  38.3 0.1 collective-permute-start.9
  38.3 0.1 copy.25.refs_11_
  38.4 0.5 %collective-permute-done.8.refs_8_ = bf16[4,224,128]{2,1,0:T(8,128)(2,1)S(1)} collective-permute-done((bf16[4,224,128]{2,1,0:T(8,128)(2,1)S(1)}, bf16[4,224,128]{2,1,0:T(8,128)(2,1)S(1)}, u32[]{:S(2)}, u32[]{:S(2)}) %collective-permute-start.8) | collective-permute-done | bytes 229408 | tf_op jit(solution)/shard_map/ppermute | solution.py:586
  38.9 0.9 %collective-permute-done.9.refs_9_ = bf16[4,224,128]{2,1,0:T(8,128)(2,1)S(1)} collective-permute-done((bf16[4,224,128]{2,1,0:T(8,128)(2,1)S(1)}, bf16[4,224,128]{2,1,0:T(8,128)(2,1)S(1)}, u32[]{:S(2)}, u32[]{:S(2)}) %collective-permute-start.9) | collective-permute-done | bytes 229408 | tf_op jit(solution)/shard_map/ppermute | solution.py:586
  39.8 10.0 %stack.6 = f32[16,128]{1,0:T(8,128)} custom-call(bf16[384,128]{1,0:T(8,128)(2,1)S(1)} %collective-permute-done.1.refs_0_, bf16[384,128]{1,0:T(8,128)(2,1)S(1)} %collective-permute-done.2.refs_1_, bf16[384,128]{1,0:T(8,128)(2,1)S(1)} %collective-permute-done.3.refs_2_, bf16[384,128]{1,0:T(8,128)(2,1)S(1)} %collective-permute-done.4.refs_3_, ...), custom_call_target="tpu_custom_call" | custom-call | tf_op jit(solution)/shard_map/stack/pallas_call | solution.py:486
  (23 shorter events, 0.2 us)
Async XLA Ops:
  0.0 1.1 %copy-start = (bf16[9,256,128]{2,1,0:T(8,128)(2,1)S(1)}, bf16[9,256,128]{2,1,0:T(8,128)(2,1)}, u32[]{:S(2)}) copy-start(bf16[9,256,128]{2,1,0:T(8,128)(2,1)} %maps_ref.1) | copy-start | bytes 1769476
  1.1 7.4 %copy-start.4 = (s32[4352]{0:T(1024)S(1)}, s32[4352]{0:T(1024)}, u32[]{:S(2)}) copy-start(s32[4352]{0:T(1024)} %constant.32.clone) | copy-start | bytes 52228
  1.1 7.4 %copy-start.5 = (s32[4352]{0:T(1024)S(1)}, s32[4352]{0:T(1024)}, u32[]{:S(2)}) copy-start(s32[4352]{0:T(1024)} %constant.31.clone) | copy-start | bytes 52228
  1.1 7.5 %copy-start.6 = (f32[2,2,64]{2,1,0:T(2,128)S(1)}, f32[2,2,64]{2,1,0:T(2,128)}, u32[]{:S(2)}) copy-start(f32[2,2,64]{2,1,0:T(2,128)} %param.14) | copy-start | bytes 3076
  1.1 7.5 %copy-start.7 = (f32[64]{0:T(128)S(1)}, f32[64]{0:T(128)}, u32[]{:S(2)}) copy-start(f32[64]{0:T(128)} %param.15) | copy-start | bytes 772
  1.1 7.5 %copy-start.8 = (f32[64]{0:T(128)S(1)}, f32[64]{0:T(128)}, u32[]{:S(2)}) copy-start(f32[64]{0:T(128)} %param.12) | copy-start | bytes 772
  1.1 7.6 %copy-start.3 = (bf16[64,144]{1,0:T(8,128)(2,1)S(1)}, bf16[64,144]{1,0:T(8,128)(2,1)}, u32[]{:S(2)}) copy-start(bf16[64,144]{1,0:T(8,128)(2,1)} %refs_10_.1) | copy-start | bytes 55300
  1.1 7.8 %copy-start.2 = (bf16[2,2,64,64,3,3]{3,2,5,4,1,0:T(8,128)(2,1)S(1)}, bf16[2,2,64,64,3,3]{3,2,5,4,1,0:T(8,128)(2,1)}, u32[]{:S(2)}) copy-start(bf16[2,2,64,64,3,3]{3,2,5,4,1,0:T(8,128)(2,1)} %param.13) | copy-start | bytes 884740
  4.1 11.5 %copy-start.1 = (bf16[9,256,128]{2,1,0:T(8,128)(2,1)S(1)}, bf16[9,256,128]{2,1,0:T(8,128)(2,1)}, u32[]{:S(2)}) copy-start(bf16[9,256,128]{2,1,0:T(8,128)(2,1)} %maps_ref.1) | copy-start | bytes 1769476
  4.1 11.5 %collective-permute-start = (bf16[1376,128]{1,0:T(8,128)(2,1)}, bf16[1376,128]{1,0:T(8,128)(2,1)S(1)}, u32[]{:S(2)}, u32[]{:S(2)}) collective-permute-start(bf16[1376,128]{1,0:T(8,128)(2,1)} %bitcast), channel_id=1, source_target_pairs={{0,1},{1,0},{2,3},{3,2},{4,5},{5,4},{6,7},{7,6},{8,9},{9,8},{10,11... | collective-permute-start | bytes 1056776 | tf_op jit(solution)/shard_map/ppermute | solution.py:524
  16.6 10.1 %collective-permute-start.1 = (bf16[384,128]{1,0:T(8,128)(2,1)S(1)}, bf16[384,128]{1,0:T(8,128)(2,1)S(1)}, u32[]{:S(2)}, u32[]{:S(2)}) collective-permute-start(bf16[384,128]{1,0:T(8,128)(2,1)S(1)} %get-tuple-element.26), channel_id=1, source_target_pairs={{0,28},{2,30},{4,24},{6,26},{8,20},{10,22},{12,16},{14,18},{16,12}... | collective-permute-start | bytes 294920 | tf_op jit(solution)/shard_map/ppermute | solution.py:575
  21.4 10.9 %collective-permute-start.2 = (bf16[384,128]{1,0:T(8,128)(2,1)S(1)}, bf16[384,128]{1,0:T(8,128)(2,1)S(1)}, u32[]{:S(2)}, u32[]{:S(2)}) collective-permute-start(bf16[384,128]{1,0:T(8,128)(2,1)S(1)} %get-tuple-element.27), channel_id=1, source_target_pairs={{0,24},{2,26},{4,28},{6,30},{8,16},{10,18},{12,20},{14,22},{16,8},... | collective-permute-start | bytes 294920 | tf_op jit(solution)/shard_map/ppermute | solution.py:575
  21.6 14.6 %collective-permute-start.3 = (bf16[384,128]{1,0:T(8,128)(2,1)S(1)}, bf16[384,128]{1,0:T(8,128)(2,1)S(1)}, u32[]{:S(2)}, u32[]{:S(2)}) collective-permute-start(bf16[384,128]{1,0:T(8,128)(2,1)S(1)} %get-tuple-element.28), channel_id=1, source_target_pairs={{0,20},{2,22},{4,16},{6,18},{8,28},{10,30},{12,24},{14,26},{16,4},... | collective-permute-start | bytes 294920 | tf_op jit(solution)/shard_map/ppermute | solution.py:575
  22.4 14.9 %collective-permute-start.4 = (bf16[384,128]{1,0:T(8,128)(2,1)S(1)}, bf16[384,128]{1,0:T(8,128)(2,1)S(1)}, u32[]{:S(2)}, u32[]{:S(2)}) collective-permute-start(bf16[384,128]{1,0:T(8,128)(2,1)S(1)} %get-tuple-element.29), channel_id=1, source_target_pairs={{0,16},{2,18},{4,20},{6,22},{8,24},{10,26},{12,28},{14,30},{16,0},... | collective-permute-start | bytes 294920 | tf_op jit(solution)/shard_map/ppermute | solution.py:575
  24.4 13.1 %collective-permute-start.5 = (bf16[384,128]{1,0:T(8,128)(2,1)S(1)}, bf16[384,128]{1,0:T(8,128)(2,1)S(1)}, u32[]{:S(2)}, u32[]{:S(2)}) collective-permute-start(bf16[384,128]{1,0:T(8,128)(2,1)S(1)} %get-tuple-element.30), channel_id=1, source_target_pairs={{0,12},{2,14},{4,8},{6,10},{8,4},{10,6},{12,0},{14,2},{16,28},{18,... | collective-permute-start | bytes 294920 | tf_op jit(solution)/shard_map/ppermute | solution.py:575
  26.7 11.5 %collective-permute-start.6 = (bf16[384,128]{1,0:T(8,128)(2,1)S(1)}, bf16[384,128]{1,0:T(8,128)(2,1)S(1)}, u32[]{:S(2)}, u32[]{:S(2)}) collective-permute-start(bf16[384,128]{1,0:T(8,128)(2,1)S(1)} %get-tuple-element.31), channel_id=1, source_target_pairs={{0,8},{2,10},{4,12},{6,14},{8,0},{10,2},{12,4},{14,6},{16,24},{18,... | collective-permute-start | bytes 294920 | tf_op jit(solution)/shard_map/ppermute | solution.py:575
  32.3 5.9 %collective-permute-start.7 = (bf16[384,128]{1,0:T(8,128)(2,1)S(1)}, bf16[384,128]{1,0:T(8,128)(2,1)S(1)}, u32[]{:S(2)}, u32[]{:S(2)}) collective-permute-start(bf16[384,128]{1,0:T(8,128)(2,1)S(1)} %get-tuple-element.32), channel_id=1, source_target_pairs={{0,4},{2,6},{4,0},{6,2},{8,12},{10,14},{12,8},{14,10},{16,20},{18,... | collective-permute-start | bytes 294920 | tf_op jit(solution)/shard_map/ppermute | solution.py:575
  37.4 1.6 %collective-permute-start.8 = (bf16[4,224,128]{2,1,0:T(8,128)(2,1)S(1)}, bf16[4,224,128]{2,1,0:T(8,128)(2,1)S(1)}, u32[]{:S(2)}, u32[]{:S(2)}) collective-permute-start(bf16[4,224,128]{2,1,0:T(8,128)(2,1)S(1)} %core_pack.2), channel_id=1, source_target_pairs={{0,2},{2,0},{4,6},{6,4},{8,10},{10,8},{12,14},{14,12},{16,18},{18,... | collective-permute-start | bytes 688136 | tf_op jit(solution)/shard_map/ppermute | solution.py:586
  38.3 1.6 %collective-permute-start.9 = (bf16[4,224,128]{2,1,0:T(8,128)(2,1)S(1)}, bf16[4,224,128]{2,1,0:T(8,128)(2,1)S(1)}, u32[]{:S(2)}, u32[]{:S(2)}) collective-permute-start(bf16[4,224,128]{2,1,0:T(8,128)(2,1)S(1)} %core_pack.3), channel_id=1, source_target_pairs={{0,2},{2,0},{4,6},{6,4},{8,10},{10,8},{12,14},{14,12},{16,18},{18,... | collective-permute-start | bytes 688136 | tf_op jit(solution)/shard_map/ppermute | solution.py:586

commit v10 on v8

--- a/solution.py
+++ b/solution.py
@@ -113,7 +113,7 @@
 
     @property
     def lanes(self):
-        return up(self.start + self.rows * self.stride, LANES) + 2 * self.chunk + 3 * LANES
+        return up(self.start + self.rows * self.stride, LANES) + 6 * self.chunk + 3 * LANES
 
 
 def partner(mine, step, count, back=False):
@@ -336,13 +336,16 @@
             ).astype(BF16)
 
 
+def lanes(base, size):
+    return pl.ds(base if isinstance(base, int) else pl.multiple_of(base, LANES), size)
+
+
 def shifted(ref, rows, base, offset, size):
-    begin = base + offset
-    low = begin // LANES * LANES
-    rest = begin - low
+    low = offset // LANES * LANES
+    rest = offset - low
     if rest == 0:
-        return ref[rows, low : low + size]
-    return pltpu.roll(ref[rows, low : low + size + LANES], size + LANES - rest, 1)[:, :size]
+        return ref[rows, lanes(base + low, size)]
+    return pltpu.roll(ref[rows, lanes(base + low, size + LANES)], size + LANES - rest, 1)[:, :size]
 
 
 def stack(plan, order, *refs):
@@ -429,21 +432,22 @@
         here = slice(i * chunk, (i + 1) * chunk)
         stream_ref[:, here] = jnp.where(mask_ref[:, here] > 0, field_ref[:, here], 0.0).astype(BF16)
 
+    chunk = 2 * chunk
     everything = slice(None)
     for n in range(plan.convs):
         source = hidden_ref if n % 2 else stream_ref
         low = (plan.start + (n + 1) * stride) // LANES * LANES
-        steps = -(-(plan.start + (rows - n - 1) * stride - low) // chunk)
+        steps = -(-(plan.start + (rows - n - 1) * stride - low + LANES) // chunk)
         offsets = vector_ref[:, n + 1 : n + 2]
 
         def multiply(base):
             window = jnp.concatenate(
                 [shifted(source, everything, base, d * stride, chunk) for d in (-1, 0, 1)], axis=0
             )
-            taps_ref[:, base : base + chunk] = dot(kernel_ref[n], window)
+            taps_ref[:, lanes(base, chunk)] = dot(kernel_ref[n], window)
 
         def finish(base):
-            here = slice(base, base + chunk)
+            here = lanes(base, chunk)
             value = taps_ref[feat : 2 * feat, here]
             value = value + shifted(taps_ref, slice(0, feat), base, -1, chunk)
             value = value + shifted(taps_ref, slice(2 * feat, 3 * feat), base, 1, chunk)
@@ -460,11 +464,15 @@
             readout = vector_ref[:, plan.convs + 1 : plan.convs + 2]
             logit_ref[0:1, here] = jnp.sum(value.astype(F32) * readout, axis=0, keepdims=True)
 
-        for i in range(steps + 1):
-            if i < steps:
-                multiply(low + i * chunk)
-            if i > 0:
-                finish(low + (i - 1) * chunk)
+        multiply(low)
+
+        def advance(i, carry):
+            base = low + i * chunk
+            finish(base - LANES)
+            multiply(base + chunk)
+            return carry
+
+        lax.fori_loop(0, steps, advance, 0)
 
     for r in range(plan.band):
         begin = plan.start + (r + halo) * stride + halo
@@ -547,9 +555,6 @@
         spots.append(functools.reduce(jnp.logical_or, hit).astype(BF16))
     spots = jnp.stack(spots)
 
-    weights = (side_weight, kernels, vectors, mask, spots)
-    received, weights = lax.optimization_barrier((received, weights))
-
     chips = plan.chips
     blocks = call(
         functools.partial(correct_pack, plan),
@@ -564,6 +569,8 @@
         arrived[step] = lax.ppermute(block, "head", pairs) if step else block
     far, near = far_near(plan)
     order = [far, near + [0]]
+    weights = (proj_weight, side_weight, kernels, vectors, mask, spots)
+    arrived[0], weights = lax.optimization_barrier((arrived[0], weights))
     swapped = []
     for steps in order:
         (packed,) = call(
@@ -577,7 +584,7 @@
     (logits,) = call(
         functools.partial(stack, plan, order),
         "stack",
-        [*arrived.values(), *swapped, proj_weight, *weights],
+        [*arrived.values(), *swapped, *weights],
         [array(F32, plan.band, cols)],
         [
             pltpu.VMEM((heads * maps * plan.rows, cols), F32),

time: 48.1 us -> 49.4 us (1.027)
  Pallas kernels: 12.4 us -> 13.5 us
    pallas_call x6, Pallas kernels: 12.4 us -> 13.5 us  [call(): pl.pallas_call(kernel, out_shape=list(outs), in_specs=[vmem] * len(args),...]
  transfers between devices with their start and end apart: 10 -> 10, of which waited for: 6 -> 5; matrix products, arithmetic and copies ran while one was open for 4% -> 4% of each run, Pallas kernels for 1% -> 2%
where the time goes in v10:
time: 49.4 us; the launch traced here: 49.2 us
  starting transfers between devices  19.8 us (40%)
  Pallas kernels  13.5 us (27%)
  waiting for transfers between devices  12.8 us (26%)
  other arithmetic  1.5 us (3%)
  local copies, waits for them, and re-layouts  1.49 us (3%)
    ppermute x7, starting transfers between devices, on_device(): arrived[step] = lax.ppermute(block, 'head', pairs) if step else block  16.7 us
    pallas_call x6, Pallas kernels, call(): pl.pallas_call(kernel, out_shape=list(outs), in_specs=[vmem] * len(args),...  13.5 us
    ppermute x1, waiting for transfers between devices, on_device(): lax.ppermute(payload[s - 1], 'tile', [(i, (i + s) % tiles) for i in range...  6.96 us
    ppermute x7, waiting for transfers between devices, on_device(): arrived[step] = lax.ppermute(block, 'head', pairs) if step else block  4.25 us
    ppermute x1, starting transfers between devices, on_device(): lax.ppermute(payload[s - 1], 'tile', [(i, (i + s) % tiles) for i in range...  3.03 us
    ppermute x2, waiting for transfers between devices, on_device(): lax.ppermute(packed, 'head', [(i, i ^ 1) for i in range(heads)])  1.59 us
    convert_element_type x1, other arithmetic, on_device(): spots.append(functools.reduce(jnp.logical_or, hit).astype(BF16))  1.47 us
    unnamed x20, local copies, waits for them, and re-layouts  1.21 us
  transfers between devices with their start and end apart: 10, of which 5 were waited for; matrix products, arithmetic and copies ran while one was open for 4% of the time, Pallas kernels for 2%

profile of v10, /device:TPU:0, one launch (start us, length us, event | category | flops | bytes accessed | tf_op | source)
XLA Modules:
  0.0 49.2 jit_solution(4861723282290316611)
XLA Ops:
  0.0 1.1 %copy-done = bf16[9,256,128]{2,1,0:T(8,128)(2,1)S(1)} copy-done((bf16[9,256,128]{2,1,0:T(8,128)(2,1)S(1)}, bf16[9,256,128]{2,1,0:T(8,128)(2,1)}, u32[]{:S(2)}) %copy-start) | copy-done | bytes 589848
  1.1 1.2 %mirror_pack.1 = (bf16[1,1376,128]{2,1,0:T(8,128)(2,1)}, f32[16,256]{1,0:T(8,128)S(1)}, f32[40,128]{1,0:T(8,128)S(1)}) custom-call(bf16[9,256,128]{2,1,0:T(8,128)(2,1)S(1)} %copy-done), custom_call_target="tpu_custom_call" | custom-call | tf_op jit(solution)/shard_map/mirror_pack/pallas_call | solution.py:486
  2.3 0.0 copy-start.2
  2.3 3.0 %collective-permute-start = (bf16[1376,128]{1,0:T(8,128)(2,1)}, bf16[1376,128]{1,0:T(8,128)(2,1)S(1)}, u32[]{:S(2)}, u32[]{:S(2)}) collective-permute-start(bf16[1376,128]{1,0:T(8,128)(2,1)} %bitcast), channel_id=1, source_target_pairs={{0,1},{1,0},{2,3},{3,2},{4,5},{5,4},{6,7},{7,6},{8,9},{9,8},{10,11... | collective-permute-start | bytes 1056776 | tf_op jit(solution)/shard_map/ppermute | solution.py:521
  5.3 1.5 %fusion.1.refs_15_ = bf16[1,128,5376]{2,1,0:T(8,128)(2,1)S(1)} fusion(s32[128]{0:T(128)} %constant.34.clone, s32[128]{0:T(128)} %constant.33.clone), kind=kLoop, calls=%fused_computation.3 | loop fusion | flops 2752512 | bytes 1377280 | tf_op jit(solution)/shard_map/convert_element_type | solution.py:555
  6.8 7.0 %collective-permute-done = bf16[1376,128]{1,0:T(8,128)(2,1)S(1)} collective-permute-done((bf16[1376,128]{1,0:T(8,128)(2,1)}, bf16[1376,128]{1,0:T(8,128)(2,1)S(1)}, u32[]{:S(2)}, u32[]{:S(2)}) %collective-permute-start) | collective-permute-done | bytes 352288 | tf_op jit(solution)/shard_map/ppermute | solution.py:521
  13.8 1.6 %correct_pack.1 = (bf16[384,128]{1,0:T(8,128)(2,1)S(1)}, bf16[384,128]{1,0:T(8,128)(2,1)S(1)}, bf16[384,128]{1,0:T(8,128)(2,1)S(1)}, bf16[384,128]{1,0:T(8,128)(...) custom-call(bf16[9,256,128]{2,1,0:T(8,128)(2,1)S(1)} %copy-done.1, ...), custom_call_target="tpu_custom_call" | custom-call | tf_op jit(solution)/shard_map/correct_pack/pallas_call | solution.py:486
  15.4 4.8 %collective-permute-start.1 = (bf16[384,128]{1,0:T(8,128)(2,1)S(1)}, bf16[384,128]{1,0:T(8,128)(2,1)S(1)}, u32[]{:S(2)}, u32[]{:S(2)}) collective-permute-start(bf16[384,128]{1,0:T(8,128)(2,1)S(1)} %get-tuple-element.26), channel_id=1, source_target_pairs={{0,28},{2,30},{4,24},{6,26},{8,20},{10,22},{12,16},{14,18},{16,12}... | collective-permute-start | bytes 294920 | tf_op jit(solution)/shard_map/ppermute | solution.py:569
  20.1 0.2 collective-permute-start.2
  20.4 0.8 %collective-permute-start.3 = (bf16[384,128]{1,0:T(8,128)(2,1)S(1)}, bf16[384,128]{1,0:T(8,128)(2,1)S(1)}, u32[]{:S(2)}, u32[]{:S(2)}) collective-permute-start(bf16[384,128]{1,0:T(8,128)(2,1)S(1)} %get-tuple-element.28), channel_id=1, source_target_pairs={{0,20},{2,22},{4,16},{6,18},{8,28},{10,30},{12,24},{14,26},{16,4},... | collective-permute-start | bytes 294920 | tf_op jit(solution)/shard_map/ppermute | solution.py:569
  21.2 1.9 %collective-permute-start.4 = (bf16[384,128]{1,0:T(8,128)(2,1)S(1)}, bf16[384,128]{1,0:T(8,128)(2,1)S(1)}, u32[]{:S(2)}, u32[]{:S(2)}) collective-permute-start(bf16[384,128]{1,0:T(8,128)(2,1)S(1)} %get-tuple-element.29), channel_id=1, source_target_pairs={{0,16},{2,18},{4,20},{6,22},{8,24},{10,26},{12,28},{14,30},{16,0},... | collective-permute-start | bytes 294920 | tf_op jit(solution)/shard_map/ppermute | solution.py:569
  23.2 2.4 %collective-permute-start.5 = (bf16[384,128]{1,0:T(8,128)(2,1)}, bf16[384,128]{1,0:T(8,128)(2,1)S(1)}, u32[]{:S(2)}, u32[]{:S(2)}) collective-permute-start(bf16[384,128]{1,0:T(8,128)(2,1)} %get-tuple-element.30), channel_id=1, source_target_pairs={{0,12},{2,14},{4,8},{6,10},{8,4},{10,6},{12,0},{14,2},{16,28},{18,... | collective-permute-start | bytes 294920 | tf_op jit(solution)/shard_map/ppermute | solution.py:569
  25.5 0.0 collective-permute-done.1.refs_0_
  25.5 5.5 %collective-permute-start.6 = (bf16[384,128]{1,0:T(8,128)(2,1)}, bf16[384,128]{1,0:T(8,128)(2,1)S(1)}, u32[]{:S(2)}, u32[]{:S(2)}) collective-permute-start(bf16[384,128]{1,0:T(8,128)(2,1)} %get-tuple-element.31), channel_id=1, source_target_pairs={{0,8},{2,10},{4,12},{6,14},{8,0},{10,2},{12,4},{14,6},{16,24},{18,... | collective-permute-start | bytes 294920 | tf_op jit(solution)/shard_map/ppermute | solution.py:569
  31.0 0.0 collective-permute-done.2.refs_1_
  31.0 1.1 %collective-permute-start.7 = (bf16[384,128]{1,0:T(8,128)(2,1)}, bf16[384,128]{1,0:T(8,128)(2,1)S(1)}, u32[]{:S(2)}, u32[]{:S(2)}) collective-permute-start(bf16[384,128]{1,0:T(8,128)(2,1)} %get-tuple-element.32), channel_id=1, source_target_pairs={{0,4},{2,6},{4,0},{6,2},{8,12},{10,14},{12,8},{14,10},{16,20},{18,... | collective-permute-start | bytes 294920 | tf_op jit(solution)/shard_map/ppermute | solution.py:569
  32.1 0.1 copy.24
  32.2 0.1 copy.21
  32.5 0.1 kernel_pack.1.refs_12_
  32.6 2.4 %collective-permute-done.3.refs_2_ = bf16[384,128]{1,0:T(8,128)(2,1)S(1)} collective-permute-done((bf16[384,128]{1,0:T(8,128)(2,1)S(1)}, bf16[384,128]{1,0:T(8,128)(2,1)S(1)}, u32[]{:S(2)}, u32[]{:S(2)}) %collective-permute-start.3) | collective-permute-done | bytes 98336 | tf_op jit(solution)/shard_map/ppermute | solution.py:569
  35.0 1.1 %collective-permute-done.4.refs_3_ = bf16[384,128]{1,0:T(8,128)(2,1)S(1)} collective-permute-done((bf16[384,128]{1,0:T(8,128)(2,1)S(1)}, bf16[384,128]{1,0:T(8,128)(2,1)S(1)}, u32[]{:S(2)}, u32[]{:S(2)}) %collective-permute-start.4) | collective-permute-done | bytes 98336 | tf_op jit(solution)/shard_map/ppermute | solution.py:569
  36.0 0.1 core_pack.2
  36.1 0.1 collective-permute-start.8
  36.2 0.0 collective-permute-done.5.refs_0_.refs_4_
  36.2 0.8 %collective-permute-done.6.refs_1_.refs_5_ = bf16[384,128]{1,0:T(8,128)(2,1)S(1)} collective-permute-done((bf16[384,128]{1,0:T(8,128)(2,1)}, bf16[384,128]{1,0:T(8,128)(2,1)S(1)}, u32[]{:S(2)}, u32[]{:S(2)}) %collective-permute-start.6) | collective-permute-done | bytes 98336 | tf_op jit(solution)/shard_map/ppermute | solution.py:569
  37.0 0.0 collective-permute-done.7.refs_2_.refs_6_
  37.0 0.8 %core_pack.3 = bf16[4,224,128]{2,1,0:T(8,128)(2,1)} custom-call(bf16[384,128]{1,0:T(8,128)(2,1)S(1)} %collective-permute-done.5.refs_0_.refs_4_, bf16[384,128]{1,0:T(8,128)(2,1)S(1)} %collective-permute-done.6.refs_1_.refs_5_, bf16[384,128]{1,0:T(8,128)(2,1)S(1)} %collective-permute-done.7.refs_2_.refs_6_, bf16[384,128]{1,0:T(8,128)(2,1)S(1)} %get-tuple-element.34.refs_3_.refs_7_), custom_call_target="tpu_custom_call" | custom-call | tf_op jit(solution)/shard_map/core_pack/pallas_call | solution.py:486
  37.8 0.0 collective-permute-start.9
  37.8 0.1 copy.25.refs_11_
  37.9 0.0 collective-permute-done.8.refs_8_
  37.9 1.6 %collective-permute-done.9.refs_9_ = bf16[4,224,128]{2,1,0:T(8,128)(2,1)S(1)} collective-permute-done((bf16[4,224,128]{2,1,0:T(8,128)(2,1)}, bf16[4,224,128]{2,1,0:T(8,128)(2,1)S(1)}, u32[]{:S(2)}, u32[]{:S(2)}) %collective-permute-start.9) | collective-permute-done | bytes 229408 | tf_op jit(solution)/shard_map/ppermute | solution.py:582
  39.5 9.8 %stack.6 = f32[16,128]{1,0:T(8,128)} custom-call(bf16[384,128]{1,0:T(8,128)(2,1)S(1)} %collective-permute-done.1.refs_0_, bf16[384,128]{1,0:T(8,128)(2,1)S(1)} %collective-permute-done.2.refs_1_, bf16[384,128]{1,0:T(8,128)(2,1)S(1)} %collective-permute-done.3.refs_2_, bf16[384,128]{1,0:T(8,128)(2,1)S(1)} %collective-permute-done.4.refs_3_, ...), custom_call_target="tpu_custom_call" | custom-call | tf_op jit(solution)/shard_map/stack/pallas_call | solution.py:486
  (23 shorter events, 0.2 us)
Async XLA Ops:
  0.0 1.1 %copy-start = (bf16[9,256,128]{2,1,0:T(8,128)(2,1)S(1)}, bf16[9,256,128]{2,1,0:T(8,128)(2,1)}, u32[]{:S(2)}) copy-start(bf16[9,256,128]{2,1,0:T(8,128)(2,1)} %maps_ref.3) | copy-start | bytes 1769476
  1.1 12.7 %copy-start.1 = (bf16[9,256,128]{2,1,0:T(8,128)(2,1)S(1)}, bf16[9,256,128]{2,1,0:T(8,128)(2,1)}, u32[]{:S(2)}) copy-start(bf16[9,256,128]{2,1,0:T(8,128)(2,1)} %maps_ref.3) | copy-start | bytes 1769476
  1.1 19.3 %copy-start.4 = (s32[5376]{0:T(1024)S(1)}, s32[5376]{0:T(1024)}, u32[]{:S(2)}) copy-start(s32[5376]{0:T(1024)} %constant.32.clone) | copy-start | bytes 64516
  1.1 19.3 %copy-start.5 = (s32[5376]{0:T(1024)S(1)}, s32[5376]{0:T(1024)}, u32[]{:S(2)}) copy-start(s32[5376]{0:T(1024)} %constant.31.clone) | copy-start | bytes 64516
  2.3 29.8 %copy-start.6 = (f32[2,2,64]{2,1,0:T(2,128)S(1)}, f32[2,2,64]{2,1,0:T(2,128)}, u32[]{:S(2)}) copy-start(f32[2,2,64]{2,1,0:T(2,128)} %param.14) | copy-start | bytes 3076
  2.3 29.8 %copy-start.7 = (f32[64]{0:T(128)S(1)}, f32[64]{0:T(128)}, u32[]{:S(2)}) copy-start(f32[64]{0:T(128)} %param.15) | copy-start | bytes 772
  2.3 29.8 %copy-start.8 = (f32[64]{0:T(128)S(1)}, f32[64]{0:T(128)}, u32[]{:S(2)}) copy-start(f32[64]{0:T(128)} %param.12) | copy-start | bytes 772
  2.3 29.9 %copy-start.3 = (bf16[64,144]{1,0:T(8,128)(2,1)S(1)}, bf16[64,144]{1,0:T(8,128)(2,1)}, u32[]{:S(2)}) copy-start(bf16[64,144]{1,0:T(8,128)(2,1)} %refs_10_) | copy-start | bytes 55300
  2.3 30.2 %copy-start.2 = (bf16[2,2,64,64,3,3]{3,2,5,4,1,0:T(8,128)(2,1)S(1)}, bf16[2,2,64,64,3,3]{3,2,5,4,1,0:T(8,128)(2,1)}, u32[]{:S(2)}) copy-start(bf16[2,2,64,64,3,3]{3,2,5,4,1,0:T(8,128)(2,1)} %param.13) | copy-start | bytes 884740
  2.3 11.5 %collective-permute-start = (bf16[1376,128]{1,0:T(8,128)(2,1)}, bf16[1376,128]{1,0:T(8,128)(2,1)S(1)}, u32[]{:S(2)}, u32[]{:S(2)}) collective-permute-start(bf16[1376,128]{1,0:T(8,128)(2,1)} %bitcast), channel_id=1, source_target_pairs={{0,1},{1,0},{2,3},{3,2},{4,5},{5,4},{6,7},{7,6},{8,9},{9,8},{10,11... | collective-permute-start | bytes 1056776 | tf_op jit(solution)/shard_map/ppermute | solution.py:521
  15.4 10.2 %collective-permute-start.1 = (bf16[384,128]{1,0:T(8,128)(2,1)S(1)}, bf16[384,128]{1,0:T(8,128)(2,1)S(1)}, u32[]{:S(2)}, u32[]{:S(2)}) collective-permute-start(bf16[384,128]{1,0:T(8,128)(2,1)S(1)} %get-tuple-element.26), channel_id=1, source_target_pairs={{0,28},{2,30},{4,24},{6,26},{8,20},{10,22},{12,16},{14,18},{16,12}... | collective-permute-start | bytes 294920 | tf_op jit(solution)/shard_map/ppermute | solution.py:569
  20.1 10.9 %collective-permute-start.2 = (bf16[384,128]{1,0:T(8,128)(2,1)S(1)}, bf16[384,128]{1,0:T(8,128)(2,1)S(1)}, u32[]{:S(2)}, u32[]{:S(2)}) collective-permute-start(bf16[384,128]{1,0:T(8,128)(2,1)S(1)} %get-tuple-element.27), channel_id=1, source_target_pairs={{0,24},{2,26},{4,28},{6,30},{8,16},{10,18},{12,20},{14,22},{16,8},... | collective-permute-start | bytes 294920 | tf_op jit(solution)/shard_map/ppermute | solution.py:569
  20.4 14.6 %collective-permute-start.3 = (bf16[384,128]{1,0:T(8,128)(2,1)S(1)}, bf16[384,128]{1,0:T(8,128)(2,1)S(1)}, u32[]{:S(2)}, u32[]{:S(2)}) collective-permute-start(bf16[384,128]{1,0:T(8,128)(2,1)S(1)} %get-tuple-element.28), channel_id=1, source_target_pairs={{0,20},{2,22},{4,16},{6,18},{8,28},{10,30},{12,24},{14,26},{16,4},... | collective-permute-start | bytes 294920 | tf_op jit(solution)/shard_map/ppermute | solution.py:569
  21.2 14.8 %collective-permute-start.4 = (bf16[384,128]{1,0:T(8,128)(2,1)S(1)}, bf16[384,128]{1,0:T(8,128)(2,1)S(1)}, u32[]{:S(2)}, u32[]{:S(2)}) collective-permute-start(bf16[384,128]{1,0:T(8,128)(2,1)S(1)} %get-tuple-element.29), channel_id=1, source_target_pairs={{0,16},{2,18},{4,20},{6,22},{8,24},{10,26},{12,28},{14,30},{16,0},... | collective-permute-start | bytes 294920 | tf_op jit(solution)/shard_map/ppermute | solution.py:569
  23.2 13.0 %collective-permute-start.5 = (bf16[384,128]{1,0:T(8,128)(2,1)}, bf16[384,128]{1,0:T(8,128)(2,1)S(1)}, u32[]{:S(2)}, u32[]{:S(2)}) collective-permute-start(bf16[384,128]{1,0:T(8,128)(2,1)} %get-tuple-element.30), channel_id=1, source_target_pairs={{0,12},{2,14},{4,8},{6,10},{8,4},{10,6},{12,0},{14,2},{16,28},{18,... | collective-permute-start | bytes 294920 | tf_op jit(solution)/shard_map/ppermute | solution.py:569
  25.5 11.5 %collective-permute-start.6 = (bf16[384,128]{1,0:T(8,128)(2,1)}, bf16[384,128]{1,0:T(8,128)(2,1)S(1)}, u32[]{:S(2)}, u32[]{:S(2)}) collective-permute-start(bf16[384,128]{1,0:T(8,128)(2,1)} %get-tuple-element.31), channel_id=1, source_target_pairs={{0,8},{2,10},{4,12},{6,14},{8,0},{10,2},{12,4},{14,6},{16,24},{18,... | collective-permute-start | bytes 294920 | tf_op jit(solution)/shard_map/ppermute | solution.py:569
  31.0 6.0 %collective-permute-start.7 = (bf16[384,128]{1,0:T(8,128)(2,1)}, bf16[384,128]{1,0:T(8,128)(2,1)S(1)}, u32[]{:S(2)}, u32[]{:S(2)}) collective-permute-start(bf16[384,128]{1,0:T(8,128)(2,1)} %get-tuple-element.32), channel_id=1, source_target_pairs={{0,4},{2,6},{4,0},{6,2},{8,12},{10,14},{12,8},{14,10},{16,20},{18,... | collective-permute-start | bytes 294920 | tf_op jit(solution)/shard_map/ppermute | solution.py:569
  36.1 1.7 %collective-permute-start.8 = (bf16[4,224,128]{2,1,0:T(8,128)(2,1)S(1)}, bf16[4,224,128]{2,1,0:T(8,128)(2,1)S(1)}, u32[]{:S(2)}, u32[]{:S(2)}) collective-permute-start(bf16[4,224,128]{2,1,0:T(8,128)(2,1)S(1)} %core_pack.2), channel_id=1, source_target_pairs={{0,2},{2,0},{4,6},{6,4},{8,10},{10,8},{12,14},{14,12},{16,18},{18,... | collective-permute-start | bytes 688136 | tf_op jit(solution)/shard_map/ppermute | solution.py:582
  37.8 1.7 %collective-permute-start.9 = (bf16[4,224,128]{2,1,0:T(8,128)(2,1)}, bf16[4,224,128]{2,1,0:T(8,128)(2,1)S(1)}, u32[]{:S(2)}, u32[]{:S(2)}) collective-permute-start(bf16[4,224,128]{2,1,0:T(8,128)(2,1)} %core_pack.3), channel_id=1, source_target_pairs={{0,2},{2,0},{4,6},{6,4},{8,10},{10,8},{12,14},{14,12},{16,18},{18,... | collective-permute-start | bytes 688136 | tf_op jit(solution)/shard_map/ppermute | solution.py:582

commit v11 on v10

--- a/solution.py
+++ b/solution.py
@@ -70,6 +70,18 @@
     @property
     def side_rows(self):
         return self.groups * self.edges
+
+    @property
+    def sets(self):
+        return self.maps // 8
+
+    @property
+    def rest(self):
+        return self.maps % 8
+
+    @property
+    def pitch(self):
+        return up(self.width + 24, 2) + 1
 
     @property
     def chips(self):
@@ -246,8 +258,11 @@
     ).astype(F32).astype(BF16)
     margin = 8 + halo
     for index in range(count):
-        field_ref[index, :16, :] = jnp.zeros((16, cols), F32)
-        field_ref[index, width + 8 :, :] = jnp.zeros((16, cols), F32)
+        origin = index * plan.pitch
+        field_ref[origin : origin + margin, :] = jnp.zeros((margin, cols), F32)
+        field_ref[origin + margin + width : origin + plan.pitch, :] = jnp.zeros(
+            (plan.pitch - margin - width, cols), F32
+        )
         for b in range(tiles):
             shift = lax.rem(b - me + tiles, tiles)
             other = recv_ref[
@@ -256,7 +271,7 @@
             own = maps_ref[index, b * cols : (b + 1) * cols, :]
             mirror = across(eye, jnp.where(shift == 0, own, other))
             column = turned_ref[b * cols : (b + 1) * cols, index : index + 1]
-            field_ref[index, margin + b * cols : margin + (b + 1) * cols, :] = (
+            field_ref[origin + margin + b * cols : origin + margin + (b + 1) * cols, :] = (
                 own.astype(F32) + mirror - column * mine[index : index + 1]
             )
 
@@ -294,11 +309,18 @@
     spare = plan.block_rows - plan.lead - plan.half_rows
     for step, out_ref in zip(step_order(plan), out_refs):
         first = partner(chip, step, plan.chips) * 2 * plan.band
-        groups = [
-            field_ref[k, pl.ds(pl.multiple_of(first + 8 + 8 * group, 8), 8), :]
-            for group in range(2 * plan.lone + plan.shared)
-            for k in range(count)
-        ]
+
+        def section(begin, size):
+            found = [
+                field_ref[pl.ds(8 * k * plan.pitch + first + 8 + begin + r, 8, stride=plan.pitch), :]
+                for r in range(size)
+                for k in range(plan.sets)
+            ]
+            for k in range(8 * plan.sets, count):
+                found.append(field_ref[pl.ds(k * plan.pitch + first + 8 + begin, size), :])
+            return found
+
+        lone, shared = 8 * plan.lone, 8 * plan.shared
         sides = []
         for core in range(2):
             side = jnp.zeros((plan.side_rows, cols), F32)
@@ -307,8 +329,8 @@
                 moved = pltpu.roll(stacks[slot], amount, 1)[:, :cols]
                 side = jnp.where((lane >= slot * rows) & (lane < (slot + 1) * rows), moved, side)
             sides.append(side)
-        lone = plan.lone * count
-        pieces = groups[:lone] + sides[:1] + groups[lone:] + sides[1:]
+        pieces = section(0, lone) + sides[:1] + section(lone, shared)
+        pieces += section(lone + shared, lone) + sides[1:]
         if spare:
             pieces.append(jnp.zeros((spare, cols), F32))
         out_ref[...] = jnp.concatenate(pieces, axis=0).astype(BF16)
@@ -353,26 +375,38 @@
     own_refs, swap_refs = refs[:chips], refs[chips : chips + len(order)]
     refs = refs[chips + len(order) :]
     proj_ref, side_ref, kernel_ref, vector_ref, mask_ref, spots_ref, out_ref = refs[:7]
-    maps_ref, sides_ref, field_ref, stream_ref, hidden_ref, taps_ref, logit_ref = refs[7:]
+    maps_ref, others_ref, sides_ref, field_ref, stream_ref, hidden_ref, taps_ref, logit_ref = refs[7:]
     count, cols, rows, halo = plan.maps, plan.cols, plan.rows, plan.halo
     heads, feat, chunk, stride = plan.heads, plan.feat, plan.chunk, plan.stride
     head = lax.axis_index("head")
     chip, core = head // 2, head % 2
-    group = plan.group_rows
+    lone, shared = 8 * plan.lone, 8 * plan.shared
+    wide = 8 * plan.sets
+
+    def rows_of(sections):
+        sets, others = [], []
+        for begin, size in sections:
+            sets += [begin + r * wide for r in range(size)]
+            others += [begin + size * wide + r for r in range(0, size, 8)]
+        return sets, others, [size for _, size in sections for _ in range(0, size, 8)]
+
+    early = rows_of([(0, lone), (plan.lead, shared)])
+    late = rows_of([(0, shared), (shared * count, lone)])
 
     def spread(block, source):
-        for k in range(plan.lone + plan.shared):
-            value = block[k * group : (k + 1) * group]
-            if k >= plan.lone:
-                late = block[plan.side_rows + k * group : plan.side_rows + (k + 1) * group]
-                value = jnp.where(core == 0, late, value)
-            place = pl.multiple_of((k * heads + source) * group, 8)
-            maps_ref[pl.ds(place, group), :] = value
-        side = jnp.where(
-            core == 0,
-            block[plan.lone * group : plan.lead],
-            block[plan.half_rows - plan.side_rows : plan.half_rows],
-        )
+        def pick(a, b, size):
+            if a == b:
+                return block[a : a + size]
+            return jnp.where(core == 0, block[a : a + size], block[b : b + size])
+
+        for r, (a, b) in enumerate(zip(early[0], late[0])):
+            place = pl.multiple_of(source * wide, 8) + r * heads * wide
+            maps_ref[pl.ds(pl.multiple_of(place, 8), wide), :] = pick(a, b, wide)
+        for k, (a, b, m, n) in enumerate(zip(early[1], late[1], early[2], late[2])):
+            for j in range(plan.rest):
+                place = (source * plan.rest + j) * rows + 8 * k
+                others_ref[pl.ds(pl.multiple_of(place, 8), 8), :] = pick(a + j * m, b + j * n, 8)
+        side = pick(lone * count, plan.half_rows - plan.side_rows, plan.side_rows)
         place = pl.multiple_of(source * plan.side_rows, 8)
         sides_ref[pl.ds(place, plan.side_rows), :] = side
 
@@ -410,12 +444,13 @@
     spot = lax.broadcasted_iota(jnp.int32, (feat, cols), 1)
     per = 2
     for r in range(0, rows, per):
-        blocks = [
-            maps_ref[
-                pl.ds((r + k) // 8 * heads * group + (r + k) % 8, heads * count, stride=8), :
-            ].astype(BF16)
-            for k in range(per)
-        ]
+        blocks = []
+        for k in range(per):
+            block = maps_ref[(r + k) * heads * wide : (r + k + 1) * heads * wide, :]
+            if plan.rest:
+                others = others_ref[pl.ds(r + k, heads * plan.rest, stride=rows), :]
+                block = jnp.concatenate([block, others], axis=0)
+            blocks.append(block.astype(BF16))
         pair = dot(weight, jnp.concatenate(blocks, axis=1)) + bias
         for k in range(per):
             begin = plan.start + (r + k) * stride + halo
@@ -437,14 +472,14 @@
     for n in range(plan.convs):
         source = hidden_ref if n % 2 else stream_ref
         low = (plan.start + (n + 1) * stride) // LANES * LANES
-        steps = -(-(plan.start + (rows - n - 1) * stride - low + LANES) // chunk)
+        steps = -(-(plan.start + (rows - n - 1) * stride - n - 1 - low) // chunk)
         offsets = vector_ref[:, n + 1 : n + 2]
 
-        def multiply(base):
+        def multiply(base, size):
             window = jnp.concatenate(
-                [shifted(source, everything, base, d * stride, chunk) for d in (-1, 0, 1)], axis=0
+                [shifted(source, everything, base, d * stride, size) for d in (-1, 0, 1)], axis=0
             )
-            taps_ref[:, lanes(base, chunk)] = dot(kernel_ref[n], window)
+            taps_ref[:, lanes(base, size)] = dot(kernel_ref[n], window)
 
         def finish(base):
             here = lanes(base, chunk)
@@ -464,15 +499,16 @@
             readout = vector_ref[:, plan.convs + 1 : plan.convs + 2]
             logit_ref[0:1, here] = jnp.sum(value.astype(F32) * readout, axis=0, keepdims=True)
 
-        multiply(low)
+        multiply(low, chunk + LANES)
 
         def advance(i, carry):
             base = low + i * chunk
-            finish(base - LANES)
-            multiply(base + chunk)
+            finish(base)
+            multiply(base + chunk + LANES, chunk)
             return carry
 
-        lax.fori_loop(0, steps, advance, 0)
+        lax.fori_loop(0, steps - 1, advance, 0)
+        finish(low + (steps - 1) * chunk)
 
     for r in range(plan.band):
         begin = plan.start + (r + halo) * stride + halo
@@ -480,12 +516,12 @@
         out_ref[r : r + 1, :] = shifted(logit_ref, slice(0, 1), low, begin - low, cols)
 
 
-def call(kernel, name, args, outs, scratch=()):
+def call(kernel, name, args, outs, scratch=(), held_out=True):
     held = sum(math.prod(x.shape) * jnp.dtype(x.dtype).itemsize for x in [*args, *outs, *scratch])
     vmem = pl.BlockSpec(memory_space=pltpu.VMEM)
     return pl.pallas_call(
         kernel,
-        out_shape=list(outs),
+        out_shape=[pltpu.VMEM(x.shape, x.dtype) if held_out else x for x in outs],
         in_specs=[vmem] * len(args),
         out_specs=[vmem] * len(outs),
         scratch_shapes=list(scratch),
@@ -555,13 +591,19 @@
         spots.append(functools.reduce(jnp.logical_or, hit).astype(BF16))
     spots = jnp.stack(spots)
 
+    by_map = proj_weight.reshape(feat, heads, maps)
+    sets = by_map[:, :, : 8 * plan.sets].reshape(feat, -1)
+    others = by_map[:, :, 8 * plan.sets :].reshape(feat, -1)
+    map_weight = jnp.concatenate([sets, others], axis=1)
+    weights = (map_weight, side_weight, kernels, vectors, mask, spots)
+    received, weights = lax.optimization_barrier((received, weights))
     chips = plan.chips
     blocks = call(
         functools.partial(correct_pack, plan),
         "correct_pack",
         [attention, received, sums, edge],
         [array(BF16, plan.block_rows, cols)] * chips,
-        [pltpu.VMEM((maps, width + 24, cols), F32), pltpu.VMEM((width, LANES), F32)],
+        [pltpu.VMEM((maps * plan.pitch, cols), F32), pltpu.VMEM((width, LANES), F32)],
     )
     arrived = {}
     for step, block in zip(step_order(plan), blocks):
@@ -569,8 +611,6 @@
         arrived[step] = lax.ppermute(block, "head", pairs) if step else block
     far, near = far_near(plan)
     order = [far, near + [0]]
-    weights = (proj_weight, side_weight, kernels, vectors, mask, spots)
-    arrived[0], weights = lax.optimization_barrier((arrived[0], weights))
     swapped = []
     for steps in order:
         (packed,) = call(
@@ -587,7 +627,8 @@
         [*arrived.values(), *swapped, *weights],
         [array(F32, plan.band, cols)],
         [
-            pltpu.VMEM((heads * maps * plan.rows, cols), F32),
+            pltpu.VMEM((heads * 8 * plan.sets * plan.rows, cols), F32),
+            pltpu.VMEM((heads * max(plan.rest, 1) * plan.rows, cols), F32),
             pltpu.VMEM((heads * plan.side_rows, cols), F32),
             pltpu.VMEM((feat, plan.lanes), F32),
             pltpu.VMEM((feat, plan.lanes), BF16),
@@ -595,6 +636,7 @@
             pltpu.VMEM((3 * feat, plan.lanes), F32),
             pltpu.VMEM((8, plan.lanes), F32),
         ],
+        held_out=False,
     )
     return logits
 

time: 49.4 us -> 48.2 us (0.976)
  local copies, waits for them, and re-layouts: 1.49 us -> 5.77 us
  waiting for transfers between devices: 12.8 us -> 9.6 us
  Pallas kernels: 13.5 us -> 10.8 us
    pallas_call x6, Pallas kernels: 13.5 us -> 10.8 us  [call(): pl.pallas_call(kernel, out_shape=[pltpu.VMEM(x.shape, x.dtype) if held_ou...]
    ppermute x1, waiting for transfers between devices: 6.96 us -> 4.87 us  [on_device(): lax.ppermute(payload[s - 1], 'tile', [(i, (i + s) % tiles) for i in range...]
    ppermute x2, waiting for transfers between devices: 1.59 us -> 0.01 us  [on_device(): lax.ppermute(packed, 'head', [(i, i ^ 1) for i in range(heads)])]
    unnamed x20 -> x25, local copies, waits for them, and re-layouts: 1.21 us -> 2.8 us
    optimization_barrier x1, local copies, waits for them, and re-layouts: 0.09 us -> 1.47 us  [on_device(): received, weights = lax.optimization_barrier((received, weights))]
    transpose x1, local copies, waits for them, and re-layouts: 0.03 us -> 0.65 us  [on_device(): side_weight = side_weight.transpose(0, 3, 1, 2).reshape(feat, -1)]
    broadcast_in_dim x1, local copies, waits for them, and re-layouts: 0.02 us -> 0.62 us  [on_device(): mask = mask.astype(F32)[None]]
  transfers between devices with their start and end apart: 10 -> 10, of which waited for: 5 -> 4; matrix products, arithmetic and copies ran while one was open for 4% -> 10% of each run, Pallas kernels for 2% -> 1%
where the time goes in v11:
time: 48.2 us; the launch traced here: 47.8 us
  starting transfers between devices  19.8 us (41%)
  Pallas kernels  10.8 us (22%)
  waiting for transfers between devices  9.6 us (20%)
  local copies, waits for them, and re-layouts  5.77 us (12%)
  other arithmetic  1.57 us (3%)
    ppermute x7, starting transfers between devices, on_device(): arrived[step] = lax.ppermute(block, 'head', pairs) if step else block  16.7 us
    pallas_call x6, Pallas kernels, call(): pl.pallas_call(kernel, out_shape=[pltpu.VMEM(x.shape, x.dtype) if held_ou...  10.8 us
    ppermute x1, waiting for transfers between devices, on_device(): lax.ppermute(payload[s - 1], 'tile', [(i, (i + s) % tiles) for i in range...  4.87 us
    ppermute x7, waiting for transfers between devices, on_device(): arrived[step] = lax.ppermute(block, 'head', pairs) if step else block  4.72 us
    ppermute x1, starting transfers between devices, on_device(): lax.ppermute(payload[s - 1], 'tile', [(i, (i + s) % tiles) for i in range...  2.97 us
    unnamed x25, local copies, waits for them, and re-layouts  2.8 us
    convert_element_type x1, other arithmetic, on_device(): spots.append(functools.reduce(jnp.logical_or, hit).astype(BF16))  1.54 us
    optimization_barrier x1, local copies, waits for them, and re-layouts, on_device(): received, weights = lax.optimization_barrier((received, weights))  1.47 us
  transfers between devices with their start and end apart: 10, of which 4 were waited for; matrix products, arithmetic and copies ran while one was open for 10% of the time, Pallas kernels for 1%

profile of v11, /device:TPU:0, one launch (start us, length us, event | category | flops | bytes accessed | tf_op | source)
XLA Modules:
  0.0 47.8 jit_solution(1565514502094576399)
XLA Ops:
  0.0 1.1 %copy-done = bf16[9,256,128]{2,1,0:T(8,128)(2,1)S(1)} copy-done((bf16[9,256,128]{2,1,0:T(8,128)(2,1)S(1)}, bf16[9,256,128]{2,1,0:T(8,128)(2,1)}, u32[]{:S(2)}) %copy-start) | copy-done | bytes 589848
  1.1 1.2 %mirror_pack.1 = (bf16[1,1376,128]{2,1,0:T(8,128)(2,1)}, f32[16,256]{1,0:T(8,128)S(1)}, f32[40,128]{1,0:T(8,128)S(1)}) custom-call(bf16[9,256,128]{2,1,0:T(8,128)(2,1)S(1)} %copy-done), custom_call_target="tpu_custom_call" | custom-call | tf_op jit(solution)/shard_map/mirror_pack/pallas_call | solution.py:522
  2.3 3.0 %collective-permute-start = (bf16[1376,128]{1,0:T(8,128)(2,1)}, bf16[1376,128]{1,0:T(8,128)(2,1)S(1)}, u32[]{:S(2)}, u32[]{:S(2)}) collective-permute-start(bf16[1376,128]{1,0:T(8,128)(2,1)} %bitcast), channel_id=1, source_target_pairs={{0,1},{1,0},{2,3},{3,2},{4,5},{5,4},{6,7},{7,6},{8,9},{9,8},{10,11... | collective-permute-start | bytes 1056776 | tf_op jit(solution)/shard_map/ppermute | solution.py:557
  5.3 1.5 %fusion.1.refs_15_ = bf16[1,128,5376]{2,1,0:T(8,128)(2,1)S(1)} fusion(s32[128]{0:T(128)} %constant.34.clone, s32[128]{0:T(128)} %constant.33.clone), kind=kLoop, calls=%fused_computation.3 | loop fusion | flops 2752512 | bytes 1377280 | tf_op jit(solution)/shard_map/convert_element_type | solution.py:591
  6.9 0.1 copy.32
  7.1 0.6 %reshape.87.refs_14_ = f32[1,5376]{1,0:T(1,128)} reshape(f32[5376]{0:T(1024)S(1)} %fusion.5) | data formatting | bytes 43008 | tf_op jit(solution)/shard_map/broadcast_in_dim | solution.py:580
  7.7 0.1 copy.37
  7.8 0.1 copy.39
  7.9 0.1 copy.34
  8.0 0.6 %copy.36 = bf16[64,5,16,2]{0,3,2,1:T(2,128)(2,1)} copy(bf16[64,5,16,2]{0,2,1,3:T(8,128)(2,1)S(1)} %bitcast.20) | data formatting | bytes 40960 | tf_op jit(solution)/shard_map/transpose | solution.py:566
  8.7 0.1 kernel_pack.1.refs_12_
  8.8 4.9 %collective-permute-done = bf16[1376,128]{1,0:T(8,128)(2,1)S(1)} collective-permute-done((bf16[1376,128]{1,0:T(8,128)(2,1)}, bf16[1376,128]{1,0:T(8,128)(2,1)S(1)}, u32[]{:S(2)}, u32[]{:S(2)}) %collective-permute-start) | collective-permute-done | bytes 352288 | tf_op jit(solution)/shard_map/ppermute | solution.py:557
  13.7 1.1 %correct_pack.1 = (bf16[384,128]{1,0:T(8,128)(2,1)S(1)}, bf16[384,128]{1,0:T(8,128)(2,1)S(1)}, bf16[384,128]{1,0:T(8,128)(2,1)S(1)}, bf16[384,128]{1,0:T(8,128)(...) custom-call(bf16[9,256,128]{2,1,0:T(8,128)(2,1)S(1)} %copy-done.1, ...), custom_call_target="tpu_custom_call" | custom-call | tf_op jit(solution)/shard_map/correct_pack/pallas_call | solution.py:522
  14.8 4.8 %collective-permute-start.1 = (bf16[384,128]{1,0:T(8,128)(2,1)S(1)}, bf16[384,128]{1,0:T(8,128)(2,1)S(1)}, u32[]{:S(2)}, u32[]{:S(2)}) collective-permute-start(bf16[384,128]{1,0:T(8,128)(2,1)S(1)} %get-tuple-element.27), channel_id=1, source_target_pairs={{0,28},{2,30},{4,24},{6,26},{8,20},{10,22},{12,16},{14,18},{16,12}... | collective-permute-start | bytes 294920 | tf_op jit(solution)/shard_map/ppermute | solution.py:611
  19.6 0.2 collective-permute-start.2
  19.8 0.8 %collective-permute-start.3 = (bf16[384,128]{1,0:T(8,128)(2,1)S(1)}, bf16[384,128]{1,0:T(8,128)(2,1)S(1)}, u32[]{:S(2)}, u32[]{:S(2)}) collective-permute-start(bf16[384,128]{1,0:T(8,128)(2,1)S(1)} %get-tuple-element.29), channel_id=1, source_target_pairs={{0,20},{2,22},{4,16},{6,18},{8,28},{10,30},{12,24},{14,26},{16,4},... | collective-permute-start | bytes 294920 | tf_op jit(solution)/shard_map/ppermute | solution.py:611
  20.6 2.0 %collective-permute-start.4 = (bf16[384,128]{1,0:T(8,128)(2,1)S(1)}, bf16[384,128]{1,0:T(8,128)(2,1)S(1)}, u32[]{:S(2)}, u32[]{:S(2)}) collective-permute-start(bf16[384,128]{1,0:T(8,128)(2,1)S(1)} %get-tuple-element.30), channel_id=1, source_target_pairs={{0,16},{2,18},{4,20},{6,22},{8,24},{10,26},{12,28},{14,30},{16,0},... | collective-permute-start | bytes 294920 | tf_op jit(solution)/shard_map/ppermute | solution.py:611
  22.6 2.3 %collective-permute-start.5 = (bf16[384,128]{1,0:T(8,128)(2,1)S(1)}, bf16[384,128]{1,0:T(8,128)(2,1)S(1)}, u32[]{:S(2)}, u32[]{:S(2)}) collective-permute-start(bf16[384,128]{1,0:T(8,128)(2,1)S(1)} %get-tuple-element.31), channel_id=1, source_target_pairs={{0,12},{2,14},{4,8},{6,10},{8,4},{10,6},{12,0},{14,2},{16,28},{18,... | collective-permute-start | bytes 294920 | tf_op jit(solution)/shard_map/ppermute | solution.py:611
  24.9 5.6 %collective-permute-start.6 = (bf16[384,128]{1,0:T(8,128)(2,1)S(1)}, bf16[384,128]{1,0:T(8,128)(2,1)S(1)}, u32[]{:S(2)}, u32[]{:S(2)}) collective-permute-start(bf16[384,128]{1,0:T(8,128)(2,1)S(1)} %get-tuple-element.32), channel_id=1, source_target_pairs={{0,8},{2,10},{4,12},{6,14},{8,0},{10,2},{12,4},{14,6},{16,24},{18,... | collective-permute-start | bytes 294920 | tf_op jit(solution)/shard_map/ppermute | solution.py:611
  30.5 0.0 collective-permute-done.2.refs_1_
  30.5 1.0 %collective-permute-start.7 = (bf16[384,128]{1,0:T(8,128)(2,1)S(1)}, bf16[384,128]{1,0:T(8,128)(2,1)S(1)}, u32[]{:S(2)}, u32[]{:S(2)}) collective-permute-start(bf16[384,128]{1,0:T(8,128)(2,1)S(1)} %get-tuple-element.33), channel_id=1, source_target_pairs={{0,4},{2,6},{4,0},{6,2},{8,12},{10,14},{12,8},{14,10},{16,20},{18,... | collective-permute-start | bytes 294920 | tf_op jit(solution)/shard_map/ppermute | solution.py:611
  31.5 2.9 %collective-permute-done.3.refs_2_ = bf16[384,128]{1,0:T(8,128)(2,1)S(1)} collective-permute-done((bf16[384,128]{1,0:T(8,128)(2,1)S(1)}, bf16[384,128]{1,0:T(8,128)(2,1)S(1)}, u32[]{:S(2)}, u32[]{:S(2)}) %collective-permute-start.3) | collective-permute-done | bytes 98336 | tf_op jit(solution)/shard_map/ppermute | solution.py:611
  34.4 1.1 %collective-permute-done.4.refs_3_ = bf16[384,128]{1,0:T(8,128)(2,1)S(1)} collective-permute-done((bf16[384,128]{1,0:T(8,128)(2,1)S(1)}, bf16[384,128]{1,0:T(8,128)(2,1)S(1)}, u32[]{:S(2)}, u32[]{:S(2)}) %collective-permute-start.4) | collective-permute-done | bytes 98336 | tf_op jit(solution)/shard_map/ppermute | solution.py:611
  35.5 0.1 core_pack.2
  35.6 0.1 collective-permute-start.8
  35.7 0.7 %collective-permute-done.6.refs_1_.refs_5_ = bf16[384,128]{1,0:T(8,128)(2,1)S(1)} collective-permute-done((bf16[384,128]{1,0:T(8,128)(2,1)S(1)}, bf16[384,128]{1,0:T(8,128)(2,1)S(1)}, u32[]{:S(2)}, u32[]{:S(2)}) %collective-permute-start.6) | collective-permute-done | bytes 98336 | tf_op jit(solution)/shard_map/ppermute | solution.py:611
  36.4 0.1 core_pack.3
  36.4 0.1 collective-permute-start.9
  36.5 1.5 %copy.38.refs_11_ = bf16[64,160]{1,0:T(8,128)(2,1)} copy(bf16[64,160]{0,1:T(8,128)(2,1)} %bitcast.19) | data formatting | bytes 40960 | tf_op jit(solution)/shard_map/optimization_barrier | solution.py:599
  38.0 0.8 %copy-done.3 = bf16[64,160]{1,0:T(8,128)(2,1)S(1)} copy-done((bf16[64,160]{1,0:T(8,128)(2,1)S(1)}, bf16[64,160]{1,0:T(8,128)(2,1)}, u32[]{:S(2)}) %copy-start.3) | copy-done | bytes 20504
  38.8 0.7 %copy-done.4 = f32[1,5376]{1,0:T(1,128)S(1)} copy-done((f32[1,5376]{1,0:T(1,128)S(1)}, f32[1,5376]{1,0:T(1,128)}, u32[]{:S(2)}) %copy-start.4) | copy-done | bytes 21528
  39.5 8.3 %stack.6 = f32[16,128]{1,0:T(8,128)} custom-call(bf16[384,128]{1,0:T(8,128)(2,1)S(1)} %collective-permute-done.1.refs_0_, bf16[384,128]{1,0:T(8,128)(2,1)S(1)} %collective-permute-done.2.refs_1_, bf16[384,128]{1,0:T(8,128)(2,1)S(1)} %collective-permute-done.3.refs_2_, bf16[384,128]{1,0:T(8,128)(2,1)S(1)} %collective-permute-done.4.refs_3_, ...), custom_call_target="tpu_custom_call" | custom-call | tf_op jit(solution)/shard_map/stack/pallas_call | solution.py:522
  (32 shorter events, 0.2 us)
Async XLA Ops:
  0.0 1.1 %copy-start = (bf16[9,256,128]{2,1,0:T(8,128)(2,1)S(1)}, bf16[9,256,128]{2,1,0:T(8,128)(2,1)}, u32[]{:S(2)}) copy-start(bf16[9,256,128]{2,1,0:T(8,128)(2,1)} %maps_ref.3) | copy-start | bytes 1769476
  1.1 5.7 %copy-start.6 = (s32[5376]{0:T(1024)S(1)}, s32[5376]{0:T(1024)}, u32[]{:S(2)}) copy-start(s32[5376]{0:T(1024)} %constant.32.clone) | copy-start | bytes 64516
  1.1 5.8 %copy-start.7 = (s32[5376]{0:T(1024)S(1)}, s32[5376]{0:T(1024)}, u32[]{:S(2)}) copy-start(s32[5376]{0:T(1024)} %constant.31.clone) | copy-start | bytes 64516
  1.1 5.8 %copy-start.8 = (f32[2,2,64]{2,1,0:T(2,128)S(1)}, f32[2,2,64]{2,1,0:T(2,128)}, u32[]{:S(2)}) copy-start(f32[2,2,64]{2,1,0:T(2,128)} %param.14) | copy-start | bytes 3076
  1.1 5.8 %copy-start.9 = (f32[64]{0:T(128)S(1)}, f32[64]{0:T(128)}, u32[]{:S(2)}) copy-start(f32[64]{0:T(128)} %param.15) | copy-start | bytes 772
  1.1 5.8 %copy-start.10 = (f32[64]{0:T(128)S(1)}, f32[64]{0:T(128)}, u32[]{:S(2)}) copy-start(f32[64]{0:T(128)} %param.12) | copy-start | bytes 772
  1.1 5.8 %copy-start.5 = (bf16[64,144]{1,0:T(8,128)(2,1)S(1)}, bf16[64,144]{1,0:T(8,128)(2,1)}, u32[]{:S(2)}) copy-start(bf16[64,144]{1,0:T(8,128)(2,1)} %param.11) | copy-start | bytes 55300
  1.1 7.6 %copy-start.2 = (bf16[2,2,64,64,3,3]{3,2,5,4,1,0:T(8,128)(2,1)S(1)}, bf16[2,2,64,64,3,3]{3,2,5,4,1,0:T(8,128)(2,1)}, u32[]{:S(2)}) copy-start(bf16[2,2,64,64,3,3]{3,2,5,4,1,0:T(8,128)(2,1)} %param.13) | copy-start | bytes 884740
  2.3 11.4 %collective-permute-start = (bf16[1376,128]{1,0:T(8,128)(2,1)}, bf16[1376,128]{1,0:T(8,128)(2,1)S(1)}, u32[]{:S(2)}, u32[]{:S(2)}) collective-permute-start(bf16[1376,128]{1,0:T(8,128)(2,1)} %bitcast), channel_id=1, source_target_pairs={{0,1},{1,0},{2,3},{3,2},{4,5},{5,4},{6,7},{7,6},{8,9},{9,8},{10,11... | collective-permute-start | bytes 1056776 | tf_op jit(solution)/shard_map/ppermute | solution.py:557
  5.3 8.4 %copy-start.1 = (bf16[9,256,128]{2,1,0:T(8,128)(2,1)S(1)}, bf16[9,256,128]{2,1,0:T(8,128)(2,1)}, u32[]{:S(2)}) copy-start(bf16[9,256,128]{2,1,0:T(8,128)(2,1)} %maps_ref.3) | copy-start | bytes 1769476
  14.8 10.1 %collective-permute-start.1 = (bf16[384,128]{1,0:T(8,128)(2,1)S(1)}, bf16[384,128]{1,0:T(8,128)(2,1)S(1)}, u32[]{:S(2)}, u32[]{:S(2)}) collective-permute-start(bf16[384,128]{1,0:T(8,128)(2,1)S(1)} %get-tuple-element.27), channel_id=1, source_target_pairs={{0,28},{2,30},{4,24},{6,26},{8,20},{10,22},{12,16},{14,18},{16,12}... | collective-permute-start | bytes 294920 | tf_op jit(solution)/shard_map/ppermute | solution.py:611
  19.6 10.9 %collective-permute-start.2 = (bf16[384,128]{1,0:T(8,128)(2,1)S(1)}, bf16[384,128]{1,0:T(8,128)(2,1)S(1)}, u32[]{:S(2)}, u32[]{:S(2)}) collective-permute-start(bf16[384,128]{1,0:T(8,128)(2,1)S(1)} %get-tuple-element.28), channel_id=1, source_target_pairs={{0,24},{2,26},{4,28},{6,30},{8,16},{10,18},{12,20},{14,22},{16,8},... | collective-permute-start | bytes 294920 | tf_op jit(solution)/shard_map/ppermute | solution.py:611
  19.8 14.6 %collective-permute-start.3 = (bf16[384,128]{1,0:T(8,128)(2,1)S(1)}, bf16[384,128]{1,0:T(8,128)(2,1)S(1)}, u32[]{:S(2)}, u32[]{:S(2)}) collective-permute-start(bf16[384,128]{1,0:T(8,128)(2,1)S(1)} %get-tuple-element.29), channel_id=1, source_target_pairs={{0,20},{2,22},{4,16},{6,18},{8,28},{10,30},{12,24},{14,26},{16,4},... | collective-permute-start | bytes 294920 | tf_op jit(solution)/shard_map/ppermute | solution.py:611
  20.6 14.9 %collective-permute-start.4 = (bf16[384,128]{1,0:T(8,128)(2,1)S(1)}, bf16[384,128]{1,0:T(8,128)(2,1)S(1)}, u32[]{:S(2)}, u32[]{:S(2)}) collective-permute-start(bf16[384,128]{1,0:T(8,128)(2,1)S(1)} %get-tuple-element.30), channel_id=1, source_target_pairs={{0,16},{2,18},{4,20},{6,22},{8,24},{10,26},{12,28},{14,30},{16,0},... | collective-permute-start | bytes 294920 | tf_op jit(solution)/shard_map/ppermute | solution.py:611
  22.6 13.1 %collective-permute-start.5 = (bf16[384,128]{1,0:T(8,128)(2,1)S(1)}, bf16[384,128]{1,0:T(8,128)(2,1)S(1)}, u32[]{:S(2)}, u32[]{:S(2)}) collective-permute-start(bf16[384,128]{1,0:T(8,128)(2,1)S(1)} %get-tuple-element.31), channel_id=1, source_target_pairs={{0,12},{2,14},{4,8},{6,10},{8,4},{10,6},{12,0},{14,2},{16,28},{18,... | collective-permute-start | bytes 294920 | tf_op jit(solution)/shard_map/ppermute | solution.py:611
  24.9 11.5 %collective-permute-start.6 = (bf16[384,128]{1,0:T(8,128)(2,1)S(1)}, bf16[384,128]{1,0:T(8,128)(2,1)S(1)}, u32[]{:S(2)}, u32[]{:S(2)}) collective-permute-start(bf16[384,128]{1,0:T(8,128)(2,1)S(1)} %get-tuple-element.32), channel_id=1, source_target_pairs={{0,8},{2,10},{4,12},{6,14},{8,0},{10,2},{12,4},{14,6},{16,24},{18,... | collective-permute-start | bytes 294920 | tf_op jit(solution)/shard_map/ppermute | solution.py:611
  30.5 5.9 %collective-permute-start.7 = (bf16[384,128]{1,0:T(8,128)(2,1)S(1)}, bf16[384,128]{1,0:T(8,128)(2,1)S(1)}, u32[]{:S(2)}, u32[]{:S(2)}) collective-permute-start(bf16[384,128]{1,0:T(8,128)(2,1)S(1)} %get-tuple-element.33), channel_id=1, source_target_pairs={{0,4},{2,6},{4,0},{6,2},{8,12},{10,14},{12,8},{14,10},{16,20},{18,... | collective-permute-start | bytes 294920 | tf_op jit(solution)/shard_map/ppermute | solution.py:611
  35.6 2.4 %collective-permute-start.8 = (bf16[4,224,128]{2,1,0:T(8,128)(2,1)S(1)}, bf16[4,224,128]{2,1,0:T(8,128)(2,1)S(1)}, u32[]{:S(2)}, u32[]{:S(2)}) collective-permute-start(bf16[4,224,128]{2,1,0:T(8,128)(2,1)S(1)} %core_pack.2), channel_id=1, source_target_pairs={{0,2},{2,0},{4,6},{6,4},{8,10},{10,8},{12,14},{14,12},{16,18},{18,... | collective-permute-start | bytes 688136 | tf_op jit(solution)/shard_map/ppermute | solution.py:622
  36.4 1.6 %collective-permute-start.9 = (bf16[4,224,128]{2,1,0:T(8,128)(2,1)S(1)}, bf16[4,224,128]{2,1,0:T(8,128)(2,1)S(1)}, u32[]{:S(2)}, u32[]{:S(2)}) collective-permute-start(bf16[4,224,128]{2,1,0:T(8,128)(2,1)S(1)} %core_pack.3), channel_id=1, source_target_pairs={{0,2},{2,0},{4,6},{6,4},{8,10},{10,8},{12,14},{14,12},{16,18},{18,... | collective-permute-start | bytes 688136 | tf_op jit(solution)/shard_map/ppermute | solution.py:622
  38.0 0.8 %copy-start.3 = (bf16[64,160]{1,0:T(8,128)(2,1)S(1)}, bf16[64,160]{1,0:T(8,128)(2,1)}, u32[]{:S(2)}) copy-start(bf16[64,160]{1,0:T(8,128)(2,1)} %copy.38.refs_11_) | copy-start | bytes 61444
  38.8 0.7 %copy-start.4 = (f32[1,5376]{1,0:T(1,128)S(1)}, f32[1,5376]{1,0:T(1,128)}, u32[]{:S(2)}) copy-start(f32[1,5376]{1,0:T(1,128)} %reshape.87.refs_14_) | copy-start | bytes 64516

commit v12 on v11

--- a/solution.py
+++ b/solution.py
@@ -343,7 +343,9 @@
         out_ref[k] = half(plan, block_ref[...].astype(F32), other).astype(BF16)
 
 
-def kernel_pack(blocks_ref, out_ref):
+def weight_pack(blocks_ref, proj_ref, set_ref, slot_ref, out_ref, map_ref, side_ref):
+    map_ref[...] = dot(proj_ref[...], set_ref[...]).astype(BF16)
+    side_ref[...] = dot(proj_ref[...], slot_ref[...]).astype(BF16)
     layers, convs, height, breadth = blocks_ref.shape[:4]
     for b in range(layers):
         for m in range(convs):
@@ -375,7 +377,7 @@
     own_refs, swap_refs = refs[:chips], refs[chips : chips + len(order)]
     refs = refs[chips + len(order) :]
     proj_ref, side_ref, kernel_ref, vector_ref, mask_ref, spots_ref, out_ref = refs[:7]
-    maps_ref, others_ref, sides_ref, field_ref, stream_ref, hidden_ref, taps_ref, logit_ref = refs[7:]
+    maps_ref, others_ref, sides_ref, stream_ref, hidden_ref, taps_ref, logit_ref = refs[7:]
     count, cols, rows, halo = plan.maps, plan.cols, plan.rows, plan.halo
     heads, feat, chunk, stride = plan.heads, plan.feat, plan.chunk, plan.stride
     head = lax.axis_index("head")
@@ -433,41 +435,48 @@
         stacked = jnp.concatenate(parts, axis=0).astype(BF16)
         placed.append((dot(side_ref[...], stacked) + bias).astype(BF16))
 
-    chunks = -(-(rows * stride + plan.start) // chunk)
-    for i in range(chunks):
-        here = slice(i * chunk, (i + 1) * chunk)
-        field_ref[:, here] = sum(
-            dot(columns, spots_ref[k, :, here]) for k, columns in enumerate(placed)
-        )
+    edge = sum(dot(columns, spots_ref[k]) for k, columns in enumerate(placed))
 
     weight = proj_ref[...]
-    spot = lax.broadcasted_iota(jnp.int32, (feat, cols), 1)
-    per = 2
-    for r in range(0, rows, per):
-        blocks = []
-        for k in range(per):
-            block = maps_ref[(r + k) * heads * wide : (r + k + 1) * heads * wide, :]
+    spot = lax.broadcasted_iota(jnp.int32, (feat, LANES), 1)
+    spans = []
+
+    def compose(tile):
+        low, value = tile * LANES, None
+        for begin, size, source, lead in spans:
+            left, right = max(begin, low), min(begin + size, low + LANES)
+            if left >= right:
+                continue
+            k = (lead + low) // LANES
+            piece = source[:, k * LANES : (k + 1) * LANES]
+            if value is None:
+                value = piece
+            else:
+                value = jnp.where((spot >= left - low) & (spot < right - low), piece, value)
+        here = slice(low, low + LANES)
+        stream_ref[:, here] = jnp.where(mask_ref[:, here] > 0, value, 0.0).astype(BF16)
+
+    done = plan.start // LANES
+    for r in range(rows + 1):
+        begin = plan.start + r * stride - halo
+        between = LANES + r * 2 * halo - halo
+        spans.append((begin, 2 * halo, edge, between - begin))
+        if r < rows:
+            block = maps_ref[r * heads * wide : (r + 1) * heads * wide, :]
             if plan.rest:
-                others = others_ref[pl.ds(r + k, heads * plan.rest, stride=rows), :]
+                others = others_ref[pl.ds(r, heads * plan.rest, stride=rows), :]
                 block = jnp.concatenate([block, others], axis=0)
-            blocks.append(block.astype(BF16))
-        pair = dot(weight, jnp.concatenate(blocks, axis=1)) + bias
-        for k in range(per):
-            begin = plan.start + (r + k) * stride + halo
-            low, rest = begin // LANES * LANES, begin % LANES
-            value = pair[:, k * cols : (k + 1) * cols]
-            if rest == 0:
-                field_ref[:, low : low + cols] += value
-                continue
-            value = pltpu.roll(value, rest, 1)
-            field_ref[:, low : low + cols] += jnp.where(spot >= rest, value, 0.0)
-            field_ref[:, low + cols : low + 2 * cols] += jnp.where(spot < rest, value, 0.0)
-
-    for i in range(chunks):
-        here = slice(i * chunk, (i + 1) * chunk)
-        stream_ref[:, here] = jnp.where(mask_ref[:, here] > 0, field_ref[:, here], 0.0).astype(BF16)
-
-    chunk = 2 * chunk
+            value = dot(weight, block.astype(BF16)) + bias
+            begin = plan.start + r * stride + halo
+            turn = begin % LANES
+            value = jnp.concatenate([value, jnp.zeros((feat, LANES), F32)], axis=1)
+            spans.append((begin, cols, pltpu.roll(value, turn, 1), turn - begin))
+        full = (plan.start + (r + 1) * stride - halo) // LANES if r < rows else done + 1
+        while done < full:
+            compose(done)
+            done += 1
+        spans = [span for span in spans if span[0] + span[1] > done * LANES]
+
     everything = slice(None)
     for n in range(plan.convs):
         source = hidden_ref if n % 2 else stream_ref
@@ -560,15 +569,29 @@
     )
 
     stride, start = plan.stride, plan.start
-    side_weight = proj_weight.reshape(feat, heads, maps)
-    side_weight = jnp.pad(side_weight, ((0, 0), (0, 0), (0, plan.groups * plan.slots - maps)))
-    side_weight = side_weight.reshape(feat, heads, plan.groups, plan.slots)
-    side_weight = side_weight.transpose(0, 3, 1, 2).reshape(feat, -1)
-    (kernels,) = call(
-        kernel_pack,
-        "kernel_pack",
-        [conv_weight.transpose(0, 1, 4, 5, 2, 3)],
-        [array(BF16, plan.convs, 3 * feat, 3 * feat)],
+    source, index = np.divmod(np.arange(heads * maps), maps)
+    wide = 8 * plan.sets
+    by_set = np.where(
+        index < wide, source * wide + index, heads * wide + source * plan.rest + index - wide
+    )
+    group, slot = np.divmod(index, plan.slots)
+    by_slot = (slot * heads + source) * plan.groups + group
+    picks = [
+        jnp.asarray(place[:, None] == np.arange(size)[None], BF16)
+        for place, size in (
+            (by_set, heads * maps),
+            (by_slot, plan.slots * heads * plan.groups),
+        )
+    ]
+    kernels, map_weight, side_weight = call(
+        weight_pack,
+        "weight_pack",
+        [conv_weight.transpose(0, 1, 4, 5, 2, 3), proj_weight, *picks],
+        [
+            array(BF16, plan.convs, 3 * feat, 3 * feat),
+            array(BF16, feat, picks[0].shape[1]),
+            array(BF16, feat, picks[1].shape[1]),
+        ],
     )
     vectors = jnp.concatenate(
         [proj_bias[None], conv_bias.reshape(-1, feat), out_weight[None]], axis=0
@@ -581,22 +604,21 @@
 
     key = np.arange(cols)
     member, line = key // plan.rows, key % plan.rows
+    lane = np.arange(up(LANES + (plan.rows + 1) * 2 * plan.halo, LANES))
     spots = []
     for first in range(0, plan.edges, plan.slots):
         column = first + member
         fits = (member < plan.slots) & (column < plan.edges)
-        places = (0, plan.halo + cols) if plan.sides == 1 else (np.where(column < plan.halo, 0, cols),)
-        target = [np.where(fits, start + line * stride + column + p, -1) for p in places]
-        hit = [jnp.arange(plan.lanes)[None] == jnp.asarray(p, jnp.int32)[:, None] for p in target]
-        spots.append(functools.reduce(jnp.logical_or, hit).astype(BF16))
-    spots = jnp.stack(spots)
-
-    by_map = proj_weight.reshape(feat, heads, maps)
-    sets = by_map[:, :, : 8 * plan.sets].reshape(feat, -1)
-    others = by_map[:, :, 8 * plan.sets :].reshape(feat, -1)
-    map_weight = jnp.concatenate([sets, others], axis=1)
-    weights = (map_weight, side_weight, kernels, vectors, mask, spots)
-    received, weights = lax.optimization_barrier((received, weights))
+        left = LANES + line * 2 * plan.halo + column
+        right = left + plan.halo
+        if plan.sides == 1:
+            places = [left, right]
+        else:
+            places = [np.where(column < plan.halo, left, right - plan.halo)]
+        hit = [np.where(fits, place, -1)[:, None] == lane[None] for place in places]
+        spots.append(functools.reduce(np.logical_or, hit))
+    spots = jnp.asarray(np.stack(spots), BF16)
+
     chips = plan.chips
     blocks = call(
         functools.partial(correct_pack, plan),
@@ -611,6 +633,7 @@
         arrived[step] = lax.ppermute(block, "head", pairs) if step else block
     far, near = far_near(plan)
     order = [far, near + [0]]
+    weights = (map_weight, side_weight, kernels, vectors, mask, spots)
     swapped = []
     for steps in order:
         (packed,) = call(
@@ -619,6 +642,8 @@
             [arrived[k] for k in steps],
             [array(BF16, len(steps), plan.half_rows, cols)],
         )
+        if steps is far:
+            packed, weights = lax.optimization_barrier((packed, weights))
         swapped.append(lax.ppermute(packed, "head", [(i, i ^ 1) for i in range(heads)]))
 
     (logits,) = call(
@@ -630,7 +655,6 @@
             pltpu.VMEM((heads * 8 * plan.sets * plan.rows, cols), F32),
             pltpu.VMEM((heads * max(plan.rest, 1) * plan.rows, cols), F32),
             pltpu.VMEM((heads * plan.side_rows, cols), F32),
-            pltpu.VMEM((feat, plan.lanes), F32),
             pltpu.VMEM((feat, plan.lanes), BF16),
             pltpu.VMEM((feat, plan.lanes), BF16),
             pltpu.VMEM((3 * feat, plan.lanes), F32),

time: 48.2 us -> 50.3 us (1.044)
  waiting for transfers between devices: 9.6 us -> 20.2 us
  starting transfers between devices: 19.8 us -> 14.5 us
  local copies, waits for them, and re-layouts: 5.77 us -> 1.23 us
  Pallas kernels: 10.8 us -> 14 us
  other arithmetic: 1.57 us -> 0.02 us
    ppermute x7, waiting for transfers between devices: 4.72 us -> 10.5 us  [on_device(): arrived[step] = lax.ppermute(block, 'head', pairs) if step else block]
    ppermute x7, starting transfers between devices: 16.7 us -> 11.4 us  [on_device(): arrived[step] = lax.ppermute(block, 'head', pairs) if step else block]
    ppermute x1, waiting for transfers between devices: 4.87 us -> 8.23 us  [on_device(): lax.ppermute(payload[s - 1], 'tile', [(i, (i + s) % tiles) for i in range...]
    pallas_call x6, Pallas kernels: 10.8 us -> 14 us  [call(): pl.pallas_call(kernel, out_shape=[pltpu.VMEM(x.shape, x.dtype) if held_ou...]
    unnamed x25 -> x24, local copies, waits for them, and re-layouts: 2.8 us -> 1.12 us
    convert_element_type x1 -> x0, other arithmetic: 1.54 us -> none  [on_device(): spots.append(functools.reduce(jnp.logical_or, hit).astype(BF16))]
    optimization_barrier x1 -> x0, local copies, waits for them, and re-layouts: 1.47 us -> none  [on_device(): received, weights = lax.optimization_barrier((received, weights))]
    ppermute x2, waiting for transfers between devices: 0.01 us -> 1.47 us  [on_device(): lax.ppermute(packed, 'head', [(i, i ^ 1) for i in range(heads)])]
  transfers between devices with their start and end apart: 10 -> 10, of which waited for: 4 -> 5; matrix products, arithmetic and copies ran while one was open for 10% -> 0% of each run, Pallas kernels for 1% -> 1%
where the time goes in v12:
time: 50.3 us; the launch traced here: 50.2 us
  waiting for transfers between devices  20.2 us (40%)
  starting transfers between devices  14.5 us (29%)
  Pallas kernels  14 us (28%)
  local copies, waits for them, and re-layouts  1.23 us (2%)
    pallas_call x6, Pallas kernels, call(): pl.pallas_call(kernel, out_shape=[pltpu.VMEM(x.shape, x.dtype) if held_ou...  14 us
    ppermute x7, starting transfers between devices, on_device(): arrived[step] = lax.ppermute(block, 'head', pairs) if step else block  11.4 us
    ppermute x7, waiting for transfers between devices, on_device(): arrived[step] = lax.ppermute(block, 'head', pairs) if step else block  10.5 us
    ppermute x1, waiting for transfers between devices, on_device(): lax.ppermute(payload[s - 1], 'tile', [(i, (i + s) % tiles) for i in range...  8.23 us
    ppermute x1, starting transfers between devices, on_device(): lax.ppermute(payload[s - 1], 'tile', [(i, (i + s) % tiles) for i in range...  3.03 us
    ppermute x2, waiting for transfers between devices, on_device(): lax.ppermute(packed, 'head', [(i, i ^ 1) for i in range(heads)])  1.47 us
    unnamed x24, local copies, waits for them, and re-layouts  1.12 us
  transfers between devices with their start and end apart: 10, of which 5 were waited for; matrix products, arithmetic and copies ran while one was open for 0% of the time, Pallas kernels for 1%

profile of v12, /device:TPU:0, one launch (start us, length us, event | category | flops | bytes accessed | tf_op | source)
XLA Modules:
  0.0 50.2 jit_solution(3785925627944671241)
XLA Ops:
  0.0 1.1 %copy-done = bf16[9,256,128]{2,1,0:T(8,128)(2,1)S(1)} copy-done((bf16[9,256,128]{2,1,0:T(8,128)(2,1)S(1)}, bf16[9,256,128]{2,1,0:T(8,128)(2,1)}, u32[]{:S(2)}) %copy-start) | copy-done | bytes 589848
  1.1 0.5 mirror_pack.1
  1.5 3.0 %collective-permute-start = (bf16[1376,128]{1,0:T(8,128)(2,1)S(1)}, bf16[1376,128]{1,0:T(8,128)(2,1)S(1)}, u32[]{:S(2)}, u32[]{:S(2)}) collective-permute-start(bf16[1376,128]{1,0:T(8,128)(2,1)S(1)} %bitcast.10), channel_id=1, source_target_pairs={{0,1},{1,0},{2,3},{3,2},{4,5},{5,4},{6,7},{7,6},{8,9},{9,8},{10,11... | collective-permute-start | bytes 1056776 | tf_op jit(solution)/shard_map/ppermute | solution.py:566
  4.6 8.2 %collective-permute-done = bf16[1376,128]{1,0:T(8,128)(2,1)S(1)} collective-permute-done((bf16[1376,128]{1,0:T(8,128)(2,1)S(1)}, bf16[1376,128]{1,0:T(8,128)(2,1)S(1)}, u32[]{:S(2)}, u32[]{:S(2)}) %collective-permute-start) | collective-permute-done | bytes 352288 | tf_op jit(solution)/shard_map/ppermute | solution.py:566
  12.8 0.0 copy-start.10
  12.8 0.0 copy-start.11
  12.8 1.1 %correct_pack.1 = (bf16[384,128]{1,0:T(8,128)(2,1)S(1)}, bf16[384,128]{1,0:T(8,128)(2,1)S(1)}, bf16[384,128]{1,0:T(8,128)(2,1)S(1)}, bf16[384,128]{1,0:T(8,128)(...) custom-call(bf16[9,256,128]{2,1,0:T(8,128)(2,1)S(1)} %copy-done.1, ...), custom_call_target="tpu_custom_call" | custom-call | tf_op jit(solution)/shard_map/correct_pack/pallas_call | solution.py:531
  13.9 2.8 %collective-permute-start.5 = (bf16[384,128]{1,0:T(8,128)(2,1)S(1)}, bf16[384,128]{1,0:T(8,128)(2,1)S(1)}, u32[]{:S(2)}, u32[]{:S(2)}) collective-permute-start(bf16[384,128]{1,0:T(8,128)(2,1)S(1)} %get-tuple-element.33), channel_id=1, source_target_pairs={{0,12},{2,14},{4,8},{6,10},{8,4},{10,6},{12,0},{14,2},{16,28},{18,... | collective-permute-start | bytes 294920 | tf_op jit(solution)/shard_map/ppermute | solution.py:633
  16.7 0.5 collective-permute-start.6
  17.2 0.0 copy-start.6
  17.2 3.6 %collective-permute-start.1 = (bf16[384,128]{1,0:T(8,128)(2,1)S(1)}, bf16[384,128]{1,0:T(8,128)(2,1)S(1)}, u32[]{:S(2)}, u32[]{:S(2)}) collective-permute-start(bf16[384,128]{1,0:T(8,128)(2,1)S(1)} %get-tuple-element.29), channel_id=1, source_target_pairs={{0,28},{2,30},{4,24},{6,26},{8,20},{10,22},{12,16},{14,18},{16,12}... | collective-permute-start | bytes 294920 | tf_op jit(solution)/shard_map/ppermute | solution.py:633
  20.8 0.1 collective-permute-start.2
  20.9 1.8 %collective-permute-start.3 = (bf16[384,128]{1,0:T(8,128)(2,1)S(1)}, bf16[384,128]{1,0:T(8,128)(2,1)S(1)}, u32[]{:S(2)}, u32[]{:S(2)}) collective-permute-start(bf16[384,128]{1,0:T(8,128)(2,1)S(1)} %get-tuple-element.31), channel_id=1, source_target_pairs={{0,20},{2,22},{4,16},{6,18},{8,28},{10,30},{12,24},{14,26},{16,4},... | collective-permute-start | bytes 294920 | tf_op jit(solution)/shard_map/ppermute | solution.py:633
  22.8 0.0 collective-permute-done.5.refs_0_.refs_4_
  22.8 2.1 %collective-permute-start.4 = (bf16[384,128]{1,0:T(8,128)(2,1)S(1)}, bf16[384,128]{1,0:T(8,128)(2,1)S(1)}, u32[]{:S(2)}, u32[]{:S(2)}) collective-permute-start(bf16[384,128]{1,0:T(8,128)(2,1)S(1)} %get-tuple-element.32), channel_id=1, source_target_pairs={{0,16},{2,18},{4,20},{6,22},{8,24},{10,26},{12,28},{14,30},{16,0},... | collective-permute-start | bytes 294920 | tf_op jit(solution)/shard_map/ppermute | solution.py:633
  24.9 0.0 collective-permute-done.6.refs_1_.refs_5_
  24.9 0.4 collective-permute-start.7
  25.4 0.1 copy.18
  25.5 0.2 weight_pack.1
  25.6 3.9 %collective-permute-done.7.refs_2_.refs_6_ = bf16[384,128]{1,0:T(8,128)(2,1)S(1)} collective-permute-done((bf16[384,128]{1,0:T(8,128)(2,1)S(1)}, bf16[384,128]{1,0:T(8,128)(2,1)S(1)}, u32[]{:S(2)}, u32[]{:S(2)}) %collective-permute-start.7) | collective-permute-done | bytes 98336 | tf_op jit(solution)/shard_map/ppermute | solution.py:633
  29.5 0.1 core_pack.3
  29.6 0.0 copy-start.3
  29.6 0.1 collective-permute-start.9
  29.7 0.0 collective-permute-done.1.refs_0_
  29.7 0.0 collective-permute-done.2.refs_1_
  29.7 6.5 %collective-permute-done.3.refs_2_ = bf16[384,128]{1,0:T(8,128)(2,1)S(1)} collective-permute-done((bf16[384,128]{1,0:T(8,128)(2,1)S(1)}, bf16[384,128]{1,0:T(8,128)(2,1)S(1)}, u32[]{:S(2)}, u32[]{:S(2)}) %collective-permute-start.3) | collective-permute-done | bytes 98336 | tf_op jit(solution)/shard_map/ppermute | solution.py:633
  36.2 0.2 collective-permute-done.4.refs_3_
  36.4 0.1 core_pack.2
  36.4 0.1 collective-permute-start.8
  36.5 0.0 collective-permute-done.9.refs_9_
  36.5 1.5 %collective-permute-done.8.refs_8_ = bf16[4,224,128]{2,1,0:T(8,128)(2,1)S(1)} collective-permute-done((bf16[4,224,128]{2,1,0:T(8,128)(2,1)S(1)}, bf16[4,224,128]{2,1,0:T(8,128)(2,1)S(1)}, u32[]{:S(2)}, u32[]{:S(2)}) %collective-permute-start.8) | collective-permute-done | bytes 229408 | tf_op jit(solution)/shard_map/ppermute | solution.py:647
  38.0 12.2 %stack.5 = f32[16,128]{1,0:T(8,128)} custom-call(bf16[384,128]{1,0:T(8,128)(2,1)S(1)} %collective-permute-done.1.refs_0_, bf16[384,128]{1,0:T(8,128)(2,1)S(1)} %collective-permute-done.2.refs_1_, bf16[384,128]{1,0:T(8,128)(2,1)S(1)} %collective-permute-done.3.refs_2_, bf16[384,128]{1,0:T(8,128)(2,1)S(1)} %collective-permute-done.4.refs_3_, ...), custom_call_target="tpu_custom_call" | custom-call | tf_op jit(solution)/shard_map/stack/pallas_call | solution.py:531
  (22 shorter events, 0.1 us)
Async XLA Ops:
  0.0 1.1 %copy-start = (bf16[9,256,128]{2,1,0:T(8,128)(2,1)S(1)}, bf16[9,256,128]{2,1,0:T(8,128)(2,1)}, u32[]{:S(2)}) copy-start(bf16[9,256,128]{2,1,0:T(8,128)(2,1)} %maps_ref.3) | copy-start | bytes 1769476
  1.1 11.7 %copy-start.1 = (bf16[9,256,128]{2,1,0:T(8,128)(2,1)S(1)}, bf16[9,256,128]{2,1,0:T(8,128)(2,1)}, u32[]{:S(2)}) copy-start(bf16[9,256,128]{2,1,0:T(8,128)(2,1)} %maps_ref.3) | copy-start | bytes 1769476
  1.5 11.3 %collective-permute-start = (bf16[1376,128]{1,0:T(8,128)(2,1)S(1)}, bf16[1376,128]{1,0:T(8,128)(2,1)S(1)}, u32[]{:S(2)}, u32[]{:S(2)}) collective-permute-start(bf16[1376,128]{1,0:T(8,128)(2,1)S(1)} %bitcast.10), channel_id=1, source_target_pairs={{0,1},{1,0},{2,3},{3,2},{4,5},{5,4},{6,7},{7,6},{8,9},{9,8},{10,11... | collective-permute-start | bytes 1056776 | tf_op jit(solution)/shard_map/ppermute | solution.py:566
  4.6 20.9 %copy-start.2 = (bf16[2,2,64,64,3,3]{3,2,5,4,1,0:T(8,128)(2,1)S(1)}, bf16[2,2,64,64,3,3]{3,2,5,4,1,0:T(8,128)(2,1)}, u32[]{:S(2)}) copy-start(bf16[2,2,64,64,3,3]{3,2,5,4,1,0:T(8,128)(2,1)} %param.14) | copy-start | bytes 884740
  12.8 4.3 %copy-start.7 = (s32[5376]{0:T(1024)S(1)}, s32[5376]{0:T(1024)}, u32[]{:S(2)}) copy-start(s32[5376]{0:T(1024)} %constant.33.clone) | copy-start | bytes 64516
  12.8 4.3 %copy-start.8 = (s32[5376]{0:T(1024)S(1)}, s32[5376]{0:T(1024)}, u32[]{:S(2)}) copy-start(s32[5376]{0:T(1024)} %constant.32.clone) | copy-start | bytes 64516
  12.8 12.5 %copy-start.9 = (f32[2,2,64]{2,1,0:T(2,128)S(1)}, f32[2,2,64]{2,1,0:T(2,128)}, u32[]{:S(2)}) copy-start(f32[2,2,64]{2,1,0:T(2,128)} %param.15) | copy-start | bytes 3076
  12.8 12.5 %copy-start.10 = (f32[64]{0:T(128)S(1)}, f32[64]{0:T(128)}, u32[]{:S(2)}) copy-start(f32[64]{0:T(128)} %param.16) | copy-start | bytes 772
  12.8 12.5 %copy-start.11 = (f32[64]{0:T(128)S(1)}, f32[64]{0:T(128)}, u32[]{:S(2)}) copy-start(f32[64]{0:T(128)} %param.13) | copy-start | bytes 772
  13.9 8.9 %collective-permute-start.5 = (bf16[384,128]{1,0:T(8,128)(2,1)S(1)}, bf16[384,128]{1,0:T(8,128)(2,1)S(1)}, u32[]{:S(2)}, u32[]{:S(2)}) collective-permute-start(bf16[384,128]{1,0:T(8,128)(2,1)S(1)} %get-tuple-element.33), channel_id=1, source_target_pairs={{0,12},{2,14},{4,8},{6,10},{8,4},{10,6},{12,0},{14,2},{16,28},{18,... | collective-permute-start | bytes 294920 | tf_op jit(solution)/shard_map/ppermute | solution.py:633
  16.7 8.8 %copy-start.4 = (bf16[144,160]{1,0:T(8,128)(2,1)S(1)}, bf16[144,160]{1,0:T(8,128)(2,1)}, u32[]{:S(2)}) copy-start(bf16[144,160]{1,0:T(8,128)(2,1)} %constant.31.clone.slot_ref) | copy-start | bytes 138244
  16.7 8.8 %copy-start.5 = (bf16[144,144]{1,0:T(8,128)(2,1)S(1)}, bf16[144,144]{1,0:T(8,128)(2,1)}, u32[]{:S(2)}) copy-start(bf16[144,144]{1,0:T(8,128)(2,1)} %constant.30.clone.set_ref) | copy-start | bytes 124420
  16.7 8.2 %collective-permute-start.6 = (bf16[384,128]{1,0:T(8,128)(2,1)S(1)}, bf16[384,128]{1,0:T(8,128)(2,1)S(1)}, u32[]{:S(2)}, u32[]{:S(2)}) collective-permute-start(bf16[384,128]{1,0:T(8,128)(2,1)S(1)} %get-tuple-element.34), channel_id=1, source_target_pairs={{0,8},{2,10},{4,12},{6,14},{8,0},{10,2},{12,4},{14,6},{16,24},{18,... | collective-permute-start | bytes 294920 | tf_op jit(solution)/shard_map/ppermute | solution.py:633
  17.2 8.3 %copy-start.6 = (bf16[64,144]{1,0:T(8,128)(2,1)S(1)}, bf16[64,144]{1,0:T(8,128)(2,1)}, u32[]{:S(2)}) copy-start(bf16[64,144]{1,0:T(8,128)(2,1)} %proj_ref.1) | copy-start | bytes 55300
  17.2 12.5 %collective-permute-start.1 = (bf16[384,128]{1,0:T(8,128)(2,1)S(1)}, bf16[384,128]{1,0:T(8,128)(2,1)S(1)}, u32[]{:S(2)}, u32[]{:S(2)}) collective-permute-start(bf16[384,128]{1,0:T(8,128)(2,1)S(1)} %get-tuple-element.29), channel_id=1, source_target_pairs={{0,28},{2,30},{4,24},{6,26},{8,20},{10,22},{12,16},{14,18},{16,12}... | collective-permute-start | bytes 294920 | tf_op jit(solution)/shard_map/ppermute | solution.py:633
  20.8 8.9 %collective-permute-start.2 = (bf16[384,128]{1,0:T(8,128)(2,1)S(1)}, bf16[384,128]{1,0:T(8,128)(2,1)S(1)}, u32[]{:S(2)}, u32[]{:S(2)}) collective-permute-start(bf16[384,128]{1,0:T(8,128)(2,1)S(1)} %get-tuple-element.30), channel_id=1, source_target_pairs={{0,24},{2,26},{4,28},{6,30},{8,16},{10,18},{12,20},{14,22},{16,8},... | collective-permute-start | bytes 294920 | tf_op jit(solution)/shard_map/ppermute | solution.py:633
  20.9 15.2 %collective-permute-start.3 = (bf16[384,128]{1,0:T(8,128)(2,1)S(1)}, bf16[384,128]{1,0:T(8,128)(2,1)S(1)}, u32[]{:S(2)}, u32[]{:S(2)}) collective-permute-start(bf16[384,128]{1,0:T(8,128)(2,1)S(1)} %get-tuple-element.31), channel_id=1, source_target_pairs={{0,20},{2,22},{4,16},{6,18},{8,28},{10,30},{12,24},{14,26},{16,4},... | collective-permute-start | bytes 294920 | tf_op jit(solution)/shard_map/ppermute | solution.py:633
  22.8 13.6 %collective-permute-start.4 = (bf16[384,128]{1,0:T(8,128)(2,1)S(1)}, bf16[384,128]{1,0:T(8,128)(2,1)S(1)}, u32[]{:S(2)}, u32[]{:S(2)}) collective-permute-start(bf16[384,128]{1,0:T(8,128)(2,1)S(1)} %get-tuple-element.32), channel_id=1, source_target_pairs={{0,16},{2,18},{4,20},{6,22},{8,24},{10,26},{12,28},{14,30},{16,0},... | collective-permute-start | bytes 294920 | tf_op jit(solution)/shard_map/ppermute | solution.py:633
  24.9 4.6 %collective-permute-start.7 = (bf16[384,128]{1,0:T(8,128)(2,1)S(1)}, bf16[384,128]{1,0:T(8,128)(2,1)S(1)}, u32[]{:S(2)}, u32[]{:S(2)}) collective-permute-start(bf16[384,128]{1,0:T(8,128)(2,1)S(1)} %get-tuple-element.35), channel_id=1, source_target_pairs={{0,4},{2,6},{4,0},{6,2},{8,12},{10,14},{12,8},{14,10},{16,20},{18,... | collective-permute-start | bytes 294920 | tf_op jit(solution)/shard_map/ppermute | solution.py:633
  29.6 8.4 %copy-start.3 = (bf16[1,128,384]{2,1,0:T(8,128)(2,1)S(1)}, bf16[1,128,384]{2,1,0:T(8,128)(2,1)}, u32[]{:S(2)}) copy-start(bf16[1,128,384]{2,1,0:T(8,128)(2,1)} %constant.34.clone.refs_15_) | copy-start | bytes 294916
  29.6 6.9 %collective-permute-start.9 = (bf16[4,224,128]{2,1,0:T(8,128)(2,1)S(1)}, bf16[4,224,128]{2,1,0:T(8,128)(2,1)S(1)}, u32[]{:S(2)}, u32[]{:S(2)}) collective-permute-start(bf16[4,224,128]{2,1,0:T(8,128)(2,1)S(1)} %core_pack.3), channel_id=1, source_target_pairs={{0,2},{2,0},{4,6},{6,4},{8,10},{10,8},{12,14},{14,12},{16,18},{18,... | collective-permute-start | bytes 688136 | tf_op jit(solution)/shard_map/ppermute | solution.py:647
  36.4 1.6 %collective-permute-start.8 = (bf16[4,224,128]{2,1,0:T(8,128)(2,1)S(1)}, bf16[4,224,128]{2,1,0:T(8,128)(2,1)S(1)}, u32[]{:S(2)}, u32[]{:S(2)}) collective-permute-start(bf16[4,224,128]{2,1,0:T(8,128)(2,1)S(1)} %core_pack.2), channel_id=1, source_target_pairs={{0,2},{2,0},{4,6},{6,4},{8,10},{10,8},{12,14},{14,12},{16,18},{18,... | collective-permute-start | bytes 688136 | tf_op jit(solution)/shard_map/ppermute | solution.py:647

commit v13 on v12

--- a/solution.py
+++ b/solution.py
@@ -120,12 +120,16 @@
         return up(self.stride, LANES) - LANES
 
     @property
+    def batch(self):
+        return 8
+
+    @property
     def chunk(self):
-        return 256
+        return 1536
 
     @property
     def lanes(self):
-        return up(self.start + self.rows * self.stride, LANES) + 6 * self.chunk + 3 * LANES
+        return up(self.start + self.rows * self.stride, LANES) + 4 * self.halo * LANES
 
 
 def partner(mine, step, count, back=False):
@@ -379,7 +383,7 @@
     proj_ref, side_ref, kernel_ref, vector_ref, mask_ref, spots_ref, out_ref = refs[:7]
     maps_ref, others_ref, sides_ref, stream_ref, hidden_ref, taps_ref, logit_ref = refs[7:]
     count, cols, rows, halo = plan.maps, plan.cols, plan.rows, plan.halo
-    heads, feat, chunk, stride = plan.heads, plan.feat, plan.chunk, plan.stride
+    heads, feat, stride = plan.heads, plan.feat, plan.stride
     head = lax.axis_index("head")
     chip, core = head // 2, head % 2
     lone, shared = 8 * plan.lone, 8 * plan.shared
@@ -456,17 +460,25 @@
         here = slice(low, low + LANES)
         stream_ref[:, here] = jnp.where(mask_ref[:, here] > 0, value, 0.0).astype(BF16)
 
+    def gather(chosen):
+        blocks = []
+        for r in chosen:
+            block = maps_ref[r * heads * wide : (r + 1) * heads * wide, :]
+            if plan.rest:
+                others = others_ref[pl.ds(r, heads * plan.rest, stride=rows), :]
+                block = jnp.concatenate([block, others], axis=0)
+            blocks.append(block.astype(BF16))
+        return jnp.concatenate(blocks, axis=1)
+
     done = plan.start // LANES
     for r in range(rows + 1):
         begin = plan.start + r * stride - halo
         between = LANES + r * 2 * halo - halo
         spans.append((begin, 2 * halo, edge, between - begin))
         if r < rows:
-            block = maps_ref[r * heads * wide : (r + 1) * heads * wide, :]
-            if plan.rest:
-                others = others_ref[pl.ds(r, heads * plan.rest, stride=rows), :]
-                block = jnp.concatenate([block, others], axis=0)
-            value = dot(weight, block.astype(BF16)) + bias
+            if r % plan.batch == 0:
+                batch = dot(weight, gather(range(r, min(r + plan.batch, rows)))) + bias
+            value = batch[:, r % plan.batch * cols : (r % plan.batch + 1) * cols]
             begin = plan.start + r * stride + halo
             turn = begin % LANES
             value = jnp.concatenate([value, jnp.zeros((feat, LANES), F32)], axis=1)
@@ -481,7 +493,9 @@
     for n in range(plan.convs):
         source = hidden_ref if n % 2 else stream_ref
         low = (plan.start + (n + 1) * stride) // LANES * LANES
-        steps = -(-(plan.start + (rows - n - 1) * stride - n - 1 - low) // chunk)
+        span = plan.start + (rows - n - 1) * stride - n - 1 - low
+        steps = -(-span // plan.chunk)
+        size = up(-(-span // steps), LANES)
         offsets = vector_ref[:, n + 1 : n + 2]
 
         def multiply(base, size):
@@ -491,10 +505,10 @@
             taps_ref[:, lanes(base, size)] = dot(kernel_ref[n], window)
 
         def finish(base):
-            here = lanes(base, chunk)
+            here = lanes(base, size)
             value = taps_ref[feat : 2 * feat, here]
-            value = value + shifted(taps_ref, slice(0, feat), base, -1, chunk)
-            value = value + shifted(taps_ref, slice(2 * feat, 3 * feat), base, 1, chunk)
+            value = value + shifted(taps_ref, slice(0, feat), base, -1, size)
+            value = value + shifted(taps_ref, slice(2 * feat, 3 * feat), base, 1, size)
             value = value + offsets
             keep = mask_ref[:, here] > 0
             if n % 2 == 0:
@@ -508,16 +522,11 @@
             readout = vector_ref[:, plan.convs + 1 : plan.convs + 2]
             logit_ref[0:1, here] = jnp.sum(value.astype(F32) * readout, axis=0, keepdims=True)
 
-        multiply(low, chunk + LANES)
-
-        def advance(i, carry):
-            base = low + i * chunk
-            finish(base)
-            multiply(base + chunk + LANES, chunk)
-            return carry
-
-        lax.fori_loop(0, steps - 1, advance, 0)
-        finish(low + (steps - 1) * chunk)
+        multiply(low, size + LANES)
+        for i in range(steps):
+            if i + 1 < steps:
+                multiply(low + (i + 1) * size + LANES, size)
+            finish(low + i * size)
 
     for r in range(plan.band):
         begin = plan.start + (r + halo) * stride + halo

time: 50.3 us -> 42.8 us (0.85)
  Pallas kernels: 14 us -> 6.47 us
    pallas_call x6, Pallas kernels: 14 us -> 6.47 us  [call(): pl.pallas_call(kernel, out_shape=[pltpu.VMEM(x.shape, x.dtype) if held_ou...]
where the time goes in v13:
time: 42.8 us; the launch traced here: 42.6 us
  waiting for transfers between devices  20.2 us (47%)
  starting transfers between devices  14.5 us (34%)
  Pallas kernels  6.47 us (15%)
  local copies, waits for them, and re-layouts  1.23 us (3%)
    ppermute x7, starting transfers between devices, on_device(): arrived[step] = lax.ppermute(block, 'head', pairs) if step else block  11.4 us
    ppermute x7, waiting for transfers between devices, on_device(): arrived[step] = lax.ppermute(block, 'head', pairs) if step else block  10.5 us
    ppermute x1, waiting for transfers between devices, on_device(): lax.ppermute(payload[s - 1], 'tile', [(i, (i + s) % tiles) for i in range...  8.23 us
    pallas_call x6, Pallas kernels, call(): pl.pallas_call(kernel, out_shape=[pltpu.VMEM(x.shape, x.dtype) if held_ou...  6.47 us
    ppermute x1, starting transfers between devices, on_device(): lax.ppermute(payload[s - 1], 'tile', [(i, (i + s) % tiles) for i in range...  3.03 us
    ppermute x2, waiting for transfers between devices, on_device(): lax.ppermute(packed, 'head', [(i, i ^ 1) for i in range(heads)])  1.47 us
    unnamed x24, local copies, waits for them, and re-layouts  1.12 us
  transfers between devices with their start and end apart: 10, of which 5 were waited for; matrix products, arithmetic and copies ran while one was open for 0% of the time, Pallas kernels for 1%

profile of v13, /device:TPU:0, one launch (start us, length us, event | category | flops | bytes accessed | tf_op | source)
XLA Modules:
  0.0 42.6 jit_solution(2120381055512684061)
XLA Ops:
  0.0 1.1 %copy-done = bf16[9,256,128]{2,1,0:T(8,128)(2,1)S(1)} copy-done((bf16[9,256,128]{2,1,0:T(8,128)(2,1)S(1)}, bf16[9,256,128]{2,1,0:T(8,128)(2,1)}, u32[]{:S(2)}) %copy-start) | copy-done | bytes 589848
  1.1 0.5 %mirror_pack.1 = (bf16[1,1376,128]{2,1,0:T(8,128)(2,1)S(1)}, f32[16,256]{1,0:T(8,128)S(1)}, f32[40,128]{1,0:T(8,128)S(1)}) custom-call(bf16[9,256,128]{2,1,0:T(8,128)(2,1)S(1)} %copy-done), custom_call_target="tpu_custom_call" | custom-call | tf_op jit(solution)/shard_map/mirror_pack/pallas_call | solution.py:540
  1.5 3.0 %collective-permute-start = (bf16[1376,128]{1,0:T(8,128)(2,1)S(1)}, bf16[1376,128]{1,0:T(8,128)(2,1)S(1)}, u32[]{:S(2)}, u32[]{:S(2)}) collective-permute-start(bf16[1376,128]{1,0:T(8,128)(2,1)S(1)} %bitcast.10), channel_id=1, source_target_pairs={{0,1},{1,0},{2,3},{3,2},{4,5},{5,4},{6,7},{7,6},{8,9},{9,8},{10,11... | collective-permute-start | bytes 1056776 | tf_op jit(solution)/shard_map/ppermute | solution.py:575
  4.6 8.2 %collective-permute-done = bf16[1376,128]{1,0:T(8,128)(2,1)S(1)} collective-permute-done((bf16[1376,128]{1,0:T(8,128)(2,1)S(1)}, bf16[1376,128]{1,0:T(8,128)(2,1)S(1)}, u32[]{:S(2)}, u32[]{:S(2)}) %collective-permute-start) | collective-permute-done | bytes 352288 | tf_op jit(solution)/shard_map/ppermute | solution.py:575
  12.8 0.0 copy-start.10
  12.8 0.0 copy-start.11
  12.8 1.1 %correct_pack.1 = (bf16[384,128]{1,0:T(8,128)(2,1)S(1)}, bf16[384,128]{1,0:T(8,128)(2,1)S(1)}, bf16[384,128]{1,0:T(8,128)(2,1)S(1)}, bf16[384,128]{1,0:T(8,128)(...) custom-call(bf16[9,256,128]{2,1,0:T(8,128)(2,1)S(1)} %copy-done.1, ...), custom_call_target="tpu_custom_call" | custom-call | tf_op jit(solution)/shard_map/correct_pack/pallas_call | solution.py:540
  13.9 2.8 %collective-permute-start.5 = (bf16[384,128]{1,0:T(8,128)(2,1)S(1)}, bf16[384,128]{1,0:T(8,128)(2,1)S(1)}, u32[]{:S(2)}, u32[]{:S(2)}) collective-permute-start(bf16[384,128]{1,0:T(8,128)(2,1)S(1)} %get-tuple-element.33), channel_id=1, source_target_pairs={{0,12},{2,14},{4,8},{6,10},{8,4},{10,6},{12,0},{14,2},{16,28},{18,... | collective-permute-start | bytes 294920 | tf_op jit(solution)/shard_map/ppermute | solution.py:642
  16.7 0.5 %collective-permute-start.6 = (bf16[384,128]{1,0:T(8,128)(2,1)S(1)}, bf16[384,128]{1,0:T(8,128)(2,1)S(1)}, u32[]{:S(2)}, u32[]{:S(2)}) collective-permute-start(bf16[384,128]{1,0:T(8,128)(2,1)S(1)} %get-tuple-element.34), channel_id=1, source_target_pairs={{0,8},{2,10},{4,12},{6,14},{8,0},{10,2},{12,4},{14,6},{16,24},{18,... | collective-permute-start | bytes 294920 | tf_op jit(solution)/shard_map/ppermute | solution.py:642
  17.2 0.0 copy-start.6
  17.2 3.6 %collective-permute-start.1 = (bf16[384,128]{1,0:T(8,128)(2,1)S(1)}, bf16[384,128]{1,0:T(8,128)(2,1)S(1)}, u32[]{:S(2)}, u32[]{:S(2)}) collective-permute-start(bf16[384,128]{1,0:T(8,128)(2,1)S(1)} %get-tuple-element.29), channel_id=1, source_target_pairs={{0,28},{2,30},{4,24},{6,26},{8,20},{10,22},{12,16},{14,18},{16,12}... | collective-permute-start | bytes 294920 | tf_op jit(solution)/shard_map/ppermute | solution.py:642
  20.8 0.1 collective-permute-start.2
  20.9 1.8 %collective-permute-start.3 = (bf16[384,128]{1,0:T(8,128)(2,1)S(1)}, bf16[384,128]{1,0:T(8,128)(2,1)S(1)}, u32[]{:S(2)}, u32[]{:S(2)}) collective-permute-start(bf16[384,128]{1,0:T(8,128)(2,1)S(1)} %get-tuple-element.31), channel_id=1, source_target_pairs={{0,20},{2,22},{4,16},{6,18},{8,28},{10,30},{12,24},{14,26},{16,4},... | collective-permute-start | bytes 294920 | tf_op jit(solution)/shard_map/ppermute | solution.py:642
  22.8 0.0 collective-permute-done.5.refs_0_.refs_4_
  22.8 2.1 %collective-permute-start.4 = (bf16[384,128]{1,0:T(8,128)(2,1)S(1)}, bf16[384,128]{1,0:T(8,128)(2,1)S(1)}, u32[]{:S(2)}, u32[]{:S(2)}) collective-permute-start(bf16[384,128]{1,0:T(8,128)(2,1)S(1)} %get-tuple-element.32), channel_id=1, source_target_pairs={{0,16},{2,18},{4,20},{6,22},{8,24},{10,26},{12,28},{14,30},{16,0},... | collective-permute-start | bytes 294920 | tf_op jit(solution)/shard_map/ppermute | solution.py:642
  24.9 0.0 collective-permute-done.6.refs_1_.refs_5_
  24.9 0.4 collective-permute-start.7
  25.4 0.1 copy.18
  25.5 0.2 weight_pack.1
  25.6 3.9 %collective-permute-done.7.refs_2_.refs_6_ = bf16[384,128]{1,0:T(8,128)(2,1)S(1)} collective-permute-done((bf16[384,128]{1,0:T(8,128)(2,1)S(1)}, bf16[384,128]{1,0:T(8,128)(2,1)S(1)}, u32[]{:S(2)}, u32[]{:S(2)}) %collective-permute-start.7) | collective-permute-done | bytes 98336 | tf_op jit(solution)/shard_map/ppermute | solution.py:642
  29.5 0.1 core_pack.3
  29.6 0.0 copy-start.3
  29.6 0.1 collective-permute-start.9
  29.7 0.0 collective-permute-done.1.refs_0_
  29.7 0.0 collective-permute-done.2.refs_1_
  29.7 6.5 %collective-permute-done.3.refs_2_ = bf16[384,128]{1,0:T(8,128)(2,1)S(1)} collective-permute-done((bf16[384,128]{1,0:T(8,128)(2,1)S(1)}, bf16[384,128]{1,0:T(8,128)(2,1)S(1)}, u32[]{:S(2)}, u32[]{:S(2)}) %collective-permute-start.3) | collective-permute-done | bytes 98336 | tf_op jit(solution)/shard_map/ppermute | solution.py:642
  36.2 0.2 collective-permute-done.4.refs_3_
  36.4 0.1 core_pack.2
  36.4 0.1 collective-permute-start.8
  36.5 0.0 collective-permute-done.9.refs_9_
  36.5 1.5 %collective-permute-done.8.refs_8_ = bf16[4,224,128]{2,1,0:T(8,128)(2,1)S(1)} collective-permute-done((bf16[4,224,128]{2,1,0:T(8,128)(2,1)S(1)}, bf16[4,224,128]{2,1,0:T(8,128)(2,1)S(1)}, u32[]{:S(2)}, u32[]{:S(2)}) %collective-permute-start.8) | collective-permute-done | bytes 229408 | tf_op jit(solution)/shard_map/ppermute | solution.py:656
  38.0 4.7 %stack.5 = f32[16,128]{1,0:T(8,128)} custom-call(bf16[384,128]{1,0:T(8,128)(2,1)S(1)} %collective-permute-done.1.refs_0_, bf16[384,128]{1,0:T(8,128)(2,1)S(1)} %collective-permute-done.2.refs_1_, bf16[384,128]{1,0:T(8,128)(2,1)S(1)} %collective-permute-done.3.refs_2_, bf16[384,128]{1,0:T(8,128)(2,1)S(1)} %collective-permute-done.4.refs_3_, ...), custom_call_target="tpu_custom_call" | custom-call | tf_op jit(solution)/shard_map/stack/pallas_call | solution.py:540
  (22 shorter events, 0.1 us)
Async XLA Ops:
  0.0 1.1 %copy-start = (bf16[9,256,128]{2,1,0:T(8,128)(2,1)S(1)}, bf16[9,256,128]{2,1,0:T(8,128)(2,1)}, u32[]{:S(2)}) copy-start(bf16[9,256,128]{2,1,0:T(8,128)(2,1)} %maps_ref.3) | copy-start | bytes 1769476
  1.1 11.7 %copy-start.1 = (bf16[9,256,128]{2,1,0:T(8,128)(2,1)S(1)}, bf16[9,256,128]{2,1,0:T(8,128)(2,1)}, u32[]{:S(2)}) copy-start(bf16[9,256,128]{2,1,0:T(8,128)(2,1)} %maps_ref.3) | copy-start | bytes 1769476
  1.5 11.3 %collective-permute-start = (bf16[1376,128]{1,0:T(8,128)(2,1)S(1)}, bf16[1376,128]{1,0:T(8,128)(2,1)S(1)}, u32[]{:S(2)}, u32[]{:S(2)}) collective-permute-start(bf16[1376,128]{1,0:T(8,128)(2,1)S(1)} %bitcast.10), channel_id=1, source_target_pairs={{0,1},{1,0},{2,3},{3,2},{4,5},{5,4},{6,7},{7,6},{8,9},{9,8},{10,11... | collective-permute-start | bytes 1056776 | tf_op jit(solution)/shard_map/ppermute | solution.py:575
  4.6 20.9 %copy-start.2 = (bf16[2,2,64,64,3,3]{3,2,5,4,1,0:T(8,128)(2,1)S(1)}, bf16[2,2,64,64,3,3]{3,2,5,4,1,0:T(8,128)(2,1)}, u32[]{:S(2)}) copy-start(bf16[2,2,64,64,3,3]{3,2,5,4,1,0:T(8,128)(2,1)} %param.14) | copy-start | bytes 884740
  12.8 4.3 %copy-start.7 = (s32[5504]{0:T(1024)S(1)}, s32[5504]{0:T(1024)}, u32[]{:S(2)}) copy-start(s32[5504]{0:T(1024)} %constant.33.clone) | copy-start | bytes 66052
  12.8 4.3 %copy-start.8 = (s32[5504]{0:T(1024)S(1)}, s32[5504]{0:T(1024)}, u32[]{:S(2)}) copy-start(s32[5504]{0:T(1024)} %constant.32.clone) | copy-start | bytes 66052
  12.8 12.5 %copy-start.9 = (f32[2,2,64]{2,1,0:T(2,128)S(1)}, f32[2,2,64]{2,1,0:T(2,128)}, u32[]{:S(2)}) copy-start(f32[2,2,64]{2,1,0:T(2,128)} %param.15) | copy-start | bytes 3076
  12.8 12.5 %copy-start.10 = (f32[64]{0:T(128)S(1)}, f32[64]{0:T(128)}, u32[]{:S(2)}) copy-start(f32[64]{0:T(128)} %param.16) | copy-start | bytes 772
  12.8 12.5 %copy-start.11 = (f32[64]{0:T(128)S(1)}, f32[64]{0:T(128)}, u32[]{:S(2)}) copy-start(f32[64]{0:T(128)} %param.13) | copy-start | bytes 772
  13.9 8.9 %collective-permute-start.5 = (bf16[384,128]{1,0:T(8,128)(2,1)S(1)}, bf16[384,128]{1,0:T(8,128)(2,1)S(1)}, u32[]{:S(2)}, u32[]{:S(2)}) collective-permute-start(bf16[384,128]{1,0:T(8,128)(2,1)S(1)} %get-tuple-element.33), channel_id=1, source_target_pairs={{0,12},{2,14},{4,8},{6,10},{8,4},{10,6},{12,0},{14,2},{16,28},{18,... | collective-permute-start | bytes 294920 | tf_op jit(solution)/shard_map/ppermute | solution.py:642
  16.7 8.8 %copy-start.4 = (bf16[144,160]{1,0:T(8,128)(2,1)S(1)}, bf16[144,160]{1,0:T(8,128)(2,1)}, u32[]{:S(2)}) copy-start(bf16[144,160]{1,0:T(8,128)(2,1)} %constant.31.clone.slot_ref) | copy-start | bytes 138244
  16.7 8.8 %copy-start.5 = (bf16[144,144]{1,0:T(8,128)(2,1)S(1)}, bf16[144,144]{1,0:T(8,128)(2,1)}, u32[]{:S(2)}) copy-start(bf16[144,144]{1,0:T(8,128)(2,1)} %constant.30.clone.set_ref) | copy-start | bytes 124420
  16.7 8.2 %collective-permute-start.6 = (bf16[384,128]{1,0:T(8,128)(2,1)S(1)}, bf16[384,128]{1,0:T(8,128)(2,1)S(1)}, u32[]{:S(2)}, u32[]{:S(2)}) collective-permute-start(bf16[384,128]{1,0:T(8,128)(2,1)S(1)} %get-tuple-element.34), channel_id=1, source_target_pairs={{0,8},{2,10},{4,12},{6,14},{8,0},{10,2},{12,4},{14,6},{16,24},{18,... | collective-permute-start | bytes 294920 | tf_op jit(solution)/shard_map/ppermute | solution.py:642
  17.2 8.3 %copy-start.6 = (bf16[64,144]{1,0:T(8,128)(2,1)S(1)}, bf16[64,144]{1,0:T(8,128)(2,1)}, u32[]{:S(2)}) copy-start(bf16[64,144]{1,0:T(8,128)(2,1)} %proj_ref.1) | copy-start | bytes 55300
  17.2 12.5 %collective-permute-start.1 = (bf16[384,128]{1,0:T(8,128)(2,1)S(1)}, bf16[384,128]{1,0:T(8,128)(2,1)S(1)}, u32[]{:S(2)}, u32[]{:S(2)}) collective-permute-start(bf16[384,128]{1,0:T(8,128)(2,1)S(1)} %get-tuple-element.29), channel_id=1, source_target_pairs={{0,28},{2,30},{4,24},{6,26},{8,20},{10,22},{12,16},{14,18},{16,12}... | collective-permute-start | bytes 294920 | tf_op jit(solution)/shard_map/ppermute | solution.py:642
  20.8 8.9 %collective-permute-start.2 = (bf16[384,128]{1,0:T(8,128)(2,1)S(1)}, bf16[384,128]{1,0:T(8,128)(2,1)S(1)}, u32[]{:S(2)}, u32[]{:S(2)}) collective-permute-start(bf16[384,128]{1,0:T(8,128)(2,1)S(1)} %get-tuple-element.30), channel_id=1, source_target_pairs={{0,24},{2,26},{4,28},{6,30},{8,16},{10,18},{12,20},{14,22},{16,8},... | collective-permute-start | bytes 294920 | tf_op jit(solution)/shard_map/ppermute | solution.py:642
  20.9 15.2 %collective-permute-start.3 = (bf16[384,128]{1,0:T(8,128)(2,1)S(1)}, bf16[384,128]{1,0:T(8,128)(2,1)S(1)}, u32[]{:S(2)}, u32[]{:S(2)}) collective-permute-start(bf16[384,128]{1,0:T(8,128)(2,1)S(1)} %get-tuple-element.31), channel_id=1, source_target_pairs={{0,20},{2,22},{4,16},{6,18},{8,28},{10,30},{12,24},{14,26},{16,4},... | collective-permute-start | bytes 294920 | tf_op jit(solution)/shard_map/ppermute | solution.py:642
  22.8 13.6 %collective-permute-start.4 = (bf16[384,128]{1,0:T(8,128)(2,1)S(1)}, bf16[384,128]{1,0:T(8,128)(2,1)S(1)}, u32[]{:S(2)}, u32[]{:S(2)}) collective-permute-start(bf16[384,128]{1,0:T(8,128)(2,1)S(1)} %get-tuple-element.32), channel_id=1, source_target_pairs={{0,16},{2,18},{4,20},{6,22},{8,24},{10,26},{12,28},{14,30},{16,0},... | collective-permute-start | bytes 294920 | tf_op jit(solution)/shard_map/ppermute | solution.py:642
  24.9 4.6 %collective-permute-start.7 = (bf16[384,128]{1,0:T(8,128)(2,1)S(1)}, bf16[384,128]{1,0:T(8,128)(2,1)S(1)}, u32[]{:S(2)}, u32[]{:S(2)}) collective-permute-start(bf16[384,128]{1,0:T(8,128)(2,1)S(1)} %get-tuple-element.35), channel_id=1, source_target_pairs={{0,4},{2,6},{4,0},{6,2},{8,12},{10,14},{12,8},{14,10},{16,20},{18,... | collective-permute-start | bytes 294920 | tf_op jit(solution)/shard_map/ppermute | solution.py:642
  29.6 8.4 %copy-start.3 = (bf16[1,128,384]{2,1,0:T(8,128)(2,1)S(1)}, bf16[1,128,384]{2,1,0:T(8,128)(2,1)}, u32[]{:S(2)}) copy-start(bf16[1,128,384]{2,1,0:T(8,128)(2,1)} %constant.34.clone.refs_15_) | copy-start | bytes 294916
  29.6 6.9 %collective-permute-start.9 = (bf16[4,224,128]{2,1,0:T(8,128)(2,1)S(1)}, bf16[4,224,128]{2,1,0:T(8,128)(2,1)S(1)}, u32[]{:S(2)}, u32[]{:S(2)}) collective-permute-start(bf16[4,224,128]{2,1,0:T(8,128)(2,1)S(1)} %core_pack.3), channel_id=1, source_target_pairs={{0,2},{2,0},{4,6},{6,4},{8,10},{10,8},{12,14},{14,12},{16,18},{18,... | collective-permute-start | bytes 688136 | tf_op jit(solution)/shard_map/ppermute | solution.py:656
  36.4 1.6 %collective-permute-start.8 = (bf16[4,224,128]{2,1,0:T(8,128)(2,1)S(1)}, bf16[4,224,128]{2,1,0:T(8,128)(2,1)S(1)}, u32[]{:S(2)}, u32[]{:S(2)}) collective-permute-start(bf16[4,224,128]{2,1,0:T(8,128)(2,1)S(1)} %core_pack.2), channel_id=1, source_target_pairs={{0,2},{2,0},{4,6},{6,4},{8,10},{10,8},{12,14},{14,12},{16,18},{18,... | collective-permute-start | bytes 688136 | tf_op jit(solution)/shard_map/ppermute | solution.py:656

commit v14 on v13

--- a/solution.py
+++ b/solution.py
@@ -109,7 +109,7 @@
 
     @property
     def block_rows(self):
-        return up(self.lead + self.half_rows, 16)
+        return self.lead + self.half_rows
 
     @property
     def stride(self):
@@ -145,7 +145,8 @@
 
 def step_order(plan):
     far, near = far_near(plan)
-    return far + near + [0]
+    middle = len(far) // 2
+    return far[:middle] + near + far[middle:] + [0]
 
 
 def half(plan, block, core):
@@ -261,6 +262,12 @@
         == lax.broadcasted_iota(jnp.int32, (cols, cols), 1)
     ).astype(F32).astype(BF16)
     margin = 8 + halo
+    mirrors = []
+    for b in range(tiles):
+        shift = lax.rem(b - me + tiles, tiles)
+        other = recv_ref[jnp.maximum(shift - 1, 0), : count * cols, :]
+        own = [maps_ref[k, b * cols : (b + 1) * cols, :] for k in range(count)]
+        mirrors.append(across(eye, jnp.where(shift == 0, jnp.concatenate(own, axis=0), other)))
     for index in range(count):
         origin = index * plan.pitch
         field_ref[origin : origin + margin, :] = jnp.zeros((margin, cols), F32)
@@ -268,12 +275,8 @@
             (plan.pitch - margin - width, cols), F32
         )
         for b in range(tiles):
-            shift = lax.rem(b - me + tiles, tiles)
-            other = recv_ref[
-                jnp.maximum(shift - 1, 0), index * cols : (index + 1) * cols, :
-            ]
             own = maps_ref[index, b * cols : (b + 1) * cols, :]
-            mirror = across(eye, jnp.where(shift == 0, own, other))
+            mirror = mirrors[b][:, index * cols : (index + 1) * cols]
             column = turned_ref[b * cols : (b + 1) * cols, index : index + 1]
             field_ref[origin + margin + b * cols : origin + margin + (b + 1) * cols, :] = (
                 own.astype(F32) + mirror - column * mine[index : index + 1]
@@ -640,8 +643,10 @@
     for step, block in zip(step_order(plan), blocks):
         pairs = [(i, 2 * partner(i // 2, step, chips) + i % 2) for i in range(heads)]
         arrived[step] = lax.ppermute(block, "head", pairs) if step else block
-    far, near = far_near(plan)
-    order = [far, near + [0]]
+    steps = step_order(plan)
+    early = steps[: chips // 2]
+    late = [step for step in steps if step not in early]
+    order = [early, late]
     weights = (map_weight, side_weight, kernels, vectors, mask, spots)
     swapped = []
     for steps in order:
@@ -651,7 +656,7 @@
             [arrived[k] for k in steps],
             [array(BF16, len(steps), plan.half_rows, cols)],
         )
-        if steps is far:
+        if steps is late:
             packed, weights = lax.optimization_barrier((packed, weights))
         swapped.append(lax.ppermute(packed, "head", [(i, i ^ 1) for i in range(heads)]))
 

time: 42.8 us -> 40.6 us (0.949)
  waiting for transfers between devices: 20.2 us -> 14.8 us
  starting transfers between devices: 14.5 us -> 17.8 us
    ppermute x7, waiting for transfers between devices: 10.5 us -> 5.11 us  [on_device(): arrived[step] = lax.ppermute(block, 'head', pairs) if step else block]
    ppermute x7, starting transfers between devices: 11.4 us -> 14.6 us  [on_device(): arrived[step] = lax.ppermute(block, 'head', pairs) if step else block]
  transfers between devices with their start and end apart: 10 -> 10, of which waited for: 5 -> 4; matrix products, arithmetic and copies ran while one was open for 0% -> 0% of each run, Pallas kernels for 1% -> 1%
where the time goes in v14:
time: 40.6 us; the launch traced here: 40.4 us
  starting transfers between devices  17.8 us (44%)
  waiting for transfers between devices  14.8 us (36%)
  Pallas kernels  6.41 us (16%)
  local copies, waits for them, and re-layouts  1.23 us (3%)
    ppermute x7, starting transfers between devices, on_device(): arrived[step] = lax.ppermute(block, 'head', pairs) if step else block  14.6 us
    ppermute x1, waiting for transfers between devices, on_device(): lax.ppermute(payload[s - 1], 'tile', [(i, (i + s) % tiles) for i in range...  8.23 us
    pallas_call x6, Pallas kernels, call(): pl.pallas_call(kernel, out_shape=[pltpu.VMEM(x.shape, x.dtype) if held_ou...  6.41 us
    ppermute x7, waiting for transfers between devices, on_device(): arrived[step] = lax.ppermute(block, 'head', pairs) if step else block  5.11 us
    ppermute x1, starting transfers between devices, on_device(): lax.ppermute(payload[s - 1], 'tile', [(i, (i + s) % tiles) for i in range...  3.03 us
    ppermute x2, waiting for transfers between devices, on_device(): lax.ppermute(packed, 'head', [(i, i ^ 1) for i in range(heads)])  1.47 us
    unnamed x24, local copies, waits for them, and re-layouts  1.11 us
  transfers between devices with their start and end apart: 10, of which 4 were waited for; matrix products, arithmetic and copies ran while one was open for 0% of the time, Pallas kernels for 1%

profile of v14, /device:TPU:0, one launch (start us, length us, event | category | flops | bytes accessed | tf_op | source)
XLA Modules:
  0.0 40.4 jit_solution(11707060419089965672)
XLA Ops:
  0.0 1.1 %copy-done = bf16[9,256,128]{2,1,0:T(8,128)(2,1)S(1)} copy-done((bf16[9,256,128]{2,1,0:T(8,128)(2,1)S(1)}, bf16[9,256,128]{2,1,0:T(8,128)(2,1)}, u32[]{:S(2)}) %copy-start) | copy-done | bytes 589848
  1.1 0.5 %mirror_pack.1 = (bf16[1,1376,128]{2,1,0:T(8,128)(2,1)S(1)}, f32[16,256]{1,0:T(8,128)S(1)}, f32[40,128]{1,0:T(8,128)S(1)}) custom-call(bf16[9,256,128]{2,1,0:T(8,128)(2,1)S(1)} %copy-done), custom_call_target="tpu_custom_call" | custom-call | tf_op jit(solution)/shard_map/mirror_pack/pallas_call | solution.py:543
  1.5 3.0 %collective-permute-start = (bf16[1376,128]{1,0:T(8,128)(2,1)S(1)}, bf16[1376,128]{1,0:T(8,128)(2,1)S(1)}, u32[]{:S(2)}, u32[]{:S(2)}) collective-permute-start(bf16[1376,128]{1,0:T(8,128)(2,1)S(1)} %bitcast.10), channel_id=1, source_target_pairs={{0,1},{1,0},{2,3},{3,2},{4,5},{5,4},{6,7},{7,6},{8,9},{9,8},{10,11... | collective-permute-start | bytes 1056776 | tf_op jit(solution)/shard_map/ppermute | solution.py:578
  4.6 8.2 %collective-permute-done = bf16[1376,128]{1,0:T(8,128)(2,1)S(1)} collective-permute-done((bf16[1376,128]{1,0:T(8,128)(2,1)S(1)}, bf16[1376,128]{1,0:T(8,128)(2,1)S(1)}, u32[]{:S(2)}, u32[]{:S(2)}) %collective-permute-start) | collective-permute-done | bytes 352288 | tf_op jit(solution)/shard_map/ppermute | solution.py:578
  12.8 0.0 copy-start.10
  12.8 0.0 copy-start.11
  12.8 1.0 %correct_pack.1 = (bf16[376,128]{1,0:T(8,128)(2,1)S(1)}, bf16[376,128]{1,0:T(8,128)(2,1)S(1)}, bf16[376,128]{1,0:T(8,128)(2,1)S(1)}, bf16[376,128]{1,0:T(8,128)(...) custom-call(bf16[9,256,128]{2,1,0:T(8,128)(2,1)S(1)} %copy-done.1, ...), custom_call_target="tpu_custom_call" | custom-call | tf_op jit(solution)/shard_map/correct_pack/pallas_call | solution.py:543
  13.8 4.8 %collective-permute-start.1 = (bf16[376,128]{1,0:T(8,128)(2,1)S(1)}, bf16[376,128]{1,0:T(8,128)(2,1)S(1)}, u32[]{:S(2)}, u32[]{:S(2)}) collective-permute-start(bf16[376,128]{1,0:T(8,128)(2,1)S(1)} %get-tuple-element.29), channel_id=1, source_target_pairs={{0,28},{2,30},{4,24},{6,26},{8,20},{10,22},{12,16},{14,18},{16,12}... | collective-permute-start | bytes 288776 | tf_op jit(solution)/shard_map/ppermute | solution.py:645
  18.6 0.2 collective-permute-start.2
  18.9 0.0 copy-start.6
  18.9 0.1 collective-permute-start.3
  19.0 1.9 %collective-permute-start.4 = (bf16[376,128]{1,0:T(8,128)(2,1)S(1)}, bf16[376,128]{1,0:T(8,128)(2,1)S(1)}, u32[]{:S(2)}, u32[]{:S(2)}) collective-permute-start(bf16[376,128]{1,0:T(8,128)(2,1)S(1)} %get-tuple-element.32), channel_id=1, source_target_pairs={{0,8},{2,10},{4,12},{6,14},{8,0},{10,2},{12,4},{14,6},{16,24},{18,... | collective-permute-start | bytes 288776 | tf_op jit(solution)/shard_map/ppermute | solution.py:645
  20.9 1.6 %collective-permute-start.5 = (bf16[376,128]{1,0:T(8,128)(2,1)S(1)}, bf16[376,128]{1,0:T(8,128)(2,1)S(1)}, u32[]{:S(2)}, u32[]{:S(2)}) collective-permute-start(bf16[376,128]{1,0:T(8,128)(2,1)S(1)} %get-tuple-element.33), channel_id=1, source_target_pairs={{0,4},{2,6},{4,0},{6,2},{8,12},{10,14},{12,8},{14,10},{16,20},{18,... | collective-permute-start | bytes 288776 | tf_op jit(solution)/shard_map/ppermute | solution.py:645
  22.5 0.0 collective-permute-done.1.refs_0_
  22.5 3.9 %collective-permute-start.6 = (bf16[376,128]{1,0:T(8,128)(2,1)S(1)}, bf16[376,128]{1,0:T(8,128)(2,1)S(1)}, u32[]{:S(2)}, u32[]{:S(2)}) collective-permute-start(bf16[376,128]{1,0:T(8,128)(2,1)S(1)} %get-tuple-element.34), channel_id=1, source_target_pairs={{0,20},{2,22},{4,16},{6,18},{8,28},{10,30},{12,24},{14,26},{16,4},... | collective-permute-start | bytes 288776 | tf_op jit(solution)/shard_map/ppermute | solution.py:645
  26.4 0.0 collective-permute-done.2.refs_1_
  26.4 2.1 %collective-permute-start.7 = (bf16[376,128]{1,0:T(8,128)(2,1)S(1)}, bf16[376,128]{1,0:T(8,128)(2,1)S(1)}, u32[]{:S(2)}, u32[]{:S(2)}) collective-permute-start(bf16[376,128]{1,0:T(8,128)(2,1)S(1)} %get-tuple-element.35), channel_id=1, source_target_pairs={{0,16},{2,18},{4,20},{6,22},{8,24},{10,26},{12,28},{14,30},{16,0},... | collective-permute-start | bytes 288776 | tf_op jit(solution)/shard_map/ppermute | solution.py:645
  28.5 0.1 copy.18
  28.6 0.0 copy-done.5
  28.7 0.2 weight_pack.1
  28.8 0.0 collective-permute-done.3.refs_2_
  28.8 0.0 collective-permute-done.4.refs_3_
  28.8 0.1 core_pack.2
  28.9 0.1 collective-permute-start.8
  29.0 0.0 collective-permute-done.5.refs_0_.refs_4_
  29.0 4.0 %collective-permute-done.6.refs_1_.refs_5_ = bf16[376,128]{1,0:T(8,128)(2,1)S(1)} collective-permute-done((bf16[376,128]{1,0:T(8,128)(2,1)S(1)}, bf16[376,128]{1,0:T(8,128)(2,1)S(1)}, u32[]{:S(2)}, u32[]{:S(2)}) %collective-permute-start.6) | collective-permute-done | bytes 96288 | tf_op jit(solution)/shard_map/ppermute | solution.py:645
  33.0 1.1 %collective-permute-done.7.refs_2_.refs_6_ = bf16[376,128]{1,0:T(8,128)(2,1)S(1)} collective-permute-done((bf16[376,128]{1,0:T(8,128)(2,1)S(1)}, bf16[376,128]{1,0:T(8,128)(2,1)S(1)}, u32[]{:S(2)}, u32[]{:S(2)}) %collective-permute-start.7) | collective-permute-done | bytes 96288 | tf_op jit(solution)/shard_map/ppermute | solution.py:645
  34.1 0.1 core_pack.3
  34.2 0.1 collective-permute-start.9
  34.3 0.0 collective-permute-done.8.refs_8_
  34.3 1.5 %collective-permute-done.9.refs_9_ = bf16[4,224,128]{2,1,0:T(8,128)(2,1)S(1)} collective-permute-done((bf16[4,224,128]{2,1,0:T(8,128)(2,1)S(1)}, bf16[4,224,128]{2,1,0:T(8,128)(2,1)S(1)}, u32[]{:S(2)}, u32[]{:S(2)}) %collective-permute-start.9) | collective-permute-done | bytes 229408 | tf_op jit(solution)/shard_map/ppermute | solution.py:661
  35.7 4.7 %stack.5 = f32[16,128]{1,0:T(8,128)} custom-call(bf16[376,128]{1,0:T(8,128)(2,1)S(1)} %collective-permute-done.1.refs_0_, bf16[376,128]{1,0:T(8,128)(2,1)S(1)} %collective-permute-done.2.refs_1_, bf16[376,128]{1,0:T(8,128)(2,1)S(1)} %collective-permute-done.3.refs_2_, bf16[376,128]{1,0:T(8,128)(2,1)S(1)} %collective-permute-done.4.refs_3_, ...), custom_call_target="tpu_custom_call" | custom-call | tf_op jit(solution)/shard_map/stack/pallas_call | solution.py:543
  (22 shorter events, 0.1 us)
Async XLA Ops:
  0.0 1.1 %copy-start = (bf16[9,256,128]{2,1,0:T(8,128)(2,1)S(1)}, bf16[9,256,128]{2,1,0:T(8,128)(2,1)}, u32[]{:S(2)}) copy-start(bf16[9,256,128]{2,1,0:T(8,128)(2,1)} %maps_ref.3) | copy-start | bytes 1769476
  1.1 11.7 %copy-start.1 = (bf16[9,256,128]{2,1,0:T(8,128)(2,1)S(1)}, bf16[9,256,128]{2,1,0:T(8,128)(2,1)}, u32[]{:S(2)}) copy-start(bf16[9,256,128]{2,1,0:T(8,128)(2,1)} %maps_ref.3) | copy-start | bytes 1769476
  1.5 11.3 %collective-permute-start = (bf16[1376,128]{1,0:T(8,128)(2,1)S(1)}, bf16[1376,128]{1,0:T(8,128)(2,1)S(1)}, u32[]{:S(2)}, u32[]{:S(2)}) collective-permute-start(bf16[1376,128]{1,0:T(8,128)(2,1)S(1)} %bitcast.10), channel_id=1, source_target_pairs={{0,1},{1,0},{2,3},{3,2},{4,5},{5,4},{6,7},{7,6},{8,9},{9,8},{10,11... | collective-permute-start | bytes 1056776 | tf_op jit(solution)/shard_map/ppermute | solution.py:578
  4.6 24.1 %copy-start.2 = (bf16[2,2,64,64,3,3]{3,2,5,4,1,0:T(8,128)(2,1)S(1)}, bf16[2,2,64,64,3,3]{3,2,5,4,1,0:T(8,128)(2,1)}, u32[]{:S(2)}) copy-start(bf16[2,2,64,64,3,3]{3,2,5,4,1,0:T(8,128)(2,1)} %param.14) | copy-start | bytes 884740
  12.8 6.1 %copy-start.7 = (s32[5504]{0:T(1024)S(1)}, s32[5504]{0:T(1024)}, u32[]{:S(2)}) copy-start(s32[5504]{0:T(1024)} %constant.33.clone) | copy-start | bytes 66052
  12.8 6.1 %copy-start.8 = (s32[5504]{0:T(1024)S(1)}, s32[5504]{0:T(1024)}, u32[]{:S(2)}) copy-start(s32[5504]{0:T(1024)} %constant.32.clone) | copy-start | bytes 66052
  12.8 15.7 %copy-start.9 = (f32[2,2,64]{2,1,0:T(2,128)S(1)}, f32[2,2,64]{2,1,0:T(2,128)}, u32[]{:S(2)}) copy-start(f32[2,2,64]{2,1,0:T(2,128)} %param.15) | copy-start | bytes 3076
  12.8 15.7 %copy-start.10 = (f32[64]{0:T(128)S(1)}, f32[64]{0:T(128)}, u32[]{:S(2)}) copy-start(f32[64]{0:T(128)} %param.16) | copy-start | bytes 772
  12.8 15.7 %copy-start.11 = (f32[64]{0:T(128)S(1)}, f32[64]{0:T(128)}, u32[]{:S(2)}) copy-start(f32[64]{0:T(128)} %param.13) | copy-start | bytes 772
  13.8 8.7 %collective-permute-start.1 = (bf16[376,128]{1,0:T(8,128)(2,1)S(1)}, bf16[376,128]{1,0:T(8,128)(2,1)S(1)}, u32[]{:S(2)}, u32[]{:S(2)}) collective-permute-start(bf16[376,128]{1,0:T(8,128)(2,1)S(1)} %get-tuple-element.29), channel_id=1, source_target_pairs={{0,28},{2,30},{4,24},{6,26},{8,20},{10,22},{12,16},{14,18},{16,12}... | collective-permute-start | bytes 288776 | tf_op jit(solution)/shard_map/ppermute | solution.py:645
  18.6 10.0 %copy-start.4 = (bf16[144,160]{1,0:T(8,128)(2,1)S(1)}, bf16[144,160]{1,0:T(8,128)(2,1)}, u32[]{:S(2)}) copy-start(bf16[144,160]{1,0:T(8,128)(2,1)} %constant.31.clone.slot_ref) | copy-start | bytes 138244
  18.6 10.0 %copy-start.5 = (bf16[144,144]{1,0:T(8,128)(2,1)S(1)}, bf16[144,144]{1,0:T(8,128)(2,1)}, u32[]{:S(2)}) copy-start(bf16[144,144]{1,0:T(8,128)(2,1)} %constant.30.clone.set_ref) | copy-start | bytes 124420
  18.6 7.8 %collective-permute-start.2 = (bf16[376,128]{1,0:T(8,128)(2,1)S(1)}, bf16[376,128]{1,0:T(8,128)(2,1)S(1)}, u32[]{:S(2)}, u32[]{:S(2)}) collective-permute-start(bf16[376,128]{1,0:T(8,128)(2,1)S(1)} %get-tuple-element.30), channel_id=1, source_target_pairs={{0,24},{2,26},{4,28},{6,30},{8,16},{10,18},{12,20},{14,22},{16,8},... | collective-permute-start | bytes 288776 | tf_op jit(solution)/shard_map/ppermute | solution.py:645
  18.9 9.7 %copy-start.6 = (bf16[64,144]{1,0:T(8,128)(2,1)S(1)}, bf16[64,144]{1,0:T(8,128)(2,1)}, u32[]{:S(2)}) copy-start(bf16[64,144]{1,0:T(8,128)(2,1)} %proj_ref.1) | copy-start | bytes 55300
  18.9 9.9 %collective-permute-start.3 = (bf16[376,128]{1,0:T(8,128)(2,1)S(1)}, bf16[376,128]{1,0:T(8,128)(2,1)S(1)}, u32[]{:S(2)}, u32[]{:S(2)}) collective-permute-start(bf16[376,128]{1,0:T(8,128)(2,1)S(1)} %get-tuple-element.31), channel_id=1, source_target_pairs={{0,12},{2,14},{4,8},{6,10},{8,4},{10,6},{12,0},{14,2},{16,28},{18,... | collective-permute-start | bytes 288776 | tf_op jit(solution)/shard_map/ppermute | solution.py:645
  19.0 9.8 %collective-permute-start.4 = (bf16[376,128]{1,0:T(8,128)(2,1)S(1)}, bf16[376,128]{1,0:T(8,128)(2,1)S(1)}, u32[]{:S(2)}, u32[]{:S(2)}) collective-permute-start(bf16[376,128]{1,0:T(8,128)(2,1)S(1)} %get-tuple-element.32), channel_id=1, source_target_pairs={{0,8},{2,10},{4,12},{6,14},{8,0},{10,2},{12,4},{14,6},{16,24},{18,... | collective-permute-start | bytes 288776 | tf_op jit(solution)/shard_map/ppermute | solution.py:645
  20.9 8.1 %collective-permute-start.5 = (bf16[376,128]{1,0:T(8,128)(2,1)S(1)}, bf16[376,128]{1,0:T(8,128)(2,1)S(1)}, u32[]{:S(2)}, u32[]{:S(2)}) collective-permute-start(bf16[376,128]{1,0:T(8,128)(2,1)S(1)} %get-tuple-element.33), channel_id=1, source_target_pairs={{0,4},{2,6},{4,0},{6,2},{8,12},{10,14},{12,8},{14,10},{16,20},{18,... | collective-permute-start | bytes 288776 | tf_op jit(solution)/shard_map/ppermute | solution.py:645
  22.5 10.6 %collective-permute-start.6 = (bf16[376,128]{1,0:T(8,128)(2,1)S(1)}, bf16[376,128]{1,0:T(8,128)(2,1)S(1)}, u32[]{:S(2)}, u32[]{:S(2)}) collective-permute-start(bf16[376,128]{1,0:T(8,128)(2,1)S(1)} %get-tuple-element.34), channel_id=1, source_target_pairs={{0,20},{2,22},{4,16},{6,18},{8,28},{10,30},{12,24},{14,26},{16,4},... | collective-permute-start | bytes 288776 | tf_op jit(solution)/shard_map/ppermute | solution.py:645
  26.4 7.7 %collective-permute-start.7 = (bf16[376,128]{1,0:T(8,128)(2,1)S(1)}, bf16[376,128]{1,0:T(8,128)(2,1)S(1)}, u32[]{:S(2)}, u32[]{:S(2)}) collective-permute-start(bf16[376,128]{1,0:T(8,128)(2,1)S(1)} %get-tuple-element.35), channel_id=1, source_target_pairs={{0,16},{2,18},{4,20},{6,22},{8,24},{10,26},{12,28},{14,30},{16,0},... | collective-permute-start | bytes 288776 | tf_op jit(solution)/shard_map/ppermute | solution.py:645
  28.9 5.3 %collective-permute-start.8 = (bf16[4,224,128]{2,1,0:T(8,128)(2,1)S(1)}, bf16[4,224,128]{2,1,0:T(8,128)(2,1)S(1)}, u32[]{:S(2)}, u32[]{:S(2)}) collective-permute-start(bf16[4,224,128]{2,1,0:T(8,128)(2,1)S(1)} %core_pack.2), channel_id=1, source_target_pairs={{0,2},{2,0},{4,6},{6,4},{8,10},{10,8},{12,14},{14,12},{16,18},{18,... | collective-permute-start | bytes 688136 | tf_op jit(solution)/shard_map/ppermute | solution.py:661
  34.1 1.6 %copy-start.3 = (bf16[1,128,384]{2,1,0:T(8,128)(2,1)S(1)}, bf16[1,128,384]{2,1,0:T(8,128)(2,1)}, u32[]{:S(2)}) copy-start(bf16[1,128,384]{2,1,0:T(8,128)(2,1)} %constant.34.clone.refs_15_) | copy-start | bytes 294916
  34.2 1.6 %collective-permute-start.9 = (bf16[4,224,128]{2,1,0:T(8,128)(2,1)S(1)}, bf16[4,224,128]{2,1,0:T(8,128)(2,1)S(1)}, u32[]{:S(2)}, u32[]{:S(2)}) collective-permute-start(bf16[4,224,128]{2,1,0:T(8,128)(2,1)S(1)} %core_pack.3), channel_id=1, source_target_pairs={{0,2},{2,0},{4,6},{6,4},{8,10},{10,8},{12,14},{14,12},{16,18},{18,... | collective-permute-start | bytes 688136 | tf_op jit(solution)/shard_map/ppermute | solution.py:661

commit v15 on v14

--- a/solution.py
+++ b/solution.py
@@ -121,11 +121,11 @@
 
     @property
     def batch(self):
-        return 8
+        return 32
 
     @property
     def chunk(self):
-        return 1536
+        return 3072
 
     @property
     def lanes(self):

time: 40.6 us -> 40.9 us (level)
  no operation moved by 1% of the time
where the time goes in v15:
time: 40.9 us; the launch traced here: 40.8 us
  starting transfers between devices  17.8 us (44%)
  waiting for transfers between devices  14.8 us (36%)
  Pallas kernels  6.79 us (17%)
  local copies, waits for them, and re-layouts  1.23 us (3%)
    ppermute x7, starting transfers between devices, on_device(): arrived[step] = lax.ppermute(block, 'head', pairs) if step else block  14.6 us
    ppermute x1, waiting for transfers between devices, on_device(): lax.ppermute(payload[s - 1], 'tile', [(i, (i + s) % tiles) for i in range...  8.23 us
    pallas_call x6, Pallas kernels, call(): pl.pallas_call(kernel, out_shape=[pltpu.VMEM(x.shape, x.dtype) if held_ou...  6.79 us
    ppermute x7, waiting for transfers between devices, on_device(): arrived[step] = lax.ppermute(block, 'head', pairs) if step else block  5.11 us
    ppermute x1, starting transfers between devices, on_device(): lax.ppermute(payload[s - 1], 'tile', [(i, (i + s) % tiles) for i in range...  3.03 us
    ppermute x2, waiting for transfers between devices, on_device(): lax.ppermute(packed, 'head', [(i, i ^ 1) for i in range(heads)])  1.47 us
    unnamed x24, local copies, waits for them, and re-layouts  1.11 us
  transfers between devices with their start and end apart: 10, of which 4 were waited for; matrix products, arithmetic and copies ran while one was open for 0% of the time, Pallas kernels for 1%

profile of v15, /device:TPU:0, one launch (start us, length us, event | category | flops | bytes accessed | tf_op | source)
XLA Modules:
  0.0 40.8 jit_solution(10757101632555693913)
XLA Ops:
  0.0 1.1 %copy-done = bf16[9,256,128]{2,1,0:T(8,128)(2,1)S(1)} copy-done((bf16[9,256,128]{2,1,0:T(8,128)(2,1)S(1)}, bf16[9,256,128]{2,1,0:T(8,128)(2,1)}, u32[]{:S(2)}) %copy-start) | copy-done | bytes 589848
  1.1 0.5 %mirror_pack.1 = (bf16[1,1376,128]{2,1,0:T(8,128)(2,1)S(1)}, f32[16,256]{1,0:T(8,128)S(1)}, f32[40,128]{1,0:T(8,128)S(1)}) custom-call(bf16[9,256,128]{2,1,0:T(8,128)(2,1)S(1)} %copy-done), custom_call_target="tpu_custom_call" | custom-call | tf_op jit(solution)/shard_map/mirror_pack/pallas_call | solution.py:543
  1.5 3.0 %collective-permute-start = (bf16[1376,128]{1,0:T(8,128)(2,1)S(1)}, bf16[1376,128]{1,0:T(8,128)(2,1)S(1)}, u32[]{:S(2)}, u32[]{:S(2)}) collective-permute-start(bf16[1376,128]{1,0:T(8,128)(2,1)S(1)} %bitcast.10), channel_id=1, source_target_pairs={{0,1},{1,0},{2,3},{3,2},{4,5},{5,4},{6,7},{7,6},{8,9},{9,8},{10,11... | collective-permute-start | bytes 1056776 | tf_op jit(solution)/shard_map/ppermute | solution.py:578
  4.6 8.2 %collective-permute-done = bf16[1376,128]{1,0:T(8,128)(2,1)S(1)} collective-permute-done((bf16[1376,128]{1,0:T(8,128)(2,1)S(1)}, bf16[1376,128]{1,0:T(8,128)(2,1)S(1)}, u32[]{:S(2)}, u32[]{:S(2)}) %collective-permute-start) | collective-permute-done | bytes 352288 | tf_op jit(solution)/shard_map/ppermute | solution.py:578
  12.8 0.0 copy-start.10
  12.8 0.0 copy-start.11
  12.8 1.0 %correct_pack.1 = (bf16[376,128]{1,0:T(8,128)(2,1)S(1)}, bf16[376,128]{1,0:T(8,128)(2,1)S(1)}, bf16[376,128]{1,0:T(8,128)(2,1)S(1)}, bf16[376,128]{1,0:T(8,128)(...) custom-call(bf16[9,256,128]{2,1,0:T(8,128)(2,1)S(1)} %copy-done.1, ...), custom_call_target="tpu_custom_call" | custom-call | tf_op jit(solution)/shard_map/correct_pack/pallas_call | solution.py:543
  13.8 4.8 %collective-permute-start.1 = (bf16[376,128]{1,0:T(8,128)(2,1)S(1)}, bf16[376,128]{1,0:T(8,128)(2,1)S(1)}, u32[]{:S(2)}, u32[]{:S(2)}) collective-permute-start(bf16[376,128]{1,0:T(8,128)(2,1)S(1)} %get-tuple-element.29), channel_id=1, source_target_pairs={{0,28},{2,30},{4,24},{6,26},{8,20},{10,22},{12,16},{14,18},{16,12}... | collective-permute-start | bytes 288776 | tf_op jit(solution)/shard_map/ppermute | solution.py:645
  18.6 0.2 collective-permute-start.2
  18.9 0.0 copy-start.6
  18.9 0.1 collective-permute-start.3
  19.0 1.9 %collective-permute-start.4 = (bf16[376,128]{1,0:T(8,128)(2,1)S(1)}, bf16[376,128]{1,0:T(8,128)(2,1)S(1)}, u32[]{:S(2)}, u32[]{:S(2)}) collective-permute-start(bf16[376,128]{1,0:T(8,128)(2,1)S(1)} %get-tuple-element.32), channel_id=1, source_target_pairs={{0,8},{2,10},{4,12},{6,14},{8,0},{10,2},{12,4},{14,6},{16,24},{18,... | collective-permute-start | bytes 288776 | tf_op jit(solution)/shard_map/ppermute | solution.py:645
  20.9 1.6 %collective-permute-start.5 = (bf16[376,128]{1,0:T(8,128)(2,1)S(1)}, bf16[376,128]{1,0:T(8,128)(2,1)S(1)}, u32[]{:S(2)}, u32[]{:S(2)}) collective-permute-start(bf16[376,128]{1,0:T(8,128)(2,1)S(1)} %get-tuple-element.33), channel_id=1, source_target_pairs={{0,4},{2,6},{4,0},{6,2},{8,12},{10,14},{12,8},{14,10},{16,20},{18,... | collective-permute-start | bytes 288776 | tf_op jit(solution)/shard_map/ppermute | solution.py:645
  22.5 0.0 collective-permute-done.1.refs_0_
  22.5 3.9 %collective-permute-start.6 = (bf16[376,128]{1,0:T(8,128)(2,1)S(1)}, bf16[376,128]{1,0:T(8,128)(2,1)S(1)}, u32[]{:S(2)}, u32[]{:S(2)}) collective-permute-start(bf16[376,128]{1,0:T(8,128)(2,1)S(1)} %get-tuple-element.34), channel_id=1, source_target_pairs={{0,20},{2,22},{4,16},{6,18},{8,28},{10,30},{12,24},{14,26},{16,4},... | collective-permute-start | bytes 288776 | tf_op jit(solution)/shard_map/ppermute | solution.py:645
  26.4 0.0 collective-permute-done.2.refs_1_
  26.4 2.1 %collective-permute-start.7 = (bf16[376,128]{1,0:T(8,128)(2,1)S(1)}, bf16[376,128]{1,0:T(8,128)(2,1)S(1)}, u32[]{:S(2)}, u32[]{:S(2)}) collective-permute-start(bf16[376,128]{1,0:T(8,128)(2,1)S(1)} %get-tuple-element.35), channel_id=1, source_target_pairs={{0,16},{2,18},{4,20},{6,22},{8,24},{10,26},{12,28},{14,30},{16,0},... | collective-permute-start | bytes 288776 | tf_op jit(solution)/shard_map/ppermute | solution.py:645
  28.5 0.0 copy-done.9
  28.5 0.1 copy.18
  28.7 0.2 weight_pack.1
  28.8 0.0 collective-permute-done.3.refs_2_
  28.8 0.0 collective-permute-done.4.refs_3_
  28.8 0.1 core_pack.2
  28.9 0.1 collective-permute-start.8
  29.0 0.0 collective-permute-done.5.refs_0_.refs_4_
  29.0 4.0 %collective-permute-done.6.refs_1_.refs_5_ = bf16[376,128]{1,0:T(8,128)(2,1)S(1)} collective-permute-done((bf16[376,128]{1,0:T(8,128)(2,1)S(1)}, bf16[376,128]{1,0:T(8,128)(2,1)S(1)}, u32[]{:S(2)}, u32[]{:S(2)}) %collective-permute-start.6) | collective-permute-done | bytes 96288 | tf_op jit(solution)/shard_map/ppermute | solution.py:645
  33.0 1.1 %collective-permute-done.7.refs_2_.refs_6_ = bf16[376,128]{1,0:T(8,128)(2,1)S(1)} collective-permute-done((bf16[376,128]{1,0:T(8,128)(2,1)S(1)}, bf16[376,128]{1,0:T(8,128)(2,1)S(1)}, u32[]{:S(2)}, u32[]{:S(2)}) %collective-permute-start.7) | collective-permute-done | bytes 96288 | tf_op jit(solution)/shard_map/ppermute | solution.py:645
  34.1 0.1 core_pack.3
  34.2 0.1 collective-permute-start.9
  34.3 0.0 collective-permute-done.8.refs_8_
  34.3 1.5 %collective-permute-done.9.refs_9_ = bf16[4,224,128]{2,1,0:T(8,128)(2,1)S(1)} collective-permute-done((bf16[4,224,128]{2,1,0:T(8,128)(2,1)S(1)}, bf16[4,224,128]{2,1,0:T(8,128)(2,1)S(1)}, u32[]{:S(2)}, u32[]{:S(2)}) %collective-permute-start.9) | collective-permute-done | bytes 229408 | tf_op jit(solution)/shard_map/ppermute | solution.py:661
  35.7 5.0 %stack.5 = f32[16,128]{1,0:T(8,128)} custom-call(bf16[376,128]{1,0:T(8,128)(2,1)S(1)} %collective-permute-done.1.refs_0_, bf16[376,128]{1,0:T(8,128)(2,1)S(1)} %collective-permute-done.2.refs_1_, bf16[376,128]{1,0:T(8,128)(2,1)S(1)} %collective-permute-done.3.refs_2_, bf16[376,128]{1,0:T(8,128)(2,1)S(1)} %collective-permute-done.4.refs_3_, ...), custom_call_target="tpu_custom_call" | custom-call | tf_op jit(solution)/shard_map/stack/pallas_call | solution.py:543
  (22 shorter events, 0.1 us)
Async XLA Ops:
  0.0 1.1 %copy-start = (bf16[9,256,128]{2,1,0:T(8,128)(2,1)S(1)}, bf16[9,256,128]{2,1,0:T(8,128)(2,1)}, u32[]{:S(2)}) copy-start(bf16[9,256,128]{2,1,0:T(8,128)(2,1)} %maps_ref.3) | copy-start | bytes 1769476
  1.1 11.7 %copy-start.1 = (bf16[9,256,128]{2,1,0:T(8,128)(2,1)S(1)}, bf16[9,256,128]{2,1,0:T(8,128)(2,1)}, u32[]{:S(2)}) copy-start(bf16[9,256,128]{2,1,0:T(8,128)(2,1)} %maps_ref.3) | copy-start | bytes 1769476
  1.5 11.3 %collective-permute-start = (bf16[1376,128]{1,0:T(8,128)(2,1)S(1)}, bf16[1376,128]{1,0:T(8,128)(2,1)S(1)}, u32[]{:S(2)}, u32[]{:S(2)}) collective-permute-start(bf16[1376,128]{1,0:T(8,128)(2,1)S(1)} %bitcast.10), channel_id=1, source_target_pairs={{0,1},{1,0},{2,3},{3,2},{4,5},{5,4},{6,7},{7,6},{8,9},{9,8},{10,11... | collective-permute-start | bytes 1056776 | tf_op jit(solution)/shard_map/ppermute | solution.py:578
  4.6 24.1 %copy-start.2 = (bf16[2,2,64,64,3,3]{3,2,5,4,1,0:T(8,128)(2,1)S(1)}, bf16[2,2,64,64,3,3]{3,2,5,4,1,0:T(8,128)(2,1)}, u32[]{:S(2)}) copy-start(bf16[2,2,64,64,3,3]{3,2,5,4,1,0:T(8,128)(2,1)} %param.14) | copy-start | bytes 884740
  12.8 6.1 %copy-start.7 = (s32[5504]{0:T(1024)S(1)}, s32[5504]{0:T(1024)}, u32[]{:S(2)}) copy-start(s32[5504]{0:T(1024)} %constant.33.clone) | copy-start | bytes 66052
  12.8 6.1 %copy-start.8 = (s32[5504]{0:T(1024)S(1)}, s32[5504]{0:T(1024)}, u32[]{:S(2)}) copy-start(s32[5504]{0:T(1024)} %constant.32.clone) | copy-start | bytes 66052
  12.8 15.7 %copy-start.9 = (f32[2,2,64]{2,1,0:T(2,128)S(1)}, f32[2,2,64]{2,1,0:T(2,128)}, u32[]{:S(2)}) copy-start(f32[2,2,64]{2,1,0:T(2,128)} %param.15) | copy-start | bytes 3076
  12.8 15.7 %copy-start.10 = (f32[64]{0:T(128)S(1)}, f32[64]{0:T(128)}, u32[]{:S(2)}) copy-start(f32[64]{0:T(128)} %param.16) | copy-start | bytes 772
  12.8 15.7 %copy-start.11 = (f32[64]{0:T(128)S(1)}, f32[64]{0:T(128)}, u32[]{:S(2)}) copy-start(f32[64]{0:T(128)} %param.13) | copy-start | bytes 772
  13.8 8.7 %collective-permute-start.1 = (bf16[376,128]{1,0:T(8,128)(2,1)S(1)}, bf16[376,128]{1,0:T(8,128)(2,1)S(1)}, u32[]{:S(2)}, u32[]{:S(2)}) collective-permute-start(bf16[376,128]{1,0:T(8,128)(2,1)S(1)} %get-tuple-element.29), channel_id=1, source_target_pairs={{0,28},{2,30},{4,24},{6,26},{8,20},{10,22},{12,16},{14,18},{16,12}... | collective-permute-start | bytes 288776 | tf_op jit(solution)/shard_map/ppermute | solution.py:645
  18.6 10.0 %copy-start.4 = (bf16[144,160]{1,0:T(8,128)(2,1)S(1)}, bf16[144,160]{1,0:T(8,128)(2,1)}, u32[]{:S(2)}) copy-start(bf16[144,160]{1,0:T(8,128)(2,1)} %constant.31.clone.slot_ref) | copy-start | bytes 138244
  18.6 10.0 %copy-start.5 = (bf16[144,144]{1,0:T(8,128)(2,1)S(1)}, bf16[144,144]{1,0:T(8,128)(2,1)}, u32[]{:S(2)}) copy-start(bf16[144,144]{1,0:T(8,128)(2,1)} %constant.30.clone.set_ref) | copy-start | bytes 124420
  18.6 7.8 %collective-permute-start.2 = (bf16[376,128]{1,0:T(8,128)(2,1)S(1)}, bf16[376,128]{1,0:T(8,128)(2,1)S(1)}, u32[]{:S(2)}, u32[]{:S(2)}) collective-permute-start(bf16[376,128]{1,0:T(8,128)(2,1)S(1)} %get-tuple-element.30), channel_id=1, source_target_pairs={{0,24},{2,26},{4,28},{6,30},{8,16},{10,18},{12,20},{14,22},{16,8},... | collective-permute-start | bytes 288776 | tf_op jit(solution)/shard_map/ppermute | solution.py:645
  18.9 9.7 %copy-start.6 = (bf16[64,144]{1,0:T(8,128)(2,1)S(1)}, bf16[64,144]{1,0:T(8,128)(2,1)}, u32[]{:S(2)}) copy-start(bf16[64,144]{1,0:T(8,128)(2,1)} %proj_ref.1) | copy-start | bytes 55300
  18.9 9.9 %collective-permute-start.3 = (bf16[376,128]{1,0:T(8,128)(2,1)S(1)}, bf16[376,128]{1,0:T(8,128)(2,1)S(1)}, u32[]{:S(2)}, u32[]{:S(2)}) collective-permute-start(bf16[376,128]{1,0:T(8,128)(2,1)S(1)} %get-tuple-element.31), channel_id=1, source_target_pairs={{0,12},{2,14},{4,8},{6,10},{8,4},{10,6},{12,0},{14,2},{16,28},{18,... | collective-permute-start | bytes 288776 | tf_op jit(solution)/shard_map/ppermute | solution.py:645
  19.0 9.8 %collective-permute-start.4 = (bf16[376,128]{1,0:T(8,128)(2,1)S(1)}, bf16[376,128]{1,0:T(8,128)(2,1)S(1)}, u32[]{:S(2)}, u32[]{:S(2)}) collective-permute-start(bf16[376,128]{1,0:T(8,128)(2,1)S(1)} %get-tuple-element.32), channel_id=1, source_target_pairs={{0,8},{2,10},{4,12},{6,14},{8,0},{10,2},{12,4},{14,6},{16,24},{18,... | collective-permute-start | bytes 288776 | tf_op jit(solution)/shard_map/ppermute | solution.py:645
  20.9 8.1 %collective-permute-start.5 = (bf16[376,128]{1,0:T(8,128)(2,1)S(1)}, bf16[376,128]{1,0:T(8,128)(2,1)S(1)}, u32[]{:S(2)}, u32[]{:S(2)}) collective-permute-start(bf16[376,128]{1,0:T(8,128)(2,1)S(1)} %get-tuple-element.33), channel_id=1, source_target_pairs={{0,4},{2,6},{4,0},{6,2},{8,12},{10,14},{12,8},{14,10},{16,20},{18,... | collective-permute-start | bytes 288776 | tf_op jit(solution)/shard_map/ppermute | solution.py:645
  22.5 10.6 %collective-permute-start.6 = (bf16[376,128]{1,0:T(8,128)(2,1)S(1)}, bf16[376,128]{1,0:T(8,128)(2,1)S(1)}, u32[]{:S(2)}, u32[]{:S(2)}) collective-permute-start(bf16[376,128]{1,0:T(8,128)(2,1)S(1)} %get-tuple-element.34), channel_id=1, source_target_pairs={{0,20},{2,22},{4,16},{6,18},{8,28},{10,30},{12,24},{14,26},{16,4},... | collective-permute-start | bytes 288776 | tf_op jit(solution)/shard_map/ppermute | solution.py:645
  26.4 7.7 %collective-permute-start.7 = (bf16[376,128]{1,0:T(8,128)(2,1)S(1)}, bf16[376,128]{1,0:T(8,128)(2,1)S(1)}, u32[]{:S(2)}, u32[]{:S(2)}) collective-permute-start(bf16[376,128]{1,0:T(8,128)(2,1)S(1)} %get-tuple-element.35), channel_id=1, source_target_pairs={{0,16},{2,18},{4,20},{6,22},{8,24},{10,26},{12,28},{14,30},{16,0},... | collective-permute-start | bytes 288776 | tf_op jit(solution)/shard_map/ppermute | solution.py:645
  28.9 5.3 %collective-permute-start.8 = (bf16[4,224,128]{2,1,0:T(8,128)(2,1)S(1)}, bf16[4,224,128]{2,1,0:T(8,128)(2,1)S(1)}, u32[]{:S(2)}, u32[]{:S(2)}) collective-permute-start(bf16[4,224,128]{2,1,0:T(8,128)(2,1)S(1)} %core_pack.2), channel_id=1, source_target_pairs={{0,2},{2,0},{4,6},{6,4},{8,10},{10,8},{12,14},{14,12},{16,18},{18,... | collective-permute-start | bytes 688136 | tf_op jit(solution)/shard_map/ppermute | solution.py:661
  34.1 1.6 %copy-start.3 = (bf16[1,128,384]{2,1,0:T(8,128)(2,1)S(1)}, bf16[1,128,384]{2,1,0:T(8,128)(2,1)}, u32[]{:S(2)}) copy-start(bf16[1,128,384]{2,1,0:T(8,128)(2,1)} %constant.34.clone.refs_15_) | copy-start | bytes 294916
  34.2 1.6 %collective-permute-start.9 = (bf16[4,224,128]{2,1,0:T(8,128)(2,1)S(1)}, bf16[4,224,128]{2,1,0:T(8,128)(2,1)S(1)}, u32[]{:S(2)}, u32[]{:S(2)}) collective-permute-start(bf16[4,224,128]{2,1,0:T(8,128)(2,1)S(1)} %core_pack.3), channel_id=1, source_target_pairs={{0,2},{2,0},{4,6},{6,4},{8,10},{10,8},{12,14},{14,12},{16,18},{18,... | collective-permute-start | bytes 688136 | tf_op jit(solution)/shard_map/ppermute | solution.py:661

commit v16 on v14

--- a/solution.py
+++ b/solution.py
@@ -198,9 +198,6 @@
         by_col = by_row = None
         for index in range(count):
             block = maps_ref[index]
-            out_ref[shift - 1, index * cols : (index + 1) * cols, :] = maps_ref[
-                index, pl.ds(pl.multiple_of(dest * cols, cols), cols), :
-            ]
             left = [pick(edge, cols, me * cols, dest, index)]
             upper = [pick(edge, width, 0, dest, index)]
             if shift == 1:
@@ -226,15 +223,15 @@
         used = (1 + tiles) * edge + 3 * tiles * head
         if plan.tail_rows > used:
             pieces.append(jnp.zeros((plan.tail_rows - used, cols), F32))
-        out_ref[shift - 1, count * cols :, :] = jnp.concatenate(pieces, axis=0).astype(BF16)
-
-
-def correct_pack(plan, maps_ref, recv_ref, sums_ref, edge_ref, *refs):
+        out_ref[shift - 1] = jnp.concatenate(pieces, axis=0).astype(BF16)
+
+
+def correct_pack(plan, maps_ref, recv_ref, tail_ref, sums_ref, edge_ref, *refs):
     *out_refs, field_ref, turned_ref = refs
     me, chip = lax.axis_index("tile"), lax.axis_index("head") // 2
     count, cols, width, tiles = plan.maps, plan.cols, plan.width, plan.tiles
     head, edge, halo = plan.map_rows, plan.edge_rows, plan.halo
-    tails = [recv_ref[k, count * cols :, :].astype(F32) for k in range(tiles - 1)]
+    tails = [tail_ref[k].astype(F32) for k in range(tiles - 1)]
 
     rowsum = []
     for b in range(tiles):
@@ -265,7 +262,7 @@
     mirrors = []
     for b in range(tiles):
         shift = lax.rem(b - me + tiles, tiles)
-        other = recv_ref[jnp.maximum(shift - 1, 0), : count * cols, :]
+        other = recv_ref[jnp.maximum(shift - 1, 0)]
         own = [maps_ref[k, b * cols : (b + 1) * cols, :] for k in range(count)]
         mirrors.append(across(eye, jnp.where(shift == 0, jnp.concatenate(own, axis=0), other)))
     for index in range(count):
@@ -563,22 +560,30 @@
     plan = Plan(maps, width, cols, tiles, heads, feat, blocks * convs)
     me, band_index = lax.axis_index("tile"), lax.axis_index("head")
 
-    payload, sums, edge = call(
+    tail, sums, edge = call(
         functools.partial(mirror_pack, plan),
         "mirror_pack",
         [attention],
         [
-            array(BF16, tiles - 1, maps * cols + plan.tail_rows, cols),
+            array(BF16, tiles - 1, plan.tail_rows, cols),
             array(F32, plan.map_rows, width),
             array(F32, plan.edge_rows, cols),
         ],
     )
-    received = jnp.stack(
-        [
-            lax.ppermute(payload[s - 1], "tile", [(i, (i + s) % tiles) for i in range(tiles)])
-            for s in range(tiles - 1, 0, -1)
-        ]
-    )
+
+    def mirror(block):
+        return jnp.stack(
+            [
+                lax.ppermute(block(s), "tile", [(i, (i + s) % tiles) for i in range(tiles)])
+                for s in range(tiles - 1, 0, -1)
+            ]
+        )
+
+    def facing(s):
+        block = lax.dynamic_slice_in_dim(attention, (me + s) % tiles * cols, cols, 1)
+        return block.reshape(maps * cols, cols)
+
+    received, tails = mirror(facing), mirror(lambda s: tail[s - 1])
 
     stride, start = plan.stride, plan.start
     source, index = np.divmod(np.arange(heads * maps), maps)
@@ -635,7 +640,7 @@
     blocks = call(
         functools.partial(correct_pack, plan),
         "correct_pack",
-        [attention, received, sums, edge],
+        [attention, received, tails, sums, edge],
         [array(BF16, plan.block_rows, cols)] * chips,
         [pltpu.VMEM((maps * plan.pitch, cols), F32), pltpu.VMEM((width, LANES), F32)],
     )

time: 40.6 us -> 40.1 us (0.988)
  waiting for transfers between devices: 14.8 us -> 14.2 us
    unnamed x24 -> x22, local copies, waits for them, and re-layouts: 1.11 us -> 0.05 us
    dynamic_slice x0 -> x1, local copies, waits for them, and re-layouts: none -> 1.05 us  [facing(): lax.dynamic_slice_in_dim(attention, (me + s) % tiles * cols, cols, 1)]
    ppermute x1 -> x2, waiting for transfers between devices: 8.23 us -> 7.65 us  [mirror(): lax.ppermute(block(s), 'tile', [(i, (i + s) % tiles) for i in range(tiles)])]
    ppermute x1 -> x2, starting transfers between devices: 3.03 us -> 3.13 us  [mirror(): lax.ppermute(block(s), 'tile', [(i, (i + s) % tiles) for i in range(tiles)])]
  transfers between devices with their start and end apart: 10 -> 11, of which waited for: 4 -> 4; matrix products, arithmetic and copies ran while one was open for 0% -> 0% of each run, Pallas kernels for 1% -> 2%
where the time goes in v16:
time: 40.1 us; the launch traced here: 39.9 us
  starting transfers between devices  17.9 us (45%)
  waiting for transfers between devices  14.2 us (35%)
  Pallas kernels  6.4 us (16%)
  local copies, waits for them, and re-layouts  1.22 us (3%)
    ppermute x7, starting transfers between devices, on_device(): arrived[step] = lax.ppermute(block, 'head', pairs) if step else block  14.6 us
    ppermute x2, waiting for transfers between devices, mirror(): lax.ppermute(block(s), 'tile', [(i, (i + s) % tiles) for i in range(tiles)])  7.65 us
    pallas_call x6, Pallas kernels, call(): pl.pallas_call(kernel, out_shape=[pltpu.VMEM(x.shape, x.dtype) if held_ou...  6.4 us
    ppermute x7, waiting for transfers between devices, on_device(): arrived[step] = lax.ppermute(block, 'head', pairs) if step else block  5.13 us
    ppermute x2, starting transfers between devices, mirror(): lax.ppermute(block(s), 'tile', [(i, (i + s) % tiles) for i in range(tiles)])  3.13 us
    ppermute x2, waiting for transfers between devices, on_device(): lax.ppermute(packed, 'head', [(i, i ^ 1) for i in range(heads)])  1.47 us
    dynamic_slice x1, local copies, waits for them, and re-layouts, facing(): lax.dynamic_slice_in_dim(attention, (me + s) % tiles * cols, cols, 1)  1.05 us
  transfers between devices with their start and end apart: 11, of which 4 were waited for; matrix products, arithmetic and copies ran while one was open for 0% of the time, Pallas kernels for 2%

profile of v16, /device:TPU:0, one launch (start us, length us, event | category | flops | bytes accessed | tf_op | source)
XLA Modules:
  0.0 39.9 jit_solution(1331327098949276228)
XLA Ops:
  0.0 1.1 %constant_dynamic-slice_fusion = bf16[9,128,128]{2,1,0:T(8,128)(2,1)S(1)} fusion(bf16[9,256,128]{2,1,0:T(8,128)(2,1)} %maps_ref.3, s32[]{:T(128)S(6)} %select_n.11), kind=kLoop, calls=%fused_computation.9 | loop fusion | bytes 589828 | tf_op jit(solution)/shard_map/dynamic_slice | solution.py:583
  1.1 3.1 %collective-permute-start = (bf16[1152,128]{1,0:T(8,128)(2,1)S(1)}, bf16[1152,128]{1,0:T(8,128)(2,1)S(1)}, u32[]{:S(2)}, u32[]{:S(2)}) collective-permute-start(bf16[1152,128]{1,0:T(8,128)(2,1)S(1)} %bitcast.14), channel_id=1, source_target_pairs={{0,1},{1,0},{2,3},{3,2},{4,5},{5,4},{6,7},{7,6},{8,9},{9,8},{10,11... | collective-permute-start | bytes 884744 | tf_op jit(solution)/shard_map/ppermute | solution.py:577
  4.1 0.5 %mirror_pack.1 = (bf16[1,224,128]{2,1,0:T(8,128)(2,1)S(1)}, f32[16,256]{1,0:T(8,128)S(1)}, f32[40,128]{1,0:T(8,128)S(1)}) custom-call(bf16[9,256,128]{2,1,0:T(8,128)(2,1)S(1)} %copy-done), custom_call_target="tpu_custom_call" | custom-call | tf_op jit(solution)/shard_map/mirror_pack/pallas_call | solution.py:540
  4.6 0.1 collective-permute-start.1
  4.7 0.0 copy-start.1
  4.7 7.6 %collective-permute-done.1 = bf16[224,128]{1,0:T(8,128)(2,1)S(1)} collective-permute-done((bf16[224,128]{1,0:T(8,128)(2,1)S(1)}, bf16[224,128]{1,0:T(8,128)(2,1)S(1)}, u32[]{:S(2)}, u32[]{:S(2)}) %collective-permute-start.1) | collective-permute-done | bytes 57376 | tf_op jit(solution)/shard_map/ppermute | solution.py:577
  12.3 0.0 collective-permute-done
  12.3 0.0 copy-start.9
  12.4 0.0 copy-start.10
  12.4 1.0 %correct_pack.1 = (bf16[376,128]{1,0:T(8,128)(2,1)S(1)}, bf16[376,128]{1,0:T(8,128)(2,1)S(1)}, bf16[376,128]{1,0:T(8,128)(2,1)S(1)}, bf16[376,128]{1,0:T(8,128)(...) custom-call(bf16[9,256,128]{2,1,0:T(8,128)(2,1)S(1)} %copy-done, ...), custom_call_target="tpu_custom_call" | custom-call | tf_op jit(solution)/shard_map/correct_pack/pallas_call | solution.py:540
  13.4 4.8 %collective-permute-start.2 = (bf16[376,128]{1,0:T(8,128)(2,1)S(1)}, bf16[376,128]{1,0:T(8,128)(2,1)S(1)}, u32[]{:S(2)}, u32[]{:S(2)}) collective-permute-start(bf16[376,128]{1,0:T(8,128)(2,1)S(1)} %get-tuple-element.29), channel_id=1, source_target_pairs={{0,28},{2,30},{4,24},{6,26},{8,20},{10,22},{12,16},{14,18},{16,12}... | collective-permute-start | bytes 288776 | tf_op jit(solution)/shard_map/ppermute | solution.py:650
  18.2 0.2 collective-permute-start.3
  18.4 0.0 copy-start.5
  18.5 0.1 collective-permute-start.4
  18.5 1.9 %collective-permute-start.5 = (bf16[376,128]{1,0:T(8,128)(2,1)S(1)}, bf16[376,128]{1,0:T(8,128)(2,1)S(1)}, u32[]{:S(2)}, u32[]{:S(2)}) collective-permute-start(bf16[376,128]{1,0:T(8,128)(2,1)S(1)} %get-tuple-element.32), channel_id=1, source_target_pairs={{0,8},{2,10},{4,12},{6,14},{8,0},{10,2},{12,4},{14,6},{16,24},{18,... | collective-permute-start | bytes 288776 | tf_op jit(solution)/shard_map/ppermute | solution.py:650
  20.4 1.6 %collective-permute-start.6 = (bf16[376,128]{1,0:T(8,128)(2,1)S(1)}, bf16[376,128]{1,0:T(8,128)(2,1)S(1)}, u32[]{:S(2)}, u32[]{:S(2)}) collective-permute-start(bf16[376,128]{1,0:T(8,128)(2,1)S(1)} %get-tuple-element.33), channel_id=1, source_target_pairs={{0,4},{2,6},{4,0},{6,2},{8,12},{10,14},{12,8},{14,10},{16,20},{18,... | collective-permute-start | bytes 288776 | tf_op jit(solution)/shard_map/ppermute | solution.py:650
  22.0 0.0 collective-permute-done.2.refs_0_
  22.0 3.9 %collective-permute-start.7 = (bf16[376,128]{1,0:T(8,128)(2,1)S(1)}, bf16[376,128]{1,0:T(8,128)(2,1)S(1)}, u32[]{:S(2)}, u32[]{:S(2)}) collective-permute-start(bf16[376,128]{1,0:T(8,128)(2,1)S(1)} %get-tuple-element.34), channel_id=1, source_target_pairs={{0,20},{2,22},{4,16},{6,18},{8,28},{10,30},{12,24},{14,26},{16,4},... | collective-permute-start | bytes 288776 | tf_op jit(solution)/shard_map/ppermute | solution.py:650
  25.9 0.0 collective-permute-done.3.refs_1_
  25.9 2.1 %collective-permute-start.8 = (bf16[376,128]{1,0:T(8,128)(2,1)S(1)}, bf16[376,128]{1,0:T(8,128)(2,1)S(1)}, u32[]{:S(2)}, u32[]{:S(2)}) collective-permute-start(bf16[376,128]{1,0:T(8,128)(2,1)S(1)} %get-tuple-element.35), channel_id=1, source_target_pairs={{0,16},{2,18},{4,20},{6,22},{8,24},{10,26},{12,28},{14,30},{16,0},... | collective-permute-start | bytes 288776 | tf_op jit(solution)/shard_map/ppermute | solution.py:650
  28.1 0.1 copy.18
  28.2 0.2 weight_pack.1
  28.4 0.1 core_pack.2
  28.4 0.1 collective-permute-start.9
  28.5 0.0 collective-permute-done.6.refs_0_.refs_4_
  28.5 4.0 %collective-permute-done.7.refs_1_.refs_5_ = bf16[376,128]{1,0:T(8,128)(2,1)S(1)} collective-permute-done((bf16[376,128]{1,0:T(8,128)(2,1)S(1)}, bf16[376,128]{1,0:T(8,128)(2,1)S(1)}, u32[]{:S(2)}, u32[]{:S(2)}) %collective-permute-start.7) | collective-permute-done | bytes 96288 | tf_op jit(solution)/shard_map/ppermute | solution.py:650
  32.6 1.1 %collective-permute-done.8.refs_2_.refs_6_ = bf16[376,128]{1,0:T(8,128)(2,1)S(1)} collective-permute-done((bf16[376,128]{1,0:T(8,128)(2,1)S(1)}, bf16[376,128]{1,0:T(8,128)(2,1)S(1)}, u32[]{:S(2)}, u32[]{:S(2)}) %collective-permute-start.8) | collective-permute-done | bytes 96288 | tf_op jit(solution)/shard_map/ppermute | solution.py:650
  33.7 0.1 core_pack.3
  33.7 0.1 collective-permute-start.10
  33.8 0.0 collective-permute-done.9.refs_8_
  33.8 1.5 %collective-permute-done.10.refs_9_ = bf16[4,224,128]{2,1,0:T(8,128)(2,1)S(1)} collective-permute-done((bf16[4,224,128]{2,1,0:T(8,128)(2,1)S(1)}, bf16[4,224,128]{2,1,0:T(8,128)(2,1)S(1)}, u32[]{:S(2)}, u32[]{:S(2)}) %collective-permute-start.10) | collective-permute-done | bytes 229408 | tf_op jit(solution)/shard_map/ppermute | solution.py:666
  35.3 4.7 %stack.9 = f32[16,128]{1,0:T(8,128)} custom-call(bf16[376,128]{1,0:T(8,128)(2,1)S(1)} %collective-permute-done.2.refs_0_, bf16[376,128]{1,0:T(8,128)(2,1)S(1)} %collective-permute-done.3.refs_1_, bf16[376,128]{1,0:T(8,128)(2,1)S(1)} %collective-permute-done.4.refs_2_, bf16[376,128]{1,0:T(8,128)(2,1)S(1)} %collective-permute-done.5.refs_3_, ...), custom_call_target="tpu_custom_call" | custom-call | tf_op jit(solution)/shard_map/stack/pallas_call | solution.py:540
  (23 shorter events, 0.1 us)
Async XLA Ops:
  0.0 4.1 %copy-start = (bf16[9,256,128]{2,1,0:T(8,128)(2,1)S(1)}, bf16[9,256,128]{2,1,0:T(8,128)(2,1)}, u32[]{:S(2)}) copy-start(bf16[9,256,128]{2,1,0:T(8,128)(2,1)} %maps_ref.3) | copy-start | bytes 1769476
  1.1 11.3 %collective-permute-start = (bf16[1152,128]{1,0:T(8,128)(2,1)S(1)}, bf16[1152,128]{1,0:T(8,128)(2,1)S(1)}, u32[]{:S(2)}, u32[]{:S(2)}) collective-permute-start(bf16[1152,128]{1,0:T(8,128)(2,1)S(1)} %bitcast.14), channel_id=1, source_target_pairs={{0,1},{1,0},{2,3},{3,2},{4,5},{5,4},{6,7},{7,6},{8,9},{9,8},{10,11... | collective-permute-start | bytes 884744 | tf_op jit(solution)/shard_map/ppermute | solution.py:577
  4.6 7.7 %collective-permute-start.1 = (bf16[224,128]{1,0:T(8,128)(2,1)S(1)}, bf16[224,128]{1,0:T(8,128)(2,1)S(1)}, u32[]{:S(2)}, u32[]{:S(2)}) collective-permute-start(bf16[224,128]{1,0:T(8,128)(2,1)S(1)} %bitcast.13), channel_id=1, source_target_pairs={{0,1},{1,0},{2,3},{3,2},{4,5},{5,4},{6,7},{7,6},{8,9},{9,8},{10,11... | collective-permute-start | bytes 172040 | tf_op jit(solution)/shard_map/ppermute | solution.py:577
  4.7 23.5 %copy-start.1 = (bf16[2,2,64,64,3,3]{3,2,5,4,1,0:T(8,128)(2,1)S(1)}, bf16[2,2,64,64,3,3]{3,2,5,4,1,0:T(8,128)(2,1)}, u32[]{:S(2)}) copy-start(bf16[2,2,64,64,3,3]{3,2,5,4,1,0:T(8,128)(2,1)} %param.14) | copy-start | bytes 884740
  12.3 6.1 %copy-start.6 = (s32[5504]{0:T(1024)S(1)}, s32[5504]{0:T(1024)}, u32[]{:S(2)}) copy-start(s32[5504]{0:T(1024)} %constant.48.clone) | copy-start | bytes 66052
  12.3 6.1 %copy-start.7 = (s32[5504]{0:T(1024)S(1)}, s32[5504]{0:T(1024)}, u32[]{:S(2)}) copy-start(s32[5504]{0:T(1024)} %constant.47.clone) | copy-start | bytes 66052
  12.3 15.7 %copy-start.8 = (f32[2,2,64]{2,1,0:T(2,128)S(1)}, f32[2,2,64]{2,1,0:T(2,128)}, u32[]{:S(2)}) copy-start(f32[2,2,64]{2,1,0:T(2,128)} %param.15) | copy-start | bytes 3076
  12.3 15.7 %copy-start.9 = (f32[64]{0:T(128)S(1)}, f32[64]{0:T(128)}, u32[]{:S(2)}) copy-start(f32[64]{0:T(128)} %param.16) | copy-start | bytes 772
  12.4 15.7 %copy-start.10 = (f32[64]{0:T(128)S(1)}, f32[64]{0:T(128)}, u32[]{:S(2)}) copy-start(f32[64]{0:T(128)} %param.13) | copy-start | bytes 772
  13.4 8.7 %collective-permute-start.2 = (bf16[376,128]{1,0:T(8,128)(2,1)S(1)}, bf16[376,128]{1,0:T(8,128)(2,1)S(1)}, u32[]{:S(2)}, u32[]{:S(2)}) collective-permute-start(bf16[376,128]{1,0:T(8,128)(2,1)S(1)} %get-tuple-element.29), channel_id=1, source_target_pairs={{0,28},{2,30},{4,24},{6,26},{8,20},{10,22},{12,16},{14,18},{16,12}... | collective-permute-start | bytes 288776 | tf_op jit(solution)/shard_map/ppermute | solution.py:650
  18.2 10.0 %copy-start.3 = (bf16[144,160]{1,0:T(8,128)(2,1)S(1)}, bf16[144,160]{1,0:T(8,128)(2,1)}, u32[]{:S(2)}) copy-start(bf16[144,160]{1,0:T(8,128)(2,1)} %constant.46.clone.slot_ref) | copy-start | bytes 138244
  18.2 10.0 %copy-start.4 = (bf16[144,144]{1,0:T(8,128)(2,1)S(1)}, bf16[144,144]{1,0:T(8,128)(2,1)}, u32[]{:S(2)}) copy-start(bf16[144,144]{1,0:T(8,128)(2,1)} %constant.45.clone.set_ref) | copy-start | bytes 124420
  18.2 7.8 %collective-permute-start.3 = (bf16[376,128]{1,0:T(8,128)(2,1)S(1)}, bf16[376,128]{1,0:T(8,128)(2,1)S(1)}, u32[]{:S(2)}, u32[]{:S(2)}) collective-permute-start(bf16[376,128]{1,0:T(8,128)(2,1)S(1)} %get-tuple-element.30), channel_id=1, source_target_pairs={{0,24},{2,26},{4,28},{6,30},{8,16},{10,18},{12,20},{14,22},{16,8},... | collective-permute-start | bytes 288776 | tf_op jit(solution)/shard_map/ppermute | solution.py:650
  18.4 9.7 %copy-start.5 = (bf16[64,144]{1,0:T(8,128)(2,1)S(1)}, bf16[64,144]{1,0:T(8,128)(2,1)}, u32[]{:S(2)}) copy-start(bf16[64,144]{1,0:T(8,128)(2,1)} %proj_ref.1) | copy-start | bytes 55300
  18.5 9.9 %collective-permute-start.4 = (bf16[376,128]{1,0:T(8,128)(2,1)S(1)}, bf16[376,128]{1,0:T(8,128)(2,1)S(1)}, u32[]{:S(2)}, u32[]{:S(2)}) collective-permute-start(bf16[376,128]{1,0:T(8,128)(2,1)S(1)} %get-tuple-element.31), channel_id=1, source_target_pairs={{0,12},{2,14},{4,8},{6,10},{8,4},{10,6},{12,0},{14,2},{16,28},{18,... | collective-permute-start | bytes 288776 | tf_op jit(solution)/shard_map/ppermute | solution.py:650
  18.5 9.8 %collective-permute-start.5 = (bf16[376,128]{1,0:T(8,128)(2,1)S(1)}, bf16[376,128]{1,0:T(8,128)(2,1)S(1)}, u32[]{:S(2)}, u32[]{:S(2)}) collective-permute-start(bf16[376,128]{1,0:T(8,128)(2,1)S(1)} %get-tuple-element.32), channel_id=1, source_target_pairs={{0,8},{2,10},{4,12},{6,14},{8,0},{10,2},{12,4},{14,6},{16,24},{18,... | collective-permute-start | bytes 288776 | tf_op jit(solution)/shard_map/ppermute | solution.py:650
  20.4 8.1 %collective-permute-start.6 = (bf16[376,128]{1,0:T(8,128)(2,1)S(1)}, bf16[376,128]{1,0:T(8,128)(2,1)S(1)}, u32[]{:S(2)}, u32[]{:S(2)}) collective-permute-start(bf16[376,128]{1,0:T(8,128)(2,1)S(1)} %get-tuple-element.33), channel_id=1, source_target_pairs={{0,4},{2,6},{4,0},{6,2},{8,12},{10,14},{12,8},{14,10},{16,20},{18,... | collective-permute-start | bytes 288776 | tf_op jit(solution)/shard_map/ppermute | solution.py:650
  22.0 10.6 %collective-permute-start.7 = (bf16[376,128]{1,0:T(8,128)(2,1)S(1)}, bf16[376,128]{1,0:T(8,128)(2,1)S(1)}, u32[]{:S(2)}, u32[]{:S(2)}) collective-permute-start(bf16[376,128]{1,0:T(8,128)(2,1)S(1)} %get-tuple-element.34), channel_id=1, source_target_pairs={{0,20},{2,22},{4,16},{6,18},{8,28},{10,30},{12,24},{14,26},{16,4},... | collective-permute-start | bytes 288776 | tf_op jit(solution)/shard_map/ppermute | solution.py:650
  25.9 7.7 %collective-permute-start.8 = (bf16[376,128]{1,0:T(8,128)(2,1)S(1)}, bf16[376,128]{1,0:T(8,128)(2,1)S(1)}, u32[]{:S(2)}, u32[]{:S(2)}) collective-permute-start(bf16[376,128]{1,0:T(8,128)(2,1)S(1)} %get-tuple-element.35), channel_id=1, source_target_pairs={{0,16},{2,18},{4,20},{6,22},{8,24},{10,26},{12,28},{14,30},{16,0},... | collective-permute-start | bytes 288776 | tf_op jit(solution)/shard_map/ppermute | solution.py:650
  28.4 5.4 %collective-permute-start.9 = (bf16[4,224,128]{2,1,0:T(8,128)(2,1)S(1)}, bf16[4,224,128]{2,1,0:T(8,128)(2,1)S(1)}, u32[]{:S(2)}, u32[]{:S(2)}) collective-permute-start(bf16[4,224,128]{2,1,0:T(8,128)(2,1)S(1)} %core_pack.2), channel_id=1, source_target_pairs={{0,2},{2,0},{4,6},{6,4},{8,10},{10,8},{12,14},{14,12},{16,18},{18,... | collective-permute-start | bytes 688136 | tf_op jit(solution)/shard_map/ppermute | solution.py:666
  33.6 1.6 %copy-start.2 = (bf16[1,128,384]{2,1,0:T(8,128)(2,1)S(1)}, bf16[1,128,384]{2,1,0:T(8,128)(2,1)}, u32[]{:S(2)}) copy-start(bf16[1,128,384]{2,1,0:T(8,128)(2,1)} %constant.49.clone.refs_15_) | copy-start | bytes 294916
  33.7 1.6 %collective-permute-start.10 = (bf16[4,224,128]{2,1,0:T(8,128)(2,1)S(1)}, bf16[4,224,128]{2,1,0:T(8,128)(2,1)S(1)}, u32[]{:S(2)}, u32[]{:S(2)}) collective-permute-start(bf16[4,224,128]{2,1,0:T(8,128)(2,1)S(1)} %core_pack.3), channel_id=1, source_target_pairs={{0,2},{2,0},{4,6},{6,4},{8,10},{10,8},{12,14},{14,12},{16,18},{18,... | collective-permute-start | bytes 688136 | tf_op jit(solution)/shard_map/ppermute | solution.py:666

commit v17 on v16

--- a/solution.py
+++ b/solution.py
@@ -125,7 +125,7 @@
 
     @property
     def chunk(self):
-        return 1536
+        return 1024
 
     @property
     def lanes(self):
@@ -226,7 +226,7 @@
         out_ref[shift - 1] = jnp.concatenate(pieces, axis=0).astype(BF16)
 
 
-def correct_pack(plan, maps_ref, recv_ref, tail_ref, sums_ref, edge_ref, *refs):
+def correct_pack(plan, maps_ref, first_ref, second_ref, tail_ref, sums_ref, edge_ref, *refs):
     *out_refs, field_ref, turned_ref = refs
     me, chip = lax.axis_index("tile"), lax.axis_index("head") // 2
     count, cols, width, tiles = plan.maps, plan.cols, plan.width, plan.tiles
@@ -262,7 +262,8 @@
     mirrors = []
     for b in range(tiles):
         shift = lax.rem(b - me + tiles, tiles)
-        other = recv_ref[jnp.maximum(shift - 1, 0)]
+        sender = jnp.maximum(shift - 1, 0)
+        other = jnp.concatenate([first_ref[sender], second_ref[sender]], axis=0)
         own = [maps_ref[k, b * cols : (b + 1) * cols, :] for k in range(count)]
         mirrors.append(across(eye, jnp.where(shift == 0, jnp.concatenate(own, axis=0), other)))
     for index in range(count):
@@ -579,11 +580,16 @@
             ]
         )
 
-    def facing(s):
-        block = lax.dynamic_slice_in_dim(attention, (me + s) % tiles * cols, cols, 1)
-        return block.reshape(maps * cols, cols)
-
-    received, tails = mirror(facing), mirror(lambda s: tail[s - 1])
+    def facing(first, count):
+        def block(s):
+            start = (first, (me + s) % tiles * cols, 0)
+            found = lax.dynamic_slice(attention, start, (count, cols, cols))
+            return found.reshape(count * cols, cols)
+
+        return block
+
+    received = [mirror(facing(0, maps // 2)), mirror(facing(maps // 2, maps - maps // 2))]
+    tails = mirror(lambda s: tail[s - 1])
 
     stride, start = plan.stride, plan.start
     source, index = np.divmod(np.arange(heads * maps), maps)
@@ -640,7 +646,7 @@
     blocks = call(
         functools.partial(correct_pack, plan),
         "correct_pack",
-        [attention, received, tails, sums, edge],
+        [attention, *received, tails, sums, edge],
         [array(BF16, plan.block_rows, cols)] * chips,
         [pltpu.VMEM((maps * plan.pitch, cols), F32), pltpu.VMEM((width, LANES), F32)],
     )

time: 40.1 us -> 40.4 us (level)
  waiting for transfers between devices: 14.2 us -> 11.3 us
  starting transfers between devices: 17.9 us -> 19.9 us
  local copies, waits for them, and re-layouts: 1.22 us -> 2.08 us
    ppermute x2 -> x3, waiting for transfers between devices: 7.65 us -> 4.7 us  [mirror(): lax.ppermute(block(s), 'tile', [(i, (i + s) % tiles) for i in range(tiles)])]
    ppermute x2 -> x3, starting transfers between devices: 3.13 us -> 5.19 us  [mirror(): lax.ppermute(block(s), 'tile', [(i, (i + s) % tiles) for i in range(tiles)])]
    dynamic_slice x1 -> x2, local copies, waits for them, and re-layouts: 1.05 us -> 1.91 us  [block(): found = lax.dynamic_slice(attention, start, (count, cols, cols))]
  transfers between devices with their start and end apart: 11 -> 12, of which waited for: 4 -> 4; matrix products, arithmetic and copies ran while one was open for 0% -> 3% of each run, Pallas kernels for 2% -> 2%
where the time goes in v17:
time: 40.4 us; the launch traced here: 40.2 us
  starting transfers between devices  19.9 us (49%)
  waiting for transfers between devices  11.3 us (28%)
  Pallas kernels  6.74 us (17%)
  local copies, waits for them, and re-layouts  2.08 us (5%)
    ppermute x7, starting transfers between devices, on_device(): arrived[step] = lax.ppermute(block, 'head', pairs) if step else block  14.6 us
    pallas_call x6, Pallas kernels, call(): pl.pallas_call(kernel, out_shape=[pltpu.VMEM(x.shape, x.dtype) if held_ou...  6.74 us
    ppermute x3, starting transfers between devices, mirror(): lax.ppermute(block(s), 'tile', [(i, (i + s) % tiles) for i in range(tiles)])  5.19 us
    ppermute x7, waiting for transfers between devices, on_device(): arrived[step] = lax.ppermute(block, 'head', pairs) if step else block  5.15 us
    ppermute x3, waiting for transfers between devices, mirror(): lax.ppermute(block(s), 'tile', [(i, (i + s) % tiles) for i in range(tiles)])  4.7 us
    dynamic_slice x2, local copies, waits for them, and re-layouts, block(): found = lax.dynamic_slice(attention, start, (count, cols, cols))  1.91 us
    ppermute x2, waiting for transfers between devices, on_device(): lax.ppermute(packed, 'head', [(i, i ^ 1) for i in range(heads)])  1.47 us
  transfers between devices with their start and end apart: 12, of which 4 were waited for; matrix products, arithmetic and copies ran while one was open for 3% of the time, Pallas kernels for 2%

profile of v17, /device:TPU:0, one launch (start us, length us, event | category | flops | bytes accessed | tf_op | source)
XLA Modules:
  0.0 40.2 jit_solution(14275869760977260310)
XLA Ops:
  0.0 1.0 %constant_dynamic-slice_fusion = bf16[5,128,128]{2,1,0:T(8,128)(2,1)S(1)} fusion(bf16[9,256,128]{2,1,0:T(8,128)(2,1)} %maps_ref.3, s32[]{:T(128)S(6)} %select_n.14), kind=kLoop, calls=%fused_computation.9 | loop fusion | bytes 327684 | tf_op jit(solution)/shard_map/dynamic_slice | solution.py:586
  1.0 3.0 %collective-permute-start.1 = (bf16[640,128]{1,0:T(8,128)(2,1)S(1)}, bf16[640,128]{1,0:T(8,128)(2,1)S(1)}, u32[]{:S(2)}, u32[]{:S(2)}) collective-permute-start(bf16[640,128]{1,0:T(8,128)(2,1)S(1)} %bitcast.17), channel_id=1, source_target_pairs={{0,1},{1,0},{2,3},{3,2},{4,5},{5,4},{6,7},{7,6},{8,9},{9,8},{10,11... | collective-permute-start | bytes 491528 | tf_op jit(solution)/shard_map/ppermute | solution.py:578
  4.0 0.9 %constant_dynamic-slice_fusion.1 = bf16[4,128,128]{2,1,0:T(8,128)(2,1)S(1)} fusion(bf16[9,256,128]{2,1,0:T(8,128)(2,1)} %maps_ref.3, s32[]{:T(128)S(6)} %select_n.14), kind=kLoop, calls=%fused_computation.10 | loop fusion | bytes 262148 | tf_op jit(solution)/shard_map/dynamic_slice | solution.py:586
  5.0 0.1 collective-permute-start
  5.0 0.5 %mirror_pack.1 = (bf16[1,224,128]{2,1,0:T(8,128)(2,1)S(1)}, f32[16,256]{1,0:T(8,128)S(1)}, f32[40,128]{1,0:T(8,128)S(1)}) custom-call(bf16[9,256,128]{2,1,0:T(8,128)(2,1)S(1)} %copy-done), custom_call_target="tpu_custom_call" | custom-call | tf_op jit(solution)/shard_map/mirror_pack/pallas_call | solution.py:541
  5.5 2.1 %collective-permute-start.2 = (bf16[224,128]{1,0:T(8,128)(2,1)S(1)}, bf16[224,128]{1,0:T(8,128)(2,1)S(1)}, u32[]{:S(2)}, u32[]{:S(2)}) collective-permute-start(bf16[224,128]{1,0:T(8,128)(2,1)S(1)} %bitcast.16), channel_id=1, source_target_pairs={{0,1},{1,0},{2,3},{3,2},{4,5},{5,4},{6,7},{7,6},{8,9},{9,8},{10,11... | collective-permute-start | bytes 172040 | tf_op jit(solution)/shard_map/ppermute | solution.py:578
  7.6 4.7 %collective-permute-done.2 = bf16[224,128]{1,0:T(8,128)(2,1)S(1)} collective-permute-done((bf16[224,128]{1,0:T(8,128)(2,1)S(1)}, bf16[224,128]{1,0:T(8,128)(2,1)S(1)}, u32[]{:S(2)}, u32[]{:S(2)}) %collective-permute-start.2) | collective-permute-done | bytes 57376 | tf_op jit(solution)/shard_map/ppermute | solution.py:578
  12.3 0.0 copy-start.7
  12.3 0.0 copy-start.8
  12.3 0.0 copy-start.9
  12.3 0.0 copy-start.10
  12.3 1.0 %correct_pack.1 = (bf16[376,128]{1,0:T(8,128)(2,1)S(1)}, bf16[376,128]{1,0:T(8,128)(2,1)S(1)}, bf16[376,128]{1,0:T(8,128)(2,1)S(1)}, bf16[376,128]{1,0:T(8,128)(...) custom-call(bf16[9,256,128]{2,1,0:T(8,128)(2,1)S(1)} %copy-done, ...), custom_call_target="tpu_custom_call" | custom-call | tf_op jit(solution)/shard_map/correct_pack/pallas_call | solution.py:541
  13.3 4.8 %collective-permute-start.3 = (bf16[376,128]{1,0:T(8,128)(2,1)S(1)}, bf16[376,128]{1,0:T(8,128)(2,1)S(1)}, u32[]{:S(2)}, u32[]{:S(2)}) collective-permute-start(bf16[376,128]{1,0:T(8,128)(2,1)S(1)} %get-tuple-element.29), channel_id=1, source_target_pairs={{0,28},{2,30},{4,24},{6,26},{8,20},{10,22},{12,16},{14,18},{16,12}... | collective-permute-start | bytes 288776 | tf_op jit(solution)/shard_map/ppermute | solution.py:656
  18.1 0.2 collective-permute-start.4
  18.4 0.0 copy-start.5
  18.4 0.1 collective-permute-start.5
  18.5 1.9 %collective-permute-start.6 = (bf16[376,128]{1,0:T(8,128)(2,1)S(1)}, bf16[376,128]{1,0:T(8,128)(2,1)S(1)}, u32[]{:S(2)}, u32[]{:S(2)}) collective-permute-start(bf16[376,128]{1,0:T(8,128)(2,1)S(1)} %get-tuple-element.32), channel_id=1, source_target_pairs={{0,8},{2,10},{4,12},{6,14},{8,0},{10,2},{12,4},{14,6},{16,24},{18,... | collective-permute-start | bytes 288776 | tf_op jit(solution)/shard_map/ppermute | solution.py:656
  20.4 1.6 %collective-permute-start.7 = (bf16[376,128]{1,0:T(8,128)(2,1)S(1)}, bf16[376,128]{1,0:T(8,128)(2,1)S(1)}, u32[]{:S(2)}, u32[]{:S(2)}) collective-permute-start(bf16[376,128]{1,0:T(8,128)(2,1)S(1)} %get-tuple-element.33), channel_id=1, source_target_pairs={{0,4},{2,6},{4,0},{6,2},{8,12},{10,14},{12,8},{14,10},{16,20},{18,... | collective-permute-start | bytes 288776 | tf_op jit(solution)/shard_map/ppermute | solution.py:656
  22.0 0.0 collective-permute-done.3.refs_0_
  22.0 3.9 %collective-permute-start.8 = (bf16[376,128]{1,0:T(8,128)(2,1)S(1)}, bf16[376,128]{1,0:T(8,128)(2,1)S(1)}, u32[]{:S(2)}, u32[]{:S(2)}) collective-permute-start(bf16[376,128]{1,0:T(8,128)(2,1)S(1)} %get-tuple-element.34), channel_id=1, source_target_pairs={{0,20},{2,22},{4,16},{6,18},{8,28},{10,30},{12,24},{14,26},{16,4},... | collective-permute-start | bytes 288776 | tf_op jit(solution)/shard_map/ppermute | solution.py:656
  25.9 0.0 collective-permute-done.4.refs_1_
  25.9 2.1 %collective-permute-start.9 = (bf16[376,128]{1,0:T(8,128)(2,1)S(1)}, bf16[376,128]{1,0:T(8,128)(2,1)S(1)}, u32[]{:S(2)}, u32[]{:S(2)}) collective-permute-start(bf16[376,128]{1,0:T(8,128)(2,1)S(1)} %get-tuple-element.35), channel_id=1, source_target_pairs={{0,16},{2,18},{4,20},{6,22},{8,24},{10,26},{12,28},{14,30},{16,0},... | collective-permute-start | bytes 288776 | tf_op jit(solution)/shard_map/ppermute | solution.py:656
  28.0 0.1 copy.18
  28.1 0.2 weight_pack.1
  28.3 0.1 core_pack.2
  28.4 0.1 collective-permute-start.10
  28.5 4.1 %collective-permute-done.8.refs_1_.refs_5_ = bf16[376,128]{1,0:T(8,128)(2,1)S(1)} collective-permute-done((bf16[376,128]{1,0:T(8,128)(2,1)S(1)}, bf16[376,128]{1,0:T(8,128)(2,1)S(1)}, u32[]{:S(2)}, u32[]{:S(2)}) %collective-permute-start.8) | collective-permute-done | bytes 96288 | tf_op jit(solution)/shard_map/ppermute | solution.py:656
  32.6 1.1 %collective-permute-done.9.refs_2_.refs_6_ = bf16[376,128]{1,0:T(8,128)(2,1)S(1)} collective-permute-done((bf16[376,128]{1,0:T(8,128)(2,1)S(1)}, bf16[376,128]{1,0:T(8,128)(2,1)S(1)}, u32[]{:S(2)}, u32[]{:S(2)}) %collective-permute-start.9) | collective-permute-done | bytes 96288 | tf_op jit(solution)/shard_map/ppermute | solution.py:656
  33.6 0.1 core_pack.3
  33.7 0.1 collective-permute-start.11
  33.8 1.5 %collective-permute-done.11.refs_9_ = bf16[4,224,128]{2,1,0:T(8,128)(2,1)S(1)} collective-permute-done((bf16[4,224,128]{2,1,0:T(8,128)(2,1)S(1)}, bf16[4,224,128]{2,1,0:T(8,128)(2,1)S(1)}, u32[]{:S(2)}, u32[]{:S(2)}) %collective-permute-start.11) | collective-permute-done | bytes 229408 | tf_op jit(solution)/shard_map/ppermute | solution.py:672
  35.2 5.0 %stack.13 = f32[16,128]{1,0:T(8,128)} custom-call(bf16[376,128]{1,0:T(8,128)(2,1)S(1)} %collective-permute-done.3.refs_0_, bf16[376,128]{1,0:T(8,128)(2,1)S(1)} %collective-permute-done.4.refs_1_, bf16[376,128]{1,0:T(8,128)(2,1)S(1)} %collective-permute-done.5.refs_2_, bf16[376,128]{1,0:T(8,128)(2,1)S(1)} %collective-permute-done.6.refs_3_, ...), custom_call_target="tpu_custom_call" | custom-call | tf_op jit(solution)/shard_map/stack/pallas_call | solution.py:541
  (26 shorter events, 0.1 us)
Async XLA Ops:
  0.0 5.0 %copy-start = (bf16[9,256,128]{2,1,0:T(8,128)(2,1)S(1)}, bf16[9,256,128]{2,1,0:T(8,128)(2,1)}, u32[]{:S(2)}) copy-start(bf16[9,256,128]{2,1,0:T(8,128)(2,1)} %maps_ref.3) | copy-start | bytes 1769476
  1.0 11.3 %collective-permute-start.1 = (bf16[640,128]{1,0:T(8,128)(2,1)S(1)}, bf16[640,128]{1,0:T(8,128)(2,1)S(1)}, u32[]{:S(2)}, u32[]{:S(2)}) collective-permute-start(bf16[640,128]{1,0:T(8,128)(2,1)S(1)} %bitcast.17), channel_id=1, source_target_pairs={{0,1},{1,0},{2,3},{3,2},{4,5},{5,4},{6,7},{7,6},{8,9},{9,8},{10,11... | collective-permute-start | bytes 491528 | tf_op jit(solution)/shard_map/ppermute | solution.py:578
  5.0 7.3 %collective-permute-start = (bf16[512,128]{1,0:T(8,128)(2,1)S(1)}, bf16[512,128]{1,0:T(8,128)(2,1)S(1)}, u32[]{:S(2)}, u32[]{:S(2)}) collective-permute-start(bf16[512,128]{1,0:T(8,128)(2,1)S(1)} %bitcast.18), channel_id=1, source_target_pairs={{0,1},{1,0},{2,3},{3,2},{4,5},{5,4},{6,7},{7,6},{8,9},{9,8},{10,11... | collective-permute-start | bytes 393224 | tf_op jit(solution)/shard_map/ppermute | solution.py:578
  5.5 6.8 %collective-permute-start.2 = (bf16[224,128]{1,0:T(8,128)(2,1)S(1)}, bf16[224,128]{1,0:T(8,128)(2,1)S(1)}, u32[]{:S(2)}, u32[]{:S(2)}) collective-permute-start(bf16[224,128]{1,0:T(8,128)(2,1)S(1)} %bitcast.16), channel_id=1, source_target_pairs={{0,1},{1,0},{2,3},{3,2},{4,5},{5,4},{6,7},{7,6},{8,9},{9,8},{10,11... | collective-permute-start | bytes 172040 | tf_op jit(solution)/shard_map/ppermute | solution.py:578
  7.6 20.5 %copy-start.1 = (bf16[2,2,64,64,3,3]{3,2,5,4,1,0:T(8,128)(2,1)S(1)}, bf16[2,2,64,64,3,3]{3,2,5,4,1,0:T(8,128)(2,1)}, u32[]{:S(2)}) copy-start(bf16[2,2,64,64,3,3]{3,2,5,4,1,0:T(8,128)(2,1)} %param.14) | copy-start | bytes 884740
  12.3 6.1 %copy-start.6 = (s32[5504]{0:T(1024)S(1)}, s32[5504]{0:T(1024)}, u32[]{:S(2)}) copy-start(s32[5504]{0:T(1024)} %constant.51.clone) | copy-start | bytes 66052
  12.3 6.1 %copy-start.7 = (s32[5504]{0:T(1024)S(1)}, s32[5504]{0:T(1024)}, u32[]{:S(2)}) copy-start(s32[5504]{0:T(1024)} %constant.50.clone) | copy-start | bytes 66052
  12.3 15.7 %copy-start.8 = (f32[2,2,64]{2,1,0:T(2,128)S(1)}, f32[2,2,64]{2,1,0:T(2,128)}, u32[]{:S(2)}) copy-start(f32[2,2,64]{2,1,0:T(2,128)} %param.15) | copy-start | bytes 3076
  12.3 15.7 %copy-start.9 = (f32[64]{0:T(128)S(1)}, f32[64]{0:T(128)}, u32[]{:S(2)}) copy-start(f32[64]{0:T(128)} %param.16) | copy-start | bytes 772
  12.3 15.7 %copy-start.10 = (f32[64]{0:T(128)S(1)}, f32[64]{0:T(128)}, u32[]{:S(2)}) copy-start(f32[64]{0:T(128)} %param.13) | copy-start | bytes 772
  13.3 8.7 %collective-permute-start.3 = (bf16[376,128]{1,0:T(8,128)(2,1)S(1)}, bf16[376,128]{1,0:T(8,128)(2,1)S(1)}, u32[]{:S(2)}, u32[]{:S(2)}) collective-permute-start(bf16[376,128]{1,0:T(8,128)(2,1)S(1)} %get-tuple-element.29), channel_id=1, source_target_pairs={{0,28},{2,30},{4,24},{6,26},{8,20},{10,22},{12,16},{14,18},{16,12}... | collective-permute-start | bytes 288776 | tf_op jit(solution)/shard_map/ppermute | solution.py:656
  18.1 10.0 %copy-start.3 = (bf16[144,160]{1,0:T(8,128)(2,1)S(1)}, bf16[144,160]{1,0:T(8,128)(2,1)}, u32[]{:S(2)}) copy-start(bf16[144,160]{1,0:T(8,128)(2,1)} %constant.49.clone.slot_ref) | copy-start | bytes 138244
  18.1 10.0 %copy-start.4 = (bf16[144,144]{1,0:T(8,128)(2,1)S(1)}, bf16[144,144]{1,0:T(8,128)(2,1)}, u32[]{:S(2)}) copy-start(bf16[144,144]{1,0:T(8,128)(2,1)} %constant.48.clone.set_ref) | copy-start | bytes 124420
  18.1 7.8 %collective-permute-start.4 = (bf16[376,128]{1,0:T(8,128)(2,1)S(1)}, bf16[376,128]{1,0:T(8,128)(2,1)S(1)}, u32[]{:S(2)}, u32[]{:S(2)}) collective-permute-start(bf16[376,128]{1,0:T(8,128)(2,1)S(1)} %get-tuple-element.30), channel_id=1, source_target_pairs={{0,24},{2,26},{4,28},{6,30},{8,16},{10,18},{12,20},{14,22},{16,8},... | collective-permute-start | bytes 288776 | tf_op jit(solution)/shard_map/ppermute | solution.py:656
  18.4 9.7 %copy-start.5 = (bf16[64,144]{1,0:T(8,128)(2,1)S(1)}, bf16[64,144]{1,0:T(8,128)(2,1)}, u32[]{:S(2)}) copy-start(bf16[64,144]{1,0:T(8,128)(2,1)} %proj_ref.1) | copy-start | bytes 55300
  18.4 9.9 %collective-permute-start.5 = (bf16[376,128]{1,0:T(8,128)(2,1)S(1)}, bf16[376,128]{1,0:T(8,128)(2,1)S(1)}, u32[]{:S(2)}, u32[]{:S(2)}) collective-permute-start(bf16[376,128]{1,0:T(8,128)(2,1)S(1)} %get-tuple-element.31), channel_id=1, source_target_pairs={{0,12},{2,14},{4,8},{6,10},{8,4},{10,6},{12,0},{14,2},{16,28},{18,... | collective-permute-start | bytes 288776 | tf_op jit(solution)/shard_map/ppermute | solution.py:656
  18.5 9.8 %collective-permute-start.6 = (bf16[376,128]{1,0:T(8,128)(2,1)S(1)}, bf16[376,128]{1,0:T(8,128)(2,1)S(1)}, u32[]{:S(2)}, u32[]{:S(2)}) collective-permute-start(bf16[376,128]{1,0:T(8,128)(2,1)S(1)} %get-tuple-element.32), channel_id=1, source_target_pairs={{0,8},{2,10},{4,12},{6,14},{8,0},{10,2},{12,4},{14,6},{16,24},{18,... | collective-permute-start | bytes 288776 | tf_op jit(solution)/shard_map/ppermute | solution.py:656
  20.4 8.1 %collective-permute-start.7 = (bf16[376,128]{1,0:T(8,128)(2,1)S(1)}, bf16[376,128]{1,0:T(8,128)(2,1)S(1)}, u32[]{:S(2)}, u32[]{:S(2)}) collective-permute-start(bf16[376,128]{1,0:T(8,128)(2,1)S(1)} %get-tuple-element.33), channel_id=1, source_target_pairs={{0,4},{2,6},{4,0},{6,2},{8,12},{10,14},{12,8},{14,10},{16,20},{18,... | collective-permute-start | bytes 288776 | tf_op jit(solution)/shard_map/ppermute | solution.py:656
  22.0 10.6 %collective-permute-start.8 = (bf16[376,128]{1,0:T(8,128)(2,1)S(1)}, bf16[376,128]{1,0:T(8,128)(2,1)S(1)}, u32[]{:S(2)}, u32[]{:S(2)}) collective-permute-start(bf16[376,128]{1,0:T(8,128)(2,1)S(1)} %get-tuple-element.34), channel_id=1, source_target_pairs={{0,20},{2,22},{4,16},{6,18},{8,28},{10,30},{12,24},{14,26},{16,4},... | collective-permute-start | bytes 288776 | tf_op jit(solution)/shard_map/ppermute | solution.py:656
  25.9 7.7 %collective-permute-start.9 = (bf16[376,128]{1,0:T(8,128)(2,1)S(1)}, bf16[376,128]{1,0:T(8,128)(2,1)S(1)}, u32[]{:S(2)}, u32[]{:S(2)}) collective-permute-start(bf16[376,128]{1,0:T(8,128)(2,1)S(1)} %get-tuple-element.35), channel_id=1, source_target_pairs={{0,16},{2,18},{4,20},{6,22},{8,24},{10,26},{12,28},{14,30},{16,0},... | collective-permute-start | bytes 288776 | tf_op jit(solution)/shard_map/ppermute | solution.py:656
  28.4 5.4 %collective-permute-start.10 = (bf16[4,224,128]{2,1,0:T(8,128)(2,1)S(1)}, bf16[4,224,128]{2,1,0:T(8,128)(2,1)S(1)}, u32[]{:S(2)}, u32[]{:S(2)}) collective-permute-start(bf16[4,224,128]{2,1,0:T(8,128)(2,1)S(1)} %core_pack.2), channel_id=1, source_target_pairs={{0,2},{2,0},{4,6},{6,4},{8,10},{10,8},{12,14},{14,12},{16,18},{18,... | collective-permute-start | bytes 688136 | tf_op jit(solution)/shard_map/ppermute | solution.py:672
  33.6 1.6 %copy-start.2 = (bf16[1,128,384]{2,1,0:T(8,128)(2,1)S(1)}, bf16[1,128,384]{2,1,0:T(8,128)(2,1)}, u32[]{:S(2)}) copy-start(bf16[1,128,384]{2,1,0:T(8,128)(2,1)} %constant.52.clone.refs_15_) | copy-start | bytes 294916
  33.7 1.6 %collective-permute-start.11 = (bf16[4,224,128]{2,1,0:T(8,128)(2,1)S(1)}, bf16[4,224,128]{2,1,0:T(8,128)(2,1)S(1)}, u32[]{:S(2)}, u32[]{:S(2)}) collective-permute-start(bf16[4,224,128]{2,1,0:T(8,128)(2,1)S(1)} %core_pack.3), channel_id=1, source_target_pairs={{0,2},{2,0},{4,6},{6,4},{8,10},{10,8},{12,14},{14,12},{16,18},{18,... | collective-permute-start | bytes 688136 | tf_op jit(solution)/shard_map/ppermute | solution.py:672

commit v18 on v16

--- a/solution.py
+++ b/solution.py
@@ -227,8 +227,8 @@
 
 
 def correct_pack(plan, maps_ref, recv_ref, tail_ref, sums_ref, edge_ref, *refs):
-    *out_refs, field_ref, turned_ref = refs
-    me, chip = lax.axis_index("tile"), lax.axis_index("head") // 2
+    *out_refs, field_ref, stack_ref, turned_ref = refs
+    me = lax.axis_index("tile")
     count, cols, width, tiles = plan.maps, plan.cols, plan.width, plan.tiles
     head, edge, halo = plan.map_rows, plan.edge_rows, plan.halo
     tails = [tail_ref[k].astype(F32) for k in range(tiles - 1)]
@@ -259,12 +259,13 @@
         == lax.broadcasted_iota(jnp.int32, (cols, cols), 1)
     ).astype(F32).astype(BF16)
     margin = 8 + halo
-    mirrors = []
+    faces = []
     for b in range(tiles):
         shift = lax.rem(b - me + tiles, tiles)
         other = recv_ref[jnp.maximum(shift - 1, 0)]
         own = [maps_ref[k, b * cols : (b + 1) * cols, :] for k in range(count)]
-        mirrors.append(across(eye, jnp.where(shift == 0, jnp.concatenate(own, axis=0), other)))
+        faces.append(jnp.where(shift == 0, jnp.concatenate(own, axis=0), other))
+    mirrors = across(eye, jnp.concatenate(faces, axis=0))
     for index in range(count):
         origin = index * plan.pitch
         field_ref[origin : origin + margin, :] = jnp.zeros((margin, cols), F32)
@@ -273,7 +274,8 @@
         )
         for b in range(tiles):
             own = maps_ref[index, b * cols : (b + 1) * cols, :]
-            mirror = mirrors[b][:, index * cols : (index + 1) * cols]
+            place = (b * count + index) * cols
+            mirror = mirrors[:, place : place + cols]
             column = turned_ref[b * cols : (b + 1) * cols, index : index + 1]
             field_ref[origin + margin + b * cols : origin + margin + (b + 1) * cols, :] = (
                 own.astype(F32) + mirror - column * mine[index : index + 1]
@@ -301,17 +303,26 @@
         strip[k * plan.edges : (k + 1) * plan.edges] - beside[:, k : k + 1] * wide[k : k + 1]
         for k in range(count)
     ]
-    rows, slots = plan.rows, plan.slots
-    stacks = []
-    for slot in range(slots):
+    for slot in range(plan.slots):
         members = []
         for group in range(plan.groups):
-            k = group * slots + slot
+            k = group * plan.slots + slot
             members.append(lines[k] if k < count else jnp.zeros((plan.edges, width), F32))
-        stacks.append(jnp.concatenate(members, axis=0))
+        stack_ref[slot] = jnp.concatenate(members, axis=0)
+    pack(plan, step_order(plan)[: len(out_refs)], out_refs, field_ref, stack_ref)
+
+
+def pack_rest(plan, field_ref, stack_ref, *out_refs):
+    pack(plan, step_order(plan)[-len(out_refs) :], out_refs, field_ref, stack_ref)
+
+
+def pack(plan, steps, out_refs, field_ref, stack_ref):
+    chip = lax.axis_index("head") // 2
+    count, cols, width, halo = plan.maps, plan.cols, plan.width, plan.halo
+    rows, slots = plan.rows, plan.slots
     lane = lax.broadcasted_iota(jnp.int32, (plan.side_rows, cols), 1)
     spare = plan.block_rows - plan.lead - plan.half_rows
-    for step, out_ref in zip(step_order(plan), out_refs):
+    for step, out_ref in zip(steps, out_refs):
         first = partner(chip, step, plan.chips) * 2 * plan.band
 
         def section(begin, size):
@@ -330,7 +341,7 @@
             side = jnp.zeros((plan.side_rows, cols), F32)
             for slot in range(slots):
                 amount = lax.rem(slot * rows + halo + width - core * plan.band - first, width)
-                moved = pltpu.roll(stacks[slot], amount, 1)[:, :cols]
+                moved = pltpu.roll(stack_ref[slot], amount, 1)[:, :cols]
                 side = jnp.where((lane >= slot * rows) & (lane < (slot + 1) * rows), moved, side)
             sides.append(side)
         pieces = section(0, lone) + sides[:1] + section(lone, shared)
@@ -637,12 +648,20 @@
     spots = jnp.asarray(np.stack(spots), BF16)
 
     chips = plan.chips
-    blocks = call(
+    ahead = chips // 4
+    *blocks, field, stacks = call(
         functools.partial(correct_pack, plan),
         "correct_pack",
         [attention, received, tails, sums, edge],
-        [array(BF16, plan.block_rows, cols)] * chips,
-        [pltpu.VMEM((maps * plan.pitch, cols), F32), pltpu.VMEM((width, LANES), F32)],
+        [array(BF16, plan.block_rows, cols)] * ahead
+        + [array(F32, maps * plan.pitch, cols), array(F32, plan.slots, plan.side_rows, width)],
+        [pltpu.VMEM((width, LANES), F32)],
+    )
+    blocks += call(
+        functools.partial(pack_rest, plan),
+        "pack_rest",
+        [field, stacks],
+        [array(BF16, plan.block_rows, cols)] * (chips - ahead),
     )
     arrived = {}
     for step, block in zip(step_order(plan), blocks):
@@ -672,8 +691,8 @@
         [array(F32, plan.band, cols)],
         [
             pltpu.VMEM((heads * 8 * plan.sets * plan.rows, cols), F32),
-            pltpu.VMEM((heads * max(plan.rest, 1) * plan.rows, cols), F32),
-            pltpu.VMEM((heads * plan.side_rows, cols), F32),
+            pltpu.VMEM(((heads * plan.rest + 1) * plan.rows, cols), F32),
+            pltpu.VMEM(((heads + 1) * plan.side_rows, cols), F32),
             pltpu.VMEM((feat, plan.lanes), BF16),
             pltpu.VMEM((feat, plan.lanes), BF16),
             pltpu.VMEM((3 * feat, plan.lanes), F32),

time: 40.1 us -> 39.7 us (0.990)
  local copies, waits for them, and re-layouts: 1.22 us -> 2.29 us
  waiting for transfers between devices: 14.2 us -> 13.2 us
    ppermute x2, waiting for transfers between devices: 7.65 us -> 6.54 us  [mirror(): lax.ppermute(block(s), 'tile', [(i, (i + s) % tiles) for i in range(tiles)])]
    unnamed x22 -> x24, local copies, waits for them, and re-layouts: 0.05 us -> 1.13 us
    pallas_call x6 -> x7, Pallas kernels: 6.4 us -> 6.38 us  [call(): pl.pallas_call(kernel, out_shape=[pltpu.VMEM(x.shape, x.dtype) if held_ou...]
  transfers between devices with their start and end apart: 11 -> 11, of which waited for: 4 -> 5; matrix products, arithmetic and copies ran while one was open for 0% -> 0% of each run, Pallas kernels for 2% -> 3%
where the time goes in v18:
time: 39.7 us; the launch traced here: 39.5 us
  starting transfers between devices  17.5 us (44%)
  waiting for transfers between devices  13.2 us (33%)
  Pallas kernels  6.38 us (16%)
  local copies, waits for them, and re-layouts  2.29 us (6%)
    ppermute x7, starting transfers between devices, on_device(): arrived[step] = lax.ppermute(block, 'head', pairs) if step else block  14.2 us
    ppermute x2, waiting for transfers between devices, mirror(): lax.ppermute(block(s), 'tile', [(i, (i + s) % tiles) for i in range(tiles)])  6.54 us
    pallas_call x7, Pallas kernels, call(): pl.pallas_call(kernel, out_shape=[pltpu.VMEM(x.shape, x.dtype) if held_ou...  6.38 us
    ppermute x7, waiting for transfers between devices, on_device(): arrived[step] = lax.ppermute(block, 'head', pairs) if step else block  5.18 us
    ppermute x2, starting transfers between devices, mirror(): lax.ppermute(block(s), 'tile', [(i, (i + s) % tiles) for i in range(tiles)])  3.11 us
    ppermute x2, waiting for transfers between devices, on_device(): lax.ppermute(packed, 'head', [(i, i ^ 1) for i in range(heads)])  1.47 us
    unnamed x24, local copies, waits for them, and re-layouts  1.13 us
    dynamic_slice x1, local copies, waits for them, and re-layouts, facing(): lax.dynamic_slice_in_dim(attention, (me + s) % tiles * cols, cols, 1)  1.05 us
  transfers between devices with their start and end apart: 11, of which 5 were waited for; matrix products, arithmetic and copies ran while one was open for 0% of the time, Pallas kernels for 3%

profile of v18, /device:TPU:0, one launch (start us, length us, event | category | flops | bytes accessed | tf_op | source)
XLA Modules:
  0.0 39.5 jit_solution(9855394277338141371)
XLA Ops:
  0.0 1.1 %constant_dynamic-slice_fusion = bf16[9,128,128]{2,1,0:T(8,128)(2,1)S(1)} fusion(bf16[9,256,128]{2,1,0:T(8,128)(2,1)} %maps_ref.3, s32[]{:T(128)S(6)} %select_n.11), kind=kLoop, calls=%fused_computation.9 | loop fusion | bytes 589828 | tf_op jit(solution)/shard_map/dynamic_slice | solution.py:594
  1.1 3.0 %collective-permute-start = (bf16[1152,128]{1,0:T(8,128)(2,1)S(1)}, bf16[1152,128]{1,0:T(8,128)(2,1)S(1)}, u32[]{:S(2)}, u32[]{:S(2)}) collective-permute-start(bf16[1152,128]{1,0:T(8,128)(2,1)S(1)} %bitcast.14), channel_id=1, source_target_pairs={{0,1},{1,0},{2,3},{3,2},{4,5},{5,4},{6,7},{7,6},{8,9},{9,8},{10,11... | collective-permute-start | bytes 884744 | tf_op jit(solution)/shard_map/ppermute | solution.py:588
  4.1 1.1 %copy-done = bf16[9,256,128]{2,1,0:T(8,128)(2,1)S(1)} copy-done((bf16[9,256,128]{2,1,0:T(8,128)(2,1)S(1)}, bf16[9,256,128]{2,1,0:T(8,128)(2,1)}, u32[]{:S(2)}) %copy-start) | copy-done | bytes 589848
  5.2 0.5 %mirror_pack.1 = (bf16[1,224,128]{2,1,0:T(8,128)(2,1)S(1)}, f32[16,256]{1,0:T(8,128)S(1)}, f32[40,128]{1,0:T(8,128)S(1)}) custom-call(bf16[9,256,128]{2,1,0:T(8,128)(2,1)S(1)} %copy-done), custom_call_target="tpu_custom_call" | custom-call | tf_op jit(solution)/shard_map/mirror_pack/pallas_call | solution.py:551
  5.6 0.0 copy-start.9
  5.6 0.0 copy-start.11
  5.7 0.0 copy-start.2
  5.7 0.0 copy-start.4
  5.7 0.0 copy-start.5
  5.7 0.1 collective-permute-start.1
  5.8 6.5 %collective-permute-done.1 = bf16[224,128]{1,0:T(8,128)(2,1)S(1)} collective-permute-done((bf16[224,128]{1,0:T(8,128)(2,1)S(1)}, bf16[224,128]{1,0:T(8,128)(2,1)S(1)}, u32[]{:S(2)}, u32[]{:S(2)}) %collective-permute-start.1) | collective-permute-done | bytes 57376 | tf_op jit(solution)/shard_map/ppermute | solution.py:588
  12.3 0.6 %correct_pack.1 = (bf16[376,128]{1,0:T(8,128)(2,1)S(1)}, bf16[376,128]{1,0:T(8,128)(2,1)S(1)}, f32[2529,128]{1,0:T(8,128)S(1)}, f32[5,8,256]{2,1,0:T(8,128)S(1)}) custom-call(bf16[9,256,128]{2,1,0:T(8,128)(2,1)S(1)} %copy-done.1, bf16[1,1152,128]{2,1,0:T(8,128)(2,1)S(1)} %bitcast.10, bf16[1,224,128]{2,1,0:T(8,128)(2,1)S(1)} %bitcast.12, ...), custom_call_target="tpu_custom_call" | custom-call | tf_op jit(solution)/shard_map/correct_pack/pallas_call | solution.py:551
  13.0 4.8 %collective-permute-start.2 = (bf16[376,128]{1,0:T(8,128)(2,1)S(1)}, bf16[376,128]{1,0:T(8,128)(2,1)S(1)}, u32[]{:S(2)}, u32[]{:S(2)}) collective-permute-start(bf16[376,128]{1,0:T(8,128)(2,1)S(1)} %get-tuple-element.31), channel_id=1, source_target_pairs={{0,28},{2,30},{4,24},{6,26},{8,20},{10,22},{12,16},{14,18},{16,12}... | collective-permute-start | bytes 288776 | tf_op jit(solution)/shard_map/ppermute | solution.py:669
  17.8 0.2 collective-permute-start.3
  18.0 0.3 pack_rest.1
  18.4 0.0 copy-start.3
  18.4 0.1 collective-permute-start.4
  18.4 1.9 %collective-permute-start.5 = (bf16[376,128]{1,0:T(8,128)(2,1)S(1)}, bf16[376,128]{1,0:T(8,128)(2,1)S(1)}, u32[]{:S(2)}, u32[]{:S(2)}) collective-permute-start(bf16[376,128]{1,0:T(8,128)(2,1)S(1)} %get-tuple-element.36), channel_id=1, source_target_pairs={{0,8},{2,10},{4,12},{6,14},{8,0},{10,2},{12,4},{14,6},{16,24},{18,... | collective-permute-start | bytes 288776 | tf_op jit(solution)/shard_map/ppermute | solution.py:669
  20.3 1.6 %collective-permute-start.6 = (bf16[376,128]{1,0:T(8,128)(2,1)S(1)}, bf16[376,128]{1,0:T(8,128)(2,1)S(1)}, u32[]{:S(2)}, u32[]{:S(2)}) collective-permute-start(bf16[376,128]{1,0:T(8,128)(2,1)S(1)} %get-tuple-element.37), channel_id=1, source_target_pairs={{0,4},{2,6},{4,0},{6,2},{8,12},{10,14},{12,8},{14,10},{16,20},{18,... | collective-permute-start | bytes 288776 | tf_op jit(solution)/shard_map/ppermute | solution.py:669
  21.9 3.6 %collective-permute-start.7 = (bf16[376,128]{1,0:T(8,128)(2,1)S(1)}, bf16[376,128]{1,0:T(8,128)(2,1)S(1)}, u32[]{:S(2)}, u32[]{:S(2)}) collective-permute-start(bf16[376,128]{1,0:T(8,128)(2,1)S(1)} %get-tuple-element.38), channel_id=1, source_target_pairs={{0,20},{2,22},{4,16},{6,18},{8,28},{10,30},{12,24},{14,26},{16,4},... | collective-permute-start | bytes 288776 | tf_op jit(solution)/shard_map/ppermute | solution.py:669
  25.6 2.0 %collective-permute-start.8 = (bf16[376,128]{1,0:T(8,128)(2,1)S(1)}, bf16[376,128]{1,0:T(8,128)(2,1)S(1)}, u32[]{:S(2)}, u32[]{:S(2)}) collective-permute-start(bf16[376,128]{1,0:T(8,128)(2,1)S(1)} %get-tuple-element.39), channel_id=1, source_target_pairs={{0,16},{2,18},{4,20},{6,22},{8,24},{10,26},{12,28},{14,30},{16,0},... | collective-permute-start | bytes 288776 | tf_op jit(solution)/shard_map/ppermute | solution.py:669
  27.6 0.1 copy.18
  27.7 0.2 weight_pack.1
  27.9 0.4 %collective-permute-done.5.refs_3_ = bf16[376,128]{1,0:T(8,128)(2,1)S(1)} collective-permute-done((bf16[376,128]{1,0:T(8,128)(2,1)S(1)}, bf16[376,128]{1,0:T(8,128)(2,1)S(1)}, u32[]{:S(2)}, u32[]{:S(2)}) %collective-permute-start.5) | collective-permute-done | bytes 96288 | tf_op jit(solution)/shard_map/ppermute | solution.py:669
  28.3 0.1 core_pack.2
  28.4 0.1 collective-permute-start.9
  28.5 3.7 %collective-permute-done.7.refs_1_.refs_5_ = bf16[376,128]{1,0:T(8,128)(2,1)S(1)} collective-permute-done((bf16[376,128]{1,0:T(8,128)(2,1)S(1)}, bf16[376,128]{1,0:T(8,128)(2,1)S(1)}, u32[]{:S(2)}, u32[]{:S(2)}) %collective-permute-start.7) | collective-permute-done | bytes 96288 | tf_op jit(solution)/shard_map/ppermute | solution.py:669
  32.2 1.1 %collective-permute-done.8.refs_2_.refs_6_ = bf16[376,128]{1,0:T(8,128)(2,1)S(1)} collective-permute-done((bf16[376,128]{1,0:T(8,128)(2,1)S(1)}, bf16[376,128]{1,0:T(8,128)(2,1)S(1)}, u32[]{:S(2)}, u32[]{:S(2)}) %collective-permute-start.8) | collective-permute-done | bytes 96288 | tf_op jit(solution)/shard_map/ppermute | solution.py:669
  33.3 0.1 core_pack.3
  33.3 0.1 collective-permute-start.10
  33.4 1.5 %collective-permute-done.10.refs_9_ = bf16[4,224,128]{2,1,0:T(8,128)(2,1)S(1)} collective-permute-done((bf16[4,224,128]{2,1,0:T(8,128)(2,1)S(1)}, bf16[4,224,128]{2,1,0:T(8,128)(2,1)S(1)}, u32[]{:S(2)}, u32[]{:S(2)}) %collective-permute-start.10) | collective-permute-done | bytes 229408 | tf_op jit(solution)/shard_map/ppermute | solution.py:685
  34.9 4.7 %stack.9 = f32[16,128]{1,0:T(8,128)} custom-call(bf16[376,128]{1,0:T(8,128)(2,1)S(1)} %collective-permute-done.2.refs_0_, bf16[376,128]{1,0:T(8,128)(2,1)S(1)} %collective-permute-done.3.refs_1_, bf16[376,128]{1,0:T(8,128)(2,1)S(1)} %collective-permute-done.4.refs_2_, bf16[376,128]{1,0:T(8,128)(2,1)S(1)} %collective-permute-done.5.refs_3_, ...), custom_call_target="tpu_custom_call" | custom-call | tf_op jit(solution)/shard_map/stack/pallas_call | solution.py:551
  (26 shorter events, 0.1 us)
Async XLA Ops:
  0.0 18.0 %copy-start.7 = (s32[5504]{0:T(1024)S(1)}, s32[5504]{0:T(1024)}, u32[]{:S(2)}) copy-start(s32[5504]{0:T(1024)} %constant.47.clone) | copy-start | bytes 66052
  0.0 12.3 %copy-start.1 = (bf16[9,256,128]{2,1,0:T(8,128)(2,1)S(1)}, bf16[9,256,128]{2,1,0:T(8,128)(2,1)}, u32[]{:S(2)}) copy-start(bf16[9,256,128]{2,1,0:T(8,128)(2,1)} %maps_ref.3) | copy-start | bytes 1769476
  1.1 11.3 %collective-permute-start = (bf16[1152,128]{1,0:T(8,128)(2,1)S(1)}, bf16[1152,128]{1,0:T(8,128)(2,1)S(1)}, u32[]{:S(2)}, u32[]{:S(2)}) collective-permute-start(bf16[1152,128]{1,0:T(8,128)(2,1)S(1)} %bitcast.14), channel_id=1, source_target_pairs={{0,1},{1,0},{2,3},{3,2},{4,5},{5,4},{6,7},{7,6},{8,9},{9,8},{10,11... | collective-permute-start | bytes 884744 | tf_op jit(solution)/shard_map/ppermute | solution.py:588
  4.1 1.1 %copy-start = (bf16[9,256,128]{2,1,0:T(8,128)(2,1)S(1)}, bf16[9,256,128]{2,1,0:T(8,128)(2,1)}, u32[]{:S(2)}) copy-start(bf16[9,256,128]{2,1,0:T(8,128)(2,1)} %maps_ref.3) | copy-start | bytes 1769476
  5.2 12.9 %copy-start.8 = (s32[5504]{0:T(1024)S(1)}, s32[5504]{0:T(1024)}, u32[]{:S(2)}) copy-start(s32[5504]{0:T(1024)} %constant.48.clone) | copy-start | bytes 66052
  5.6 21.9 %copy-start.9 = (f32[2,2,64]{2,1,0:T(2,128)S(1)}, f32[2,2,64]{2,1,0:T(2,128)}, u32[]{:S(2)}) copy-start(f32[2,2,64]{2,1,0:T(2,128)} %param.15) | copy-start | bytes 3076
  5.6 21.9 %copy-start.10 = (f32[64]{0:T(128)S(1)}, f32[64]{0:T(128)}, u32[]{:S(2)}) copy-start(f32[64]{0:T(128)} %param.16) | copy-start | bytes 772
  5.6 21.9 %copy-start.11 = (f32[64]{0:T(128)S(1)}, f32[64]{0:T(128)}, u32[]{:S(2)}) copy-start(f32[64]{0:T(128)} %param.13) | copy-start | bytes 772
  5.7 22.1 %copy-start.2 = (bf16[2,2,64,64,3,3]{3,2,5,4,1,0:T(8,128)(2,1)S(1)}, bf16[2,2,64,64,3,3]{3,2,5,4,1,0:T(8,128)(2,1)}, u32[]{:S(2)}) copy-start(bf16[2,2,64,64,3,3]{3,2,5,4,1,0:T(8,128)(2,1)} %param.14) | copy-start | bytes 884740
  5.7 22.0 %copy-start.4 = (bf16[144,144]{1,0:T(8,128)(2,1)S(1)}, bf16[144,144]{1,0:T(8,128)(2,1)}, u32[]{:S(2)}) copy-start(bf16[144,144]{1,0:T(8,128)(2,1)} %constant.45.clone.set_ref) | copy-start | bytes 124420
  5.7 22.0 %copy-start.5 = (bf16[144,160]{1,0:T(8,128)(2,1)S(1)}, bf16[144,160]{1,0:T(8,128)(2,1)}, u32[]{:S(2)}) copy-start(bf16[144,160]{1,0:T(8,128)(2,1)} %constant.46.clone.slot_ref) | copy-start | bytes 138244
  5.7 22.0 %copy-start.6 = (bf16[64,144]{1,0:T(8,128)(2,1)S(1)}, bf16[64,144]{1,0:T(8,128)(2,1)}, u32[]{:S(2)}) copy-start(bf16[64,144]{1,0:T(8,128)(2,1)} %proj_ref.1) | copy-start | bytes 55300
  5.7 6.6 %collective-permute-start.1 = (bf16[224,128]{1,0:T(8,128)(2,1)S(1)}, bf16[224,128]{1,0:T(8,128)(2,1)S(1)}, u32[]{:S(2)}, u32[]{:S(2)}) collective-permute-start(bf16[224,128]{1,0:T(8,128)(2,1)S(1)} %bitcast.13), channel_id=1, source_target_pairs={{0,1},{1,0},{2,3},{3,2},{4,5},{5,4},{6,7},{7,6},{8,9},{9,8},{10,11... | collective-permute-start | bytes 172040 | tf_op jit(solution)/shard_map/ppermute | solution.py:588
  13.0 8.9 %collective-permute-start.2 = (bf16[376,128]{1,0:T(8,128)(2,1)S(1)}, bf16[376,128]{1,0:T(8,128)(2,1)S(1)}, u32[]{:S(2)}, u32[]{:S(2)}) collective-permute-start(bf16[376,128]{1,0:T(8,128)(2,1)S(1)} %get-tuple-element.31), channel_id=1, source_target_pairs={{0,28},{2,30},{4,24},{6,26},{8,20},{10,22},{12,16},{14,18},{16,12}... | collective-permute-start | bytes 288776 | tf_op jit(solution)/shard_map/ppermute | solution.py:669
  17.8 7.8 %collective-permute-start.3 = (bf16[376,128]{1,0:T(8,128)(2,1)S(1)}, bf16[376,128]{1,0:T(8,128)(2,1)S(1)}, u32[]{:S(2)}, u32[]{:S(2)}) collective-permute-start(bf16[376,128]{1,0:T(8,128)(2,1)S(1)} %get-tuple-element.32), channel_id=1, source_target_pairs={{0,24},{2,26},{4,28},{6,30},{8,16},{10,18},{12,20},{14,22},{16,8},... | collective-permute-start | bytes 288776 | tf_op jit(solution)/shard_map/ppermute | solution.py:669
  18.4 16.5 %copy-start.3 = (bf16[1,128,384]{2,1,0:T(8,128)(2,1)S(1)}, bf16[1,128,384]{2,1,0:T(8,128)(2,1)}, u32[]{:S(2)}) copy-start(bf16[1,128,384]{2,1,0:T(8,128)(2,1)} %constant.49.clone.refs_15_) | copy-start | bytes 294916
  18.4 9.5 %collective-permute-start.4 = (bf16[376,128]{1,0:T(8,128)(2,1)S(1)}, bf16[376,128]{1,0:T(8,128)(2,1)S(1)}, u32[]{:S(2)}, u32[]{:S(2)}) collective-permute-start(bf16[376,128]{1,0:T(8,128)(2,1)S(1)} %get-tuple-element.35), channel_id=1, source_target_pairs={{0,12},{2,14},{4,8},{6,10},{8,4},{10,6},{12,0},{14,2},{16,28},{18,... | collective-permute-start | bytes 288776 | tf_op jit(solution)/shard_map/ppermute | solution.py:669
  18.4 9.9 %collective-permute-start.5 = (bf16[376,128]{1,0:T(8,128)(2,1)S(1)}, bf16[376,128]{1,0:T(8,128)(2,1)S(1)}, u32[]{:S(2)}, u32[]{:S(2)}) collective-permute-start(bf16[376,128]{1,0:T(8,128)(2,1)S(1)} %get-tuple-element.36), channel_id=1, source_target_pairs={{0,8},{2,10},{4,12},{6,14},{8,0},{10,2},{12,4},{14,6},{16,24},{18,... | collective-permute-start | bytes 288776 | tf_op jit(solution)/shard_map/ppermute | solution.py:669
  20.3 8.2 %collective-permute-start.6 = (bf16[376,128]{1,0:T(8,128)(2,1)S(1)}, bf16[376,128]{1,0:T(8,128)(2,1)S(1)}, u32[]{:S(2)}, u32[]{:S(2)}) collective-permute-start(bf16[376,128]{1,0:T(8,128)(2,1)S(1)} %get-tuple-element.37), channel_id=1, source_target_pairs={{0,4},{2,6},{4,0},{6,2},{8,12},{10,14},{12,8},{14,10},{16,20},{18,... | collective-permute-start | bytes 288776 | tf_op jit(solution)/shard_map/ppermute | solution.py:669
  21.9 10.3 %collective-permute-start.7 = (bf16[376,128]{1,0:T(8,128)(2,1)S(1)}, bf16[376,128]{1,0:T(8,128)(2,1)S(1)}, u32[]{:S(2)}, u32[]{:S(2)}) collective-permute-start(bf16[376,128]{1,0:T(8,128)(2,1)S(1)} %get-tuple-element.38), channel_id=1, source_target_pairs={{0,20},{2,22},{4,16},{6,18},{8,28},{10,30},{12,24},{14,26},{16,4},... | collective-permute-start | bytes 288776 | tf_op jit(solution)/shard_map/ppermute | solution.py:669
  25.6 7.7 %collective-permute-start.8 = (bf16[376,128]{1,0:T(8,128)(2,1)S(1)}, bf16[376,128]{1,0:T(8,128)(2,1)S(1)}, u32[]{:S(2)}, u32[]{:S(2)}) collective-permute-start(bf16[376,128]{1,0:T(8,128)(2,1)S(1)} %get-tuple-element.39), channel_id=1, source_target_pairs={{0,16},{2,18},{4,20},{6,22},{8,24},{10,26},{12,28},{14,30},{16,0},... | collective-permute-start | bytes 288776 | tf_op jit(solution)/shard_map/ppermute | solution.py:669
  28.4 5.0 %collective-permute-start.9 = (bf16[4,224,128]{2,1,0:T(8,128)(2,1)S(1)}, bf16[4,224,128]{2,1,0:T(8,128)(2,1)S(1)}, u32[]{:S(2)}, u32[]{:S(2)}) collective-permute-start(bf16[4,224,128]{2,1,0:T(8,128)(2,1)S(1)} %core_pack.2), channel_id=1, source_target_pairs={{0,2},{2,0},{4,6},{6,4},{8,10},{10,8},{12,14},{14,12},{16,18},{18,... | collective-permute-start | bytes 688136 | tf_op jit(solution)/shard_map/ppermute | solution.py:685
  33.3 1.6 %collective-permute-start.10 = (bf16[4,224,128]{2,1,0:T(8,128)(2,1)S(1)}, bf16[4,224,128]{2,1,0:T(8,128)(2,1)S(1)}, u32[]{:S(2)}, u32[]{:S(2)}) collective-permute-start(bf16[4,224,128]{2,1,0:T(8,128)(2,1)S(1)} %core_pack.3), channel_id=1, source_target_pairs={{0,2},{2,0},{4,6},{6,4},{8,10},{10,8},{12,14},{14,12},{16,18},{18,... | collective-permute-start | bytes 688136 | tf_op jit(solution)/shard_map/ppermute | solution.py:685

commit v19 on v18

--- a/solution.py
+++ b/solution.py
@@ -500,44 +500,49 @@
             done += 1
         spans = [span for span in spans if span[0] + span[1] > done * LANES]
 
-    everything = slice(None)
-    for n in range(plan.convs):
+    everything, convs = slice(None), range(plan.convs)
+    slack = 2 * LANES + stride // LANES * LANES
+    lows = [(plan.start + (n + 1) * stride) // LANES * LANES for n in convs]
+    ends = [up(plan.start + (rows - n - 1) * stride - n - 1, LANES) for n in convs]
+    steps = -(-(ends[0] - lows[0]) // plan.chunk)
+    size = up(-(-(ends[0] - lows[0]) // steps), LANES)
+    lead = lows[0] + size + up(slack * (plan.convs - 1) // 2, LANES)
+    cuts = [[lows[n], *(lead + j * size - n * slack for j in range(steps - 1)), ends[n]] for n in convs]
+
+    def multiply(n, j):
         source = hidden_ref if n % 2 else stream_ref
-        low = (plan.start + (n + 1) * stride) // LANES * LANES
-        span = plan.start + (rows - n - 1) * stride - n - 1 - low
-        steps = -(-span // plan.chunk)
-        size = up(-(-span // steps), LANES)
-        offsets = vector_ref[:, n + 1 : n + 2]
-
-        def multiply(base, size):
-            window = jnp.concatenate(
-                [shifted(source, everything, base, d * stride, size) for d in (-1, 0, 1)], axis=0
-            )
-            taps_ref[:, lanes(base, size)] = dot(kernel_ref[n], window)
-
-        def finish(base):
-            here = lanes(base, size)
-            value = taps_ref[feat : 2 * feat, here]
-            value = value + shifted(taps_ref, slice(0, feat), base, -1, size)
-            value = value + shifted(taps_ref, slice(2 * feat, 3 * feat), base, 1, size)
-            value = value + offsets
-            keep = mask_ref[:, here] > 0
-            if n % 2 == 0:
-                value = jnp.where(value > 0, value, jnp.exp(jnp.minimum(value, 0.0)) - 1.0)
-                hidden_ref[:, here] = jnp.where(keep, value, 0.0).astype(BF16)
-                return
-            value = (stream_ref[:, here].astype(F32) + value).astype(BF16)
-            if n < plan.convs - 1:
-                stream_ref[:, here] = jnp.where(keep, value.astype(F32), 0.0).astype(BF16)
-                return
-            readout = vector_ref[:, plan.convs + 1 : plan.convs + 2]
-            logit_ref[0:1, here] = jnp.sum(value.astype(F32) * readout, axis=0, keepdims=True)
-
-        multiply(low, size + LANES)
-        for i in range(steps):
-            if i + 1 < steps:
-                multiply(low + (i + 1) * size + LANES, size)
-            finish(low + i * size)
+        base = cuts[n][j] + (LANES if j else 0)
+        size = cuts[n][j + 1] + LANES - base
+        window = jnp.concatenate(
+            [shifted(source, everything, base, d * stride, size) for d in (-1, 0, 1)], axis=0
+        )
+        taps_ref[:, lanes(base, size)] = dot(kernel_ref[n], window)
+
+    def finish(n, j):
+        base, size = cuts[n][j], cuts[n][j + 1] - cuts[n][j]
+        here = lanes(base, size)
+        value = taps_ref[feat : 2 * feat, here]
+        value = value + shifted(taps_ref, slice(0, feat), base, -1, size)
+        value = value + shifted(taps_ref, slice(2 * feat, 3 * feat), base, 1, size)
+        value = value + vector_ref[:, n + 1 : n + 2]
+        keep = mask_ref[:, here] > 0
+        if n % 2 == 0:
+            value = jnp.where(value > 0, value, jnp.exp(jnp.minimum(value, 0.0)) - 1.0)
+            hidden_ref[:, here] = jnp.where(keep, value, 0.0).astype(BF16)
+            return
+        value = (stream_ref[:, here].astype(F32) + value).astype(BF16)
+        if n < plan.convs - 1:
+            stream_ref[:, here] = jnp.where(keep, value.astype(F32), 0.0).astype(BF16)
+            return
+        readout = vector_ref[:, plan.convs + 1 : plan.convs + 2]
+        logit_ref[0:1, here] = jnp.sum(value.astype(F32) * readout, axis=0, keepdims=True)
+
+    for turn in range(plan.convs + steps - 1):
+        together = [(n, turn - n) for n in convs if 0 <= turn - n < steps]
+        for n, j in together:
+            multiply(n, j)
+        for n, j in together:
+            finish(n, j)
 
     for r in range(plan.band):
         begin = plan.start + (r + halo) * stride + halo

time: 39.7 us -> 40.1 us (1.010)
  Pallas kernels: 6.38 us -> 6.79 us
    pallas_call x7, Pallas kernels: 6.38 us -> 6.79 us  [call(): pl.pallas_call(kernel, out_shape=[pltpu.VMEM(x.shape, x.dtype) if held_ou...]
where the time goes in v19:
time: 40.1 us; the launch traced here: 40 us
  starting transfers between devices  17.5 us (44%)
  waiting for transfers between devices  13.2 us (33%)
  Pallas kernels  6.79 us (17%)
  local copies, waits for them, and re-layouts  2.29 us (6%)
    ppermute x7, starting transfers between devices, on_device(): arrived[step] = lax.ppermute(block, 'head', pairs) if step else block  14.2 us
    pallas_call x7, Pallas kernels, call(): pl.pallas_call(kernel, out_shape=[pltpu.VMEM(x.shape, x.dtype) if held_ou...  6.79 us
    ppermute x2, waiting for transfers between devices, mirror(): lax.ppermute(block(s), 'tile', [(i, (i + s) % tiles) for i in range(tiles)])  6.54 us
    ppermute x7, waiting for transfers between devices, on_device(): arrived[step] = lax.ppermute(block, 'head', pairs) if step else block  5.18 us
    ppermute x2, starting transfers between devices, mirror(): lax.ppermute(block(s), 'tile', [(i, (i + s) % tiles) for i in range(tiles)])  3.11 us
    ppermute x2, waiting for transfers between devices, on_device(): lax.ppermute(packed, 'head', [(i, i ^ 1) for i in range(heads)])  1.47 us
    unnamed x24, local copies, waits for them, and re-layouts  1.13 us
    dynamic_slice x1, local copies, waits for them, and re-layouts, facing(): lax.dynamic_slice_in_dim(attention, (me + s) % tiles * cols, cols, 1)  1.05 us
  transfers between devices with their start and end apart: 11, of which 5 were waited for; matrix products, arithmetic and copies ran while one was open for 0% of the time, Pallas kernels for 3%

profile of v19, /device:TPU:0, one launch (start us, length us, event | category | flops | bytes accessed | tf_op | source)
XLA Modules:
  0.0 40.0 jit_solution(17278453041746809020)
XLA Ops:
  0.0 1.1 %constant_dynamic-slice_fusion = bf16[9,128,128]{2,1,0:T(8,128)(2,1)S(1)} fusion(bf16[9,256,128]{2,1,0:T(8,128)(2,1)} %maps_ref.3, s32[]{:T(128)S(6)} %select_n.11), kind=kLoop, calls=%fused_computation.9 | loop fusion | bytes 589828 | tf_op jit(solution)/shard_map/dynamic_slice | solution.py:599
  1.1 3.0 %collective-permute-start = (bf16[1152,128]{1,0:T(8,128)(2,1)S(1)}, bf16[1152,128]{1,0:T(8,128)(2,1)S(1)}, u32[]{:S(2)}, u32[]{:S(2)}) collective-permute-start(bf16[1152,128]{1,0:T(8,128)(2,1)S(1)} %bitcast.14), channel_id=1, source_target_pairs={{0,1},{1,0},{2,3},{3,2},{4,5},{5,4},{6,7},{7,6},{8,9},{9,8},{10,11... | collective-permute-start | bytes 884744 | tf_op jit(solution)/shard_map/ppermute | solution.py:593
  4.1 1.1 %copy-done = bf16[9,256,128]{2,1,0:T(8,128)(2,1)S(1)} copy-done((bf16[9,256,128]{2,1,0:T(8,128)(2,1)S(1)}, bf16[9,256,128]{2,1,0:T(8,128)(2,1)}, u32[]{:S(2)}) %copy-start) | copy-done | bytes 589848
  5.2 0.5 %mirror_pack.1 = (bf16[1,224,128]{2,1,0:T(8,128)(2,1)S(1)}, f32[16,256]{1,0:T(8,128)S(1)}, f32[40,128]{1,0:T(8,128)S(1)}) custom-call(bf16[9,256,128]{2,1,0:T(8,128)(2,1)S(1)} %copy-done), custom_call_target="tpu_custom_call" | custom-call | tf_op jit(solution)/shard_map/mirror_pack/pallas_call | solution.py:556
  5.6 0.0 copy-start.9
  5.6 0.0 copy-start.11
  5.7 0.0 copy-start.2
  5.7 0.0 copy-start.4
  5.7 0.0 copy-start.5
  5.7 0.1 collective-permute-start.1
  5.8 6.5 %collective-permute-done.1 = bf16[224,128]{1,0:T(8,128)(2,1)S(1)} collective-permute-done((bf16[224,128]{1,0:T(8,128)(2,1)S(1)}, bf16[224,128]{1,0:T(8,128)(2,1)S(1)}, u32[]{:S(2)}, u32[]{:S(2)}) %collective-permute-start.1) | collective-permute-done | bytes 57376 | tf_op jit(solution)/shard_map/ppermute | solution.py:593
  12.3 0.6 %correct_pack.1 = (bf16[376,128]{1,0:T(8,128)(2,1)S(1)}, bf16[376,128]{1,0:T(8,128)(2,1)S(1)}, f32[2529,128]{1,0:T(8,128)S(1)}, f32[5,8,256]{2,1,0:T(8,128)S(1)}) custom-call(bf16[9,256,128]{2,1,0:T(8,128)(2,1)S(1)} %copy-done.1, bf16[1,1152,128]{2,1,0:T(8,128)(2,1)S(1)} %bitcast.10, bf16[1,224,128]{2,1,0:T(8,128)(2,1)S(1)} %bitcast.12, ...), custom_call_target="tpu_custom_call" | custom-call | tf_op jit(solution)/shard_map/correct_pack/pallas_call | solution.py:556
  13.0 4.8 %collective-permute-start.2 = (bf16[376,128]{1,0:T(8,128)(2,1)S(1)}, bf16[376,128]{1,0:T(8,128)(2,1)S(1)}, u32[]{:S(2)}, u32[]{:S(2)}) collective-permute-start(bf16[376,128]{1,0:T(8,128)(2,1)S(1)} %get-tuple-element.31), channel_id=1, source_target_pairs={{0,28},{2,30},{4,24},{6,26},{8,20},{10,22},{12,16},{14,18},{16,12}... | collective-permute-start | bytes 288776 | tf_op jit(solution)/shard_map/ppermute | solution.py:674
  17.8 0.2 collective-permute-start.3
  18.0 0.3 pack_rest.1
  18.4 0.0 copy-start.3
  18.4 0.1 collective-permute-start.4
  18.4 1.9 %collective-permute-start.5 = (bf16[376,128]{1,0:T(8,128)(2,1)S(1)}, bf16[376,128]{1,0:T(8,128)(2,1)S(1)}, u32[]{:S(2)}, u32[]{:S(2)}) collective-permute-start(bf16[376,128]{1,0:T(8,128)(2,1)S(1)} %get-tuple-element.36), channel_id=1, source_target_pairs={{0,8},{2,10},{4,12},{6,14},{8,0},{10,2},{12,4},{14,6},{16,24},{18,... | collective-permute-start | bytes 288776 | tf_op jit(solution)/shard_map/ppermute | solution.py:674
  20.3 1.6 %collective-permute-start.6 = (bf16[376,128]{1,0:T(8,128)(2,1)S(1)}, bf16[376,128]{1,0:T(8,128)(2,1)S(1)}, u32[]{:S(2)}, u32[]{:S(2)}) collective-permute-start(bf16[376,128]{1,0:T(8,128)(2,1)S(1)} %get-tuple-element.37), channel_id=1, source_target_pairs={{0,4},{2,6},{4,0},{6,2},{8,12},{10,14},{12,8},{14,10},{16,20},{18,... | collective-permute-start | bytes 288776 | tf_op jit(solution)/shard_map/ppermute | solution.py:674
  21.9 3.6 %collective-permute-start.7 = (bf16[376,128]{1,0:T(8,128)(2,1)S(1)}, bf16[376,128]{1,0:T(8,128)(2,1)S(1)}, u32[]{:S(2)}, u32[]{:S(2)}) collective-permute-start(bf16[376,128]{1,0:T(8,128)(2,1)S(1)} %get-tuple-element.38), channel_id=1, source_target_pairs={{0,20},{2,22},{4,16},{6,18},{8,28},{10,30},{12,24},{14,26},{16,4},... | collective-permute-start | bytes 288776 | tf_op jit(solution)/shard_map/ppermute | solution.py:674
  25.6 2.0 %collective-permute-start.8 = (bf16[376,128]{1,0:T(8,128)(2,1)S(1)}, bf16[376,128]{1,0:T(8,128)(2,1)S(1)}, u32[]{:S(2)}, u32[]{:S(2)}) collective-permute-start(bf16[376,128]{1,0:T(8,128)(2,1)S(1)} %get-tuple-element.39), channel_id=1, source_target_pairs={{0,16},{2,18},{4,20},{6,22},{8,24},{10,26},{12,28},{14,30},{16,0},... | collective-permute-start | bytes 288776 | tf_op jit(solution)/shard_map/ppermute | solution.py:674
  27.6 0.1 copy.18
  27.7 0.2 weight_pack.1
  27.9 0.4 %collective-permute-done.5.refs_3_ = bf16[376,128]{1,0:T(8,128)(2,1)S(1)} collective-permute-done((bf16[376,128]{1,0:T(8,128)(2,1)S(1)}, bf16[376,128]{1,0:T(8,128)(2,1)S(1)}, u32[]{:S(2)}, u32[]{:S(2)}) %collective-permute-start.5) | collective-permute-done | bytes 96288 | tf_op jit(solution)/shard_map/ppermute | solution.py:674
  28.3 0.1 core_pack.2
  28.4 0.1 collective-permute-start.9
  28.5 3.7 %collective-permute-done.7.refs_1_.refs_5_ = bf16[376,128]{1,0:T(8,128)(2,1)S(1)} collective-permute-done((bf16[376,128]{1,0:T(8,128)(2,1)S(1)}, bf16[376,128]{1,0:T(8,128)(2,1)S(1)}, u32[]{:S(2)}, u32[]{:S(2)}) %collective-permute-start.7) | collective-permute-done | bytes 96288 | tf_op jit(solution)/shard_map/ppermute | solution.py:674
  32.2 1.1 %collective-permute-done.8.refs_2_.refs_6_ = bf16[376,128]{1,0:T(8,128)(2,1)S(1)} collective-permute-done((bf16[376,128]{1,0:T(8,128)(2,1)S(1)}, bf16[376,128]{1,0:T(8,128)(2,1)S(1)}, u32[]{:S(2)}, u32[]{:S(2)}) %collective-permute-start.8) | collective-permute-done | bytes 96288 | tf_op jit(solution)/shard_map/ppermute | solution.py:674
  33.3 0.1 core_pack.3
  33.3 0.1 collective-permute-start.10
  33.4 1.5 %collective-permute-done.10.refs_9_ = bf16[4,224,128]{2,1,0:T(8,128)(2,1)S(1)} collective-permute-done((bf16[4,224,128]{2,1,0:T(8,128)(2,1)S(1)}, bf16[4,224,128]{2,1,0:T(8,128)(2,1)S(1)}, u32[]{:S(2)}, u32[]{:S(2)}) %collective-permute-start.10) | collective-permute-done | bytes 229408 | tf_op jit(solution)/shard_map/ppermute | solution.py:690
  34.9 5.1 %stack.9 = f32[16,128]{1,0:T(8,128)} custom-call(bf16[376,128]{1,0:T(8,128)(2,1)S(1)} %collective-permute-done.2.refs_0_, bf16[376,128]{1,0:T(8,128)(2,1)S(1)} %collective-permute-done.3.refs_1_, bf16[376,128]{1,0:T(8,128)(2,1)S(1)} %collective-permute-done.4.refs_2_, bf16[376,128]{1,0:T(8,128)(2,1)S(1)} %collective-permute-done.5.refs_3_, ...), custom_call_target="tpu_custom_call" | custom-call | tf_op jit(solution)/shard_map/stack/pallas_call | solution.py:556
  (26 shorter events, 0.1 us)
Async XLA Ops:
  0.0 18.0 %copy-start.7 = (s32[5504]{0:T(1024)S(1)}, s32[5504]{0:T(1024)}, u32[]{:S(2)}) copy-start(s32[5504]{0:T(1024)} %constant.47.clone) | copy-start | bytes 66052
  0.0 12.3 %copy-start.1 = (bf16[9,256,128]{2,1,0:T(8,128)(2,1)S(1)}, bf16[9,256,128]{2,1,0:T(8,128)(2,1)}, u32[]{:S(2)}) copy-start(bf16[9,256,128]{2,1,0:T(8,128)(2,1)} %maps_ref.3) | copy-start | bytes 1769476
  1.1 11.3 %collective-permute-start = (bf16[1152,128]{1,0:T(8,128)(2,1)S(1)}, bf16[1152,128]{1,0:T(8,128)(2,1)S(1)}, u32[]{:S(2)}, u32[]{:S(2)}) collective-permute-start(bf16[1152,128]{1,0:T(8,128)(2,1)S(1)} %bitcast.14), channel_id=1, source_target_pairs={{0,1},{1,0},{2,3},{3,2},{4,5},{5,4},{6,7},{7,6},{8,9},{9,8},{10,11... | collective-permute-start | bytes 884744 | tf_op jit(solution)/shard_map/ppermute | solution.py:593
  4.1 1.1 %copy-start = (bf16[9,256,128]{2,1,0:T(8,128)(2,1)S(1)}, bf16[9,256,128]{2,1,0:T(8,128)(2,1)}, u32[]{:S(2)}) copy-start(bf16[9,256,128]{2,1,0:T(8,128)(2,1)} %maps_ref.3) | copy-start | bytes 1769476
  5.2 12.9 %copy-start.8 = (s32[5504]{0:T(1024)S(1)}, s32[5504]{0:T(1024)}, u32[]{:S(2)}) copy-start(s32[5504]{0:T(1024)} %constant.48.clone) | copy-start | bytes 66052
  5.6 21.9 %copy-start.9 = (f32[2,2,64]{2,1,0:T(2,128)S(1)}, f32[2,2,64]{2,1,0:T(2,128)}, u32[]{:S(2)}) copy-start(f32[2,2,64]{2,1,0:T(2,128)} %param.15) | copy-start | bytes 3076
  5.6 21.9 %copy-start.10 = (f32[64]{0:T(128)S(1)}, f32[64]{0:T(128)}, u32[]{:S(2)}) copy-start(f32[64]{0:T(128)} %param.16) | copy-start | bytes 772
  5.6 21.9 %copy-start.11 = (f32[64]{0:T(128)S(1)}, f32[64]{0:T(128)}, u32[]{:S(2)}) copy-start(f32[64]{0:T(128)} %param.13) | copy-start | bytes 772
  5.7 22.1 %copy-start.2 = (bf16[2,2,64,64,3,3]{3,2,5,4,1,0:T(8,128)(2,1)S(1)}, bf16[2,2,64,64,3,3]{3,2,5,4,1,0:T(8,128)(2,1)}, u32[]{:S(2)}) copy-start(bf16[2,2,64,64,3,3]{3,2,5,4,1,0:T(8,128)(2,1)} %param.14) | copy-start | bytes 884740
  5.7 22.0 %copy-start.4 = (bf16[144,144]{1,0:T(8,128)(2,1)S(1)}, bf16[144,144]{1,0:T(8,128)(2,1)}, u32[]{:S(2)}) copy-start(bf16[144,144]{1,0:T(8,128)(2,1)} %constant.45.clone.set_ref) | copy-start | bytes 124420
  5.7 22.0 %copy-start.5 = (bf16[144,160]{1,0:T(8,128)(2,1)S(1)}, bf16[144,160]{1,0:T(8,128)(2,1)}, u32[]{:S(2)}) copy-start(bf16[144,160]{1,0:T(8,128)(2,1)} %constant.46.clone.slot_ref) | copy-start | bytes 138244
  5.7 22.0 %copy-start.6 = (bf16[64,144]{1,0:T(8,128)(2,1)S(1)}, bf16[64,144]{1,0:T(8,128)(2,1)}, u32[]{:S(2)}) copy-start(bf16[64,144]{1,0:T(8,128)(2,1)} %proj_ref.1) | copy-start | bytes 55300
  5.7 6.6 %collective-permute-start.1 = (bf16[224,128]{1,0:T(8,128)(2,1)S(1)}, bf16[224,128]{1,0:T(8,128)(2,1)S(1)}, u32[]{:S(2)}, u32[]{:S(2)}) collective-permute-start(bf16[224,128]{1,0:T(8,128)(2,1)S(1)} %bitcast.13), channel_id=1, source_target_pairs={{0,1},{1,0},{2,3},{3,2},{4,5},{5,4},{6,7},{7,6},{8,9},{9,8},{10,11... | collective-permute-start | bytes 172040 | tf_op jit(solution)/shard_map/ppermute | solution.py:593
  13.0 8.9 %collective-permute-start.2 = (bf16[376,128]{1,0:T(8,128)(2,1)S(1)}, bf16[376,128]{1,0:T(8,128)(2,1)S(1)}, u32[]{:S(2)}, u32[]{:S(2)}) collective-permute-start(bf16[376,128]{1,0:T(8,128)(2,1)S(1)} %get-tuple-element.31), channel_id=1, source_target_pairs={{0,28},{2,30},{4,24},{6,26},{8,20},{10,22},{12,16},{14,18},{16,12}... | collective-permute-start | bytes 288776 | tf_op jit(solution)/shard_map/ppermute | solution.py:674
  17.8 7.8 %collective-permute-start.3 = (bf16[376,128]{1,0:T(8,128)(2,1)S(1)}, bf16[376,128]{1,0:T(8,128)(2,1)S(1)}, u32[]{:S(2)}, u32[]{:S(2)}) collective-permute-start(bf16[376,128]{1,0:T(8,128)(2,1)S(1)} %get-tuple-element.32), channel_id=1, source_target_pairs={{0,24},{2,26},{4,28},{6,30},{8,16},{10,18},{12,20},{14,22},{16,8},... | collective-permute-start | bytes 288776 | tf_op jit(solution)/shard_map/ppermute | solution.py:674
  18.4 16.5 %copy-start.3 = (bf16[1,128,384]{2,1,0:T(8,128)(2,1)S(1)}, bf16[1,128,384]{2,1,0:T(8,128)(2,1)}, u32[]{:S(2)}) copy-start(bf16[1,128,384]{2,1,0:T(8,128)(2,1)} %constant.49.clone.refs_15_) | copy-start | bytes 294916
  18.4 9.5 %collective-permute-start.4 = (bf16[376,128]{1,0:T(8,128)(2,1)S(1)}, bf16[376,128]{1,0:T(8,128)(2,1)S(1)}, u32[]{:S(2)}, u32[]{:S(2)}) collective-permute-start(bf16[376,128]{1,0:T(8,128)(2,1)S(1)} %get-tuple-element.35), channel_id=1, source_target_pairs={{0,12},{2,14},{4,8},{6,10},{8,4},{10,6},{12,0},{14,2},{16,28},{18,... | collective-permute-start | bytes 288776 | tf_op jit(solution)/shard_map/ppermute | solution.py:674
  18.4 9.9 %collective-permute-start.5 = (bf16[376,128]{1,0:T(8,128)(2,1)S(1)}, bf16[376,128]{1,0:T(8,128)(2,1)S(1)}, u32[]{:S(2)}, u32[]{:S(2)}) collective-permute-start(bf16[376,128]{1,0:T(8,128)(2,1)S(1)} %get-tuple-element.36), channel_id=1, source_target_pairs={{0,8},{2,10},{4,12},{6,14},{8,0},{10,2},{12,4},{14,6},{16,24},{18,... | collective-permute-start | bytes 288776 | tf_op jit(solution)/shard_map/ppermute | solution.py:674
  20.3 8.2 %collective-permute-start.6 = (bf16[376,128]{1,0:T(8,128)(2,1)S(1)}, bf16[376,128]{1,0:T(8,128)(2,1)S(1)}, u32[]{:S(2)}, u32[]{:S(2)}) collective-permute-start(bf16[376,128]{1,0:T(8,128)(2,1)S(1)} %get-tuple-element.37), channel_id=1, source_target_pairs={{0,4},{2,6},{4,0},{6,2},{8,12},{10,14},{12,8},{14,10},{16,20},{18,... | collective-permute-start | bytes 288776 | tf_op jit(solution)/shard_map/ppermute | solution.py:674
  21.9 10.3 %collective-permute-start.7 = (bf16[376,128]{1,0:T(8,128)(2,1)S(1)}, bf16[376,128]{1,0:T(8,128)(2,1)S(1)}, u32[]{:S(2)}, u32[]{:S(2)}) collective-permute-start(bf16[376,128]{1,0:T(8,128)(2,1)S(1)} %get-tuple-element.38), channel_id=1, source_target_pairs={{0,20},{2,22},{4,16},{6,18},{8,28},{10,30},{12,24},{14,26},{16,4},... | collective-permute-start | bytes 288776 | tf_op jit(solution)/shard_map/ppermute | solution.py:674
  25.6 7.7 %collective-permute-start.8 = (bf16[376,128]{1,0:T(8,128)(2,1)S(1)}, bf16[376,128]{1,0:T(8,128)(2,1)S(1)}, u32[]{:S(2)}, u32[]{:S(2)}) collective-permute-start(bf16[376,128]{1,0:T(8,128)(2,1)S(1)} %get-tuple-element.39), channel_id=1, source_target_pairs={{0,16},{2,18},{4,20},{6,22},{8,24},{10,26},{12,28},{14,30},{16,0},... | collective-permute-start | bytes 288776 | tf_op jit(solution)/shard_map/ppermute | solution.py:674
  28.4 5.0 %collective-permute-start.9 = (bf16[4,224,128]{2,1,0:T(8,128)(2,1)S(1)}, bf16[4,224,128]{2,1,0:T(8,128)(2,1)S(1)}, u32[]{:S(2)}, u32[]{:S(2)}) collective-permute-start(bf16[4,224,128]{2,1,0:T(8,128)(2,1)S(1)} %core_pack.2), channel_id=1, source_target_pairs={{0,2},{2,0},{4,6},{6,4},{8,10},{10,8},{12,14},{14,12},{16,18},{18,... | collective-permute-start | bytes 688136 | tf_op jit(solution)/shard_map/ppermute | solution.py:690
  33.3 1.6 %collective-permute-start.10 = (bf16[4,224,128]{2,1,0:T(8,128)(2,1)S(1)}, bf16[4,224,128]{2,1,0:T(8,128)(2,1)S(1)}, u32[]{:S(2)}, u32[]{:S(2)}) collective-permute-start(bf16[4,224,128]{2,1,0:T(8,128)(2,1)S(1)} %core_pack.3), channel_id=1, source_target_pairs={{0,2},{2,0},{4,6},{6,4},{8,10},{10,8},{12,14},{14,12},{16,18},{18,... | collective-permute-start | bytes 688136 | tf_op jit(solution)/shard_map/ppermute | solution.py:690

commit v20 on v18

--- a/solution.py
+++ b/solution.py
@@ -49,7 +49,11 @@
 
     @property
     def tail_rows(self):
-        return up((1 + self.tiles) * self.edge_rows + 3 * self.tiles * self.map_rows, 16)
+        return up((1 + self.tiles) * self.edge_rows + self.sum_rows, 16)
+
+    @property
+    def sum_rows(self):
+        return 3 * self.tiles * 8 * self.sets + up(3 * self.tiles * self.rest, 8)
 
     @property
     def band(self):
@@ -218,9 +222,21 @@
             middle = (sums - high).astype(BF16).astype(F32)
             low = sums - high - middle
         pieces = [by_row[:edge]]
-        for wide in (by_col[:edge], high, middle, low):
-            pieces += [wide[:, k * cols : (k + 1) * cols] for k in range(tiles)]
-        used = (1 + tiles) * edge + 3 * tiles * head
+        pieces += [by_col[:edge, k * cols : (k + 1) * cols] for k in range(tiles)]
+        parts = [
+            part[:, k * cols : (k + 1) * cols] for part in (high, middle, low) for k in range(tiles)
+        ]
+        sets, rest = 8 * plan.sets, plan.rest
+        pieces += [part[:sets] for part in parts if sets]
+        if rest:
+            spare = up(len(parts) * rest, 8)
+            row = lax.broadcasted_iota(jnp.int32, (spare, cols), 0)
+            others = jnp.zeros((spare, cols), F32)
+            for k, part in enumerate(parts):
+                for j in range(rest):
+                    others = jnp.where(row == k * rest + j, part[sets + j : sets + j + 1], others)
+            pieces.append(others)
+        used = (1 + tiles) * edge + plan.sum_rows
         if plan.tail_rows > used:
             pieces.append(jnp.zeros((plan.tail_rows - used, cols), F32))
         out_ref[shift - 1] = jnp.concatenate(pieces, axis=0).astype(BF16)
@@ -233,15 +249,22 @@
     head, edge, halo = plan.map_rows, plan.edge_rows, plan.halo
     tails = [tail_ref[k].astype(F32) for k in range(tiles - 1)]
 
+    sets, rest = 8 * plan.sets, plan.rest
+    line = lax.broadcasted_iota(jnp.int32, (head - sets, cols), 0)
+
+    def sums_of(tail, k):
+        base = (1 + tiles) * edge
+        begin = base + 3 * tiles * sets + k * rest
+        others = jnp.zeros((head - sets, cols), F32)
+        for j in range(rest):
+            others = jnp.where(line == j, tail[begin + j : begin + j + 1], others)
+        return jnp.concatenate([tail[base + k * sets : base + (k + 1) * sets], others], axis=0)
+
     rowsum = []
     for b in range(tiles):
         value = sums_ref[:, b * cols : (b + 1) * cols]
         for tail in tails:
-            base = (1 + tiles) * edge
-            parts = [
-                tail[base + (k * tiles + b) * head : base + (k * tiles + b + 1) * head]
-                for k in range(3)
-            ]
+            parts = [sums_of(tail, k * tiles + b) for k in range(3)]
             value = value + ((parts[0] + parts[1]) + parts[2])
         rowsum.append(value)
     grand = sum(jnp.sum(value, axis=1, keepdims=True) for value in rowsum)

time: 39.7 us -> 39.5 us (level)
  no operation moved by 1% of the time
where the time goes in v20:
time: 39.5 us; the launch traced here: 39.3 us
  starting transfers between devices  17.5 us (44%)
  waiting for transfers between devices  12.9 us (33%)
  Pallas kernels  6.37 us (16%)
  local copies, waits for them, and re-layouts  2.29 us (6%)
    ppermute x7, starting transfers between devices, on_device(): arrived[step] = lax.ppermute(block, 'head', pairs) if step else block  14.2 us
    pallas_call x7, Pallas kernels, call(): pl.pallas_call(kernel, out_shape=[pltpu.VMEM(x.shape, x.dtype) if held_ou...  6.37 us
    ppermute x2, waiting for transfers between devices, mirror(): lax.ppermute(block(s), 'tile', [(i, (i + s) % tiles) for i in range(tiles)])  6.27 us
    ppermute x7, waiting for transfers between devices, on_device(): arrived[step] = lax.ppermute(block, 'head', pairs) if step else block  5.19 us
    ppermute x2, starting transfers between devices, mirror(): lax.ppermute(block(s), 'tile', [(i, (i + s) % tiles) for i in range(tiles)])  3.12 us
    ppermute x2, waiting for transfers between devices, on_device(): lax.ppermute(packed, 'head', [(i, i ^ 1) for i in range(heads)])  1.47 us
    unnamed x24, local copies, waits for them, and re-layouts  1.13 us
    dynamic_slice x1, local copies, waits for them, and re-layouts, facing(): lax.dynamic_slice_in_dim(attention, (me + s) % tiles * cols, cols, 1)  1.05 us
  transfers between devices with their start and end apart: 11, of which 5 were waited for; matrix products, arithmetic and copies ran while one was open for 0% of the time, Pallas kernels for 3%

profile of v20, /device:TPU:0, one launch (start us, length us, event | category | flops | bytes accessed | tf_op | source)
XLA Modules:
  0.0 39.3 jit_solution(16460778234203192786)
XLA Ops:
  0.0 1.1 %constant_dynamic-slice_fusion = bf16[9,128,128]{2,1,0:T(8,128)(2,1)S(1)} fusion(bf16[9,256,128]{2,1,0:T(8,128)(2,1)} %maps_ref.3, s32[]{:T(128)S(6)} %select_n.11), kind=kLoop, calls=%fused_computation.9 | loop fusion | bytes 589828 | tf_op jit(solution)/shard_map/dynamic_slice | solution.py:617
  1.1 3.0 %collective-permute-start = (bf16[1152,128]{1,0:T(8,128)(2,1)S(1)}, bf16[1152,128]{1,0:T(8,128)(2,1)S(1)}, u32[]{:S(2)}, u32[]{:S(2)}) collective-permute-start(bf16[1152,128]{1,0:T(8,128)(2,1)S(1)} %bitcast.14), channel_id=1, source_target_pairs={{0,1},{1,0},{2,3},{3,2},{4,5},{5,4},{6,7},{7,6},{8,9},{9,8},{10,11... | collective-permute-start | bytes 884744 | tf_op jit(solution)/shard_map/ppermute | solution.py:611
  4.1 1.1 %copy-done = bf16[9,256,128]{2,1,0:T(8,128)(2,1)S(1)} copy-done((bf16[9,256,128]{2,1,0:T(8,128)(2,1)S(1)}, bf16[9,256,128]{2,1,0:T(8,128)(2,1)}, u32[]{:S(2)}) %copy-start) | copy-done | bytes 589848
  5.2 0.5 %mirror_pack.1 = (bf16[1,176,128]{2,1,0:T(8,128)(2,1)S(1)}, f32[16,256]{1,0:T(8,128)S(1)}, f32[40,128]{1,0:T(8,128)S(1)}) custom-call(bf16[9,256,128]{2,1,0:T(8,128)(2,1)S(1)} %copy-done), custom_call_target="tpu_custom_call" | custom-call | tf_op jit(solution)/shard_map/mirror_pack/pallas_call | solution.py:574
  5.6 0.0 copy-start.9
  5.7 0.0 copy-start.2
  5.7 0.0 copy-start.4
  5.7 0.0 copy-start.5
  5.7 0.0 copy-start.6
  5.7 0.1 collective-permute-start.1
  5.8 6.3 %collective-permute-done.1 = bf16[176,128]{1,0:T(8,128)(2,1)S(1)} collective-permute-done((bf16[176,128]{1,0:T(8,128)(2,1)S(1)}, bf16[176,128]{1,0:T(8,128)(2,1)S(1)}, u32[]{:S(2)}, u32[]{:S(2)}) %collective-permute-start.1) | collective-permute-done | bytes 45088 | tf_op jit(solution)/shard_map/ppermute | solution.py:611
  12.1 0.6 %correct_pack.1 = (bf16[376,128]{1,0:T(8,128)(2,1)S(1)}, bf16[376,128]{1,0:T(8,128)(2,1)S(1)}, f32[2529,128]{1,0:T(8,128)S(1)}, f32[5,8,256]{2,1,0:T(8,128)S(1)}) custom-call(bf16[9,256,128]{2,1,0:T(8,128)(2,1)S(1)} %copy-done.1, bf16[1,1152,128]{2,1,0:T(8,128)(2,1)S(1)} %bitcast.10, bf16[1,176,128]{2,1,0:T(8,128)(2,1)S(1)} %bitcast.12, ...), custom_call_target="tpu_custom_call" | custom-call | tf_op jit(solution)/shard_map/correct_pack/pallas_call | solution.py:574
  12.7 4.8 %collective-permute-start.2 = (bf16[376,128]{1,0:T(8,128)(2,1)S(1)}, bf16[376,128]{1,0:T(8,128)(2,1)S(1)}, u32[]{:S(2)}, u32[]{:S(2)}) collective-permute-start(bf16[376,128]{1,0:T(8,128)(2,1)S(1)} %get-tuple-element.31), channel_id=1, source_target_pairs={{0,28},{2,30},{4,24},{6,26},{8,20},{10,22},{12,16},{14,18},{16,12}... | collective-permute-start | bytes 288776 | tf_op jit(solution)/shard_map/ppermute | solution.py:692
  17.5 0.2 collective-permute-start.3
  17.8 0.3 pack_rest.1
  18.1 0.0 copy-start.3
  18.1 0.1 collective-permute-start.4
  18.2 1.9 %collective-permute-start.5 = (bf16[376,128]{1,0:T(8,128)(2,1)S(1)}, bf16[376,128]{1,0:T(8,128)(2,1)S(1)}, u32[]{:S(2)}, u32[]{:S(2)}) collective-permute-start(bf16[376,128]{1,0:T(8,128)(2,1)S(1)} %get-tuple-element.36), channel_id=1, source_target_pairs={{0,8},{2,10},{4,12},{6,14},{8,0},{10,2},{12,4},{14,6},{16,24},{18,... | collective-permute-start | bytes 288776 | tf_op jit(solution)/shard_map/ppermute | solution.py:692
  20.1 1.6 %collective-permute-start.6 = (bf16[376,128]{1,0:T(8,128)(2,1)S(1)}, bf16[376,128]{1,0:T(8,128)(2,1)S(1)}, u32[]{:S(2)}, u32[]{:S(2)}) collective-permute-start(bf16[376,128]{1,0:T(8,128)(2,1)S(1)} %get-tuple-element.37), channel_id=1, source_target_pairs={{0,4},{2,6},{4,0},{6,2},{8,12},{10,14},{12,8},{14,10},{16,20},{18,... | collective-permute-start | bytes 288776 | tf_op jit(solution)/shard_map/ppermute | solution.py:692
  21.7 3.6 %collective-permute-start.7 = (bf16[376,128]{1,0:T(8,128)(2,1)S(1)}, bf16[376,128]{1,0:T(8,128)(2,1)S(1)}, u32[]{:S(2)}, u32[]{:S(2)}) collective-permute-start(bf16[376,128]{1,0:T(8,128)(2,1)S(1)} %get-tuple-element.38), channel_id=1, source_target_pairs={{0,20},{2,22},{4,16},{6,18},{8,28},{10,30},{12,24},{14,26},{16,4},... | collective-permute-start | bytes 288776 | tf_op jit(solution)/shard_map/ppermute | solution.py:692
  25.3 2.0 %collective-permute-start.8 = (bf16[376,128]{1,0:T(8,128)(2,1)S(1)}, bf16[376,128]{1,0:T(8,128)(2,1)S(1)}, u32[]{:S(2)}, u32[]{:S(2)}) collective-permute-start(bf16[376,128]{1,0:T(8,128)(2,1)S(1)} %get-tuple-element.39), channel_id=1, source_target_pairs={{0,16},{2,18},{4,20},{6,22},{8,24},{10,26},{12,28},{14,30},{16,0},... | collective-permute-start | bytes 288776 | tf_op jit(solution)/shard_map/ppermute | solution.py:692
  27.3 0.1 copy.18
  27.5 0.2 weight_pack.1
  27.6 0.4 %collective-permute-done.5.refs_3_ = bf16[376,128]{1,0:T(8,128)(2,1)S(1)} collective-permute-done((bf16[376,128]{1,0:T(8,128)(2,1)S(1)}, bf16[376,128]{1,0:T(8,128)(2,1)S(1)}, u32[]{:S(2)}, u32[]{:S(2)}) %collective-permute-start.5) | collective-permute-done | bytes 96288 | tf_op jit(solution)/shard_map/ppermute | solution.py:692
  28.1 0.1 core_pack.2
  28.2 0.1 collective-permute-start.9
  28.2 3.7 %collective-permute-done.7.refs_1_.refs_5_ = bf16[376,128]{1,0:T(8,128)(2,1)S(1)} collective-permute-done((bf16[376,128]{1,0:T(8,128)(2,1)S(1)}, bf16[376,128]{1,0:T(8,128)(2,1)S(1)}, u32[]{:S(2)}, u32[]{:S(2)}) %collective-permute-start.7) | collective-permute-done | bytes 96288 | tf_op jit(solution)/shard_map/ppermute | solution.py:692
  31.9 1.1 %collective-permute-done.8.refs_2_.refs_6_ = bf16[376,128]{1,0:T(8,128)(2,1)S(1)} collective-permute-done((bf16[376,128]{1,0:T(8,128)(2,1)S(1)}, bf16[376,128]{1,0:T(8,128)(2,1)S(1)}, u32[]{:S(2)}, u32[]{:S(2)}) %collective-permute-start.8) | collective-permute-done | bytes 96288 | tf_op jit(solution)/shard_map/ppermute | solution.py:692
  33.0 0.1 core_pack.3
  33.1 0.1 collective-permute-start.10
  33.2 1.5 %collective-permute-done.10.refs_9_ = bf16[4,224,128]{2,1,0:T(8,128)(2,1)S(1)} collective-permute-done((bf16[4,224,128]{2,1,0:T(8,128)(2,1)S(1)}, bf16[4,224,128]{2,1,0:T(8,128)(2,1)S(1)}, u32[]{:S(2)}, u32[]{:S(2)}) %collective-permute-start.10) | collective-permute-done | bytes 229408 | tf_op jit(solution)/shard_map/ppermute | solution.py:708
  34.6 4.7 %stack.9 = f32[16,128]{1,0:T(8,128)} custom-call(bf16[376,128]{1,0:T(8,128)(2,1)S(1)} %collective-permute-done.2.refs_0_, bf16[376,128]{1,0:T(8,128)(2,1)S(1)} %collective-permute-done.3.refs_1_, bf16[376,128]{1,0:T(8,128)(2,1)S(1)} %collective-permute-done.4.refs_2_, bf16[376,128]{1,0:T(8,128)(2,1)S(1)} %collective-permute-done.5.refs_3_, ...), custom_call_target="tpu_custom_call" | custom-call | tf_op jit(solution)/shard_map/stack/pallas_call | solution.py:574
  (26 shorter events, 0.1 us)
Async XLA Ops:
  0.0 17.8 %copy-start.7 = (s32[5504]{0:T(1024)S(1)}, s32[5504]{0:T(1024)}, u32[]{:S(2)}) copy-start(s32[5504]{0:T(1024)} %constant.47.clone) | copy-start | bytes 66052
  0.0 12.1 %copy-start.1 = (bf16[9,256,128]{2,1,0:T(8,128)(2,1)S(1)}, bf16[9,256,128]{2,1,0:T(8,128)(2,1)}, u32[]{:S(2)}) copy-start(bf16[9,256,128]{2,1,0:T(8,128)(2,1)} %maps_ref.3) | copy-start | bytes 1769476
  1.1 11.0 %collective-permute-start = (bf16[1152,128]{1,0:T(8,128)(2,1)S(1)}, bf16[1152,128]{1,0:T(8,128)(2,1)S(1)}, u32[]{:S(2)}, u32[]{:S(2)}) collective-permute-start(bf16[1152,128]{1,0:T(8,128)(2,1)S(1)} %bitcast.14), channel_id=1, source_target_pairs={{0,1},{1,0},{2,3},{3,2},{4,5},{5,4},{6,7},{7,6},{8,9},{9,8},{10,11... | collective-permute-start | bytes 884744 | tf_op jit(solution)/shard_map/ppermute | solution.py:611
  4.1 1.1 %copy-start = (bf16[9,256,128]{2,1,0:T(8,128)(2,1)S(1)}, bf16[9,256,128]{2,1,0:T(8,128)(2,1)}, u32[]{:S(2)}) copy-start(bf16[9,256,128]{2,1,0:T(8,128)(2,1)} %maps_ref.3) | copy-start | bytes 1769476
  5.2 12.6 %copy-start.8 = (s32[5504]{0:T(1024)S(1)}, s32[5504]{0:T(1024)}, u32[]{:S(2)}) copy-start(s32[5504]{0:T(1024)} %constant.48.clone) | copy-start | bytes 66052
  5.6 21.7 %copy-start.9 = (f32[2,2,64]{2,1,0:T(2,128)S(1)}, f32[2,2,64]{2,1,0:T(2,128)}, u32[]{:S(2)}) copy-start(f32[2,2,64]{2,1,0:T(2,128)} %param.15) | copy-start | bytes 3076
  5.6 21.7 %copy-start.10 = (f32[64]{0:T(128)S(1)}, f32[64]{0:T(128)}, u32[]{:S(2)}) copy-start(f32[64]{0:T(128)} %param.16) | copy-start | bytes 772
  5.6 21.7 %copy-start.11 = (f32[64]{0:T(128)S(1)}, f32[64]{0:T(128)}, u32[]{:S(2)}) copy-start(f32[64]{0:T(128)} %param.13) | copy-start | bytes 772
  5.7 21.8 %copy-start.2 = (bf16[2,2,64,64,3,3]{3,2,5,4,1,0:T(8,128)(2,1)S(1)}, bf16[2,2,64,64,3,3]{3,2,5,4,1,0:T(8,128)(2,1)}, u32[]{:S(2)}) copy-start(bf16[2,2,64,64,3,3]{3,2,5,4,1,0:T(8,128)(2,1)} %param.14) | copy-start | bytes 884740
  5.7 21.8 %copy-start.4 = (bf16[144,144]{1,0:T(8,128)(2,1)S(1)}, bf16[144,144]{1,0:T(8,128)(2,1)}, u32[]{:S(2)}) copy-start(bf16[144,144]{1,0:T(8,128)(2,1)} %constant.45.clone.set_ref) | copy-start | bytes 124420
  5.7 21.8 %copy-start.5 = (bf16[144,160]{1,0:T(8,128)(2,1)S(1)}, bf16[144,160]{1,0:T(8,128)(2,1)}, u32[]{:S(2)}) copy-start(bf16[144,160]{1,0:T(8,128)(2,1)} %constant.46.clone.slot_ref) | copy-start | bytes 138244
  5.7 21.8 %copy-start.6 = (bf16[64,144]{1,0:T(8,128)(2,1)S(1)}, bf16[64,144]{1,0:T(8,128)(2,1)}, u32[]{:S(2)}) copy-start(bf16[64,144]{1,0:T(8,128)(2,1)} %proj_ref.1) | copy-start | bytes 55300
  5.7 6.4 %collective-permute-start.1 = (bf16[176,128]{1,0:T(8,128)(2,1)S(1)}, bf16[176,128]{1,0:T(8,128)(2,1)S(1)}, u32[]{:S(2)}, u32[]{:S(2)}) collective-permute-start(bf16[176,128]{1,0:T(8,128)(2,1)S(1)} %bitcast.13), channel_id=1, source_target_pairs={{0,1},{1,0},{2,3},{3,2},{4,5},{5,4},{6,7},{7,6},{8,9},{9,8},{10,11... | collective-permute-start | bytes 135176 | tf_op jit(solution)/shard_map/ppermute | solution.py:611
  12.7 9.0 %collective-permute-start.2 = (bf16[376,128]{1,0:T(8,128)(2,1)S(1)}, bf16[376,128]{1,0:T(8,128)(2,1)S(1)}, u32[]{:S(2)}, u32[]{:S(2)}) collective-permute-start(bf16[376,128]{1,0:T(8,128)(2,1)S(1)} %get-tuple-element.31), channel_id=1, source_target_pairs={{0,28},{2,30},{4,24},{6,26},{8,20},{10,22},{12,16},{14,18},{16,12}... | collective-permute-start | bytes 288776 | tf_op jit(solution)/shard_map/ppermute | solution.py:692
  17.5 7.8 %collective-permute-start.3 = (bf16[376,128]{1,0:T(8,128)(2,1)S(1)}, bf16[376,128]{1,0:T(8,128)(2,1)S(1)}, u32[]{:S(2)}, u32[]{:S(2)}) collective-permute-start(bf16[376,128]{1,0:T(8,128)(2,1)S(1)} %get-tuple-element.32), channel_id=1, source_target_pairs={{0,24},{2,26},{4,28},{6,30},{8,16},{10,18},{12,20},{14,22},{16,8},... | collective-permute-start | bytes 288776 | tf_op jit(solution)/shard_map/ppermute | solution.py:692
  18.1 16.5 %copy-start.3 = (bf16[1,128,384]{2,1,0:T(8,128)(2,1)S(1)}, bf16[1,128,384]{2,1,0:T(8,128)(2,1)}, u32[]{:S(2)}) copy-start(bf16[1,128,384]{2,1,0:T(8,128)(2,1)} %constant.49.clone.refs_15_) | copy-start | bytes 294916
  18.1 9.5 %collective-permute-start.4 = (bf16[376,128]{1,0:T(8,128)(2,1)S(1)}, bf16[376,128]{1,0:T(8,128)(2,1)S(1)}, u32[]{:S(2)}, u32[]{:S(2)}) collective-permute-start(bf16[376,128]{1,0:T(8,128)(2,1)S(1)} %get-tuple-element.35), channel_id=1, source_target_pairs={{0,12},{2,14},{4,8},{6,10},{8,4},{10,6},{12,0},{14,2},{16,28},{18,... | collective-permute-start | bytes 288776 | tf_op jit(solution)/shard_map/ppermute | solution.py:692
  18.2 9.9 %collective-permute-start.5 = (bf16[376,128]{1,0:T(8,128)(2,1)S(1)}, bf16[376,128]{1,0:T(8,128)(2,1)S(1)}, u32[]{:S(2)}, u32[]{:S(2)}) collective-permute-start(bf16[376,128]{1,0:T(8,128)(2,1)S(1)} %get-tuple-element.36), channel_id=1, source_target_pairs={{0,8},{2,10},{4,12},{6,14},{8,0},{10,2},{12,4},{14,6},{16,24},{18,... | collective-permute-start | bytes 288776 | tf_op jit(solution)/shard_map/ppermute | solution.py:692
  20.1 8.2 %collective-permute-start.6 = (bf16[376,128]{1,0:T(8,128)(2,1)S(1)}, bf16[376,128]{1,0:T(8,128)(2,1)S(1)}, u32[]{:S(2)}, u32[]{:S(2)}) collective-permute-start(bf16[376,128]{1,0:T(8,128)(2,1)S(1)} %get-tuple-element.37), channel_id=1, source_target_pairs={{0,4},{2,6},{4,0},{6,2},{8,12},{10,14},{12,8},{14,10},{16,20},{18,... | collective-permute-start | bytes 288776 | tf_op jit(solution)/shard_map/ppermute | solution.py:692
  21.7 10.3 %collective-permute-start.7 = (bf16[376,128]{1,0:T(8,128)(2,1)S(1)}, bf16[376,128]{1,0:T(8,128)(2,1)S(1)}, u32[]{:S(2)}, u32[]{:S(2)}) collective-permute-start(bf16[376,128]{1,0:T(8,128)(2,1)S(1)} %get-tuple-element.38), channel_id=1, source_target_pairs={{0,20},{2,22},{4,16},{6,18},{8,28},{10,30},{12,24},{14,26},{16,4},... | collective-permute-start | bytes 288776 | tf_op jit(solution)/shard_map/ppermute | solution.py:692
  25.3 7.7 %collective-permute-start.8 = (bf16[376,128]{1,0:T(8,128)(2,1)S(1)}, bf16[376,128]{1,0:T(8,128)(2,1)S(1)}, u32[]{:S(2)}, u32[]{:S(2)}) collective-permute-start(bf16[376,128]{1,0:T(8,128)(2,1)S(1)} %get-tuple-element.39), channel_id=1, source_target_pairs={{0,16},{2,18},{4,20},{6,22},{8,24},{10,26},{12,28},{14,30},{16,0},... | collective-permute-start | bytes 288776 | tf_op jit(solution)/shard_map/ppermute | solution.py:692
  28.2 5.0 %collective-permute-start.9 = (bf16[4,224,128]{2,1,0:T(8,128)(2,1)S(1)}, bf16[4,224,128]{2,1,0:T(8,128)(2,1)S(1)}, u32[]{:S(2)}, u32[]{:S(2)}) collective-permute-start(bf16[4,224,128]{2,1,0:T(8,128)(2,1)S(1)} %core_pack.2), channel_id=1, source_target_pairs={{0,2},{2,0},{4,6},{6,4},{8,10},{10,8},{12,14},{14,12},{16,18},{18,... | collective-permute-start | bytes 688136 | tf_op jit(solution)/shard_map/ppermute | solution.py:708
  33.1 1.6 %collective-permute-start.10 = (bf16[4,224,128]{2,1,0:T(8,128)(2,1)S(1)}, bf16[4,224,128]{2,1,0:T(8,128)(2,1)S(1)}, u32[]{:S(2)}, u32[]{:S(2)}) collective-permute-start(bf16[4,224,128]{2,1,0:T(8,128)(2,1)S(1)} %core_pack.3), channel_id=1, source_target_pairs={{0,2},{2,0},{4,6},{6,4},{8,10},{10,8},{12,14},{14,12},{16,18},{18,... | collective-permute-start | bytes 688136 | tf_op jit(solution)/shard_map/ppermute | solution.py:708

commit v21 on v20

--- a/solution.py
+++ b/solution.py
@@ -125,7 +125,7 @@
 
     @property
     def batch(self):
-        return 8
+        return 12
 
     @property
     def chunk(self):

time: 39.5 us -> 39.5 us (level)
  no operation moved by 1% of the time
where the time goes in v21:
time: 39.5 us; the launch traced here: 39.3 us
  starting transfers between devices  17.5 us (44%)
  waiting for transfers between devices  12.9 us (33%)
  Pallas kernels  6.37 us (16%)
  local copies, waits for them, and re-layouts  2.29 us (6%)
    ppermute x7, starting transfers between devices, on_device(): arrived[step] = lax.ppermute(block, 'head', pairs) if step else block  14.2 us
    pallas_call x7, Pallas kernels, call(): pl.pallas_call(kernel, out_shape=[pltpu.VMEM(x.shape, x.dtype) if held_ou...  6.37 us
    ppermute x2, waiting for transfers between devices, mirror(): lax.ppermute(block(s), 'tile', [(i, (i + s) % tiles) for i in range(tiles)])  6.27 us
    ppermute x7, waiting for transfers between devices, on_device(): arrived[step] = lax.ppermute(block, 'head', pairs) if step else block  5.19 us
    ppermute x2, starting transfers between devices, mirror(): lax.ppermute(block(s), 'tile', [(i, (i + s) % tiles) for i in range(tiles)])  3.12 us
    ppermute x2, waiting for transfers between devices, on_device(): lax.ppermute(packed, 'head', [(i, i ^ 1) for i in range(heads)])  1.47 us
    unnamed x24, local copies, waits for them, and re-layouts  1.13 us
    dynamic_slice x1, local copies, waits for them, and re-layouts, facing(): lax.dynamic_slice_in_dim(attention, (me + s) % tiles * cols, cols, 1)  1.05 us
  transfers between devices with their start and end apart: 11, of which 5 were waited for; matrix products, arithmetic and copies ran while one was open for 0% of the time, Pallas kernels for 3%

profile of v21, /device:TPU:0, one launch (start us, length us, event | category | flops | bytes accessed | tf_op | source)
XLA Modules:
  0.0 39.3 jit_solution(16460778234203192786)
XLA Ops:
  0.0 1.1 %constant_dynamic-slice_fusion = bf16[9,128,128]{2,1,0:T(8,128)(2,1)S(1)} fusion(bf16[9,256,128]{2,1,0:T(8,128)(2,1)} %maps_ref.3, s32[]{:T(128)S(6)} %select_n.11), kind=kLoop, calls=%fused_computation.9 | loop fusion | bytes 589828 | tf_op jit(solution)/shard_map/dynamic_slice | solution.py:617
  1.1 3.0 %collective-permute-start = (bf16[1152,128]{1,0:T(8,128)(2,1)S(1)}, bf16[1152,128]{1,0:T(8,128)(2,1)S(1)}, u32[]{:S(2)}, u32[]{:S(2)}) collective-permute-start(bf16[1152,128]{1,0:T(8,128)(2,1)S(1)} %bitcast.14), channel_id=1, source_target_pairs={{0,1},{1,0},{2,3},{3,2},{4,5},{5,4},{6,7},{7,6},{8,9},{9,8},{10,11... | collective-permute-start | bytes 884744 | tf_op jit(solution)/shard_map/ppermute | solution.py:611
  4.1 1.1 %copy-done = bf16[9,256,128]{2,1,0:T(8,128)(2,1)S(1)} copy-done((bf16[9,256,128]{2,1,0:T(8,128)(2,1)S(1)}, bf16[9,256,128]{2,1,0:T(8,128)(2,1)}, u32[]{:S(2)}) %copy-start) | copy-done | bytes 589848
  5.2 0.5 %mirror_pack.1 = (bf16[1,176,128]{2,1,0:T(8,128)(2,1)S(1)}, f32[16,256]{1,0:T(8,128)S(1)}, f32[40,128]{1,0:T(8,128)S(1)}) custom-call(bf16[9,256,128]{2,1,0:T(8,128)(2,1)S(1)} %copy-done), custom_call_target="tpu_custom_call" | custom-call | tf_op jit(solution)/shard_map/mirror_pack/pallas_call | solution.py:574
  5.6 0.0 copy-start.9
  5.7 0.0 copy-start.2
  5.7 0.0 copy-start.4
  5.7 0.0 copy-start.5
  5.7 0.0 copy-start.6
  5.7 0.1 collective-permute-start.1
  5.8 6.3 %collective-permute-done.1 = bf16[176,128]{1,0:T(8,128)(2,1)S(1)} collective-permute-done((bf16[176,128]{1,0:T(8,128)(2,1)S(1)}, bf16[176,128]{1,0:T(8,128)(2,1)S(1)}, u32[]{:S(2)}, u32[]{:S(2)}) %collective-permute-start.1) | collective-permute-done | bytes 45088 | tf_op jit(solution)/shard_map/ppermute | solution.py:611
  12.1 0.6 %correct_pack.1 = (bf16[376,128]{1,0:T(8,128)(2,1)S(1)}, bf16[376,128]{1,0:T(8,128)(2,1)S(1)}, f32[2529,128]{1,0:T(8,128)S(1)}, f32[5,8,256]{2,1,0:T(8,128)S(1)}) custom-call(bf16[9,256,128]{2,1,0:T(8,128)(2,1)S(1)} %copy-done.1, bf16[1,1152,128]{2,1,0:T(8,128)(2,1)S(1)} %bitcast.10, bf16[1,176,128]{2,1,0:T(8,128)(2,1)S(1)} %bitcast.12, ...), custom_call_target="tpu_custom_call" | custom-call | tf_op jit(solution)/shard_map/correct_pack/pallas_call | solution.py:574
  12.7 4.8 %collective-permute-start.2 = (bf16[376,128]{1,0:T(8,128)(2,1)S(1)}, bf16[376,128]{1,0:T(8,128)(2,1)S(1)}, u32[]{:S(2)}, u32[]{:S(2)}) collective-permute-start(bf16[376,128]{1,0:T(8,128)(2,1)S(1)} %get-tuple-element.31), channel_id=1, source_target_pairs={{0,28},{2,30},{4,24},{6,26},{8,20},{10,22},{12,16},{14,18},{16,12}... | collective-permute-start | bytes 288776 | tf_op jit(solution)/shard_map/ppermute | solution.py:692
  17.5 0.2 collective-permute-start.3
  17.8 0.3 pack_rest.1
  18.1 0.0 copy-start.3
  18.1 0.1 collective-permute-start.4
  18.2 1.9 %collective-permute-start.5 = (bf16[376,128]{1,0:T(8,128)(2,1)S(1)}, bf16[376,128]{1,0:T(8,128)(2,1)S(1)}, u32[]{:S(2)}, u32[]{:S(2)}) collective-permute-start(bf16[376,128]{1,0:T(8,128)(2,1)S(1)} %get-tuple-element.36), channel_id=1, source_target_pairs={{0,8},{2,10},{4,12},{6,14},{8,0},{10,2},{12,4},{14,6},{16,24},{18,... | collective-permute-start | bytes 288776 | tf_op jit(solution)/shard_map/ppermute | solution.py:692
  20.1 1.6 %collective-permute-start.6 = (bf16[376,128]{1,0:T(8,128)(2,1)S(1)}, bf16[376,128]{1,0:T(8,128)(2,1)S(1)}, u32[]{:S(2)}, u32[]{:S(2)}) collective-permute-start(bf16[376,128]{1,0:T(8,128)(2,1)S(1)} %get-tuple-element.37), channel_id=1, source_target_pairs={{0,4},{2,6},{4,0},{6,2},{8,12},{10,14},{12,8},{14,10},{16,20},{18,... | collective-permute-start | bytes 288776 | tf_op jit(solution)/shard_map/ppermute | solution.py:692
  21.7 3.6 %collective-permute-start.7 = (bf16[376,128]{1,0:T(8,128)(2,1)S(1)}, bf16[376,128]{1,0:T(8,128)(2,1)S(1)}, u32[]{:S(2)}, u32[]{:S(2)}) collective-permute-start(bf16[376,128]{1,0:T(8,128)(2,1)S(1)} %get-tuple-element.38), channel_id=1, source_target_pairs={{0,20},{2,22},{4,16},{6,18},{8,28},{10,30},{12,24},{14,26},{16,4},... | collective-permute-start | bytes 288776 | tf_op jit(solution)/shard_map/ppermute | solution.py:692
  25.3 2.0 %collective-permute-start.8 = (bf16[376,128]{1,0:T(8,128)(2,1)S(1)}, bf16[376,128]{1,0:T(8,128)(2,1)S(1)}, u32[]{:S(2)}, u32[]{:S(2)}) collective-permute-start(bf16[376,128]{1,0:T(8,128)(2,1)S(1)} %get-tuple-element.39), channel_id=1, source_target_pairs={{0,16},{2,18},{4,20},{6,22},{8,24},{10,26},{12,28},{14,30},{16,0},... | collective-permute-start | bytes 288776 | tf_op jit(solution)/shard_map/ppermute | solution.py:692
  27.3 0.1 copy.18
  27.5 0.2 weight_pack.1
  27.6 0.4 %collective-permute-done.5.refs_3_ = bf16[376,128]{1,0:T(8,128)(2,1)S(1)} collective-permute-done((bf16[376,128]{1,0:T(8,128)(2,1)S(1)}, bf16[376,128]{1,0:T(8,128)(2,1)S(1)}, u32[]{:S(2)}, u32[]{:S(2)}) %collective-permute-start.5) | collective-permute-done | bytes 96288 | tf_op jit(solution)/shard_map/ppermute | solution.py:692
  28.1 0.1 core_pack.2
  28.2 0.1 collective-permute-start.9
  28.2 3.7 %collective-permute-done.7.refs_1_.refs_5_ = bf16[376,128]{1,0:T(8,128)(2,1)S(1)} collective-permute-done((bf16[376,128]{1,0:T(8,128)(2,1)S(1)}, bf16[376,128]{1,0:T(8,128)(2,1)S(1)}, u32[]{:S(2)}, u32[]{:S(2)}) %collective-permute-start.7) | collective-permute-done | bytes 96288 | tf_op jit(solution)/shard_map/ppermute | solution.py:692
  31.9 1.1 %collective-permute-done.8.refs_2_.refs_6_ = bf16[376,128]{1,0:T(8,128)(2,1)S(1)} collective-permute-done((bf16[376,128]{1,0:T(8,128)(2,1)S(1)}, bf16[376,128]{1,0:T(8,128)(2,1)S(1)}, u32[]{:S(2)}, u32[]{:S(2)}) %collective-permute-start.8) | collective-permute-done | bytes 96288 | tf_op jit(solution)/shard_map/ppermute | solution.py:692
  33.0 0.1 core_pack.3
  33.1 0.1 collective-permute-start.10
  33.2 1.5 %collective-permute-done.10.refs_9_ = bf16[4,224,128]{2,1,0:T(8,128)(2,1)S(1)} collective-permute-done((bf16[4,224,128]{2,1,0:T(8,128)(2,1)S(1)}, bf16[4,224,128]{2,1,0:T(8,128)(2,1)S(1)}, u32[]{:S(2)}, u32[]{:S(2)}) %collective-permute-start.10) | collective-permute-done | bytes 229408 | tf_op jit(solution)/shard_map/ppermute | solution.py:708
  34.6 4.7 %stack.9 = f32[16,128]{1,0:T(8,128)} custom-call(bf16[376,128]{1,0:T(8,128)(2,1)S(1)} %collective-permute-done.2.refs_0_, bf16[376,128]{1,0:T(8,128)(2,1)S(1)} %collective-permute-done.3.refs_1_, bf16[376,128]{1,0:T(8,128)(2,1)S(1)} %collective-permute-done.4.refs_2_, bf16[376,128]{1,0:T(8,128)(2,1)S(1)} %collective-permute-done.5.refs_3_, ...), custom_call_target="tpu_custom_call" | custom-call | tf_op jit(solution)/shard_map/stack/pallas_call | solution.py:574
  (26 shorter events, 0.1 us)
Async XLA Ops:
  0.0 17.8 %copy-start.7 = (s32[5504]{0:T(1024)S(1)}, s32[5504]{0:T(1024)}, u32[]{:S(2)}) copy-start(s32[5504]{0:T(1024)} %constant.47.clone) | copy-start | bytes 66052
  0.0 12.1 %copy-start.1 = (bf16[9,256,128]{2,1,0:T(8,128)(2,1)S(1)}, bf16[9,256,128]{2,1,0:T(8,128)(2,1)}, u32[]{:S(2)}) copy-start(bf16[9,256,128]{2,1,0:T(8,128)(2,1)} %maps_ref.3) | copy-start | bytes 1769476
  1.1 11.0 %collective-permute-start = (bf16[1152,128]{1,0:T(8,128)(2,1)S(1)}, bf16[1152,128]{1,0:T(8,128)(2,1)S(1)}, u32[]{:S(2)}, u32[]{:S(2)}) collective-permute-start(bf16[1152,128]{1,0:T(8,128)(2,1)S(1)} %bitcast.14), channel_id=1, source_target_pairs={{0,1},{1,0},{2,3},{3,2},{4,5},{5,4},{6,7},{7,6},{8,9},{9,8},{10,11... | collective-permute-start | bytes 884744 | tf_op jit(solution)/shard_map/ppermute | solution.py:611
  4.1 1.1 %copy-start = (bf16[9,256,128]{2,1,0:T(8,128)(2,1)S(1)}, bf16[9,256,128]{2,1,0:T(8,128)(2,1)}, u32[]{:S(2)}) copy-start(bf16[9,256,128]{2,1,0:T(8,128)(2,1)} %maps_ref.3) | copy-start | bytes 1769476
  5.2 12.6 %copy-start.8 = (s32[5504]{0:T(1024)S(1)}, s32[5504]{0:T(1024)}, u32[]{:S(2)}) copy-start(s32[5504]{0:T(1024)} %constant.48.clone) | copy-start | bytes 66052
  5.6 21.7 %copy-start.9 = (f32[2,2,64]{2,1,0:T(2,128)S(1)}, f32[2,2,64]{2,1,0:T(2,128)}, u32[]{:S(2)}) copy-start(f32[2,2,64]{2,1,0:T(2,128)} %param.15) | copy-start | bytes 3076
  5.6 21.7 %copy-start.10 = (f32[64]{0:T(128)S(1)}, f32[64]{0:T(128)}, u32[]{:S(2)}) copy-start(f32[64]{0:T(128)} %param.16) | copy-start | bytes 772
  5.6 21.7 %copy-start.11 = (f32[64]{0:T(128)S(1)}, f32[64]{0:T(128)}, u32[]{:S(2)}) copy-start(f32[64]{0:T(128)} %param.13) | copy-start | bytes 772
  5.7 21.8 %copy-start.2 = (bf16[2,2,64,64,3,3]{3,2,5,4,1,0:T(8,128)(2,1)S(1)}, bf16[2,2,64,64,3,3]{3,2,5,4,1,0:T(8,128)(2,1)}, u32[]{:S(2)}) copy-start(bf16[2,2,64,64,3,3]{3,2,5,4,1,0:T(8,128)(2,1)} %param.14) | copy-start | bytes 884740
  5.7 21.8 %copy-start.4 = (bf16[144,144]{1,0:T(8,128)(2,1)S(1)}, bf16[144,144]{1,0:T(8,128)(2,1)}, u32[]{:S(2)}) copy-start(bf16[144,144]{1,0:T(8,128)(2,1)} %constant.45.clone.set_ref) | copy-start | bytes 124420
  5.7 21.8 %copy-start.5 = (bf16[144,160]{1,0:T(8,128)(2,1)S(1)}, bf16[144,160]{1,0:T(8,128)(2,1)}, u32[]{:S(2)}) copy-start(bf16[144,160]{1,0:T(8,128)(2,1)} %constant.46.clone.slot_ref) | copy-start | bytes 138244
  5.7 21.8 %copy-start.6 = (bf16[64,144]{1,0:T(8,128)(2,1)S(1)}, bf16[64,144]{1,0:T(8,128)(2,1)}, u32[]{:S(2)}) copy-start(bf16[64,144]{1,0:T(8,128)(2,1)} %proj_ref.1) | copy-start | bytes 55300
  5.7 6.4 %collective-permute-start.1 = (bf16[176,128]{1,0:T(8,128)(2,1)S(1)}, bf16[176,128]{1,0:T(8,128)(2,1)S(1)}, u32[]{:S(2)}, u32[]{:S(2)}) collective-permute-start(bf16[176,128]{1,0:T(8,128)(2,1)S(1)} %bitcast.13), channel_id=1, source_target_pairs={{0,1},{1,0},{2,3},{3,2},{4,5},{5,4},{6,7},{7,6},{8,9},{9,8},{10,11... | collective-permute-start | bytes 135176 | tf_op jit(solution)/shard_map/ppermute | solution.py:611
  12.7 9.0 %collective-permute-start.2 = (bf16[376,128]{1,0:T(8,128)(2,1)S(1)}, bf16[376,128]{1,0:T(8,128)(2,1)S(1)}, u32[]{:S(2)}, u32[]{:S(2)}) collective-permute-start(bf16[376,128]{1,0:T(8,128)(2,1)S(1)} %get-tuple-element.31), channel_id=1, source_target_pairs={{0,28},{2,30},{4,24},{6,26},{8,20},{10,22},{12,16},{14,18},{16,12}... | collective-permute-start | bytes 288776 | tf_op jit(solution)/shard_map/ppermute | solution.py:692
  17.5 7.8 %collective-permute-start.3 = (bf16[376,128]{1,0:T(8,128)(2,1)S(1)}, bf16[376,128]{1,0:T(8,128)(2,1)S(1)}, u32[]{:S(2)}, u32[]{:S(2)}) collective-permute-start(bf16[376,128]{1,0:T(8,128)(2,1)S(1)} %get-tuple-element.32), channel_id=1, source_target_pairs={{0,24},{2,26},{4,28},{6,30},{8,16},{10,18},{12,20},{14,22},{16,8},... | collective-permute-start | bytes 288776 | tf_op jit(solution)/shard_map/ppermute | solution.py:692
  18.1 16.5 %copy-start.3 = (bf16[1,128,384]{2,1,0:T(8,128)(2,1)S(1)}, bf16[1,128,384]{2,1,0:T(8,128)(2,1)}, u32[]{:S(2)}) copy-start(bf16[1,128,384]{2,1,0:T(8,128)(2,1)} %constant.49.clone.refs_15_) | copy-start | bytes 294916
  18.1 9.5 %collective-permute-start.4 = (bf16[376,128]{1,0:T(8,128)(2,1)S(1)}, bf16[376,128]{1,0:T(8,128)(2,1)S(1)}, u32[]{:S(2)}, u32[]{:S(2)}) collective-permute-start(bf16[376,128]{1,0:T(8,128)(2,1)S(1)} %get-tuple-element.35), channel_id=1, source_target_pairs={{0,12},{2,14},{4,8},{6,10},{8,4},{10,6},{12,0},{14,2},{16,28},{18,... | collective-permute-start | bytes 288776 | tf_op jit(solution)/shard_map/ppermute | solution.py:692
  18.2 9.9 %collective-permute-start.5 = (bf16[376,128]{1,0:T(8,128)(2,1)S(1)}, bf16[376,128]{1,0:T(8,128)(2,1)S(1)}, u32[]{:S(2)}, u32[]{:S(2)}) collective-permute-start(bf16[376,128]{1,0:T(8,128)(2,1)S(1)} %get-tuple-element.36), channel_id=1, source_target_pairs={{0,8},{2,10},{4,12},{6,14},{8,0},{10,2},{12,4},{14,6},{16,24},{18,... | collective-permute-start | bytes 288776 | tf_op jit(solution)/shard_map/ppermute | solution.py:692
  20.1 8.2 %collective-permute-start.6 = (bf16[376,128]{1,0:T(8,128)(2,1)S(1)}, bf16[376,128]{1,0:T(8,128)(2,1)S(1)}, u32[]{:S(2)}, u32[]{:S(2)}) collective-permute-start(bf16[376,128]{1,0:T(8,128)(2,1)S(1)} %get-tuple-element.37), channel_id=1, source_target_pairs={{0,4},{2,6},{4,0},{6,2},{8,12},{10,14},{12,8},{14,10},{16,20},{18,... | collective-permute-start | bytes 288776 | tf_op jit(solution)/shard_map/ppermute | solution.py:692
  21.7 10.3 %collective-permute-start.7 = (bf16[376,128]{1,0:T(8,128)(2,1)S(1)}, bf16[376,128]{1,0:T(8,128)(2,1)S(1)}, u32[]{:S(2)}, u32[]{:S(2)}) collective-permute-start(bf16[376,128]{1,0:T(8,128)(2,1)S(1)} %get-tuple-element.38), channel_id=1, source_target_pairs={{0,20},{2,22},{4,16},{6,18},{8,28},{10,30},{12,24},{14,26},{16,4},... | collective-permute-start | bytes 288776 | tf_op jit(solution)/shard_map/ppermute | solution.py:692
  25.3 7.7 %collective-permute-start.8 = (bf16[376,128]{1,0:T(8,128)(2,1)S(1)}, bf16[376,128]{1,0:T(8,128)(2,1)S(1)}, u32[]{:S(2)}, u32[]{:S(2)}) collective-permute-start(bf16[376,128]{1,0:T(8,128)(2,1)S(1)} %get-tuple-element.39), channel_id=1, source_target_pairs={{0,16},{2,18},{4,20},{6,22},{8,24},{10,26},{12,28},{14,30},{16,0},... | collective-permute-start | bytes 288776 | tf_op jit(solution)/shard_map/ppermute | solution.py:692
  28.2 5.0 %collective-permute-start.9 = (bf16[4,224,128]{2,1,0:T(8,128)(2,1)S(1)}, bf16[4,224,128]{2,1,0:T(8,128)(2,1)S(1)}, u32[]{:S(2)}, u32[]{:S(2)}) collective-permute-start(bf16[4,224,128]{2,1,0:T(8,128)(2,1)S(1)} %core_pack.2), channel_id=1, source_target_pairs={{0,2},{2,0},{4,6},{6,4},{8,10},{10,8},{12,14},{14,12},{16,18},{18,... | collective-permute-start | bytes 688136 | tf_op jit(solution)/shard_map/ppermute | solution.py:708
  33.1 1.6 %collective-permute-start.10 = (bf16[4,224,128]{2,1,0:T(8,128)(2,1)S(1)}, bf16[4,224,128]{2,1,0:T(8,128)(2,1)S(1)}, u32[]{:S(2)}, u32[]{:S(2)}) collective-permute-start(bf16[4,224,128]{2,1,0:T(8,128)(2,1)S(1)} %core_pack.3), channel_id=1, source_target_pairs={{0,2},{2,0},{4,6},{6,4},{8,10},{10,8},{12,14},{14,12},{16,18},{18,... | collective-permute-start | bytes 688136 | tf_op jit(solution)/shard_map/ppermute | solution.py:708

commit v22 on v21

--- a/solution.py
+++ b/solution.py
@@ -558,9 +558,9 @@
 
         multiply(low, size + LANES)
         for i in range(steps):
+            finish(low + i * size)
             if i + 1 < steps:
                 multiply(low + (i + 1) * size + LANES, size)
-            finish(low + i * size)
 
     for r in range(plan.band):
         begin = plan.start + (r + halo) * stride + halo

time: 39.5 us -> 40 us (1.013)
  Pallas kernels: 6.37 us -> 6.9 us
    pallas_call x7, Pallas kernels: 6.37 us -> 6.9 us  [call(): pl.pallas_call(kernel, out_shape=[pltpu.VMEM(x.shape, x.dtype) if held_ou...]
where the time goes in v22:
time: 40 us; the launch traced here: 39.8 us
  starting transfers between devices  17.5 us (44%)
  waiting for transfers between devices  12.9 us (32%)
  Pallas kernels  6.9 us (17%)
  local copies, waits for them, and re-layouts  2.29 us (6%)
    ppermute x7, starting transfers between devices, on_device(): arrived[step] = lax.ppermute(block, 'head', pairs) if step else block  14.2 us
    pallas_call x7, Pallas kernels, call(): pl.pallas_call(kernel, out_shape=[pltpu.VMEM(x.shape, x.dtype) if held_ou...  6.9 us
    ppermute x2, waiting for transfers between devices, mirror(): lax.ppermute(block(s), 'tile', [(i, (i + s) % tiles) for i in range(tiles)])  6.27 us
    ppermute x7, waiting for transfers between devices, on_device(): arrived[step] = lax.ppermute(block, 'head', pairs) if step else block  5.19 us
    ppermute x2, starting transfers between devices, mirror(): lax.ppermute(block(s), 'tile', [(i, (i + s) % tiles) for i in range(tiles)])  3.12 us
    ppermute x2, waiting for transfers between devices, on_device(): lax.ppermute(packed, 'head', [(i, i ^ 1) for i in range(heads)])  1.47 us
    unnamed x24, local copies, waits for them, and re-layouts  1.13 us
    dynamic_slice x1, local copies, waits for them, and re-layouts, facing(): lax.dynamic_slice_in_dim(attention, (me + s) % tiles * cols, cols, 1)  1.05 us
  transfers between devices with their start and end apart: 11, of which 5 were waited for; matrix products, arithmetic and copies ran while one was open for 0% of the time, Pallas kernels for 3%

profile of v22, /device:TPU:0, one launch (start us, length us, event | category | flops | bytes accessed | tf_op | source)
XLA Modules:
  0.0 39.8 jit_solution(14486371508770074655)
XLA Ops:
  0.0 1.1 %constant_dynamic-slice_fusion = bf16[9,128,128]{2,1,0:T(8,128)(2,1)S(1)} fusion(bf16[9,256,128]{2,1,0:T(8,128)(2,1)} %maps_ref.3, s32[]{:T(128)S(6)} %select_n.11), kind=kLoop, calls=%fused_computation.9 | loop fusion | bytes 589828 | tf_op jit(solution)/shard_map/dynamic_slice | solution.py:617
  1.1 3.0 %collective-permute-start = (bf16[1152,128]{1,0:T(8,128)(2,1)S(1)}, bf16[1152,128]{1,0:T(8,128)(2,1)S(1)}, u32[]{:S(2)}, u32[]{:S(2)}) collective-permute-start(bf16[1152,128]{1,0:T(8,128)(2,1)S(1)} %bitcast.14), channel_id=1, source_target_pairs={{0,1},{1,0},{2,3},{3,2},{4,5},{5,4},{6,7},{7,6},{8,9},{9,8},{10,11... | collective-permute-start | bytes 884744 | tf_op jit(solution)/shard_map/ppermute | solution.py:611
  4.1 1.1 %copy-done = bf16[9,256,128]{2,1,0:T(8,128)(2,1)S(1)} copy-done((bf16[9,256,128]{2,1,0:T(8,128)(2,1)S(1)}, bf16[9,256,128]{2,1,0:T(8,128)(2,1)}, u32[]{:S(2)}) %copy-start) | copy-done | bytes 589848
  5.2 0.5 %mirror_pack.1 = (bf16[1,176,128]{2,1,0:T(8,128)(2,1)S(1)}, f32[16,256]{1,0:T(8,128)S(1)}, f32[40,128]{1,0:T(8,128)S(1)}) custom-call(bf16[9,256,128]{2,1,0:T(8,128)(2,1)S(1)} %copy-done), custom_call_target="tpu_custom_call" | custom-call | tf_op jit(solution)/shard_map/mirror_pack/pallas_call | solution.py:574
  5.6 0.0 copy-start.9
  5.6 0.0 copy-start.10
  5.6 0.0 copy-start.11
  5.7 0.0 copy-start.4
  5.7 0.0 copy-start.5
  5.7 0.1 collective-permute-start.1
  5.8 6.3 %collective-permute-done.1 = bf16[176,128]{1,0:T(8,128)(2,1)S(1)} collective-permute-done((bf16[176,128]{1,0:T(8,128)(2,1)S(1)}, bf16[176,128]{1,0:T(8,128)(2,1)S(1)}, u32[]{:S(2)}, u32[]{:S(2)}) %collective-permute-start.1) | collective-permute-done | bytes 45088 | tf_op jit(solution)/shard_map/ppermute | solution.py:611
  12.1 0.6 %correct_pack.1 = (bf16[376,128]{1,0:T(8,128)(2,1)S(1)}, bf16[376,128]{1,0:T(8,128)(2,1)S(1)}, f32[2529,128]{1,0:T(8,128)S(1)}, f32[5,8,256]{2,1,0:T(8,128)S(1)}) custom-call(bf16[9,256,128]{2,1,0:T(8,128)(2,1)S(1)} %copy-done.1, bf16[1,1152,128]{2,1,0:T(8,128)(2,1)S(1)} %bitcast.10, bf16[1,176,128]{2,1,0:T(8,128)(2,1)S(1)} %bitcast.12, ...), custom_call_target="tpu_custom_call" | custom-call | tf_op jit(solution)/shard_map/correct_pack/pallas_call | solution.py:574
  12.7 4.8 %collective-permute-start.2 = (bf16[376,128]{1,0:T(8,128)(2,1)S(1)}, bf16[376,128]{1,0:T(8,128)(2,1)S(1)}, u32[]{:S(2)}, u32[]{:S(2)}) collective-permute-start(bf16[376,128]{1,0:T(8,128)(2,1)S(1)} %get-tuple-element.31), channel_id=1, source_target_pairs={{0,28},{2,30},{4,24},{6,26},{8,20},{10,22},{12,16},{14,18},{16,12}... | collective-permute-start | bytes 288776 | tf_op jit(solution)/shard_map/ppermute | solution.py:692
  17.5 0.2 collective-permute-start.3
  17.8 0.3 pack_rest.1
  18.1 0.0 copy-start.3
  18.1 0.1 collective-permute-start.4
  18.2 1.9 %collective-permute-start.5 = (bf16[376,128]{1,0:T(8,128)(2,1)S(1)}, bf16[376,128]{1,0:T(8,128)(2,1)S(1)}, u32[]{:S(2)}, u32[]{:S(2)}) collective-permute-start(bf16[376,128]{1,0:T(8,128)(2,1)S(1)} %get-tuple-element.36), channel_id=1, source_target_pairs={{0,8},{2,10},{4,12},{6,14},{8,0},{10,2},{12,4},{14,6},{16,24},{18,... | collective-permute-start | bytes 288776 | tf_op jit(solution)/shard_map/ppermute | solution.py:692
  20.1 1.6 %collective-permute-start.6 = (bf16[376,128]{1,0:T(8,128)(2,1)S(1)}, bf16[376,128]{1,0:T(8,128)(2,1)S(1)}, u32[]{:S(2)}, u32[]{:S(2)}) collective-permute-start(bf16[376,128]{1,0:T(8,128)(2,1)S(1)} %get-tuple-element.37), channel_id=1, source_target_pairs={{0,4},{2,6},{4,0},{6,2},{8,12},{10,14},{12,8},{14,10},{16,20},{18,... | collective-permute-start | bytes 288776 | tf_op jit(solution)/shard_map/ppermute | solution.py:692
  21.7 3.6 %collective-permute-start.7 = (bf16[376,128]{1,0:T(8,128)(2,1)S(1)}, bf16[376,128]{1,0:T(8,128)(2,1)S(1)}, u32[]{:S(2)}, u32[]{:S(2)}) collective-permute-start(bf16[376,128]{1,0:T(8,128)(2,1)S(1)} %get-tuple-element.38), channel_id=1, source_target_pairs={{0,20},{2,22},{4,16},{6,18},{8,28},{10,30},{12,24},{14,26},{16,4},... | collective-permute-start | bytes 288776 | tf_op jit(solution)/shard_map/ppermute | solution.py:692
  25.3 2.0 %collective-permute-start.8 = (bf16[376,128]{1,0:T(8,128)(2,1)S(1)}, bf16[376,128]{1,0:T(8,128)(2,1)S(1)}, u32[]{:S(2)}, u32[]{:S(2)}) collective-permute-start(bf16[376,128]{1,0:T(8,128)(2,1)S(1)} %get-tuple-element.39), channel_id=1, source_target_pairs={{0,16},{2,18},{4,20},{6,22},{8,24},{10,26},{12,28},{14,30},{16,0},... | collective-permute-start | bytes 288776 | tf_op jit(solution)/shard_map/ppermute | solution.py:692
  27.3 0.1 copy.18
  27.5 0.2 weight_pack.1
  27.6 0.4 %collective-permute-done.5.refs_3_ = bf16[376,128]{1,0:T(8,128)(2,1)S(1)} collective-permute-done((bf16[376,128]{1,0:T(8,128)(2,1)S(1)}, bf16[376,128]{1,0:T(8,128)(2,1)S(1)}, u32[]{:S(2)}, u32[]{:S(2)}) %collective-permute-start.5) | collective-permute-done | bytes 96288 | tf_op jit(solution)/shard_map/ppermute | solution.py:692
  28.1 0.1 core_pack.2
  28.2 0.1 collective-permute-start.9
  28.2 3.7 %collective-permute-done.7.refs_1_.refs_5_ = bf16[376,128]{1,0:T(8,128)(2,1)S(1)} collective-permute-done((bf16[376,128]{1,0:T(8,128)(2,1)S(1)}, bf16[376,128]{1,0:T(8,128)(2,1)S(1)}, u32[]{:S(2)}, u32[]{:S(2)}) %collective-permute-start.7) | collective-permute-done | bytes 96288 | tf_op jit(solution)/shard_map/ppermute | solution.py:692
  31.9 1.1 %collective-permute-done.8.refs_2_.refs_6_ = bf16[376,128]{1,0:T(8,128)(2,1)S(1)} collective-permute-done((bf16[376,128]{1,0:T(8,128)(2,1)S(1)}, bf16[376,128]{1,0:T(8,128)(2,1)S(1)}, u32[]{:S(2)}, u32[]{:S(2)}) %collective-permute-start.8) | collective-permute-done | bytes 96288 | tf_op jit(solution)/shard_map/ppermute | solution.py:692
  33.0 0.1 core_pack.3
  33.1 0.1 collective-permute-start.10
  33.2 1.5 %collective-permute-done.10.refs_9_ = bf16[4,224,128]{2,1,0:T(8,128)(2,1)S(1)} collective-permute-done((bf16[4,224,128]{2,1,0:T(8,128)(2,1)S(1)}, bf16[4,224,128]{2,1,0:T(8,128)(2,1)S(1)}, u32[]{:S(2)}, u32[]{:S(2)}) %collective-permute-start.10) | collective-permute-done | bytes 229408 | tf_op jit(solution)/shard_map/ppermute | solution.py:708
  34.6 5.2 %stack.9 = f32[16,128]{1,0:T(8,128)} custom-call(bf16[376,128]{1,0:T(8,128)(2,1)S(1)} %collective-permute-done.2.refs_0_, bf16[376,128]{1,0:T(8,128)(2,1)S(1)} %collective-permute-done.3.refs_1_, bf16[376,128]{1,0:T(8,128)(2,1)S(1)} %collective-permute-done.4.refs_2_, bf16[376,128]{1,0:T(8,128)(2,1)S(1)} %collective-permute-done.5.refs_3_, ...), custom_call_target="tpu_custom_call" | custom-call | tf_op jit(solution)/shard_map/stack/pallas_call | solution.py:574
  (26 shorter events, 0.1 us)
Async XLA Ops:
  0.0 17.8 %copy-start.7 = (s32[5504]{0:T(1024)S(1)}, s32[5504]{0:T(1024)}, u32[]{:S(2)}) copy-start(s32[5504]{0:T(1024)} %constant.47.clone) | copy-start | bytes 66052
  0.0 12.1 %copy-start.1 = (bf16[9,256,128]{2,1,0:T(8,128)(2,1)S(1)}, bf16[9,256,128]{2,1,0:T(8,128)(2,1)}, u32[]{:S(2)}) copy-start(bf16[9,256,128]{2,1,0:T(8,128)(2,1)} %maps_ref.3) | copy-start | bytes 1769476
  1.1 11.0 %collective-permute-start = (bf16[1152,128]{1,0:T(8,128)(2,1)S(1)}, bf16[1152,128]{1,0:T(8,128)(2,1)S(1)}, u32[]{:S(2)}, u32[]{:S(2)}) collective-permute-start(bf16[1152,128]{1,0:T(8,128)(2,1)S(1)} %bitcast.14), channel_id=1, source_target_pairs={{0,1},{1,0},{2,3},{3,2},{4,5},{5,4},{6,7},{7,6},{8,9},{9,8},{10,11... | collective-permute-start | bytes 884744 | tf_op jit(solution)/shard_map/ppermute | solution.py:611
  4.1 1.1 %copy-start = (bf16[9,256,128]{2,1,0:T(8,128)(2,1)S(1)}, bf16[9,256,128]{2,1,0:T(8,128)(2,1)}, u32[]{:S(2)}) copy-start(bf16[9,256,128]{2,1,0:T(8,128)(2,1)} %maps_ref.3) | copy-start | bytes 1769476
  5.2 12.6 %copy-start.8 = (s32[5504]{0:T(1024)S(1)}, s32[5504]{0:T(1024)}, u32[]{:S(2)}) copy-start(s32[5504]{0:T(1024)} %constant.48.clone) | copy-start | bytes 66052
  5.6 21.7 %copy-start.9 = (f32[2,2,64]{2,1,0:T(2,128)S(1)}, f32[2,2,64]{2,1,0:T(2,128)}, u32[]{:S(2)}) copy-start(f32[2,2,64]{2,1,0:T(2,128)} %param.15) | copy-start | bytes 3076
  5.6 21.7 %copy-start.10 = (f32[64]{0:T(128)S(1)}, f32[64]{0:T(128)}, u32[]{:S(2)}) copy-start(f32[64]{0:T(128)} %param.16) | copy-start | bytes 772
  5.6 21.7 %copy-start.11 = (f32[64]{0:T(128)S(1)}, f32[64]{0:T(128)}, u32[]{:S(2)}) copy-start(f32[64]{0:T(128)} %param.13) | copy-start | bytes 772
  5.7 21.8 %copy-start.2 = (bf16[2,2,64,64,3,3]{3,2,5,4,1,0:T(8,128)(2,1)S(1)}, bf16[2,2,64,64,3,3]{3,2,5,4,1,0:T(8,128)(2,1)}, u32[]{:S(2)}) copy-start(bf16[2,2,64,64,3,3]{3,2,5,4,1,0:T(8,128)(2,1)} %param.14) | copy-start | bytes 884740
  5.7 21.8 %copy-start.4 = (bf16[144,144]{1,0:T(8,128)(2,1)S(1)}, bf16[144,144]{1,0:T(8,128)(2,1)}, u32[]{:S(2)}) copy-start(bf16[144,144]{1,0:T(8,128)(2,1)} %constant.45.clone.set_ref) | copy-start | bytes 124420
  5.7 21.8 %copy-start.5 = (bf16[144,160]{1,0:T(8,128)(2,1)S(1)}, bf16[144,160]{1,0:T(8,128)(2,1)}, u32[]{:S(2)}) copy-start(bf16[144,160]{1,0:T(8,128)(2,1)} %constant.46.clone.slot_ref) | copy-start | bytes 138244
  5.7 21.8 %copy-start.6 = (bf16[64,144]{1,0:T(8,128)(2,1)S(1)}, bf16[64,144]{1,0:T(8,128)(2,1)}, u32[]{:S(2)}) copy-start(bf16[64,144]{1,0:T(8,128)(2,1)} %proj_ref.1) | copy-start | bytes 55300
  5.7 6.4 %collective-permute-start.1 = (bf16[176,128]{1,0:T(8,128)(2,1)S(1)}, bf16[176,128]{1,0:T(8,128)(2,1)S(1)}, u32[]{:S(2)}, u32[]{:S(2)}) collective-permute-start(bf16[176,128]{1,0:T(8,128)(2,1)S(1)} %bitcast.13), channel_id=1, source_target_pairs={{0,1},{1,0},{2,3},{3,2},{4,5},{5,4},{6,7},{7,6},{8,9},{9,8},{10,11... | collective-permute-start | bytes 135176 | tf_op jit(solution)/shard_map/ppermute | solution.py:611
  12.7 9.0 %collective-permute-start.2 = (bf16[376,128]{1,0:T(8,128)(2,1)S(1)}, bf16[376,128]{1,0:T(8,128)(2,1)S(1)}, u32[]{:S(2)}, u32[]{:S(2)}) collective-permute-start(bf16[376,128]{1,0:T(8,128)(2,1)S(1)} %get-tuple-element.31), channel_id=1, source_target_pairs={{0,28},{2,30},{4,24},{6,26},{8,20},{10,22},{12,16},{14,18},{16,12}... | collective-permute-start | bytes 288776 | tf_op jit(solution)/shard_map/ppermute | solution.py:692
  17.5 7.8 %collective-permute-start.3 = (bf16[376,128]{1,0:T(8,128)(2,1)S(1)}, bf16[376,128]{1,0:T(8,128)(2,1)S(1)}, u32[]{:S(2)}, u32[]{:S(2)}) collective-permute-start(bf16[376,128]{1,0:T(8,128)(2,1)S(1)} %get-tuple-element.32), channel_id=1, source_target_pairs={{0,24},{2,26},{4,28},{6,30},{8,16},{10,18},{12,20},{14,22},{16,8},... | collective-permute-start | bytes 288776 | tf_op jit(solution)/shard_map/ppermute | solution.py:692
  18.1 16.5 %copy-start.3 = (bf16[1,128,384]{2,1,0:T(8,128)(2,1)S(1)}, bf16[1,128,384]{2,1,0:T(8,128)(2,1)}, u32[]{:S(2)}) copy-start(bf16[1,128,384]{2,1,0:T(8,128)(2,1)} %constant.49.clone.refs_15_) | copy-start | bytes 294916
  18.1 9.5 %collective-permute-start.4 = (bf16[376,128]{1,0:T(8,128)(2,1)S(1)}, bf16[376,128]{1,0:T(8,128)(2,1)S(1)}, u32[]{:S(2)}, u32[]{:S(2)}) collective-permute-start(bf16[376,128]{1,0:T(8,128)(2,1)S(1)} %get-tuple-element.35), channel_id=1, source_target_pairs={{0,12},{2,14},{4,8},{6,10},{8,4},{10,6},{12,0},{14,2},{16,28},{18,... | collective-permute-start | bytes 288776 | tf_op jit(solution)/shard_map/ppermute | solution.py:692
  18.2 9.9 %collective-permute-start.5 = (bf16[376,128]{1,0:T(8,128)(2,1)S(1)}, bf16[376,128]{1,0:T(8,128)(2,1)S(1)}, u32[]{:S(2)}, u32[]{:S(2)}) collective-permute-start(bf16[376,128]{1,0:T(8,128)(2,1)S(1)} %get-tuple-element.36), channel_id=1, source_target_pairs={{0,8},{2,10},{4,12},{6,14},{8,0},{10,2},{12,4},{14,6},{16,24},{18,... | collective-permute-start | bytes 288776 | tf_op jit(solution)/shard_map/ppermute | solution.py:692
  20.1 8.2 %collective-permute-start.6 = (bf16[376,128]{1,0:T(8,128)(2,1)S(1)}, bf16[376,128]{1,0:T(8,128)(2,1)S(1)}, u32[]{:S(2)}, u32[]{:S(2)}) collective-permute-start(bf16[376,128]{1,0:T(8,128)(2,1)S(1)} %get-tuple-element.37), channel_id=1, source_target_pairs={{0,4},{2,6},{4,0},{6,2},{8,12},{10,14},{12,8},{14,10},{16,20},{18,... | collective-permute-start | bytes 288776 | tf_op jit(solution)/shard_map/ppermute | solution.py:692
  21.7 10.3 %collective-permute-start.7 = (bf16[376,128]{1,0:T(8,128)(2,1)S(1)}, bf16[376,128]{1,0:T(8,128)(2,1)S(1)}, u32[]{:S(2)}, u32[]{:S(2)}) collective-permute-start(bf16[376,128]{1,0:T(8,128)(2,1)S(1)} %get-tuple-element.38), channel_id=1, source_target_pairs={{0,20},{2,22},{4,16},{6,18},{8,28},{10,30},{12,24},{14,26},{16,4},... | collective-permute-start | bytes 288776 | tf_op jit(solution)/shard_map/ppermute | solution.py:692
  25.3 7.7 %collective-permute-start.8 = (bf16[376,128]{1,0:T(8,128)(2,1)S(1)}, bf16[376,128]{1,0:T(8,128)(2,1)S(1)}, u32[]{:S(2)}, u32[]{:S(2)}) collective-permute-start(bf16[376,128]{1,0:T(8,128)(2,1)S(1)} %get-tuple-element.39), channel_id=1, source_target_pairs={{0,16},{2,18},{4,20},{6,22},{8,24},{10,26},{12,28},{14,30},{16,0},... | collective-permute-start | bytes 288776 | tf_op jit(solution)/shard_map/ppermute | solution.py:692
  28.2 5.0 %collective-permute-start.9 = (bf16[4,224,128]{2,1,0:T(8,128)(2,1)S(1)}, bf16[4,224,128]{2,1,0:T(8,128)(2,1)S(1)}, u32[]{:S(2)}, u32[]{:S(2)}) collective-permute-start(bf16[4,224,128]{2,1,0:T(8,128)(2,1)S(1)} %core_pack.2), channel_id=1, source_target_pairs={{0,2},{2,0},{4,6},{6,4},{8,10},{10,8},{12,14},{14,12},{16,18},{18,... | collective-permute-start | bytes 688136 | tf_op jit(solution)/shard_map/ppermute | solution.py:708
  33.1 1.6 %collective-permute-start.10 = (bf16[4,224,128]{2,1,0:T(8,128)(2,1)S(1)}, bf16[4,224,128]{2,1,0:T(8,128)(2,1)S(1)}, u32[]{:S(2)}, u32[]{:S(2)}) collective-permute-start(bf16[4,224,128]{2,1,0:T(8,128)(2,1)S(1)} %core_pack.3), channel_id=1, source_target_pairs={{0,2},{2,0},{4,6},{6,4},{8,10},{10,8},{12,14},{14,12},{16,18},{18,... | collective-permute-start | bytes 688136 | tf_op jit(solution)/shard_map/ppermute | solution.py:708
